TPU v7x, 32 devices: a whole 2x2x4 slice. The times are simulated.
32 devices in a mesh: var: 8 (over z, y), samp: 4 (over x, core).
Axes of the slice: x: 2, y: 2, z: 4, core: 2. Of those that a mesh axis runs over, the one named last changes fastest.
Arguments:
- dosage: bfloat16 [16384, 4096], P('samp', 'var'), may hold values from 0 to 2
- pair_offsets: int32 [8, 3], P('var'), may hold values from -1 to 2, as said below
- live_counts: int32 [8], P('var'), may hold values from 256 to 512, as said below
Outputs:
- ld_upper: bfloat16 [8, 3, 512, 512], P('var', None, 'samp')
- ld_mirror: bfloat16 [8, 2, 512, 512], P('var', None, 'samp')
Inputs may be any that keep to these rules, and one draw needn't show every extreme that they name: `pair_offsets`: row i lists distinct offsets in increasing order, first always 0, each with i + offset < 8; unused slots at the end hold -1. The first live_counts[i] variants of block i are real, the rest of the block is padding and is left out.
All inputs are finite; a program needn't handle non-finite values.
Results may differ from a plain program's by a relative error of at most 0.0034.
Values may be sent and summed in bfloat16 or wider, within the bound.
No kernel may reach another device: no remote copies, remote signals or barrier semaphores. Data moves between devices by JAX's collectives and lax.ppermute only.
A program may use at most 320 MiB of HBM per device.

v0:
```python
import jax
import jax.numpy as jnp
from jax import lax
from jax.sharding import PartitionSpec as P

BAND = 2
SLOTS = 3


def passed_along(value, axis, steps):
    count = lax.axis_size(axis)
    first, last = (max(0, -steps), min(count, count - steps))
    return lax.ppermute(value, axis, [(source, source + steps) for source in range(first, last)])


def body(dosage, pair_offsets, live_counts):
    samples_all = dosage.shape[0] * lax.axis_size("samp")
    width = dosage.shape[1]
    values = dosage.astype(jnp.float32)
    totals = lax.psum(jnp.sum(values, axis=0), "samp")
    mean = totals / samples_all
    centered = values - mean
    spread = lax.psum(jnp.sum(centered * centered, axis=0), "samp") / samples_all
    position = jnp.arange(width, dtype=jnp.int32)
    live = position < live_counts[0]
    std_dose = jnp.where(live, centered * lax.rsqrt(spread + 1e-05), 0.0).astype(jnp.bfloat16)
    fetched = [std_dose]
    for step in range(1, BAND + 1):
        fetched.append(passed_along(std_dose, "var", -step))
    stacked = jnp.stack(fetched)
    scale_inv = 1.0 / samples_all

    def make_tile(offset):
        partner = lax.dynamic_index_in_dim(stacked, jnp.maximum(offset, 0), 0, keepdims=False)
        product = lax.dot_general(
            std_dose, partner, (((0,), (0,)), ((), ())), preferred_element_type=jnp.float32
        )
        return product * scale_inv

    def empty_tile(offset):
        return jnp.zeros((width, width), jnp.float32)

    tiles = []
    for slot in range(SLOTS):
        offset = pair_offsets[0, slot]
        tiles.append(lax.cond(offset >= 0, make_tile, empty_tile, offset))

    def pick(source, step):
        picked = jnp.zeros(source.shape[1:], jnp.bfloat16)
        for slot in range(SLOTS):
            picked = jnp.where(pair_offsets[0, slot] == step, source[slot], picked)
        return picked

    both = jnp.stack([jnp.stack([tile, tile.T]) for tile in tiles])
    shared = lax.psum_scatter(both, "samp", scatter_dimension=2, tiled=True)
    ld_upper = shared[:, 0].astype(jnp.bfloat16)
    turned = shared[:, 1].astype(jnp.bfloat16)
    flipped = [pick(turned, step) for step in range(1, BAND + 1)]
    mirrors = []
    for step in range(1, BAND + 1):
        mirrors.append(passed_along(flipped[step - 1], "var", step))
    ld_mirror = jnp.stack(mirrors)
    return (ld_upper[None], ld_mirror[None])


def solution(mesh):
    in_specs = (P("samp", "var"), P("var", None), P("var"))
    out_specs = (P("var", None, "samp", None), P("var", None, "samp", None))
    return jax.shard_map(body, mesh=mesh, in_specs=in_specs, out_specs=out_specs, check_vma=False)
```

profile of v0, /device:TPU:0, one launch (start us, length us, event | category | flops | bytes accessed | tf_op | source)
XLA Modules:
  0.0 338.5 jit_solution(5814475762643090175)
XLA Ops:
  7.2 0.0 reduce-scatter.2.cloned.1.call-start
  7.2 2.8 convert_reduce_fusion
  10.0 8.3 %psum.14 = f32[512]{0:T(512)S(1)} all-reduce(f32[512]{0:T(512)S(1)} %convert_reduce_fusion), channel_id=1, replica_groups=mesh['var'=8,'samp'=4] {'samp'}, use_global_device_ids=true, to_apply=%region_1.0 | all-reduce | flops 512 | bytes 4096 | tf_op jit(solution)/shard_map/psum | solution.py:20
  18.4 3.3 fusion.23
  21.7 5.8 %psum.15 = f32[512]{0:T(512)S(1)} all-reduce(f32[512]{0:T(512)S(1)} %fusion.23), channel_id=1, replica_groups=mesh['var'=8,'samp'=4] {'samp'}, use_global_device_ids=true, to_apply=%region_3.0 | all-reduce | flops 512 | bytes 4096 | tf_op jit(solution)/shard_map/psum | solution.py:23
  28.1 0.0 copy-start
  28.1 5.4 %fusion.25 = bf16[4096,512]{1,0:T(8,128)(2,1)} fusion(bf16[4096,512]{1,0:T(8,128)(2,1)} %param.9, f32[512]{0:T(512)S(1)} %add_rsqrt_fusion, f32[512]{0:T(512)S(1)} %broadcast_multiply_fusion, pred[512]{0:T(512)(128)(4,1)S(1)} %iota_compare_fusion), kind=kLoop, calls=%fused_computation.22 | loop fusion | flops 10485760 | bytes 8393216 | tf_op jit(solution)/shard_map/convert_element_type | solution.py:26
  33.5 1.3 collective-permute-start
  34.8 1.3 collective-permute-start.1
  36.1 0.0 copy-done
  36.1 0.6 fusion.26
  38.6 3.5 %fusion.30 = bf16[1,4096,512]{2,1,0:T(8,128)(2,1)S(1)} fusion(f32[512]{0:T(512)S(1)} %add_rsqrt_fusion, f32[512]{0:T(512)S(1)} %broadcast_multiply_fusion, bf16[4096,512]{1,0:T(8,128)(2,1)} %param.9, pred[512]{0:T(512)(128)(4,1)S(1)} %iota_compare_fusion), kind=kLoop, calls=%fused_computation.35 | loop fusion | flops 10485760 | bytes 8393216 | tf_op jit(solution)/shard_map/stack | solution.py:30
  42.1 85.9 %collective-permute-done = bf16[4096,512]{1,0:T(8,128)(2,1)} collective-permute-done((bf16[4096,512]{1,0:T(8,128)(2,1)}, bf16[4096,512]{1,0:T(8,128)(2,1)}, u32[]{:S(2)}, u32[]{:S(2)}) %collective-permute-start) | collective-permute-done | bytes 4194336 | tf_op jit(solution)/shard_map/ppermute | solution.py:13
  128.0 90.8 %collective-permute-done.1 = bf16[4096,512]{1,0:T(8,128)(2,1)} collective-permute-done((bf16[4096,512]{1,0:T(8,128)(2,1)}, bf16[4096,512]{1,0:T(8,128)(2,1)}, u32[]{:S(2)}, u32[]{:S(2)}) %collective-permute-start.1) | collective-permute-done | bytes 4194336 | tf_op jit(solution)/shard_map/ppermute | solution.py:13
  218.8 9.3 %pad_maximum_fusion = bf16[3,4096,512]{2,1,0:T(8,128)(2,1)} fusion(bf16[1,4096,512]{2,1,0:T(8,128)(2,1)} %bitcast.13, bf16[1,4096,512]{2,1,0:T(8,128)(2,1)} %bitcast.12, bf16[1,4096,512]{2,1,0:T(8,128)(2,1)S(1)} %fusion.30), kind=kLoop, calls=%fused_computation.15 | loop fusion | flops 12582912 | bytes 25165824 | tf_op jit(solution)/shard_map/stack | solution.py:30
  228.1 9.0 %conditional.5 = (f32[512,512]{0,1:T(8,128)}, f32[1,512,512]{2,1,0:T(8,128)S(1)}) conditional(s32[]{:T(128)} %convert_element_type.32, () %tuple.42, (s32[]{:T(128)}, bf16[3,4096,512]{2,1,0:T(8,128)(2,1)}, bf16[4096,512]{1,0:T(8,128)(2,1)}) %tuple.43), branch_computations={%region_8.9_spmd, %region_9.10_spmd} | conditional | flops 2147745792 | bytes 11534368 | solution.py:46
  228.7 6.8 %fusion.17 = f32[512,512]{1,0:T(8,128)} fusion(bf16[4096,512]{1,0:T(8,128)(2,1)} %get-tuple-element.32, bf16[3,4096,512]{2,1,0:T(8,128)(2,1)} %get-tuple-element.30, s32[]{:T(128)S(6)} %max.8), kind=kOutput, calls=%fused_computation.13 | convolution fusion | flops 2147745792 | bytes 9437188 | tf_op jit(solution)/shard_map/cond/branch_1_fun/dot_general | solution.py:35
  235.5 1.6 copy.13
  237.1 1.4 maximum_bitcast_fusion.2
  238.5 9.0 %conditional.4 = (f32[512,512]{0,1:T(8,128)}, f32[1,512,512]{2,1,0:T(8,128)S(1)}) conditional(s32[]{:T(128)} %convert_element_type.31, () %tuple.40, (s32[]{:T(128)}, bf16[3,4096,512]{2,1,0:T(8,128)(2,1)}, bf16[4096,512]{1,0:T(8,128)(2,1)}) %tuple.41), branch_computations={%region_6.7_spmd, %region_7.8_spmd} | conditional | flops 2147745792 | bytes 11534368 | solution.py:46
  239.1 6.8 %fusion.10 = f32[512,512]{1,0:T(8,128)} fusion(bf16[4096,512]{1,0:T(8,128)(2,1)} %get-tuple-element.29, bf16[3,4096,512]{2,1,0:T(8,128)(2,1)} %get-tuple-element.27, s32[]{:T(128)S(6)} %max.7), kind=kOutput, calls=%fused_computation.8 | convolution fusion | flops 2147745792 | bytes 9437188 | tf_op jit(solution)/shard_map/cond/branch_1_fun/dot_general | solution.py:35
  245.9 1.6 copy.11
  247.5 10.0 %conditional.3 = (f32[512,512]{0,1:T(8,128)}, f32[1,512,512]{2,1,0:T(8,128)}) conditional(s32[]{:T(128)} %convert_element_type.28, () %tuple.38, (s32[]{:T(128)}, bf16[3,4096,512]{2,1,0:T(8,128)(2,1)}, bf16[4096,512]{1,0:T(8,128)(2,1)}) %tuple.39), branch_computations={%region_4.5_spmd, %region_5.6_spmd} | conditional | flops 2147745792 | bytes 11534368 | solution.py:46
  248.2 6.8 %fusion.3 = f32[512,512]{1,0:T(8,128)} fusion(bf16[4096,512]{1,0:T(8,128)(2,1)} %get-tuple-element.26, bf16[3,4096,512]{2,1,0:T(8,128)(2,1)} %get-tuple-element.24, s32[]{:T(128)S(6)} %max.6), kind=kOutput, calls=%fused_computation.3 | convolution fusion | flops 2147745792 | bytes 9437188 | tf_op jit(solution)/shard_map/cond/branch_1_fun/dot_general | solution.py:35
  255.0 2.6 copy.9
  257.5 2.3 maximum_bitcast_fusion
  259.8 3.4 pad_maximum_fusion.1
  263.2 0.0 reduce-scatter.2.cloned.1.call-update
  267.0 53.1 %reduce-scatter.2.cloned.1.call-done = f32[3,2,128,512]{3,2,1,0:T(8,128)} async-done(((f32[3,2,512,512]{3,2,1,0:T(8,128)}), f32[3,2,128,512]{3,2,1,0:T(8,128)}) %reduce-scatter.2.cloned.1.call-update) | async-done | bytes 1572880 | tf_op jit(solution)/shard_map/reduce_scatter | solution.py:55
  320.1 1.5 convert.4
  321.6 3.4 %collective-permute-start.2 = (bf16[128,512]{1,0:T(8,128)(2,1)S(1)}, bf16[128,512]{1,0:T(8,128)(2,1)S(1)}, u32[]{:S(2)}, u32[]{:S(2)}) collective-permute-start(bf16[128,512]{1,0:T(8,128)(2,1)S(1)} %get-tuple-element.50), channel_id=1, source_target_pairs={{0,4},{4,8},{8,12},{12,16},{16,20},{20,24},{24,28},{1,5},{5,9},{9,... | collective-permute-start | bytes 393224 | tf_op jit(solution)/shard_map/ppermute | solution.py:13
  325.0 3.4 collective-permute-start.3
  328.4 0.8 slice_bitcast_fusion
  329.2 0.0 collective-permute-done.2
  329.2 1.7 collective-permute-done.3
  330.9 0.7 maximum_bitcast_fusion.3
  (4 shorter events, 0.1 us)
Async XLA Ops:
  7.2 312.9 %reduce-scatter.2.cloned.1.call-start = ((), (), s32[]{:S(2)}) async-start(), calls=%async_computation.1 | async-start | bytes 7864320 | tf_op jit(solution)/shard_map/reduce_scatter | solution.py:55
  28.1 8.0 %copy-start = (s32[1,3]{1,0:T(1,128)S(1)}, s32[1,3]{1,0:T(1,128)}, u32[]{:S(2)}) copy-start(s32[1,3]{1,0:T(1,128)} %param.10) | copy-start | bytes 40
  33.5 94.4 %collective-permute-start = (bf16[4096,512]{1,0:T(8,128)(2,1)}, bf16[4096,512]{1,0:T(8,128)(2,1)}, u32[]{:S(2)}, u32[]{:S(2)}) collective-permute-start(bf16[4096,512]{1,0:T(8,128)(2,1)} %fusion.25), channel_id=1, source_target_pairs={{4,0},{8,4},{12,8},{16,12},{20,16},{24,20},{28,24},{5,1},{9,5},{13... | collective-permute-start | bytes 12582920 | tf_op jit(solution)/shard_map/ppermute | solution.py:13
  34.8 184.0 %collective-permute-start.1 = (bf16[4096,512]{1,0:T(8,128)(2,1)}, bf16[4096,512]{1,0:T(8,128)(2,1)}, u32[]{:S(2)}, u32[]{:S(2)}) collective-permute-start(bf16[4096,512]{1,0:T(8,128)(2,1)} %fusion.25), channel_id=1, source_target_pairs={{8,0},{12,4},{16,8},{20,12},{24,16},{28,20},{9,1},{13,5},{17,9},{2... | collective-permute-start | bytes 12582920 | tf_op jit(solution)/shard_map/ppermute | solution.py:13
  321.6 7.6 %collective-permute-start.2 = (bf16[128,512]{1,0:T(8,128)(2,1)S(1)}, bf16[128,512]{1,0:T(8,128)(2,1)S(1)}, u32[]{:S(2)}, u32[]{:S(2)}) collective-permute-start(bf16[128,512]{1,0:T(8,128)(2,1)S(1)} %get-tuple-element.50), channel_id=1, source_target_pairs={{0,4},{4,8},{8,12},{12,16},{16,20},{20,24},{24,28},{1,5},{5,9},{9,... | collective-permute-start | bytes 393224 | tf_op jit(solution)/shard_map/ppermute | solution.py:13
  325.0 5.9 %collective-permute-start.3 = (bf16[128,512]{1,0:T(8,128)(2,1)S(1)}, bf16[128,512]{1,0:T(8,128)(2,1)S(1)}, u32[]{:S(2)}, u32[]{:S(2)}) collective-permute-start(bf16[128,512]{1,0:T(8,128)(2,1)S(1)} %get-tuple-element.51), channel_id=1, source_target_pairs={{0,8},{4,12},{8,16},{12,20},{16,24},{20,28},{1,9},{5,13},{9,17},{1... | collective-permute-start | bytes 393224 | tf_op jit(solution)/shard_map/ppermute | solution.py:13
Sparse Core Ops, SparseCore 0:
  263.3 56.6 reduce-scatter.1
where the time goes:
time: 339 us; the launch traced here: 338 us
  waiting for transfers between devices  232 us (68%)
  other arithmetic  33.6 us (10%)
  matrix products  20.4 us (6%)
  between operations  20.4 us (6%)
  blocking collectives  14.1 us (4%)
  starting transfers between devices  9.37 us (3%)
  local copies, waits for them, and re-layouts  7.06 us (2%)
    ppermute x4, waiting for transfers between devices, passed_along(): lax.ppermute(value, axis, [(source, source + steps) for source in range(f...  178 us
    reduce_scatter x1, waiting for transfers between devices, body(): shared = lax.psum_scatter(both, 'samp', scatter_dimension=2, tiled=True)  53.1 us
    dot_general x3, matrix products, make_tile(): lax.dot_general(std_dose, partner, (((0,), (0,)), ((), ())), preferred_el...  20.4 us
    another operation x2, other arithmetic, body(): stacked = jnp.stack(fetched)  12.7 us
    ppermute x4, starting transfers between devices, passed_along(): lax.ppermute(value, axis, [(source, source + steps) for source in range(f...  9.34 us
    psum x1, blocking collectives, body(): totals = lax.psum(jnp.sum(values, axis=0), 'samp')  8.33 us
    another operation x3, other arithmetic, body(): both = jnp.stack([jnp.stack([tile, tile.T]) for tile in tiles])  7.05 us
  transfers between devices with their start and end apart: 5, of which 4 were waited for; matrix products, arithmetic and copies ran while one was open for 1% of the time, Pallas kernels for 0%

commit v1 on v0

v1 whole, which is shorter than its diff:
```python
import functools

import jax
import jax.numpy as jnp
from jax import lax
from jax.experimental import pallas as pl
from jax.experimental.pallas import tpu as pltpu
from jax.sharding import PartitionSpec as P

SLOTS = 3
AXES = ("var", "samp")
F32 = jnp.float32
BF16 = jnp.bfloat16
VMEM = pl.BlockSpec(memory_space=pltpu.VMEM)
SMEM = pl.BlockSpec(memory_space=pltpu.SMEM)


def dot(a, b):
    return jnp.dot(a, b, preferred_element_type=F32)


def standardized(raw, mean, inv):
    return ((raw.astype(F32) - mean) * inv).astype(BF16)


def own_kernel(x_ref, stat_ref, turned_ref, tile_ref, acc):
    step = pl.program_id(0)
    z = standardized(x_ref[...], stat_ref[0:1, :], stat_ref[1:2, :])
    zt = z.T
    turned_ref[...] = zt
    part = dot(zt, z)

    @pl.when(step == 0)
    def _():
        acc[...] = part

    @pl.when(step > 0)
    def _():
        acc[...] += part

    @pl.when(step == pl.num_programs(0) - 1)
    def _():
        tile_ref[...] = acc[...]


def pair_kernel(pos_ref, scale_ref, turned_ref, y_ref, w_ref, ystat_ref, wstat_ref,
                keep_c, send_c, keep_bd, send_bd, acc):
    step = pl.program_id(0)
    last = pl.num_programs(0) - 1
    active = pos_ref[1]
    half = acc.shape[1] // 2

    @pl.when(step == 0)
    def _():
        acc[...] = jnp.zeros_like(acc)

    zt = turned_ref[...]
    w = standardized(w_ref[...], wstat_ref[0:1, :], wstat_ref[1:2, :])
    acc[1] += dot(zt, w)

    @pl.when(active == 1)
    def _():
        y = standardized(y_ref[...], ystat_ref[0:1, :], ystat_ref[1:2, :])
        acc[0] += dot(zt, y)
        acc[2] += dot(y.T, w)

    @pl.when(step == last)
    def _():
        here = pl.multiple_of(pos_ref[0] * half, half)
        there = pl.multiple_of((1 - pos_ref[0]) * half, half)

        def quarters(tile, keep, send):
            scale = scale_ref[tile]
            ours = ((here, here), (here, there), (there, here))
            theirs = ((there, there), (there, here), (here, there))
            for index in range(3):
                for (row, col), out in ((ours[index], keep), (theirs[index], send)):
                    out[index] = acc[tile, pl.ds(row, half), pl.ds(col, half)] * scale

        quarters(1, keep_c.at[0], send_c.at[0])

        @pl.when(active == 1)
        def _():
            quarters(0, keep_bd.at[0], send_bd.at[0])
            quarters(2, keep_bd.at[1], send_bd.at[1])


def strips_kernel(pos_ref, keep_c, got_c, keep_bd, got_bd, own, sib, y_same, y_cross, z_same, z_cross, turn):
    half = keep_c.shape[-1]
    rows = half // 2
    here = pl.multiple_of(pos_ref[0] * half, half)
    there = pl.multiple_of((1 - pos_ref[0]) * half, half)
    mine = pl.multiple_of(pos_ref[2] * rows, rows)
    other = pl.multiple_of((1 - pos_ref[2]) * rows, rows)

    def cut(keep, got, row_out, col_out):
        turn[0, :, pl.ds(here, half)] = keep[0] + got[0]
        turn[0, :, pl.ds(there, half)] = keep[1] + got[1]
        turn[1, :, pl.ds(here, half)] = (keep[0] + got[0]).T
        turn[1, :, pl.ds(there, half)] = (keep[2] + got[2]).T
        for which, outs in ((0, row_out), (1, col_out)):
            for start, out in zip((mine, other), outs):
                out[...] = turn[which, pl.ds(start, rows), :]

    cut(keep_c.at[0], got_c.at[0], (own.at[1], sib.at[1]), (z_same.at[0], z_cross.at[0]))

    @pl.when(pos_ref[1] == 1)
    def _():
        cut(keep_bd.at[0], got_bd.at[0], (own.at[0], sib.at[0]), (y_same.at[0], y_cross.at[0]))
        cut(keep_bd.at[1], got_bd.at[1], (y_same.at[1], y_cross.at[1]), (z_same.at[1], z_cross.at[1]))


def finish_kernel(pos_ref, offsets_ref, diag, own, sib, y_a, y_b, z_same, z_cross, upper, mirror):
    active = pos_ref[1] == 1
    first_core = pos_ref[2] == 0
    even = pos_ref[3] == 0
    count_inv = pos_ref[4]

    def pick(cond, a, b):
        return jnp.where(cond, a, b)

    side = pick(active, y_b[0], y_a[0])
    side_d = pick(active, y_b[1], y_a[1])
    below_c = pick(first_core, z_same[0], z_cross[0])
    above_c = pick(first_core, z_cross[0], z_same[0])
    near_d = pick(first_core == even, z_same[1], z_cross[1])
    held = pick(active, own[0], sib[0]) + side
    far = side_d + near_d
    upper_1 = pick(even, held, far)
    mirror_1 = pick(even, far, held)
    upper_2 = pick(first_core, own[1], sib[1]) + above_c
    mirror_2 = pick(first_core, sib[1], own[1]) + below_c
    mirror[0, 0] = mirror_1.astype(BF16)
    mirror[0, 1] = mirror_2.astype(BF16)
    self_tile = diag[...] * (1.0 / count_inv.astype(F32))
    for slot in range(SLOTS):
        offset = offsets_ref[0, slot]
        tile = pick(offset == 0, self_tile, pick(offset == 1, upper_1, pick(offset == 2, upper_2, 0.0)))
        upper[0, slot] = tile.astype(BF16)


def body(dosage, pair_offsets, live_counts):
    n_var = lax.axis_size("var")
    n_samp = lax.axis_size("samp")
    depth, width = dosage.shape
    half = width // 2
    strip = width // n_samp
    samples_all = depth * n_samp
    v = lax.axis_index("var")
    s = lax.axis_index("samp")
    x, core, odd = s // 2, s % 2, v % 2
    active = (core == odd).astype(jnp.int32)

    def at(var, samp):
        return var * n_samp + samp

    def active_on(var, samp):
        return var % 2 == samp % 2

    everyone = [(var, samp) for var in range(n_var) for samp in range(n_samp)]
    z_same = [(at(a, b), at(a - 2 if b % 2 == 0 else a + 2, b)) for a, b in everyone
              if 0 <= (a - 2 if b % 2 == 0 else a + 2) < n_var]
    y_same = [(at(a, b), at(a ^ 1, b)) for a, b in everyone if not active_on(a, b)]

    def send(value, pairs):
        return lax.ppermute(value, AXES, pairs)

    w_raw = send(dosage, z_same)
    y_raw = send(dosage, y_same)

    values = dosage.astype(F32)
    mean = lax.psum(jnp.sum(values, axis=0), "samp") / samples_all
    centered = values - mean
    spread = lax.psum(jnp.sum(centered * centered, axis=0), "samp") / samples_all
    live = jnp.arange(width, dtype=jnp.int32) < live_counts[0]
    inv = jnp.where(live, lax.rsqrt(spread + 1e-05), 0.0)
    lists = [jnp.any(pair_offsets[0] == step).astype(F32) for step in (1, 2)]
    stat = jnp.stack([mean, inv] + [jnp.full((width,), flag) for flag in lists])
    w_stat = send(stat, z_same)
    y_stat = send(stat, y_same)
    first = core == 0
    scale = jnp.stack([
        jnp.where(first, lists[0], y_stat[2, 0]),
        jnp.where(first, lists[1], w_stat[3, 0]),
        jnp.where(first, y_stat[2, 0], w_stat[2, 0]),
    ]) / samples_all
    pos = jnp.stack([x, active, core, odd, jnp.int32(samples_all)]).astype(jnp.int32)

    step_rows = min(512, depth)
    steps = depth // step_rows
    turned, tile = pl.pallas_call(
        own_kernel,
        grid=(steps,),
        in_specs=[pl.BlockSpec((step_rows, width), lambda k: (k, 0)), pl.BlockSpec((4, width), lambda k: (0, 0))],
        out_specs=[pl.BlockSpec((width, step_rows), lambda k: (0, k)), pl.BlockSpec((width, width), lambda k: (0, 0))],
        out_shape=[jax.ShapeDtypeStruct((width, depth), BF16), jax.ShapeDtypeStruct((width, width), F32)],
        scratch_shapes=[pltpu.VMEM((width, width), F32)],
        compiler_params=pltpu.CompilerParams(vmem_limit_bytes=24 << 20),
        cost_estimate=pl.CostEstimate(flops=2 * depth * width * width, bytes_accessed=4 * depth * width, transcendentals=0),
        name="own_tile",
    )(dosage, stat)
    diag = lax.psum_scatter(tile, "samp", scatter_dimension=0, tiled=True)

    quarter = lambda n: jax.ShapeDtypeStruct((n, 3, half, half), F32)
    whole = lambda n: pl.BlockSpec((n, 3, half, half), lambda k: (0, 0, 0, 0))
    keep_c, send_c, keep_bd, send_bd = pl.pallas_call(
        pair_kernel,
        grid=(steps,),
        in_specs=[SMEM, SMEM, pl.BlockSpec((width, step_rows), lambda k: (0, k)),
                  pl.BlockSpec((step_rows, width), lambda k: (k, 0)), pl.BlockSpec((step_rows, width), lambda k: (k, 0)),
                  pl.BlockSpec((4, width), lambda k: (0, 0)), pl.BlockSpec((4, width), lambda k: (0, 0))],
        out_specs=[whole(1), whole(1), whole(2), whole(2)],
        out_shape=[quarter(1), quarter(1), quarter(2), quarter(2)],
        scratch_shapes=[pltpu.VMEM((3, width, width), F32)],
        compiler_params=pltpu.CompilerParams(vmem_limit_bytes=32 << 20),
        cost_estimate=pl.CostEstimate(flops=6 * depth * width * width, bytes_accessed=6 * depth * width, transcendentals=0),
        name="pair_tiles",
    )(pos, scale, turned, y_raw, w_raw, y_stat, w_stat)

    across = [(at(a, b), at(a, b ^ 2)) for a, b in everyone]
    across_active = [(at(a, b), at(a, b ^ 2)) for a, b in everyone if active_on(a, b)]
    got_c = send(send_c, across)
    got_bd = send(send_bd, across_active)

    two = jax.ShapeDtypeStruct((2, strip, width), F32)
    own, sib, to_y_same, to_y_cross, to_z_same, to_z_cross = pl.pallas_call(
        strips_kernel,
        in_specs=[SMEM] + [VMEM] * 4,
        out_specs=[VMEM] * 6,
        out_shape=[two] * 6,
        scratch_shapes=[pltpu.VMEM((2, half, width), F32)],
        compiler_params=pltpu.CompilerParams(vmem_limit_bytes=24 << 20),
        name="strips",
    )(pos, keep_c, got_c, keep_bd, got_bd)

    got_sib = send(sib, [(at(a, b), at(a, b ^ 1)) for a, b in everyone])
    got_y_same = send(to_y_same, [(at(a, b), at(a ^ 1, b)) for a, b in everyone if active_on(a, b)])
    got_y_cross = send(to_y_cross, [(at(a, b), at(a ^ 1, b ^ 1)) for a, b in everyone if active_on(a, b)])
    z_up_down = [(a, b, a + 2 if b % 2 == 0 else a - 2) for a, b in everyone]
    got_z_same = send(to_z_same, [(at(a, b), at(t, b)) for a, b, t in z_up_down if 0 <= t < n_var])
    got_z_cross = send(to_z_cross, [(at(a, b), at(t, b ^ 1)) for a, b, t in z_up_down if 0 <= t < n_var])

    return pl.pallas_call(
        finish_kernel,
        in_specs=[SMEM, SMEM] + [VMEM] * 7,
        out_specs=[VMEM, VMEM],
        out_shape=[jax.ShapeDtypeStruct((1, SLOTS, strip, width), BF16),
                   jax.ShapeDtypeStruct((1, 2, strip, width), BF16)],
        compiler_params=pltpu.CompilerParams(vmem_limit_bytes=24 << 20),
        name="finish",
    )(pos, pair_offsets, diag, own, got_sib, got_y_same, got_y_cross, got_z_same, got_z_cross)


def solution(mesh):
    in_specs = (P("samp", "var"), P("var", None), P("var"))
    out_specs = (P("var", None, "samp", None), P("var", None, "samp", None))
    return jax.shard_map(body, mesh=mesh, in_specs=in_specs, out_specs=out_specs, check_vma=False)
```

time: 339 us -> 161 us (0.47)
  waiting for transfers between devices: 232 us -> 52.4 us
  other arithmetic: 33.6 us -> 7.68 us
  Pallas kernels: 0 us -> 22.9 us
  matrix products: 20.4 us -> 0 us
  starting transfers between devices: 9.37 us -> 22.1 us
  blocking collectives: 14.1 us -> 22.2 us
  local copies, waits for them, and re-layouts: 7.06 us -> 14.3 us
    ppermute x4 -> x11, waiting for transfers between devices: 178 us -> 52.4 us  [send(): return lax.ppermute(value, AXES, pairs)]
    reduce_scatter x1, waiting for transfers between devices: 53.1 us -> 0.02 us  [body(): diag = lax.psum_scatter(tile, 'samp', scatter_dimension=0, tiled=True)]
    pallas_call x0 -> x4, Pallas kernels: none -> 22.9 us  [the longest x1 13.2 us: body(): pl.pallas_call(pair_kernel, grid=(steps,), in_specs=[SMEM, SMEM, pl.Block...]
    another operation x6 -> x1, other arithmetic: 21.3 us -> 0.08 us  [body(): stat = jnp.stack([mean, inv] + [jnp.full((width,), flag) for flag in lists])]
    dot_general x3 -> x0, matrix products: 20.4 us -> none  [make_tile(): lax.dot_general(std_dose, partner, (((0,), (0,)), ((), ())), preferred_el...]
    unnamed x2 -> x22, local copies, waits for them, and re-layouts: 0.01 us -> 13.1 us
    ppermute x4 -> x11, starting transfers between devices: 9.34 us -> 22.1 us  [send(): return lax.ppermute(value, AXES, pairs)]
    psum x1, blocking collectives: 8.33 us -> 16.1 us  [body(): mean = lax.psum(jnp.sum(values, axis=0), 'samp') / samples_all]
  transfers between devices with their start and end apart: 5 -> 12, of which waited for: 4 -> 6; matrix products, arithmetic and copies ran while one was open for 1% -> 6% of each run, Pallas kernels for 0% -> 5%
where the time goes in v1:
time: 161 us; the launch traced here: 160 us
  waiting for transfers between devices  52.4 us (33%)
  Pallas kernels  22.9 us (14%)
  blocking collectives  22.2 us (14%)
  starting transfers between devices  22.1 us (14%)
  between operations  18.7 us (12%)
  local copies, waits for them, and re-layouts  14.3 us (9%)
  other arithmetic  7.68 us (5%)
    ppermute x11, waiting for transfers between devices, send(): return lax.ppermute(value, AXES, pairs)  52.4 us
    ppermute x11, starting transfers between devices, send(): return lax.ppermute(value, AXES, pairs)  22.1 us
    psum x1, blocking collectives, body(): mean = lax.psum(jnp.sum(values, axis=0), 'samp') / samples_all  16.1 us
    pallas_call x1, Pallas kernels, body(): pl.pallas_call(pair_kernel, grid=(steps,), in_specs=[SMEM, SMEM, pl.Block...  13.2 us
    unnamed x22, local copies, waits for them, and re-layouts  13.1 us
    psum x1, blocking collectives, body(): lax.psum(jnp.sum(centered * centered, axis=0), 'samp') / samples_all  6.06 us
    pallas_call x1, Pallas kernels, body(): pl.pallas_call(own_kernel, grid=(steps,), in_specs=[pl.BlockSpec((step_ro...  4.99 us
    reduce_sum x1, other arithmetic, body(): jnp.sum(centered * centered, axis=0)  3.34 us
  transfers between devices with their start and end apart: 12, of which 6 were waited for; matrix products, arithmetic and copies ran while one was open for 6% of the time, Pallas kernels for 5%

profile of v1, /device:TPU:0, one launch (start us, length us, event | category | flops | bytes accessed | tf_op | source)
XLA Modules:
  0.0 160.3 jit_solution(11118823337752426920)
XLA Ops:
  7.2 0.0 reduce-scatter.2.cloned.1.call-start
  7.2 1.3 collective-permute-start.2
  8.5 1.3 collective-permute-start.3
  10.5 1.4 compare_reduce_fusion.1
  13.2 0.1 pad.6.clone
  13.2 0.1 pad.5.clone
  13.3 2.8 %convert_reduce_fusion = f32[512]{0:T(512)S(1)} fusion(bf16[4096,512]{1,0:T(8,128)(2,1)} %x_ref.1), kind=kLoop, calls=%fused_computation.1 | loop fusion | flops 4193792 | bytes 4196352 | tf_op jit(solution)/shard_map/reduce_sum | solution.py:172
  16.1 16.1 %psum.14 = f32[512]{0:T(512)S(1)} all-reduce(f32[512]{0:T(512)S(1)} %convert_reduce_fusion), channel_id=1, replica_groups=mesh['var'=8,'samp'=4] {'samp'}, use_global_device_ids=true, to_apply=%region_1.2 | all-reduce | flops 512 | bytes 4096 | tf_op jit(solution)/shard_map/psum | solution.py:172
  32.2 3.3 %fusion.1 = f32[512]{0:T(512)S(1)} fusion(bf16[4096,512]{1,0:T(8,128)(2,1)} %x_ref.1, f32[512]{0:T(512)S(1)} %broadcast_multiply_fusion), kind=kLoop, calls=%fused_computation.3 | loop fusion | flops 8388096 | bytes 4198400 | tf_op jit(solution)/shard_map/reduce_sum | solution.py:174
  35.6 6.1 %psum.15 = f32[512]{0:T(512)S(1)} all-reduce(f32[512]{0:T(512)S(1)} %fusion.1), channel_id=1, replica_groups=mesh['var'=8,'samp'=4] {'samp'}, use_global_device_ids=true, to_apply=%region_3.4 | all-reduce | flops 512 | bytes 4096 | tf_op jit(solution)/shard_map/psum | solution.py:174
  41.6 0.1 maximum_maximum_fusion.stat_ref
  41.7 1.3 collective-permute-start
  43.0 1.3 collective-permute-start.1
  44.3 0.0 copy-start
  44.3 2.2 %copy-done = bf16[4096,512]{1,0:T(8,128)(2,1)S(1)} copy-done((bf16[4096,512]{1,0:T(8,128)(2,1)S(1)}, bf16[4096,512]{1,0:T(8,128)(2,1)}, u32[]{:S(2)}) %copy-start) | copy-done | bytes 4194328
  46.5 5.0 %own_tile.1 = (bf16[512,4096]{1,0:T(8,128)(2,1)S(1)}, f32[512,512]{1,0:T(8,128)S(1)}) custom-call(bf16[4096,512]{1,0:T(8,128)(2,1)S(1)} %copy-done, f32[4,512]{1,0:T(4,128)S(1)} %maximum_maximum_fusion.stat_ref), custom_call_target="tpu_custom_call" | custom-call | flops 2147483648 | bytes 8388608 | tf_op jit(solution)/shard_map/own_tile/pallas_call | solution.py:191
  51.5 1.0 copy-done.1
  52.5 2.0 %copy-done.9 = bf16[512,4096]{1,0:T(8,128)(2,1)} copy-done((bf16[512,4096]{1,0:T(8,128)(2,1)}, bf16[512,4096]{1,0:T(8,128)(2,1)S(1)}, u32[]{:S(2)}) %copy-start.9) | copy-done | bytes 4194328
  54.5 0.1 stack.44.pos_ref
  54.6 3.7 %collective-permute-done.ystat_ref = f32[4,512]{1,0:T(4,128)S(1)} collective-permute-done((f32[4,512]{1,0:T(4,128)S(1)}, f32[4,512]{1,0:T(4,128)S(1)}, u32[]{:S(2)}, u32[]{:S(2)}) %collective-permute-start) | collective-permute-done | bytes 8224 | tf_op jit(solution)/shard_map/ppermute | solution.py:166
  58.3 0.5 slice.13
  59.4 0.8 collective-permute-done.1.wstat_ref
  60.2 0.5 fusion.2
  62.6 0.1 maximum_multiply_fusion.scale_ref
  62.7 0.0 collective-permute-done.2.y_ref
  62.7 0.0 collective-permute-done.3.w_ref
  62.7 2.2 %copy-done.10 = bf16[512,4096]{1,0:T(8,128)(2,1)S(1)} copy-done((bf16[512,4096]{1,0:T(8,128)(2,1)S(1)}, bf16[512,4096]{1,0:T(8,128)(2,1)}, u32[]{:S(2)}) %copy-start.10) | copy-done | bytes 4194328
  64.9 13.2 %pair_tiles.1 = (f32[1,3,256,256]{3,2,1,0:T(8,128)S(1)}, f32[1,3,256,256]{3,2,1,0:T(8,128)S(1)}, f32[2,3,256,256]{3,2,1,0:T(8,128)S(1)}, f32[2,3,256,256]{3,2,1,0:T(8,128)}) custom-call(s32[5]{0:T(128)S(1)} %stack.44.pos_ref, f32[3]{0:T(128)S(1)} %maximum_multiply_fusion.scale_ref, bf16[512,4096]{1,0:T(8,128)(2,1)S(1)} %copy-done.10, ...), custom_call_target="tpu_custom_call" | custom-call | flops 6442450944 | bytes 12582912 | tf_op jit(solution)/shard_map/pair_tiles/pallas_call | solution.py:206
  78.1 0.9 copy-done.2
  79.0 0.9 copy-done.8
  79.9 4.0 %collective-permute-start.5 = (f32[2,3,256,256]{3,2,1,0:T(8,128)}, f32[2,3,256,256]{3,2,1,0:T(8,128)S(1)}, u32[]{:S(2)}, u32[]{:S(2)}) collective-permute-start(f32[2,3,256,256]{3,2,1,0:T(8,128)} %get-tuple-element.19), channel_id=1, source_target_pairs={{0,2},{2,0},{5,7},{7,5},{8,10},{10,8},{13,15},{15,13},{16,18},{18,... | collective-permute-start | bytes 4718600 | tf_op jit(solution)/shard_map/ppermute | solution.py:166
  83.9 0.0 reduce-scatter.2.cloned.1.call-update
  83.9 0.2 collective-permute-start.4
  84.1 37.3 %collective-permute-done.4.got_c = f32[1,3,256,256]{3,2,1,0:T(8,128)S(1)} collective-permute-done((f32[1,3,256,256]{3,2,1,0:T(8,128)}, f32[1,3,256,256]{3,2,1,0:T(8,128)S(1)}, u32[]{:S(2)}, u32[]{:S(2)}) %collective-permute-start.4) | collective-permute-done | bytes 786464 | tf_op jit(solution)/shard_map/ppermute | solution.py:166
  121.4 1.1 copy-done.3
  122.5 2.8 %strips.1 = (f32[2,128,512]{2,1,0:T(8,128)S(1)}, f32[2,128,512]{2,1,0:T(8,128)}, f32[2,128,512]{2,1,0:T(8,128)}, f32[2,128,512]{2,1,0:T(8,128)}, f32[2,128,512]{2,1,0:T(8,128)}, /*index=5*/f32[2,128,512]{2,1,0:T(8,128)}) custom-call(s32[5]{0:T(128)S(1)} %stack.44.pos_ref, f32[1,3,256,256]{3,2,1,0:T(8,128)S(1)} %copy-done.3, ...), custom_call_target="tpu_custom_call" | custom-call | tf_op jit(solution)/shard_map/strips/pallas_call | solution.py:226
  125.3 0.8 copy-done.4
  126.1 5.0 %collective-permute-start.7 = (f32[2,128,512]{2,1,0:T(8,128)}, f32[2,128,512]{2,1,0:T(8,128)S(1)}, u32[]{:S(2)}, u32[]{:S(2)}) collective-permute-start(f32[2,128,512]{2,1,0:T(8,128)} %get-tuple-element.22), channel_id=1, source_target_pairs={{0,4},{2,6},{5,1},{7,3},{8,12},{10,14},{13,9},{15,11},{16,20},{18,... | collective-permute-start | bytes 1572872 | tf_op jit(solution)/shard_map/ppermute | solution.py:166
  131.1 1.9 %collective-permute-start.8 = (f32[2,128,512]{2,1,0:T(8,128)}, f32[2,128,512]{2,1,0:T(8,128)S(1)}, u32[]{:S(2)}, u32[]{:S(2)}) collective-permute-start(f32[2,128,512]{2,1,0:T(8,128)} %get-tuple-element.23), channel_id=1, source_target_pairs={{0,5},{2,7},{5,0},{7,2},{8,13},{10,15},{13,8},{15,10},{16,21},{18,... | collective-permute-start | bytes 1572872 | tf_op jit(solution)/shard_map/ppermute | solution.py:166
  133.1 4.0 %collective-permute-start.9 = (f32[2,128,512]{2,1,0:T(8,128)}, f32[2,128,512]{2,1,0:T(8,128)S(1)}, u32[]{:S(2)}, u32[]{:S(2)}) collective-permute-start(f32[2,128,512]{2,1,0:T(8,128)} %get-tuple-element.24), channel_id=1, source_target_pairs={{0,8},{2,10},{4,12},{6,14},{8,16},{9,1},{10,18},{11,3},{12,20},{13... | collective-permute-start | bytes 1572872 | tf_op jit(solution)/shard_map/ppermute | solution.py:166
  137.1 1.9 %collective-permute-start.10 = (f32[2,128,512]{2,1,0:T(8,128)}, f32[2,128,512]{2,1,0:T(8,128)S(1)}, u32[]{:S(2)}, u32[]{:S(2)}) collective-permute-start(f32[2,128,512]{2,1,0:T(8,128)} %get-tuple-element.25), channel_id=1, source_target_pairs={{0,9},{2,11},{4,13},{6,15},{8,17},{9,0},{10,19},{11,2},{12,21},{13... | collective-permute-start | bytes 1572872 | tf_op jit(solution)/shard_map/ppermute | solution.py:166
  139.0 0.0 reduce-scatter.2.cloned.1.call-done.diag
  139.0 4.7 %collective-permute-done.8.y_b = f32[2,128,512]{2,1,0:T(8,128)S(1)} collective-permute-done((f32[2,128,512]{2,1,0:T(8,128)}, f32[2,128,512]{2,1,0:T(8,128)S(1)}, u32[]{:S(2)}, u32[]{:S(2)}) %collective-permute-start.8) | collective-permute-done | bytes 524320 | tf_op jit(solution)/shard_map/ppermute | solution.py:166
  143.7 0.3 collective-permute-done.9.z_same
  144.0 5.6 %collective-permute-done.10.z_cross = f32[2,128,512]{2,1,0:T(8,128)S(1)} collective-permute-done((f32[2,128,512]{2,1,0:T(8,128)}, f32[2,128,512]{2,1,0:T(8,128)S(1)}, u32[]{:S(2)}, u32[]{:S(2)}) %collective-permute-start.10) | collective-permute-done | bytes 524320 | tf_op jit(solution)/shard_map/ppermute | solution.py:166
  149.6 1.0 copy-done.5
  150.7 0.9 copy-done.6
  151.6 1.9 %finish.1 = (bf16[1,3,128,512]{3,2,1,0:T(8,128)(2,1)}, bf16[1,2,128,512]{3,2,1,0:T(8,128)(2,1)}) custom-call(s32[5]{0:T(128)S(1)} %stack.44.pos_ref, s32[1,3]{1,0:T(1,128)S(1)} %copy-done.7, f32[128,512]{1,0:T(8,128)S(1)} %copy-done.6, f32[2,128,512]{2,1,0:T(8,128)S(1)} %copy-done.5, f32[2,128,512]{2,1,0:T(8,128)S(1)} %collective-permute-done.6.sib, ...), custom_call_target="tpu_custom_call" | custom-call | tf_op jit(solution)/shard_map/finish/pallas_call | solution.py:243
  (17 shorter events, 0.0 us)
Async XLA Ops:
  7.2 131.8 %reduce-scatter.2.cloned.1.call-start = ((), (), s32[]{:S(2)}) async-start(), calls=%async_computation.1 | async-start | bytes 1310720 | tf_op jit(solution)/shard_map/reduce_scatter | solution.py:202
  7.2 55.5 %collective-permute-start.2 = (bf16[4096,512]{1,0:T(8,128)(2,1)}, bf16[4096,512]{1,0:T(8,128)(2,1)}, u32[]{:S(2)}, u32[]{:S(2)}) collective-permute-start(bf16[4096,512]{1,0:T(8,128)(2,1)} %x_ref.1), channel_id=1, source_target_pairs={{1,5},{3,7},{4,0},{6,2},{9,13},{11,15},{12,8},{14,10},{17,21},{19,... | collective-permute-start | bytes 12582920 | tf_op jit(solution)/shard_map/ppermute | solution.py:166
  8.5 54.2 %collective-permute-start.3 = (bf16[4096,512]{1,0:T(8,128)(2,1)}, bf16[4096,512]{1,0:T(8,128)(2,1)}, u32[]{:S(2)}, u32[]{:S(2)}) collective-permute-start(bf16[4096,512]{1,0:T(8,128)(2,1)} %x_ref.1), channel_id=1, source_target_pairs={{1,9},{3,11},{5,13},{7,15},{8,0},{9,17},{10,2},{11,19},{12,4},{13,... | collective-permute-start | bytes 12582920 | tf_op jit(solution)/shard_map/ppermute | solution.py:166
  41.7 16.5 %collective-permute-start = (f32[4,512]{1,0:T(4,128)S(1)}, f32[4,512]{1,0:T(4,128)S(1)}, u32[]{:S(2)}, u32[]{:S(2)}) collective-permute-start(f32[4,512]{1,0:T(4,128)S(1)} %maximum_maximum_fusion.stat_ref), channel_id=1, source_target_pairs={{1,5},{3,7},{4,0},{6,2},{9,13},{11,15},{12,8},{14,10},{17,21},{19,... | collective-permute-start | bytes 24584 | tf_op jit(solution)/shard_map/ppermute | solution.py:166
  43.0 17.2 %collective-permute-start.1 = (f32[4,512]{1,0:T(4,128)S(1)}, f32[4,512]{1,0:T(4,128)S(1)}, u32[]{:S(2)}, u32[]{:S(2)}) collective-permute-start(f32[4,512]{1,0:T(4,128)S(1)} %maximum_maximum_fusion.stat_ref), channel_id=1, source_target_pairs={{1,9},{3,11},{5,13},{7,15},{8,0},{9,17},{10,2},{11,19},{12,4},{13,... | collective-permute-start | bytes 24584 | tf_op jit(solution)/shard_map/ppermute | solution.py:166
  44.3 2.2 %copy-start = (bf16[4096,512]{1,0:T(8,128)(2,1)S(1)}, bf16[4096,512]{1,0:T(8,128)(2,1)}, u32[]{:S(2)}) copy-start(bf16[4096,512]{1,0:T(8,128)(2,1)} %x_ref.1) | copy-start | bytes 12582916
  51.5 1.0 copy-start.1
  52.5 2.0 %copy-start.9 = (bf16[512,4096]{1,0:T(8,128)(2,1)}, bf16[512,4096]{1,0:T(8,128)(2,1)S(1)}, u32[]{:S(2)}) copy-start(bf16[512,4096]{1,0:T(8,128)(2,1)S(1)} %get-tuple-element.15.turned_ref) | copy-start | bytes 12582916
  62.7 2.2 %copy-start.10 = (bf16[512,4096]{1,0:T(8,128)(2,1)S(1)}, bf16[512,4096]{1,0:T(8,128)(2,1)}, u32[]{:S(2)}) copy-start(bf16[512,4096]{1,0:T(8,128)(2,1)} %copy-done.9) | copy-start | bytes 12582916
  78.1 0.9 copy-start.2
  79.0 0.9 copy-start.8
  79.9 69.7 %copy-start.7 = (s32[1,3]{1,0:T(1,128)S(1)}, s32[1,3]{1,0:T(1,128)}, u32[]{:S(2)}) copy-start(s32[1,3]{1,0:T(1,128)} %offsets_ref.1) | copy-start | bytes 40
  79.9 41.4 %collective-permute-start.5 = (f32[2,3,256,256]{3,2,1,0:T(8,128)}, f32[2,3,256,256]{3,2,1,0:T(8,128)S(1)}, u32[]{:S(2)}, u32[]{:S(2)}) collective-permute-start(f32[2,3,256,256]{3,2,1,0:T(8,128)} %get-tuple-element.19), channel_id=1, source_target_pairs={{0,2},{2,0},{5,7},{7,5},{8,10},{10,8},{13,15},{15,13},{16,18},{18,... | collective-permute-start | bytes 4718600 | tf_op jit(solution)/shard_map/ppermute | solution.py:166
  83.9 37.4 %collective-permute-start.4 = (f32[1,3,256,256]{3,2,1,0:T(8,128)}, f32[1,3,256,256]{3,2,1,0:T(8,128)S(1)}, u32[]{:S(2)}, u32[]{:S(2)}) collective-permute-start(f32[1,3,256,256]{3,2,1,0:T(8,128)} %copy-done.8), channel_id=1, source_target_pairs={{0,2},{1,3},{2,0},{3,1},{4,6},{5,7},{6,4},{7,5},{8,10},{9,11},{10,... | collective-permute-start | bytes 2359304 | tf_op jit(solution)/shard_map/ppermute | solution.py:166
  121.4 1.1 copy-start.3
  125.3 0.8 copy-start.4
  126.1 12.9 %collective-permute-start.6 = (f32[2,128,512]{2,1,0:T(8,128)}, f32[2,128,512]{2,1,0:T(8,128)S(1)}, u32[]{:S(2)}, u32[]{:S(2)}) collective-permute-start(f32[2,128,512]{2,1,0:T(8,128)} %get-tuple-element.21), channel_id=1, source_target_pairs={{0,1},{1,0},{2,3},{3,2},{4,5},{5,4},{6,7},{7,6},{8,9},{9,8},{10,11... | collective-permute-start | bytes 1572872 | tf_op jit(solution)/shard_map/ppermute | solution.py:166
  126.1 12.9 %collective-permute-start.7 = (f32[2,128,512]{2,1,0:T(8,128)}, f32[2,128,512]{2,1,0:T(8,128)S(1)}, u32[]{:S(2)}, u32[]{:S(2)}) collective-permute-start(f32[2,128,512]{2,1,0:T(8,128)} %get-tuple-element.22), channel_id=1, source_target_pairs={{0,4},{2,6},{5,1},{7,3},{8,12},{10,14},{13,9},{15,11},{16,20},{18,... | collective-permute-start | bytes 1572872 | tf_op jit(solution)/shard_map/ppermute | solution.py:166
  131.1 12.6 %collective-permute-start.8 = (f32[2,128,512]{2,1,0:T(8,128)}, f32[2,128,512]{2,1,0:T(8,128)S(1)}, u32[]{:S(2)}, u32[]{:S(2)}) collective-permute-start(f32[2,128,512]{2,1,0:T(8,128)} %get-tuple-element.23), channel_id=1, source_target_pairs={{0,5},{2,7},{5,0},{7,2},{8,13},{10,15},{13,8},{15,10},{16,21},{18,... | collective-permute-start | bytes 1572872 | tf_op jit(solution)/shard_map/ppermute | solution.py:166
  133.1 10.9 %collective-permute-start.9 = (f32[2,128,512]{2,1,0:T(8,128)}, f32[2,128,512]{2,1,0:T(8,128)S(1)}, u32[]{:S(2)}, u32[]{:S(2)}) collective-permute-start(f32[2,128,512]{2,1,0:T(8,128)} %get-tuple-element.24), channel_id=1, source_target_pairs={{0,8},{2,10},{4,12},{6,14},{8,16},{9,1},{10,18},{11,3},{12,20},{13... | collective-permute-start | bytes 1572872 | tf_op jit(solution)/shard_map/ppermute | solution.py:166
  137.1 12.6 %collective-permute-start.10 = (f32[2,128,512]{2,1,0:T(8,128)}, f32[2,128,512]{2,1,0:T(8,128)S(1)}, u32[]{:S(2)}, u32[]{:S(2)}) collective-permute-start(f32[2,128,512]{2,1,0:T(8,128)} %get-tuple-element.25), channel_id=1, source_target_pairs={{0,9},{2,11},{4,13},{6,15},{8,17},{9,0},{10,19},{11,2},{12,21},{13... | collective-permute-start | bytes 1572872 | tf_op jit(solution)/shard_map/ppermute | solution.py:166
  149.6 1.0 copy-start.5
  150.7 0.9 copy-start.6
Sparse Core Ops, SparseCore 0:
  84.0 26.9 reduce-scatter.1

commit v2 on v1

v2 whole, which is shorter than its diff:
```python
import jax
import jax.numpy as jnp
from jax import lax
from jax.experimental import pallas as pl
from jax.experimental.pallas import tpu as pltpu
from jax.sharding import PartitionSpec as P

SLOTS = 3
AXES = ("var", "samp")
F32 = jnp.float32
BF16 = jnp.bfloat16
VMEM = pl.BlockSpec(memory_space=pltpu.VMEM)
SMEM = pl.BlockSpec(memory_space=pltpu.SMEM)
BIG = pltpu.CompilerParams(vmem_limit_bytes=56 << 20)
D_BLOCKS = {0: [(0, 0)], 1: [(0, 1), (1, 0), (1, 1)]}


def dot(a, b):
    return jnp.dot(a, b, preferred_element_type=F32)


def standardized(raw, stat_ref):
    return ((raw.astype(F32) - stat_ref[0:1, :]) * stat_ref[1:2, :]).astype(BF16)


def stats_kernel(x_ref, out_ref):
    step = pl.program_id(0)
    rows = x_ref.shape[0]
    x = x_ref[...].astype(F32)
    mean = jnp.sum(x, axis=0, keepdims=True) * (1.0 / rows)
    centered = x - mean
    square = jnp.sum(centered * centered, axis=0, keepdims=True)

    @pl.when(step == 0)
    def _():
        out_ref[0:1, :] = mean
        out_ref[1:2, :] = square

    @pl.when(step > 0)
    def _():
        before = step.astype(F32)
        share = 1.0 / (before + 1.0)
        delta = mean - out_ref[0:1, :]
        out_ref[0:1, :] += delta * share
        out_ref[1:2, :] += square + delta * delta * (rows * before * share)


def own_kernel(pos_ref, x_ref, stat_ref, turned_ref, keep_ref, send_ref, acc):
    step = pl.program_id(0)
    z = standardized(x_ref[...], stat_ref)
    zt = z.T
    turned_ref[...] = zt
    part = dot(zt, z)

    @pl.when(step == 0)
    def _():
        acc[...] = part

    @pl.when(step > 0)
    def _():
        acc[...] += part

    @pl.when(step == pl.num_programs(0) - 1)
    def _():
        half = keep_ref.shape[0]
        keep_ref[...] = acc[pl.ds(pl.multiple_of(pos_ref[0] * half, half), half), :]
        send_ref[...] = acc[pl.ds(pl.multiple_of((1 - pos_ref[0]) * half, half), half), :]


def diag_kernel(pos_ref, keep_ref, got_ref, mine_ref, other_ref):
    rows = mine_ref.shape[0]
    for core, out in ((pos_ref[2], mine_ref), (1 - pos_ref[2], other_ref)):
        at = pl.ds(pl.multiple_of(core * rows, rows), rows)
        out[...] = keep_ref[at, :] + got_ref[at, :]


def put_blocks(x, source, base, out_keep, out_send, first, parts):
    size = out_keep.shape[-1]
    for out, near in ((out_keep, x), (out_send, 1 - x)):
        index = first
        for r, h in ((near, near), (near, 1 - near), (1 - near, near)):
            for part in range(parts):
                row = pl.multiple_of(r * parts * size + part * size, size)
                col = pl.multiple_of(base + h * size, size)
                out[index] = source[pl.ds(row, size), pl.ds(col, size)]
                index += 1


def pair_kernel(chunk, *refs):
    (pos_ref, scale_ref, turned_ref, y_ref, w_ref, ystat_ref, wstat_ref), refs = refs[:7], refs[7:]
    if chunk == 0:
        keep_c, send_c, keep_bd, send_bd, yt_out, w_out, acc_b, acc_c, acc_d = refs
    else:
        yt_old, w_old, keep_c, send_c, keep_bd, send_bd, acc_b, acc_c, acc_d, acc_e = refs
    step = pl.program_id(0)
    last = pl.num_programs(0) - 1
    x = pos_ref[0]
    active = pos_ref[1] == 1
    size = keep_c.shape[-1]

    @pl.when(step == 0)
    def _():
        for acc in (acc_b, acc_c, acc_d) + (() if chunk == 0 else (acc_e,)):
            acc[...] = jnp.zeros_like(acc)

    zt = turned_ref[...]
    w = standardized(w_ref[...], wstat_ref)
    acc_c[...] += dot(zt, w)
    if chunk == 0:
        w_out[...] = w

    @pl.when(active)
    def _():
        y = standardized(y_ref[...], ystat_ref)
        yt = y.T
        acc_b[...] += dot(zt, y)
        if chunk == 0:
            yt_out[...] = yt
            acc_d[...] += dot(yt, w)
        else:
            acc_e[...] += dot(yt_old[...], w)
            acc_d[:, :2 * size] += dot(yt, w_old[...])
            acc_d[:, 2 * size:] += dot(yt, w)

    @pl.when(step == last)
    def _():
        acc_c[...] *= scale_ref[1]
        put_blocks(x, acc_c, 0, keep_c, send_c, 0, 2)

        @pl.when(active)
        def _():
            acc_b[...] *= scale_ref[0]
            acc_d[...] *= scale_ref[2]
            put_blocks(x, acc_b, 0, keep_bd, send_bd, 0, 2)
            if chunk == 0:
                put_blocks(x, acc_d, 0, keep_bd, send_bd, 6, 1)
            else:
                acc_e[...] *= scale_ref[2]
                put_blocks(x, acc_e, 0, keep_bd, send_bd, 6, 1)
                put_blocks(x, acc_d, 0, keep_bd, send_bd, 9, 1)
                put_blocks(x, acc_d, 2 * size, keep_bd, send_bd, 12, 1)


def strips_kernel(pos_ref, keep_c0, got_c0, keep_bd0, got_bd0, keep_c1, got_c1, keep_bd1, got_bd1,
                  own, sib, y_same, y_cross, z_same, z_cross):
    size = keep_c0.shape[-1]
    x = pos_ref[0]

    def columns(half, part):
        return pl.ds(pl.multiple_of(half * 2 * size + part * size, size), size)

    def wide(keeps, gots, mine, row_out, col_out):
        for core, rows, cols in ((mine, row_out[0], col_out[0]), (1 - mine, row_out[1], col_out[1])):
            for part in range(2):
                rows[:, columns(x, part)] = keeps[part][core] + gots[part][core]
                rows[:, columns(1 - x, part)] = keeps[part][2 + core] + gots[part][2 + core]
                cols[:, columns(x, part)] = (keeps[core][part] + gots[core][part]).T
                cols[:, columns(1 - x, part)] = (keeps[core][4 + part] + gots[core][4 + part]).T

    def cross(keeps, gots, mine, row_out, col_out):
        def block(a, b, which):
            chunk = max(a, b)
            index = 6 + 3 * D_BLOCKS[chunk].index((a, b)) + which
            return keeps[chunk][index] + gots[chunk][index]

        for core, rows, cols in ((mine, row_out[0], col_out[0]), (1 - mine, row_out[1], col_out[1])):
            for part in range(2):
                rows[:, columns(x, part)] = block(core, part, 0)
                rows[:, columns(1 - x, part)] = block(core, part, 1)
                cols[:, columns(x, part)] = block(part, core, 0).T
                cols[:, columns(1 - x, part)] = block(part, core, 2).T

    for mine in range(2):
        @pl.when(pos_ref[2] == mine)
        def _():
            wide((keep_c0, keep_c1), (got_c0, got_c1), mine, (own.at[1], sib.at[1]), (z_same.at[0], z_cross.at[0]))

            @pl.when(pos_ref[1] == 1)
            def _():
                keeps, gots = (keep_bd0, keep_bd1), (got_bd0, got_bd1)
                wide(keeps, gots, mine, (own.at[0], sib.at[0]), (y_same.at[0], y_cross.at[0]))
                cross(keeps, gots, mine, (y_same.at[1], y_cross.at[1]), (z_same.at[1], z_cross.at[1]))


def finish_kernel(pos_ref, offsets_ref, diag_mine, diag_got, own, sib, y_a, y_b, z_same, z_cross, upper, mirror):
    active = pos_ref[1] == 1
    first_core = pos_ref[2] == 0
    even = pos_ref[3] == 0
    pick = jnp.where
    side = pick(active, y_b[0], y_a[0])
    side_d = pick(active, y_b[1], y_a[1])
    below_c = pick(first_core, z_same[0], z_cross[0])
    above_c = pick(first_core, z_cross[0], z_same[0])
    near_d = pick(first_core == even, z_same[1], z_cross[1])
    held = pick(active, own[0], sib[0]) + side
    far = side_d + near_d
    upper_1 = pick(even, held, far)
    mirror_1 = pick(even, far, held)
    upper_2 = pick(first_core, own[1], sib[1]) + above_c
    mirror_2 = pick(first_core, sib[1], own[1]) + below_c
    mirror[0, 0] = mirror_1.astype(BF16)
    mirror[0, 1] = mirror_2.astype(BF16)
    self_tile = (diag_mine[...] + diag_got[...]) * (1.0 / pos_ref[4].astype(F32))
    for slot in range(SLOTS):
        offset = offsets_ref[0, slot]
        tile = pick(offset == 0, self_tile, pick(offset == 1, upper_1, pick(offset == 2, upper_2, 0.0)))
        upper[0, slot] = tile.astype(BF16)


def body(dosage, pair_offsets, live_counts):
    n_var = lax.axis_size("var")
    n_samp = lax.axis_size("samp")
    depth, width = dosage.shape
    half = width // 2
    strip = width // n_samp
    samples_all = depth * n_samp
    v = lax.axis_index("var")
    s = lax.axis_index("samp")
    x, core, odd = s // 2, s % 2, v % 2
    active = (core == odd).astype(jnp.int32)

    def at(var, samp):
        return var * n_samp + samp

    def active_on(var, samp):
        return var % 2 == samp % 2

    everyone = [(var, samp) for var in range(n_var) for samp in range(n_samp)]
    z_main = [(at(a, b), at(a - 2 if b % 2 == 0 else a + 2, b)) for a, b in everyone
              if 0 <= (a - 2 if b % 2 == 0 else a + 2) < n_var]
    y_main = [(at(a, b), at(a ^ 1, b)) for a, b in everyone if not active_on(a, b)]
    across = [(at(a, b), at(a, b ^ 2)) for a, b in everyone]
    across_active = [(at(a, b), at(a, b ^ 2)) for a, b in everyone if active_on(a, b)]
    sibling = [(at(a, b), at(a, b ^ 1)) for a, b in everyone]

    def send(value, pairs):
        return lax.ppermute(value, AXES, pairs)

    chunks = []
    for part in range(2):
        pieces = [dosage[:, h * half + part * strip:h * half + (part + 1) * strip] for h in range(2)]
        chunks.append(jnp.concatenate(pieces, axis=1))
    w_raw = [send(chunk, z_main) for chunk in chunks]
    y_raw = [send(chunk, y_main) for chunk in chunks]

    step_rows = min(512, depth)
    local = pl.pallas_call(
        stats_kernel,
        grid=(depth // step_rows,),
        in_specs=[pl.BlockSpec((step_rows, width), lambda k: (k, 0))],
        out_specs=pl.BlockSpec((2, width), lambda k: (0, 0)),
        out_shape=jax.ShapeDtypeStruct((2, width), F32),
        compiler_params=BIG,
        cost_estimate=pl.CostEstimate(flops=5 * depth * width, bytes_accessed=2 * depth * width, transcendentals=0),
        name="local_stats",
    )(dosage)
    mask = (jnp.arange(n_samp) == s).astype(F32)
    gathered = lax.psum(mask[:, None, None] * local[None], "samp")
    mean = jnp.sum(gathered[:, 0], axis=0) * (1.0 / n_samp)
    between = jnp.sum(jnp.square(gathered[:, 0] - mean), axis=0) * depth
    spread = (jnp.sum(gathered[:, 1], axis=0) + between) / samples_all
    live = jnp.arange(width, dtype=jnp.int32) < live_counts[0]
    inv = jnp.where(live, lax.rsqrt(spread + 1e-05), 0.0)
    lists = [jnp.any(pair_offsets[0] == step).astype(F32) for step in (1, 2)]
    stat = jnp.stack([mean, inv] + [jnp.full((width,), flag) for flag in lists])
    z_step = [(a, b, a + 2 if b % 2 == 0 else a - 2) for a, b in everyone]
    z_cross = [(at(a, b), at(t, b ^ 1)) for a, b, t in z_step if 0 <= t < n_var]
    y_cross = [(at(a, b), at(a ^ 1, b ^ 1)) for a, b in everyone if active_on(a, b)]
    w_stat, y_stat = send(stat, z_cross), send(stat, y_cross)

    first = core == 0
    scale = jnp.stack([
        jnp.where(first, lists[0], y_stat[2, 0]),
        jnp.where(first, lists[1], w_stat[3, 0]),
        jnp.where(first, y_stat[2, 0], w_stat[2, 0]),
    ]) / samples_all
    pos = jnp.stack([x, active, core, odd, jnp.int32(samples_all)]).astype(jnp.int32)

    def by_chunk(table):
        perm = [h * half + part * strip for part in range(2) for h in range(2)]
        return [jnp.concatenate([table[:, at:at + strip] for at in perm[2 * part:2 * part + 2]], axis=1)
                for part in range(2)]

    w_stats, y_stats = by_chunk(w_stat), by_chunk(y_stat)

    turned, diag_keep, diag_send = pl.pallas_call(
        own_kernel,
        grid=(depth // step_rows,),
        in_specs=[SMEM, pl.BlockSpec((step_rows, width), lambda k: (k, 0)), pl.BlockSpec((4, width), lambda k: (0, 0))],
        out_specs=[pl.BlockSpec((width, step_rows), lambda k: (0, k))]
        + [pl.BlockSpec((half, width), lambda k: (0, 0))] * 2,
        out_shape=[jax.ShapeDtypeStruct((width, depth), BF16)] + [jax.ShapeDtypeStruct((half, width), F32)] * 2,
        scratch_shapes=[pltpu.VMEM((width, width), F32)],
        compiler_params=BIG,
        cost_estimate=pl.CostEstimate(flops=2 * depth * width * width, bytes_accessed=4 * depth * width, transcendentals=0),
        name="own_tile",
    )(pos, dosage, stat)
    diag_across = send(diag_send, across)
    pair_rows = min(1024, depth)
    steps = depth // pair_rows
    blocks = lambda n: jax.ShapeDtypeStruct((n, strip, strip), F32)
    whole = lambda *shape: pl.BlockSpec(shape, lambda k: (0,) * len(shape))
    tall = pl.BlockSpec((pair_rows, half), lambda k: (k, 0))
    flat = lambda rows: pl.BlockSpec((rows, pair_rows), lambda k: (0, k))
    keeps, arrived, passed, before = [], [], [], [diag_across]
    for part in range(2):
        n_bd = 6 + 3 * len(D_BLOCKS[part])
        in_specs = [SMEM, SMEM, flat(width), tall, tall, whole(4, half), whole(4, half)]
        out_specs = [whole(6, strip, strip)] * 2 + [whole(n_bd, strip, strip)] * 2
        out_shape = [blocks(6)] * 2 + [blocks(n_bd)] * 2
        scratch = [pltpu.VMEM((width, half), F32)] * 2
        if part == 0:
            out_specs += [flat(half), tall]
            out_shape += [jax.ShapeDtypeStruct((half, depth), BF16), jax.ShapeDtypeStruct((depth, half), BF16)]
            scratch += [pltpu.VMEM((half, half), F32)]
        else:
            in_specs += [flat(half), tall]
            scratch += [pltpu.VMEM((half, width), F32), pltpu.VMEM((half, half), F32)]
        keep_c, send_c, keep_bd, send_bd, *passed = pl.pallas_call(
            lambda *refs, part=part: pair_kernel(part, *refs),
            grid=(steps,),
            in_specs=in_specs,
            out_specs=out_specs,
            out_shape=out_shape,
            scratch_shapes=scratch,
            compiler_params=BIG,
            cost_estimate=pl.CostEstimate(flops=3 * depth * width * width, bytes_accessed=4 * depth * width, transcendentals=0),
            name=f"pair_tiles_{part}",
        )(pos, scale, turned, y_raw[part], w_raw[part], y_stats[part], w_stats[part], *passed)
        send_bd, send_c, *before = lax.optimization_barrier((send_bd, send_c, *before))
        arrived += before
        before = [send(send_bd, across_active), send(send_c, across)]
        keeps.append((keep_bd, keep_c))
    arrived += before

    diag_mine, diag_other = pl.pallas_call(
        diag_kernel,
        in_specs=[SMEM, VMEM, VMEM],
        out_specs=[VMEM, VMEM],
        out_shape=[jax.ShapeDtypeStruct((strip, width), F32)] * 2,
        name="diag_strips",
    )(pos, diag_keep, arrived[0])
    diag_got = send(diag_other, sibling)

    held = []
    for part, (keep_bd, keep_c) in enumerate(keeps):
        held += [keep_c, arrived[2 + 2 * part], keep_bd, arrived[1 + 2 * part]]
    two = jax.ShapeDtypeStruct((2, strip, width), F32)
    own, sib, to_y_same, to_y_cross, to_z_same, to_z_cross = pl.pallas_call(
        strips_kernel,
        in_specs=[SMEM] + [VMEM] * 8,
        out_specs=[VMEM] * 6,
        out_shape=[two] * 6,
        name="strips",
    )(pos, *held)

    got_z_cross = send(to_z_cross, z_cross)
    got_z_same = send(to_z_same, [(at(a, b), at(t, b)) for a, b, t in z_step if 0 <= t < n_var])
    got_y_same = send(to_y_same, [(at(a, b), at(a ^ 1, b)) for a, b in everyone if active_on(a, b)])
    got_y_cross = send(to_y_cross, y_cross)
    got_sib = send(sib, sibling)

    return pl.pallas_call(
        finish_kernel,
        in_specs=[SMEM, SMEM] + [VMEM] * 8,
        out_specs=[VMEM, VMEM],
        out_shape=[jax.ShapeDtypeStruct((1, SLOTS, strip, width), BF16),
                   jax.ShapeDtypeStruct((1, 2, strip, width), BF16)],
        name="finish",
    )(pos, pair_offsets, diag_mine, diag_got, own, got_sib, got_y_same, got_y_cross, got_z_same, got_z_cross)


def solution(mesh):
    in_specs = (P("samp", "var"), P("var", None), P("var"))
    out_specs = (P("var", None, "samp", None), P("var", None, "samp", None))
    return jax.shard_map(body, mesh=mesh, in_specs=in_specs, out_specs=out_specs, check_vma=False)
```

time: 161 us -> 150 us (0.932)
  Pallas kernels: 22.9 us -> 44.9 us
  waiting for transfers between devices: 52.4 us -> 33.2 us
  between operations: 18.7 us -> 5.58 us
  starting transfers between devices: 22.1 us -> 29.8 us
  local copies, waits for them, and re-layouts: 14.3 us -> 7.02 us
  other arithmetic: 7.68 us -> 5.2 us
    pallas_call x4 -> x7, Pallas kernels: 22.9 us -> 44.9 us  [the longest x2 19.1 us: body(): pl.pallas_call(lambda *refs, part=part: pair_kernel(part, *refs), grid=(s...]
    ppermute x11 -> x17, waiting for transfers between devices: 52.4 us -> 33.2 us  [send(): return lax.ppermute(value, AXES, pairs)]
    unnamed x22 -> x26, local copies, waits for them, and re-layouts: 13.1 us -> 2.66 us
    ppermute x11 -> x17, starting transfers between devices: 22.1 us -> 29.8 us  [send(): return lax.ppermute(value, AXES, pairs)]
    reduce_sum x2, other arithmetic: 6.14 us -> 0.04 us  [the longest x1 0.02 us: body(): mean = jnp.sum(gathered[:, 0], axis=0) * (1.0 / n_samp)]
    concatenate x0 -> x4, other arithmetic: none -> 2.97 us  [the longest x2 1.77 us: body(): chunks.append(jnp.concatenate(pieces, axis=1))]
    slice x0 -> x3, local copies, waits for them, and re-layouts: none -> 2.51 us  [the longest x1 2.5 us: body(): dosage[:, h * half + part * strip:h * half + (part + 1) * strip]]
    psum x2 -> x1, blocking collectives: 22.2 us -> 22.9 us  [body(): gathered = lax.psum(mask[:, None, None] * local[None], 'samp')]
  transfers between devices with their start and end apart: 12 -> 17, of which waited for: 6 -> 6; matrix products, arithmetic and copies ran while one was open for 6% -> 4% of each run, Pallas kernels for 5% -> 28%
where the time goes in v2:
time: 150 us; the launch traced here: 149 us
  Pallas kernels  44.9 us (30%)
  waiting for transfers between devices  33.2 us (22%)
  starting transfers between devices  29.8 us (20%)
  blocking collectives  22.9 us (15%)
  local copies, waits for them, and re-layouts  7.02 us (5%)
  between operations  5.58 us (4%)
  other arithmetic  5.2 us (3%)
    ppermute x17, waiting for transfers between devices, send(): return lax.ppermute(value, AXES, pairs)  33.2 us
    ppermute x17, starting transfers between devices, send(): return lax.ppermute(value, AXES, pairs)  29.8 us
    psum x1, blocking collectives, body(): gathered = lax.psum(mask[:, None, None] * local[None], 'samp')  22.9 us
    pallas_call x2, Pallas kernels, body(): pl.pallas_call(lambda *refs, part=part: pair_kernel(part, *refs), grid=(s...  19.1 us
    pallas_call x1, Pallas kernels, body(): pl.pallas_call(own_kernel, grid=(depth // step_rows,), in_specs=[SMEM, pl...  9.09 us
    pallas_call x1, Pallas kernels, body(): pl.pallas_call(stats_kernel, grid=(depth // step_rows,), in_specs=[pl.Blo...  6.48 us
    pallas_call x1, Pallas kernels, body(): pl.pallas_call(strips_kernel, in_specs=[SMEM] + [VMEM] * 8, out_specs=[VM...  4.81 us
    pallas_call x1, Pallas kernels, body(): pl.pallas_call(finish_kernel, in_specs=[SMEM, SMEM] + [VMEM] * 8, out_spe...  3.3 us
  transfers between devices with their start and end apart: 17, of which 6 were waited for; matrix products, arithmetic and copies ran while one was open for 4% of the time, Pallas kernels for 28%

profile of v2, /device:TPU:0, one launch (start us, length us, event | category | flops | bytes accessed | tf_op | source)
XLA Modules:
  0.0 148.6 jit_solution(9009037014694073189)
XLA Ops:
  0.6 2.5 %fusion.2 = (bf16[4096,128]{1,0:T(8,128)(2,1)S(1)}, bf16[4096,128]{1,0:T(8,128)(2,1)S(1)}, bf16[4096,128]{1,0:T(8,128)(2,1)S(1)}, bf16[4096,128]{1,0:T(8,128)(2,1)S(1)}) fusion(bf16[4096,512]{1,0:T(8,128)(2,1)} %x_ref.3), kind=kLoop, calls=%fused_computation.20 | loop fusion | bytes 8388608 | tf_op jit(solution)/shard_map/slice | solution.py:241
  3.1 1.5 %pad_maximum_fusion = bf16[4096,256]{1,0:T(8,128)(2,1)} fusion(bf16[4096,128]{1,0:T(8,128)(2,1)S(1)} %get-tuple-element.63, bf16[4096,128]{1,0:T(8,128)(2,1)S(1)} %get-tuple-element.64), kind=kLoop, calls=%fused_computation | loop fusion | flops 4194304 | bytes 4194304 | tf_op jit(solution)/shard_map/concatenate | solution.py:242
  4.7 1.3 collective-permute-start.2
  6.0 1.3 collective-permute-start.3
  7.3 0.2 pad_maximum_fusion.1
  7.5 1.3 collective-permute-start.6
  8.8 1.3 collective-permute-start.7
  10.1 0.0 copy-start.12
  10.1 6.5 %local_stats.1 = f32[2,512]{1,0:T(2,128)} custom-call(bf16[4096,512]{1,0:T(8,128)(2,1)} %x_ref.3), custom_call_target="tpu_custom_call" | custom-call | flops 10485760 | bytes 4194304 | tf_op jit(solution)/shard_map/local_stats/pallas_call | solution.py:247
  16.6 0.8 broadcast_multiply_fusion
  17.4 22.9 %psum.7 = f32[4,2,512]{2,0,1:T(4,128)S(1)} all-reduce(f32[4,2,512]{2,0,1:T(4,128)S(1)} %broadcast_multiply_fusion), channel_id=1, replica_groups=mesh['var'=8,'samp'=4] {'samp'}, use_global_device_ids=true, to_apply=%region_0.1 | all-reduce | flops 4096 | bytes 32768 | tf_op jit(solution)/shard_map/psum | solution.py:258
  41.0 0.7 compare_reduce_fusion.1
  43.1 0.1 pad.18.clone
  43.2 0.1 pad.17.clone
  43.2 0.1 maximum_maximum_fusion.stat_ref
  43.3 1.9 %collective-permute-start = (f32[4,512]{1,0:T(4,128)S(1)}, f32[4,512]{1,0:T(4,128)S(1)}, u32[]{:S(2)}, u32[]{:S(2)}) collective-permute-start(f32[4,512]{1,0:T(4,128)S(1)} %maximum_maximum_fusion.stat_ref), channel_id=1, source_target_pairs={{0,5},{2,7},{5,0},{7,2},{8,13},{10,15},{13,8},{15,10},{16,21},{18,... | collective-permute-start | bytes 24584 | tf_op jit(solution)/shard_map/ppermute | solution.py:237
  45.3 0.6 stack.40.pos_ref.refs_0_
  45.9 2.6 %collective-permute-done = f32[4,512]{1,0:T(4,128)S(1)} collective-permute-done((f32[4,512]{1,0:T(4,128)S(1)}, f32[4,512]{1,0:T(4,128)S(1)}, u32[]{:S(2)}, u32[]{:S(2)}) %collective-permute-start) | collective-permute-done | bytes 8224 | tf_op jit(solution)/shard_map/ppermute | solution.py:237
  48.4 1.9 %collective-permute-start.1 = (f32[4,512]{1,0:T(4,128)S(1)}, f32[4,512]{1,0:T(4,128)S(1)}, u32[]{:S(2)}, u32[]{:S(2)}) collective-permute-start(f32[4,512]{1,0:T(4,128)S(1)} %maximum_maximum_fusion.stat_ref), channel_id=1, source_target_pairs={{0,9},{2,11},{4,13},{6,15},{8,17},{9,0},{10,19},{11,2},{12,21},{13... | collective-permute-start | bytes 24584 | tf_op jit(solution)/shard_map/ppermute | solution.py:237
  50.4 9.1 %own_tile.1 = (bf16[512,4096]{1,0:T(8,128)(2,1)}, f32[256,512]{1,0:T(8,128)}, f32[256,512]{1,0:T(8,128)}) custom-call(s32[5]{0:T(128)} %stack.40.pos_ref.refs_0_, bf16[4096,512]{1,0:T(8,128)(2,1)} %x_ref.3, f32[4,512]{1,0:T(4,128)} %copy-done.11), custom_call_target="tpu_custom_call" | custom-call | flops 2147483648 | bytes 8388608 | tf_op jit(solution)/shard_map/own_tile/pallas_call | solution.py:286
  59.4 0.5 slice.72
  60.6 0.6 collective-permute-start.4
  61.2 0.6 fusion.5
  63.8 0.6 maximum_multiply_fusion.refs_1_
  64.4 0.6 pad_maximum_fusion.2
  65.1 9.0 %pair_tiles_0.1 = (f32[6,128,128]{2,1,0:T(8,128)}, f32[6,128,128]{2,1,0:T(8,128)}, f32[9,128,128]{2,1,0:T(8,128)}, f32[9,128,128]{2,1,0:T(8,128)}, bf16[256,4096]{1,0:T(8,128)(2,1)}, /*index=5*/bf16[4096,256]{1,0:T(8,128)(2,1)}) custom-call(s32[5]{0:T(128)} %stack.40.pos_ref.refs_0_, f32[3]{0:T(128)} %maximum_multiply_fusion.refs_1_, ...), custom_call_target="tpu_custom_call" | custom-call | flops 3221225472 | bytes 8388608 | tf_op jit(solution)/shard_map/pair_tiles_0/pallas_call | solution.py:319
  74.1 3.4 %collective-permute-start.8 = (f32[9,128,128]{2,1,0:T(8,128)}, f32[9,128,128]{2,1,0:T(8,128)S(1)}, u32[]{:S(2)}, u32[]{:S(2)}) collective-permute-start(f32[9,128,128]{2,1,0:T(8,128)} %get-tuple-element.43), channel_id=1, source_target_pairs={{0,2},{2,0},{5,7},{7,5},{8,10},{10,8},{13,15},{15,13},{16,18},{18,... | collective-permute-start | bytes 1769480 | tf_op jit(solution)/shard_map/ppermute | solution.py:237
  77.5 0.6 collective-permute-start.9
  78.1 0.6 pad_maximum_fusion.4
  78.7 10.1 %pair_tiles_1.1 = (f32[6,128,128]{2,1,0:T(8,128)}, f32[6,128,128]{2,1,0:T(8,128)}, f32[15,128,128]{2,1,0:T(8,128)}, f32[15,128,128]{2,1,0:T(8,128)}) custom-call(s32[5]{0:T(128)} %stack.40.pos_ref.refs_0_, f32[3]{0:T(128)} %maximum_multiply_fusion.refs_1_, bf16[512,4096]{1,0:T(8,128)(2,1)} %get-tuple-element.31.refs_2_, ...), custom_call_target="tpu_custom_call" | custom-call | flops 3221225472 | bytes 8388608 | tf_op jit(solution)/shard_map/pair_tiles_1/pallas_call | solution.py:319
  88.8 5.7 %collective-permute-done.9.got_c0 = f32[6,128,128]{2,1,0:T(8,128)S(1)} collective-permute-done((f32[6,128,128]{2,1,0:T(8,128)}, f32[6,128,128]{2,1,0:T(8,128)S(1)}, u32[]{:S(2)}, u32[]{:S(2)}) %collective-permute-start.9) | collective-permute-done | bytes 393248 | tf_op jit(solution)/shard_map/ppermute | solution.py:237
  94.5 0.8 copy-done.8
  95.2 3.4 %collective-permute-start.11 = (f32[15,128,128]{2,1,0:T(8,128)}, f32[15,128,128]{2,1,0:T(8,128)S(1)}, u32[]{:S(2)}, u32[]{:S(2)}) collective-permute-start(f32[15,128,128]{2,1,0:T(8,128)} %get-tuple-element.51), channel_id=1, source_target_pairs={{0,2},{2,0},{5,7},{7,5},{8,10},{10,8},{13,15},{15,13},{16,18},{18,... | collective-permute-start | bytes 2949128 | tf_op jit(solution)/shard_map/ppermute | solution.py:237
  98.6 0.6 collective-permute-start.10
  99.2 2.1 %diag_strips.1 = (f32[128,512]{1,0:T(8,128)}, f32[128,512]{1,0:T(8,128)}) custom-call(s32[5]{0:T(128)} %stack.40.pos_ref.refs_0_, f32[256,512]{1,0:T(8,128)} %get-tuple-element.30.keep_ref, f32[256,512]{1,0:T(8,128)} %copy-done.2), custom_call_target="tpu_custom_call" | custom-call | tf_op jit(solution)/shard_map/diag_strips/pallas_call | solution.py:336
  101.3 14.3 %collective-permute-done.10.got_c1 = f32[6,128,128]{2,1,0:T(8,128)S(1)} collective-permute-done((f32[6,128,128]{2,1,0:T(8,128)}, f32[6,128,128]{2,1,0:T(8,128)S(1)}, u32[]{:S(2)}, u32[]{:S(2)}) %collective-permute-start.10) | collective-permute-done | bytes 393248 | tf_op jit(solution)/shard_map/ppermute | solution.py:237
  115.7 0.7 copy-done.9
  116.4 0.4 copy-done
  116.7 4.8 %strips.1 = (f32[2,128,512]{2,1,0:T(8,128)}, f32[2,128,512]{2,1,0:T(8,128)}, f32[2,128,512]{2,1,0:T(8,128)}, f32[2,128,512]{2,1,0:T(8,128)}, f32[2,128,512]{2,1,0:T(8,128)}, /*index=5*/f32[2,128,512]{2,1,0:T(8,128)}) custom-call(s32[5]{0:T(128)} %stack.40.pos_ref.refs_0_, f32[6,128,128]{2,1,0:T(8,128)} %get-tuple-element.38.keep_c0, ...), custom_call_target="tpu_custom_call" | custom-call | tf_op jit(solution)/shard_map/strips/pallas_call | solution.py:349
  121.6 1.3 collective-permute-start.13
  122.9 4.4 %collective-permute-start.14 = (f32[2,128,512]{2,1,0:T(8,128)}, f32[2,128,512]{2,1,0:T(8,128)S(1)}, u32[]{:S(2)}, u32[]{:S(2)}) collective-permute-start(f32[2,128,512]{2,1,0:T(8,128)} %get-tuple-element.55), channel_id=1, source_target_pairs={{0,5},{2,7},{5,0},{7,2},{8,13},{10,15},{13,8},{15,10},{16,21},{18,... | collective-permute-start | bytes 1572872 | tf_op jit(solution)/shard_map/ppermute | solution.py:237
  127.3 4.7 %collective-permute-start.15 = (f32[2,128,512]{2,1,0:T(8,128)}, f32[2,128,512]{2,1,0:T(8,128)S(1)}, u32[]{:S(2)}, u32[]{:S(2)}) collective-permute-start(f32[2,128,512]{2,1,0:T(8,128)} %get-tuple-element.56), channel_id=1, source_target_pairs={{0,8},{2,10},{4,12},{6,14},{8,16},{9,1},{10,18},{11,3},{12,20},{13... | collective-permute-start | bytes 1572872 | tf_op jit(solution)/shard_map/ppermute | solution.py:237
  131.9 1.9 %collective-permute-start.16 = (f32[2,128,512]{2,1,0:T(8,128)}, f32[2,128,512]{2,1,0:T(8,128)S(1)}, u32[]{:S(2)}, u32[]{:S(2)}) collective-permute-start(f32[2,128,512]{2,1,0:T(8,128)} %get-tuple-element.57), channel_id=1, source_target_pairs={{0,9},{2,11},{4,13},{6,15},{8,17},{9,0},{10,19},{11,2},{12,21},{13... | collective-permute-start | bytes 1572872 | tf_op jit(solution)/shard_map/ppermute | solution.py:237
  133.9 4.1 %collective-permute-done.14.y_b = f32[2,128,512]{2,1,0:T(8,128)S(1)} collective-permute-done((f32[2,128,512]{2,1,0:T(8,128)}, f32[2,128,512]{2,1,0:T(8,128)S(1)}, u32[]{:S(2)}, u32[]{:S(2)}) %collective-permute-start.14) | collective-permute-done | bytes 524320 | tf_op jit(solution)/shard_map/ppermute | solution.py:237
  138.0 0.9 collective-permute-done.15.z_same
  138.9 5.6 %collective-permute-done.16.z_cross = f32[2,128,512]{2,1,0:T(8,128)S(1)} collective-permute-done((f32[2,128,512]{2,1,0:T(8,128)}, f32[2,128,512]{2,1,0:T(8,128)S(1)}, u32[]{:S(2)}, u32[]{:S(2)}) %collective-permute-start.16) | collective-permute-done | bytes 524320 | tf_op jit(solution)/shard_map/ppermute | solution.py:237
  144.5 0.8 copy-done.7
  145.3 3.3 %finish.1 = (bf16[1,3,128,512]{3,2,1,0:T(8,128)(2,1)}, bf16[1,2,128,512]{3,2,1,0:T(8,128)(2,1)}) custom-call(s32[5]{0:T(128)} %stack.40.pos_ref.refs_0_, s32[1,3]{1,0:T(1,128)} %offsets_ref.1, f32[128,512]{1,0:T(8,128)} %get-tuple-element.36.diag_mine, f32[128,512]{1,0:T(8,128)} %copy-done.10, f32[2,128,512]{2,1,0:T(8,128)} %get-tuple-element.52.own, ...), custom_call_target="tpu_custom_call" | custom-call | tf_op jit(solution)/shard_map/finish/pallas_call | solution.py:363
  (42 shorter events, 0.1 us)
Async XLA Ops:
  4.7 60.4 %collective-permute-start.2 = (bf16[4096,256]{1,0:T(8,128)(2,1)}, bf16[4096,256]{1,0:T(8,128)(2,1)}, u32[]{:S(2)}, u32[]{:S(2)}) collective-permute-start(bf16[4096,256]{1,0:T(8,128)(2,1)} %pad_maximum_fusion), channel_id=1, source_target_pairs={{1,5},{3,7},{4,0},{6,2},{9,13},{11,15},{12,8},{14,10},{17,21},{19,... | collective-permute-start | bytes 6291464 | tf_op jit(solution)/shard_map/ppermute | solution.py:237
  6.0 59.1 %collective-permute-start.3 = (bf16[4096,256]{1,0:T(8,128)(2,1)}, bf16[4096,256]{1,0:T(8,128)(2,1)}, u32[]{:S(2)}, u32[]{:S(2)}) collective-permute-start(bf16[4096,256]{1,0:T(8,128)(2,1)} %pad_maximum_fusion), channel_id=1, source_target_pairs={{1,9},{3,11},{5,13},{7,15},{8,0},{9,17},{10,2},{11,19},{12,4},{13,... | collective-permute-start | bytes 6291464 | tf_op jit(solution)/shard_map/ppermute | solution.py:237
  7.5 71.2 %collective-permute-start.6 = (bf16[4096,256]{1,0:T(8,128)(2,1)S(1)}, bf16[4096,256]{1,0:T(8,128)(2,1)}, u32[]{:S(2)}, u32[]{:S(2)}) collective-permute-start(bf16[4096,256]{1,0:T(8,128)(2,1)S(1)} %pad_maximum_fusion.1), channel_id=1, source_target_pairs={{1,5},{3,7},{4,0},{6,2},{9,13},{11,15},{12,8},{14,10},{17,21},{19,... | collective-permute-start | bytes 6291464 | tf_op jit(solution)/shard_map/ppermute | solution.py:237
  8.8 69.9 %collective-permute-start.7 = (bf16[4096,256]{1,0:T(8,128)(2,1)S(1)}, bf16[4096,256]{1,0:T(8,128)(2,1)}, u32[]{:S(2)}, u32[]{:S(2)}) collective-permute-start(bf16[4096,256]{1,0:T(8,128)(2,1)S(1)} %pad_maximum_fusion.1), channel_id=1, source_target_pairs={{1,9},{3,11},{5,13},{7,15},{8,0},{9,17},{10,2},{11,19},{12,4},{13,... | collective-permute-start | bytes 6291464 | tf_op jit(solution)/shard_map/ppermute | solution.py:237
  10.1 30.9 %copy-start.12 = (s32[1,3]{1,0:T(1,128)S(1)}, s32[1,3]{1,0:T(1,128)}, u32[]{:S(2)}) copy-start(s32[1,3]{1,0:T(1,128)} %offsets_ref.1) | copy-start | bytes 40
  43.3 7.0 %copy-start.11 = (f32[4,512]{1,0:T(4,128)}, f32[4,512]{1,0:T(4,128)S(1)}, u32[]{:S(2)}) copy-start(f32[4,512]{1,0:T(4,128)S(1)} %maximum_maximum_fusion.stat_ref) | copy-start | bytes 24580
  43.3 5.1 %collective-permute-start = (f32[4,512]{1,0:T(4,128)S(1)}, f32[4,512]{1,0:T(4,128)S(1)}, u32[]{:S(2)}, u32[]{:S(2)}) collective-permute-start(f32[4,512]{1,0:T(4,128)S(1)} %maximum_maximum_fusion.stat_ref), channel_id=1, source_target_pairs={{0,5},{2,7},{5,0},{7,2},{8,13},{10,15},{13,8},{15,10},{16,21},{18,... | collective-permute-start | bytes 24584 | tf_op jit(solution)/shard_map/ppermute | solution.py:237
  48.4 12.2 %collective-permute-start.1 = (f32[4,512]{1,0:T(4,128)S(1)}, f32[4,512]{1,0:T(4,128)S(1)}, u32[]{:S(2)}, u32[]{:S(2)}) collective-permute-start(f32[4,512]{1,0:T(4,128)S(1)} %maximum_maximum_fusion.stat_ref), channel_id=1, source_target_pairs={{0,9},{2,11},{4,13},{6,15},{8,17},{9,0},{10,19},{11,2},{12,21},{13... | collective-permute-start | bytes 24584 | tf_op jit(solution)/shard_map/ppermute | solution.py:237
  60.6 13.4 %collective-permute-start.4 = (f32[256,512]{1,0:T(8,128)}, f32[256,512]{1,0:T(8,128)S(1)}, u32[]{:S(2)}, u32[]{:S(2)}) collective-permute-start(f32[256,512]{1,0:T(8,128)} %get-tuple-element.34), channel_id=1, source_target_pairs={{0,2},{1,3},{2,0},{3,1},{4,6},{5,7},{6,4},{7,5},{8,10},{9,11},{10,... | collective-permute-start | bytes 1572872 | tf_op jit(solution)/shard_map/ppermute | solution.py:237
  74.0 14.8 %copy-start.2 = (f32[256,512]{1,0:T(8,128)}, f32[256,512]{1,0:T(8,128)S(1)}, u32[]{:S(2)}) copy-start(f32[256,512]{1,0:T(8,128)S(1)} %collective-permute-done.4.got_ref) | copy-start | bytes 1572868
  74.1 20.4 %collective-permute-start.8 = (f32[9,128,128]{2,1,0:T(8,128)}, f32[9,128,128]{2,1,0:T(8,128)S(1)}, u32[]{:S(2)}, u32[]{:S(2)}) collective-permute-start(f32[9,128,128]{2,1,0:T(8,128)} %get-tuple-element.43), channel_id=1, source_target_pairs={{0,2},{2,0},{5,7},{7,5},{8,10},{10,8},{13,15},{15,13},{16,18},{18,... | collective-permute-start | bytes 1769480 | tf_op jit(solution)/shard_map/ppermute | solution.py:237
  77.5 17.0 %collective-permute-start.9 = (f32[6,128,128]{2,1,0:T(8,128)}, f32[6,128,128]{2,1,0:T(8,128)S(1)}, u32[]{:S(2)}, u32[]{:S(2)}) collective-permute-start(f32[6,128,128]{2,1,0:T(8,128)} %get-tuple-element.44), channel_id=1, source_target_pairs={{0,2},{1,3},{2,0},{3,1},{4,6},{5,7},{6,4},{7,5},{8,10},{9,11},{10,... | collective-permute-start | bytes 1179656 | tf_op jit(solution)/shard_map/ppermute | solution.py:237
  94.5 0.8 copy-start.8
  94.5 21.2 %copy-start.1 = (f32[9,128,128]{2,1,0:T(8,128)}, f32[9,128,128]{2,1,0:T(8,128)S(1)}, u32[]{:S(2)}) copy-start(f32[9,128,128]{2,1,0:T(8,128)S(1)} %collective-permute-done.8.got_bd0) | copy-start | bytes 1769476
  95.2 20.4 %collective-permute-start.11 = (f32[15,128,128]{2,1,0:T(8,128)}, f32[15,128,128]{2,1,0:T(8,128)S(1)}, u32[]{:S(2)}, u32[]{:S(2)}) collective-permute-start(f32[15,128,128]{2,1,0:T(8,128)} %get-tuple-element.51), channel_id=1, source_target_pairs={{0,2},{2,0},{5,7},{7,5},{8,10},{10,8},{13,15},{15,13},{16,18},{18,... | collective-permute-start | bytes 2949128 | tf_op jit(solution)/shard_map/ppermute | solution.py:237
  98.6 17.0 %collective-permute-start.10 = (f32[6,128,128]{2,1,0:T(8,128)}, f32[6,128,128]{2,1,0:T(8,128)S(1)}, u32[]{:S(2)}, u32[]{:S(2)}) collective-permute-start(f32[6,128,128]{2,1,0:T(8,128)} %get-tuple-element.49), channel_id=1, source_target_pairs={{0,2},{1,3},{2,0},{3,1},{4,6},{5,7},{6,4},{7,5},{8,10},{9,11},{10,... | collective-permute-start | bytes 1179656 | tf_op jit(solution)/shard_map/ppermute | solution.py:237
  101.3 30.6 %collective-permute-start.5 = (f32[128,512]{1,0:T(8,128)}, f32[128,512]{1,0:T(8,128)S(1)}, u32[]{:S(2)}, u32[]{:S(2)}) collective-permute-start(f32[128,512]{1,0:T(8,128)} %get-tuple-element.37), channel_id=1, source_target_pairs={{0,1},{1,0},{2,3},{3,2},{4,5},{5,4},{6,7},{7,6},{8,9},{9,8},{10,11... | collective-permute-start | bytes 786440 | tf_op jit(solution)/shard_map/ppermute | solution.py:237
  115.6 0.7 copy-start.9
  115.6 1.1 copy-start
  121.6 12.3 %collective-permute-start.12 = (f32[2,128,512]{2,1,0:T(8,128)}, f32[2,128,512]{2,1,0:T(8,128)S(1)}, u32[]{:S(2)}, u32[]{:S(2)}) collective-permute-start(f32[2,128,512]{2,1,0:T(8,128)} %get-tuple-element.53), channel_id=1, source_target_pairs={{0,1},{1,0},{2,3},{3,2},{4,5},{5,4},{6,7},{7,6},{8,9},{9,8},{10,11... | collective-permute-start | bytes 1572872 | tf_op jit(solution)/shard_map/ppermute | solution.py:237
  121.6 12.3 %collective-permute-start.13 = (f32[2,128,512]{2,1,0:T(8,128)}, f32[2,128,512]{2,1,0:T(8,128)S(1)}, u32[]{:S(2)}, u32[]{:S(2)}) collective-permute-start(f32[2,128,512]{2,1,0:T(8,128)} %get-tuple-element.54), channel_id=1, source_target_pairs={{0,4},{2,6},{5,1},{7,3},{8,12},{10,14},{13,9},{15,11},{16,20},{18,... | collective-permute-start | bytes 1572872 | tf_op jit(solution)/shard_map/ppermute | solution.py:237
  122.9 15.1 %collective-permute-start.14 = (f32[2,128,512]{2,1,0:T(8,128)}, f32[2,128,512]{2,1,0:T(8,128)S(1)}, u32[]{:S(2)}, u32[]{:S(2)}) collective-permute-start(f32[2,128,512]{2,1,0:T(8,128)} %get-tuple-element.55), channel_id=1, source_target_pairs={{0,5},{2,7},{5,0},{7,2},{8,13},{10,15},{13,8},{15,10},{16,21},{18,... | collective-permute-start | bytes 1572872 | tf_op jit(solution)/shard_map/ppermute | solution.py:237
  127.3 11.6 %collective-permute-start.15 = (f32[2,128,512]{2,1,0:T(8,128)}, f32[2,128,512]{2,1,0:T(8,128)S(1)}, u32[]{:S(2)}, u32[]{:S(2)}) collective-permute-start(f32[2,128,512]{2,1,0:T(8,128)} %get-tuple-element.56), channel_id=1, source_target_pairs={{0,8},{2,10},{4,12},{6,14},{8,16},{9,1},{10,18},{11,3},{12,20},{13... | collective-permute-start | bytes 1572872 | tf_op jit(solution)/shard_map/ppermute | solution.py:237
  131.9 12.6 %copy-start.10 = (f32[128,512]{1,0:T(8,128)}, f32[128,512]{1,0:T(8,128)S(1)}, u32[]{:S(2)}) copy-start(f32[128,512]{1,0:T(8,128)S(1)} %collective-permute-done.5.diag_got) | copy-start | bytes 786436
  131.9 12.6 %collective-permute-start.16 = (f32[2,128,512]{2,1,0:T(8,128)}, f32[2,128,512]{2,1,0:T(8,128)S(1)}, u32[]{:S(2)}, u32[]{:S(2)}) collective-permute-start(f32[2,128,512]{2,1,0:T(8,128)} %get-tuple-element.57), channel_id=1, source_target_pairs={{0,9},{2,11},{4,13},{6,15},{8,17},{9,0},{10,19},{11,2},{12,21},{13... | collective-permute-start | bytes 1572872 | tf_op jit(solution)/shard_map/ppermute | solution.py:237
  133.9 10.6 %copy-start.3 = (f32[2,128,512]{2,1,0:T(8,128)}, f32[2,128,512]{2,1,0:T(8,128)S(1)}, u32[]{:S(2)}) copy-start(f32[2,128,512]{2,1,0:T(8,128)S(1)} %collective-permute-done.12.sib) | copy-start | bytes 1572868
  133.9 10.6 %copy-start.4 = (f32[2,128,512]{2,1,0:T(8,128)}, f32[2,128,512]{2,1,0:T(8,128)S(1)}, u32[]{:S(2)}) copy-start(f32[2,128,512]{2,1,0:T(8,128)S(1)} %collective-permute-done.13.y_a) | copy-start | bytes 1572868
  138.0 6.5 %copy-start.5 = (f32[2,128,512]{2,1,0:T(8,128)}, f32[2,128,512]{2,1,0:T(8,128)S(1)}, u32[]{:S(2)}) copy-start(f32[2,128,512]{2,1,0:T(8,128)S(1)} %collective-permute-done.14.y_b) | copy-start | bytes 1572868
  138.9 5.6 %copy-start.6 = (f32[2,128,512]{2,1,0:T(8,128)}, f32[2,128,512]{2,1,0:T(8,128)S(1)}, u32[]{:S(2)}) copy-start(f32[2,128,512]{2,1,0:T(8,128)S(1)} %collective-permute-done.15.z_same) | copy-start | bytes 1572868
  144.5 0.8 copy-start.7

commit v3 on v0

v3 whole, which is shorter than its diff:
```python
import jax
import jax.numpy as jnp
from jax import lax
from jax.experimental import pallas as pl
from jax.experimental.pallas import tpu as pltpu
from jax.sharding import PartitionSpec as P

SLOTS = 3
AXES = ("var", "samp")
F32 = jnp.float32
BF16 = jnp.bfloat16
VMEM = pl.BlockSpec(memory_space=pltpu.VMEM)
SMEM = pl.BlockSpec(memory_space=pltpu.SMEM)
SOME = pltpu.CompilerParams(vmem_limit_bytes=24 << 20)
C_TYPE, BD_TYPE = F32, BF16


def dot(a, b):
    return jnp.dot(a, b, preferred_element_type=F32)


def standardized(raw, stat_ref):
    return ((raw.astype(F32) - stat_ref[0:1, :]) * stat_ref[1:2, :]).astype(BF16)


def local_kernel(steps, x_ref, out_ref, center, total, square):
    step = pl.program_id(0)
    rows, width = x_ref.shape
    group = min(64, rows)

    @pl.when(step == 0)
    def _():
        center[...] = jnp.mean(x_ref[:group, :].astype(F32), axis=0, keepdims=True)
        total[...] = jnp.zeros_like(total)
        square[...] = jnp.zeros_like(square)

    middle = center[...]

    def add(i, sums):
        x = x_ref[pl.ds(pl.multiple_of(i * group, group), group), :].astype(F32) - middle
        x = x.reshape(group // 8, 8, width)
        return sums[0] + jnp.sum(x, axis=0), sums[1] + jnp.sum(x * x, axis=0)

    sums = lax.fori_loop(0, rows // group, add, (total[...], square[...]))
    total[...], square[...] = sums

    @pl.when(step == steps - 1)
    def _():
        count = float(rows * steps)
        shift = jnp.sum(total[...], axis=0, keepdims=True) * (1.0 / count)
        around = jnp.sum(square[...], axis=0, keepdims=True) - shift * shift * count
        out_ref[0:1, :] = middle + shift
        out_ref[1:2, :] = jnp.maximum(around, 0.0)


def stat_kernel(pos_ref, live_ref, offsets_ref, own_ref, sib_ref, far_ref, cross_ref, stat_ref):
    width = own_ref.shape[1]
    samples = pos_ref[4].astype(F32)

    def merged(values):
        return (values[0] + values[1]) + (values[2] + values[3])

    groups = (own_ref, sib_ref, far_ref, cross_ref)
    mean = merged([ref[0:1, :] for ref in groups]) * 0.25
    between = merged([jnp.square(ref[0:1, :] - mean) for ref in groups]) * (samples * 0.25)
    spread = (merged([ref[1:2, :] for ref in groups]) + between) / samples
    live = lax.broadcasted_iota(jnp.int32, (1, width), 1) < live_ref[0]
    stat_ref[0:1, :] = mean
    stat_ref[1:2, :] = jnp.where(live, lax.rsqrt(spread + 1e-05), 0.0)
    for step in (1, 2):
        listed = offsets_ref[0, 0] == step
        for slot in range(1, SLOTS):
            listed = jnp.logical_or(listed, offsets_ref[0, slot] == step)
        stat_ref[1 + step:2 + step, :] = jnp.full((1, width), jnp.where(listed, 1.0, 0.0), F32)


def own_kernel(pos_ref, x_ref, stat_ref, turned_ref, keep_ref, send_ref, acc):
    step = pl.program_id(0)
    z = standardized(x_ref[...], stat_ref)
    zt = z.T
    turned_ref[...] = zt
    part = dot(zt, z)

    @pl.when(step == 0)
    def _():
        acc[...] = part

    @pl.when(step > 0)
    def _():
        acc[...] += part

    @pl.when(step == pl.num_programs(0) - 1)
    def _():
        rows = keep_ref.shape[1]
        for far in range(2):
            for core, out in ((pos_ref[2], keep_ref), (1 - pos_ref[2], send_ref)):
                out[far] = acc[pl.ds(pl.multiple_of((2 * far + core) * rows, rows), rows), :]


def diag_kernel(pos_ref, keep_ref, got_ref, mine_ref, send_ref):
    mine_ref[...] = keep_ref[pos_ref[0]] + got_ref[pos_ref[0]]
    send_ref[...] = keep_ref[1 - pos_ref[0]] + got_ref[1 - pos_ref[0]]


def put_quarters(x, source, keep, send):
    half = keep.shape[-1]
    for out, near in ((keep, x), (send, 1 - x)):
        for index, (row, col) in enumerate(((near, near), (near, 1 - near), (1 - near, near))):
            rows = pl.ds(pl.multiple_of(row * half, half), half)
            cols = pl.ds(pl.multiple_of(col * half, half), half)
            out[index] = source[rows, cols].astype(out.dtype)


def far_kernel(pos_ref, turned_ref, w_ref, stat_ref, wstat_ref, keep_ref, send_ref, w_out, acc):
    step = pl.program_id(0)

    @pl.when(step == 0)
    def _():
        acc[...] = jnp.zeros_like(acc)

    w = standardized(w_ref[...], wstat_ref)
    w_out[...] = w
    acc[...] += dot(turned_ref[...], w)

    @pl.when(step == pl.num_programs(0) - 1)
    def _():
        listed = jnp.where(pos_ref[2] == 0, stat_ref[3:4, :], wstat_ref[3:4, :])
        acc[...] *= listed * (1.0 / pos_ref[4].astype(F32))
        put_quarters(pos_ref[0], acc, keep_ref, send_ref)


def near_kernel(pos_ref, turned_ref, y_ref, w_ref, stat_ref, ystat_ref, wstat_ref, keep_ref, send_ref, acc_b, acc_d):
    step = pl.program_id(0)

    @pl.when(pos_ref[1] == 1)
    def _():
        @pl.when(step == 0)
        def _():
            acc_b[...] = jnp.zeros_like(acc_b)
            acc_d[...] = jnp.zeros_like(acc_d)

        y = standardized(y_ref[...], ystat_ref)
        acc_b[...] += dot(turned_ref[...], y)
        acc_d[...] += dot(y.T, w_ref[...])

        @pl.when(step == pl.num_programs(0) - 1)
        def _():
            first = pos_ref[2] == 0
            share = 1.0 / pos_ref[4].astype(F32)
            acc_b[...] *= jnp.where(first, stat_ref[2:3, :], ystat_ref[2:3, :]) * share
            acc_d[...] *= jnp.where(first, ystat_ref[2:3, :], wstat_ref[2:3, :]) * share
            put_quarters(pos_ref[0], acc_b, keep_ref.at[0], send_ref.at[0])
            put_quarters(pos_ref[0], acc_d, keep_ref.at[1], send_ref.at[1])


def add_halves(x, keep, got, rows_out, cols_out):
    half = keep.shape[-1]
    here = pl.ds(pl.multiple_of(x * half, half), half)
    there = pl.ds(pl.multiple_of((1 - x) * half, half), half)
    corner = keep[0] + got[0].astype(F32)
    rows_out[:, here] = corner.astype(rows_out.dtype)
    rows_out[:, there] = (keep[1] + got[1].astype(F32)).astype(rows_out.dtype)
    cols_out[:, here] = corner.T.astype(cols_out.dtype)
    cols_out[:, there] = (keep[2] + got[2].astype(F32)).T.astype(cols_out.dtype)


def far_strips_kernel(pos_ref, keep, got, held, to_z):
    add_halves(pos_ref[0], keep, got, held, to_z)


def near_strips_kernel(pos_ref, keep, got, held, to_y, to_z):
    @pl.when(pos_ref[1] == 1)
    def _():
        add_halves(pos_ref[0], keep.at[0], got.at[0], held, to_y.at[0])
        add_halves(pos_ref[0], keep.at[1], got.at[1], to_y.at[1], to_z)


def combine_kernel(pos_ref, held_b, held_c, from_y, from_z_c, from_z_d, mine, sib):
    rows = mine.shape[1]
    for core, out in ((pos_ref[2], mine), (1 - pos_ref[2], sib)):
        at = pl.ds(pl.multiple_of(core * rows, rows), rows)
        out[1] = held_c[at, :] + from_z_c[at, :].astype(F32)

        @pl.when(pos_ref[1] == 1)
        def _():
            out[0] = held_b[at, :] + from_y[0, at, :].astype(F32)
            out[2] = from_y[1, at, :].astype(F32)

        @pl.when(pos_ref[1] == 0)
        def _():
            out[2] = from_z_d[at, :].astype(F32)


def finish_kernel(pos_ref, offsets_ref, diag_mine, diag_got, mine, sib, upper, mirror):
    active = pos_ref[1] == 1
    first_core = pos_ref[2] == 0
    even = pos_ref[3] == 0
    pick = jnp.where
    near = pick(active, mine[0], sib[0])
    far = mine[2] + sib[2]
    upper_1 = pick(even, near, far)
    upper_2 = pick(first_core, mine[1], sib[1])
    mirror[0, 0] = pick(even, far, near).astype(BF16)
    mirror[0, 1] = pick(first_core, sib[1], mine[1]).astype(BF16)
    self_tile = (diag_mine[...] + diag_got[...]) * (1.0 / pos_ref[4].astype(F32))
    for slot in range(SLOTS):
        offset = offsets_ref[0, slot]
        tile = pick(offset == 0, self_tile, pick(offset == 1, upper_1, pick(offset == 2, upper_2, 0.0)))
        upper[0, slot] = tile.astype(BF16)


def body(dosage, pair_offsets, live_counts):
    n_var = lax.axis_size("var")
    n_samp = lax.axis_size("samp")
    depth, width = dosage.shape
    half = width // 2
    strip = width // n_samp
    samples_all = depth * n_samp
    v = lax.axis_index("var")
    s = lax.axis_index("samp")
    x, core, odd = s // 2, s % 2, v % 2
    active = (core == odd).astype(jnp.int32)

    def at(var, samp):
        return var * n_samp + samp

    def active_on(var, samp):
        return var % 2 == samp % 2

    def send(value, pairs):
        return lax.ppermute(value, AXES, pairs)

    def shape(*dims, dtype=F32):
        return jax.ShapeDtypeStruct(dims, dtype)

    everyone = [(var, samp) for var in range(n_var) for samp in range(n_samp)]
    z_main = [(at(a, b), at(a - 2 if b % 2 == 0 else a + 2, b)) for a, b in everyone
              if 0 <= (a - 2 if b % 2 == 0 else a + 2) < n_var]
    y_main = [(at(a, b), at(a ^ 1, b)) for a, b in everyone if not active_on(a, b)]
    z_step = [(a, b, a + 2 if b % 2 == 0 else a - 2) for a, b in everyone]
    z_cross = [(at(a, b), at(t, b ^ 1)) for a, b, t in z_step if 0 <= t < n_var]
    z_cross_active = [(at(a, b), at(t, b ^ 1)) for a, b, t in z_step if 0 <= t < n_var and active_on(a, b)]
    y_cross = [(at(a, b), at(a ^ 1, b ^ 1)) for a, b in everyone if active_on(a, b)]
    across = [(at(a, b), at(a, b ^ 2)) for a, b in everyone]
    across_active = [(at(a, b), at(a, b ^ 2)) for a, b in everyone if active_on(a, b)]
    sibling = [(at(a, b), at(a, b ^ 1)) for a, b in everyone]

    w_raw, y_raw = send(dosage, z_main), send(dosage, y_main)

    pos = jnp.stack([x, active, core, odd, jnp.int32(samples_all)]).astype(jnp.int32)
    step_rows = min(1024, depth)
    steps = depth // step_rows
    wide = pl.BlockSpec((step_rows, width), lambda k: (k, 0))
    flat = pl.BlockSpec((width, step_rows), lambda k: (0, k))
    whole = lambda *dims: pl.BlockSpec(dims, lambda k: (0,) * len(dims))

    def call(kernel, name, grid, in_specs, out_specs, out_shape, scratch=(), flops=0, moved=0):
        return pl.pallas_call(
            kernel, grid=grid, in_specs=in_specs, out_specs=out_specs, out_shape=out_shape, scratch_shapes=scratch,
            compiler_params=SOME, name=name,
            cost_estimate=pl.CostEstimate(flops=flops, bytes_accessed=moved, transcendentals=0))

    bytes_block, tile_flops = 2 * depth * width, 2 * depth * width * width
    local = call(lambda *refs: local_kernel(steps, *refs), "local_stats", (steps,), [wide], whole(2, width), shape(2, width),
                 [pltpu.VMEM((1, width), F32)] + [pltpu.VMEM((8, width), F32)] * 2, 5 * depth * width, bytes_block)(dosage)
    others = [send(local, [(at(a, b), at(a, b ^ flip)) for a, b in everyone]) for flip in (1, 2, 3)]
    stat = call(stat_kernel, "stats", (), [SMEM] * 3 + [VMEM] * 4, VMEM, shape(4, width))(
        pos, live_counts, pair_offsets, local, *others)
    w_stat, y_stat = send(stat, z_cross), send(stat, y_cross)

    turned, diag_keep, diag_send = call(
        own_kernel, "own_tile", (steps,), [SMEM, wide, whole(4, width)],
        [flat, whole(2, strip, width), whole(2, strip, width)],
        [shape(width, depth, dtype=BF16), shape(2, strip, width), shape(2, strip, width)],
        [pltpu.VMEM((width, width), F32)], tile_flops, 2 * bytes_block)(pos, dosage, stat)
    diag_mine, diag_other = call(diag_kernel, "own_tile_strips", (), [SMEM, VMEM, VMEM], [VMEM] * 2, [shape(strip, width)] * 2)(
        pos, diag_keep, send(diag_send, sibling))
    diag_got = send(diag_other, across)

    keep_c, send_c, w = call(
        far_kernel, "far_tile", (steps,), [SMEM, flat, wide, whole(4, width), whole(4, width)],
        [whole(3, half, half)] * 2 + [wide],
        [shape(3, half, half), shape(3, half, half, dtype=C_TYPE), shape(depth, width, dtype=BF16)],
        [pltpu.VMEM((width, width), F32)], tile_flops, 3 * bytes_block)(pos, turned, w_raw, stat, w_stat)
    send_c, diag_got = lax.optimization_barrier((send_c, diag_got))
    got_c = send(send_c, across)

    keep_bd, send_bd = call(
        near_kernel, "near_tiles", (steps,), [SMEM, flat, wide, wide] + [whole(4, width)] * 3,
        [whole(2, 3, half, half)] * 2,
        [shape(2, 3, half, half), shape(2, 3, half, half, dtype=BD_TYPE)],
        [pltpu.VMEM((width, width), F32)] * 2, 2 * tile_flops, 3 * bytes_block)(pos, turned, y_raw, w, stat, y_stat, w_stat)
    got_bd = send(send_bd, across_active)

    held_c, to_z_c = call(far_strips_kernel, "far_strips", (), [SMEM] + [VMEM] * 2, [VMEM] * 2,
                          [shape(half, width), shape(half, width, dtype=C_TYPE)])(pos, keep_c, got_c)
    from_z_c = send(to_z_c, z_cross)
    held_b, to_y, to_z_d = call(
        near_strips_kernel, "near_strips", (), [SMEM] + [VMEM] * 2, [VMEM] * 3,
        [shape(half, width), shape(2, half, width, dtype=BD_TYPE), shape(half, width, dtype=BD_TYPE)])(pos, keep_bd, got_bd)
    from_y, from_z_d = send(to_y, y_cross), send(to_z_d, z_cross_active)

    mine, sib = call(combine_kernel, "combine", (), [SMEM] + [VMEM] * 5, [VMEM] * 2, [shape(3, strip, width)] * 2)(
        pos, held_b, held_c, from_y, from_z_c, from_z_d)
    return call(finish_kernel, "finish", (), [SMEM] * 2 + [VMEM] * 4, [VMEM] * 2,
                [shape(1, SLOTS, strip, width, dtype=BF16), shape(1, 2, strip, width, dtype=BF16)])(
        pos, pair_offsets, diag_mine, diag_got, mine, send(sib, sibling))


def solution(mesh):
    in_specs = (P("samp", "var"), P("var", None), P("var"))
    out_specs = (P("var", None, "samp", None), P("var", None, "samp", None))
    return jax.shard_map(body, mesh=mesh, in_specs=in_specs, out_specs=out_specs, check_vma=False)
```

time: 339 us -> 101 us (0.30)
  waiting for transfers between devices: 232 us -> 42.3 us
  other arithmetic: 33.6 us -> 0 us
  Pallas kernels: 0 us -> 23.9 us
  matrix products: 20.4 us -> 0 us
  between operations: 20.4 us -> 1.45 us
  starting transfers between devices: 9.37 us -> 28.1 us
  blocking collectives: 14.1 us -> 0 us
    ppermute x4 -> x15, waiting for transfers between devices: 178 us -> 42.3 us  [send(): return lax.ppermute(value, AXES, pairs)]
    reduce_scatter x1 -> x0, waiting for transfers between devices: 53.1 us -> none  [body(): shared = lax.psum_scatter(both, 'samp', scatter_dimension=2, tiled=True)]
    pallas_call x0 -> x10, Pallas kernels: none -> 23.9 us  [the longest x1 7.33 us: body(): call(near_kernel, 'near_tiles', (steps,), [SMEM, flat, wide, wide] + [who...]
    another operation x6 -> x0, other arithmetic: 21.3 us -> none  [the longest x2 12.7 us: body(): stacked = jnp.stack(fetched)]
    dot_general x3 -> x0, matrix products: 20.4 us -> none  [make_tile(): lax.dot_general(std_dose, partner, (((0,), (0,)), ((), ())), preferred_el...]
    ppermute x4 -> x15, starting transfers between devices: 9.34 us -> 28.1 us  [send(): return lax.ppermute(value, AXES, pairs)]
    psum x2 -> x0, blocking collectives: 14.1 us -> none  [the longest x1 8.33 us: body(): totals = lax.psum(jnp.sum(values, axis=0), 'samp')]
    reduce_sum x2 -> x0, other arithmetic: 6.14 us -> none  [the longest x1 3.34 us: body(): jnp.sum(centered * centered, axis=0)]
  transfers between devices with their start and end apart: 5 -> 15, of which waited for: 4 -> 10; matrix products, arithmetic and copies ran while one was open for 1% -> 0% of each run, Pallas kernels for 0% -> 22%
where the time goes in v3:
time: 101 us; the launch traced here: 100 us
  waiting for transfers between devices  42.3 us (42%)
  starting transfers between devices  28.1 us (28%)
  Pallas kernels  23.9 us (24%)
  local copies, waits for them, and re-layouts  4.46 us (4%)
  between operations  1.45 us (1%)
    ppermute x15, waiting for transfers between devices, send(): return lax.ppermute(value, AXES, pairs)  42.3 us
    ppermute x15, starting transfers between devices, send(): return lax.ppermute(value, AXES, pairs)  28.1 us
    pallas_call x1, Pallas kernels, body(): call(near_kernel, 'near_tiles', (steps,), [SMEM, flat, wide, wide] + [who...  7.33 us
    pallas_call x1, Pallas kernels, body(): call(far_kernel, 'far_tile', (steps,), [SMEM, flat, wide, whole(4, width)...  5.35 us
    unnamed x6, local copies, waits for them, and re-layouts  4.37 us
    pallas_call x1, Pallas kernels, body(): call(own_kernel, 'own_tile', (steps,), [SMEM, wide, whole(4, width)], [fl...  4.3 us
  transfers between devices with their start and end apart: 15, of which 10 were waited for; matrix products, arithmetic and copies ran while one was open for 0% of the time, Pallas kernels for 22%

profile of v3, /device:TPU:0, one launch (start us, length us, event | category | flops | bytes accessed | tf_op | source)
XLA Modules:
  0.0 100.3 jit_solution(14896522068418416720)
XLA Ops:
  0.6 1.3 %collective-permute-start.4 = (bf16[4096,512]{1,0:T(8,128)(2,1)}, bf16[4096,512]{1,0:T(8,128)(2,1)}, u32[]{:S(2)}, u32[]{:S(2)}) collective-permute-start(bf16[4096,512]{1,0:T(8,128)(2,1)} %x_ref.1), channel_id=1, source_target_pairs={{1,9},{3,11},{5,13},{7,15},{8,0},{9,17},{10,2},{11,19},{12,4},{13,... | collective-permute-start | bytes 12582920 | tf_op jit(solution)/shard_map/ppermute | solution.py:231
  1.9 1.3 %collective-permute-start.7 = (bf16[4096,512]{1,0:T(8,128)(2,1)}, bf16[4096,512]{1,0:T(8,128)(2,1)}, u32[]{:S(2)}, u32[]{:S(2)}) collective-permute-start(bf16[4096,512]{1,0:T(8,128)(2,1)} %x_ref.1), channel_id=1, source_target_pairs={{1,5},{3,7},{4,0},{6,2},{9,13},{11,15},{12,8},{14,10},{17,21},{19,... | collective-permute-start | bytes 12582920 | tf_op jit(solution)/shard_map/ppermute | solution.py:231
  3.2 0.0 copy-start
  3.2 2.2 %copy-done = bf16[4096,512]{1,0:T(8,128)(2,1)S(1)} copy-done((bf16[4096,512]{1,0:T(8,128)(2,1)S(1)}, bf16[4096,512]{1,0:T(8,128)(2,1)}, u32[]{:S(2)}) %copy-start) | copy-done | bytes 4194328
  5.4 0.0 copy-start.2
  5.4 1.9 %local_stats.1.own_ref = f32[2,512]{1,0:T(2,128)S(1)} custom-call(bf16[4096,512]{1,0:T(8,128)(2,1)S(1)} %copy-done), custom_call_target="tpu_custom_call" | custom-call | flops 10485760 | bytes 4194304 | tf_op jit(solution)/shard_map/local_stats/pallas_call | solution.py:264
  7.3 9.0 %collective-permute-start = (f32[2,512]{1,0:T(2,128)S(1)}, f32[2,512]{1,0:T(2,128)S(1)}, u32[]{:S(2)}, u32[]{:S(2)}) collective-permute-start(f32[2,512]{1,0:T(2,128)S(1)} %local_stats.1.own_ref), channel_id=1, source_target_pairs={{0,1},{1,0},{2,3},{3,2},{4,5},{5,4},{6,7},{7,6},{8,9},{9,8},{10,11... | collective-permute-start | bytes 12296 | tf_op jit(solution)/shard_map/ppermute | solution.py:231
  16.3 1.5 %collective-permute-start.1 = (f32[2,512]{1,0:T(2,128)S(1)}, f32[2,512]{1,0:T(2,128)S(1)}, u32[]{:S(2)}, u32[]{:S(2)}) collective-permute-start(f32[2,512]{1,0:T(2,128)S(1)} %local_stats.1.own_ref), channel_id=1, source_target_pairs={{0,2},{1,3},{2,0},{3,1},{4,6},{5,7},{6,4},{7,5},{8,10},{9,11},{10,... | collective-permute-start | bytes 12296 | tf_op jit(solution)/shard_map/ppermute | solution.py:231
  17.8 0.0 collective-permute-start.2
  18.5 0.1 stack.23.pos_ref
  18.6 0.0 collective-permute-done.sib_ref
  18.6 1.4 %collective-permute-done.1.far_ref = f32[2,512]{1,0:T(2,128)S(1)} collective-permute-done((f32[2,512]{1,0:T(2,128)S(1)}, f32[2,512]{1,0:T(2,128)S(1)}, u32[]{:S(2)}, u32[]{:S(2)}) %collective-permute-start.1) | collective-permute-done | bytes 4128 | tf_op jit(solution)/shard_map/ppermute | solution.py:231
  19.9 0.9 collective-permute-done.2.cross_ref
  20.9 0.0 copy-done.2
  20.9 0.6 stats.1.stat_ref
  21.5 0.0 copy-start.1
  21.5 2.2 %copy-done.1 = bf16[4096,512]{1,0:T(8,128)(2,1)S(1)} copy-done((bf16[4096,512]{1,0:T(8,128)(2,1)S(1)}, bf16[4096,512]{1,0:T(8,128)(2,1)}, u32[]{:S(2)}) %copy-start.1) | copy-done | bytes 4194328
  23.7 4.3 %own_tile.1 = (bf16[512,4096]{1,0:T(8,128)(2,1)S(1)}, f32[2,128,512]{2,1,0:T(8,128)S(1)}, f32[2,128,512]{2,1,0:T(8,128)S(1)}) custom-call(s32[5]{0:T(128)S(1)} %stack.23.pos_ref, bf16[4096,512]{1,0:T(8,128)(2,1)S(1)} %copy-done.1, f32[4,512]{1,0:T(4,128)S(1)} %stats.1.stat_ref), custom_call_target="tpu_custom_call" | custom-call | flops 2147483648 | bytes 8388608 | tf_op jit(solution)/shard_map/own_tile/pallas_call | solution.py:271
  28.0 0.3 collective-permute-start.3
  28.2 1.7 %collective-permute-done.3.got_ref = f32[2,128,512]{2,1,0:T(8,128)S(1)} collective-permute-done((f32[2,128,512]{2,1,0:T(8,128)S(1)}, f32[2,128,512]{2,1,0:T(8,128)S(1)}, u32[]{:S(2)}, u32[]{:S(2)}) %collective-permute-start.3) | collective-permute-done | bytes 524320 | tf_op jit(solution)/shard_map/ppermute | solution.py:231
  29.9 0.6 own_tile_strips.1
  30.5 0.6 collective-permute-start.6
  31.2 1.9 %collective-permute-start.5 = (f32[4,512]{1,0:T(4,128)S(1)}, f32[4,512]{1,0:T(4,128)S(1)}, u32[]{:S(2)}, u32[]{:S(2)}) collective-permute-start(f32[4,512]{1,0:T(4,128)S(1)} %stats.1.stat_ref), channel_id=1, source_target_pairs={{0,9},{2,11},{4,13},{6,15},{8,17},{9,0},{10,19},{11,2},{12,21},{13... | collective-permute-start | bytes 24584 | tf_op jit(solution)/shard_map/ppermute | solution.py:231
  33.1 1.9 %collective-permute-start.8 = (f32[4,512]{1,0:T(4,128)S(1)}, f32[4,512]{1,0:T(4,128)S(1)}, u32[]{:S(2)}, u32[]{:S(2)}) collective-permute-start(f32[4,512]{1,0:T(4,128)S(1)} %stats.1.stat_ref), channel_id=1, source_target_pairs={{0,5},{2,7},{5,0},{7,2},{8,13},{10,15},{13,8},{15,10},{16,21},{18,... | collective-permute-start | bytes 24584 | tf_op jit(solution)/shard_map/ppermute | solution.py:231
  35.0 1.3 %collective-permute-done.5.wstat_ref = f32[4,512]{1,0:T(4,128)S(1)} collective-permute-done((f32[4,512]{1,0:T(4,128)S(1)}, f32[4,512]{1,0:T(4,128)S(1)}, u32[]{:S(2)}, u32[]{:S(2)}) %collective-permute-start.5) | collective-permute-done | bytes 8224 | tf_op jit(solution)/shard_map/ppermute | solution.py:231
  36.3 16.2 %collective-permute-done.4.w_ref = bf16[4096,512]{1,0:T(8,128)(2,1)} collective-permute-done((bf16[4096,512]{1,0:T(8,128)(2,1)}, bf16[4096,512]{1,0:T(8,128)(2,1)}, u32[]{:S(2)}, u32[]{:S(2)}) %collective-permute-start.4) | collective-permute-done | bytes 4194336 | tf_op jit(solution)/shard_map/ppermute | solution.py:231
  52.4 5.3 %far_tile.1 = (f32[3,256,256]{2,1,0:T(8,128)S(1)}, f32[3,256,256]{2,1,0:T(8,128)S(1)}, bf16[4096,512]{1,0:T(8,128)(2,1)S(1)}) custom-call(s32[5]{0:T(128)S(1)} %stack.23.pos_ref, bf16[512,4096]{1,0:T(8,128)(2,1)S(1)} %get-tuple-element.24.turned_ref, bf16[4096,512]{1,0:T(8,128)(2,1)} %collective-permute-done.4.w_ref, f32[4,512]{1,0:T(4,128)S(1)} %stats.1.stat_ref, ...), custom_call_target="tpu_custom_call" | custom-call | flops 2147483648 | bytes 12582912 | tf_op jit(solution)/shard_map/far_tile/pallas_call | solution.py:280
  57.8 0.0 collective-permute-done.6.diag_got
  57.8 2.0 %collective-permute-start.10 = (f32[3,256,256]{2,1,0:T(8,128)S(1)}, f32[3,256,256]{2,1,0:T(8,128)S(1)}, u32[]{:S(2)}, u32[]{:S(2)}) collective-permute-start(f32[3,256,256]{2,1,0:T(8,128)S(1)} %get-tuple-element.33), channel_id=1, source_target_pairs={{0,2},{1,3},{2,0},{3,1},{4,6},{5,7},{6,4},{7,5},{8,10},{9,11},{10,... | collective-permute-start | bytes 2359304 | tf_op jit(solution)/shard_map/ppermute | solution.py:231
  59.8 0.0 collective-permute-done.8.ystat_ref
  59.8 0.0 collective-permute-done.7.y_ref
  59.8 7.3 %near_tiles.1 = (f32[2,3,256,256]{3,2,1,0:T(8,128)S(1)}, bf16[2,3,256,256]{3,2,1,0:T(8,128)(2,1)S(1)}) custom-call(s32[5]{0:T(128)S(1)} %stack.23.pos_ref, bf16[512,4096]{1,0:T(8,128)(2,1)S(1)} %get-tuple-element.24.turned_ref, bf16[4096,512]{1,0:T(8,128)(2,1)} %collective-permute-done.7.y_ref, bf16[4096,512]{1,0:T(8,128)(2,1)S(1)} %get-tuple-element.28.w_ref, ...), custom_call_target="tpu_custom_call" | custom-call | flops 4294967296 | bytes 12582912 | tf_op jit(solution)/shard_map/near_tiles/pallas_call | solution.py:288
  67.1 2.0 %collective-permute-start.9 = (bf16[2,3,256,256]{3,2,1,0:T(8,128)(2,1)S(1)}, bf16[2,3,256,256]{3,2,1,0:T(8,128)(2,1)S(1)}, u32[]{:S(2)}, u32[]{:S(2)}) collective-permute-start(bf16[2,3,256,256]{3,2,1,0:T(8,128)(2,1)S(1)} %get-tuple-element.30), channel_id=1, source_target_pairs={{0,2},{2,0},{5,7},{7,5},{8,10},{10,8},{13,15},{15,13},{16,18},{18,... | collective-permute-start | bytes 2359304 | tf_op jit(solution)/shard_map/ppermute | solution.py:231
  69.2 6.7 %collective-permute-done.10.got = f32[3,256,256]{2,1,0:T(8,128)S(1)} collective-permute-done((f32[3,256,256]{2,1,0:T(8,128)S(1)}, f32[3,256,256]{2,1,0:T(8,128)S(1)}, u32[]{:S(2)}, u32[]{:S(2)}) %collective-permute-start.10) | collective-permute-done | bytes 786464 | tf_op jit(solution)/shard_map/ppermute | solution.py:231
  75.8 0.7 far_strips.1
  76.6 2.1 %collective-permute-start.12 = (f32[256,512]{1,0:T(8,128)S(1)}, f32[256,512]{1,0:T(8,128)S(1)}, u32[]{:S(2)}, u32[]{:S(2)}) collective-permute-start(f32[256,512]{1,0:T(8,128)S(1)} %get-tuple-element.36), channel_id=1, source_target_pairs={{0,9},{2,11},{4,13},{6,15},{8,17},{9,0},{10,19},{11,2},{12,21},{13... | collective-permute-start | bytes 1572872 | tf_op jit(solution)/shard_map/ppermute | solution.py:231
  78.7 5.6 %collective-permute-done.9.got = bf16[2,3,256,256]{3,2,1,0:T(8,128)(2,1)S(1)} collective-permute-done((bf16[2,3,256,256]{3,2,1,0:T(8,128)(2,1)S(1)}, bf16[2,3,256,256]{3,2,1,0:T(8,128)(2,1)S(1)}, u32[]{:S(2)}, u32[]{:S(2)}) %collective-permute-start.9) | collective-permute-done | bytes 786464 | tf_op jit(solution)/shard_map/ppermute | solution.py:231
  84.3 0.8 near_strips.1
  85.1 2.8 %collective-permute-start.11 = (bf16[2,256,512]{2,1,0:T(8,128)(2,1)S(1)}, bf16[2,256,512]{2,1,0:T(8,128)(2,1)S(1)}, u32[]{:S(2)}, u32[]{:S(2)}) collective-permute-start(bf16[2,256,512]{2,1,0:T(8,128)(2,1)S(1)} %get-tuple-element.35), channel_id=1, source_target_pairs={{0,5},{2,7},{5,0},{7,2},{8,13},{10,15},{13,8},{15,10},{16,21},{18,... | collective-permute-start | bytes 1572872 | tf_op jit(solution)/shard_map/ppermute | solution.py:231
  87.9 1.3 %collective-permute-start.13 = (bf16[256,512]{1,0:T(8,128)(2,1)S(1)}, bf16[256,512]{1,0:T(8,128)(2,1)S(1)}, u32[]{:S(2)}, u32[]{:S(2)}) collective-permute-start(bf16[256,512]{1,0:T(8,128)(2,1)S(1)} %get-tuple-element.37), channel_id=1, source_target_pairs={{0,9},{2,11},{8,17},{10,19},{13,4},{15,6},{16,25},{18,27},{21,12},... | collective-permute-start | bytes 786440 | tf_op jit(solution)/shard_map/ppermute | solution.py:231
  89.2 3.9 %collective-permute-done.13.from_z_d = bf16[256,512]{1,0:T(8,128)(2,1)S(1)} collective-permute-done((bf16[256,512]{1,0:T(8,128)(2,1)S(1)}, bf16[256,512]{1,0:T(8,128)(2,1)S(1)}, u32[]{:S(2)}, u32[]{:S(2)}) %collective-permute-start.13) | collective-permute-done | bytes 262176 | tf_op jit(solution)/shard_map/ppermute | solution.py:231
  93.1 0.0 collective-permute-done.12.from_z_c
  93.1 2.5 %collective-permute-done.11.from_y = bf16[2,256,512]{2,1,0:T(8,128)(2,1)S(1)} collective-permute-done((bf16[2,256,512]{2,1,0:T(8,128)(2,1)S(1)}, bf16[2,256,512]{2,1,0:T(8,128)(2,1)S(1)}, u32[]{:S(2)}, u32[]{:S(2)}) %collective-permute-start.11) | collective-permute-done | bytes 524320 | tf_op jit(solution)/shard_map/ppermute | solution.py:231
  95.6 0.7 combine.1
  96.3 0.1 collective-permute-start.14
  96.4 2.3 %collective-permute-done.14.sib = f32[3,128,512]{2,1,0:T(8,128)S(1)} collective-permute-done((f32[3,128,512]{2,1,0:T(8,128)S(1)}, f32[3,128,512]{2,1,0:T(8,128)S(1)}, u32[]{:S(2)}, u32[]{:S(2)}) %collective-permute-start.14) | collective-permute-done | bytes 786464 | tf_op jit(solution)/shard_map/ppermute | solution.py:231
  98.6 1.7 %finish.1 = (bf16[1,3,128,512]{3,2,1,0:T(8,128)(2,1)}, bf16[1,2,128,512]{3,2,1,0:T(8,128)(2,1)}) custom-call(s32[5]{0:T(128)S(1)} %stack.23.pos_ref, s32[1,3]{1,0:T(1,128)S(1)} %copy-done.2, f32[128,512]{1,0:T(8,128)S(1)} %get-tuple-element.23.diag_mine, f32[128,512]{1,0:T(8,128)S(1)} %collective-permute-done.6.diag_got, ...), custom_call_target="tpu_custom_call" | custom-call | tf_op jit(solution)/shard_map/finish/pallas_call | solution.py:305
Async XLA Ops:
  0.6 51.8 %collective-permute-start.4 = (bf16[4096,512]{1,0:T(8,128)(2,1)}, bf16[4096,512]{1,0:T(8,128)(2,1)}, u32[]{:S(2)}, u32[]{:S(2)}) collective-permute-start(bf16[4096,512]{1,0:T(8,128)(2,1)} %x_ref.1), channel_id=1, source_target_pairs={{1,9},{3,11},{5,13},{7,15},{8,0},{9,17},{10,2},{11,19},{12,4},{13,... | collective-permute-start | bytes 12582920 | tf_op jit(solution)/shard_map/ppermute | solution.py:231
  1.9 57.9 %collective-permute-start.7 = (bf16[4096,512]{1,0:T(8,128)(2,1)}, bf16[4096,512]{1,0:T(8,128)(2,1)}, u32[]{:S(2)}, u32[]{:S(2)}) collective-permute-start(bf16[4096,512]{1,0:T(8,128)(2,1)} %x_ref.1), channel_id=1, source_target_pairs={{1,5},{3,7},{4,0},{6,2},{9,13},{11,15},{12,8},{14,10},{17,21},{19,... | collective-permute-start | bytes 12582920 | tf_op jit(solution)/shard_map/ppermute | solution.py:231
  3.2 2.2 %copy-start = (bf16[4096,512]{1,0:T(8,128)(2,1)S(1)}, bf16[4096,512]{1,0:T(8,128)(2,1)}, u32[]{:S(2)}) copy-start(bf16[4096,512]{1,0:T(8,128)(2,1)} %x_ref.1) | copy-start | bytes 12582916
  5.4 15.5 %copy-start.2 = (s32[1,3]{1,0:T(1,128)S(1)}, s32[1,3]{1,0:T(1,128)}, u32[]{:S(2)}) copy-start(s32[1,3]{1,0:T(1,128)} %offsets_ref.3) | copy-start | bytes 40
  7.3 11.3 %collective-permute-start = (f32[2,512]{1,0:T(2,128)S(1)}, f32[2,512]{1,0:T(2,128)S(1)}, u32[]{:S(2)}, u32[]{:S(2)}) collective-permute-start(f32[2,512]{1,0:T(2,128)S(1)} %local_stats.1.own_ref), channel_id=1, source_target_pairs={{0,1},{1,0},{2,3},{3,2},{4,5},{5,4},{6,7},{7,6},{8,9},{9,8},{10,11... | collective-permute-start | bytes 12296 | tf_op jit(solution)/shard_map/ppermute | solution.py:231
  16.3 3.6 %collective-permute-start.1 = (f32[2,512]{1,0:T(2,128)S(1)}, f32[2,512]{1,0:T(2,128)S(1)}, u32[]{:S(2)}, u32[]{:S(2)}) collective-permute-start(f32[2,512]{1,0:T(2,128)S(1)} %local_stats.1.own_ref), channel_id=1, source_target_pairs={{0,2},{1,3},{2,0},{3,1},{4,6},{5,7},{6,4},{7,5},{8,10},{9,11},{10,... | collective-permute-start | bytes 12296 | tf_op jit(solution)/shard_map/ppermute | solution.py:231
  17.8 3.1 %collective-permute-start.2 = (f32[2,512]{1,0:T(2,128)S(1)}, f32[2,512]{1,0:T(2,128)S(1)}, u32[]{:S(2)}, u32[]{:S(2)}) collective-permute-start(f32[2,512]{1,0:T(2,128)S(1)} %local_stats.1.own_ref), channel_id=1, source_target_pairs={{0,3},{1,2},{2,1},{3,0},{4,7},{5,6},{6,5},{7,4},{8,11},{9,10},{10,... | collective-permute-start | bytes 12296 | tf_op jit(solution)/shard_map/ppermute | solution.py:231
  21.5 2.2 %copy-start.1 = (bf16[4096,512]{1,0:T(8,128)(2,1)S(1)}, bf16[4096,512]{1,0:T(8,128)(2,1)}, u32[]{:S(2)}) copy-start(bf16[4096,512]{1,0:T(8,128)(2,1)} %x_ref.1) | copy-start | bytes 12582916
  28.0 2.0 %collective-permute-start.3 = (f32[2,128,512]{2,1,0:T(8,128)S(1)}, f32[2,128,512]{2,1,0:T(8,128)S(1)}, u32[]{:S(2)}, u32[]{:S(2)}) collective-permute-start(f32[2,128,512]{2,1,0:T(8,128)S(1)} %get-tuple-element.22), channel_id=1, source_target_pairs={{0,1},{1,0},{2,3},{3,2},{4,5},{5,4},{6,7},{7,6},{8,9},{9,8},{10,11... | collective-permute-start | bytes 1572872 | tf_op jit(solution)/shard_map/ppermute | solution.py:231
  30.5 27.3 %collective-permute-start.6 = (f32[128,512]{1,0:T(8,128)S(1)}, f32[128,512]{1,0:T(8,128)S(1)}, u32[]{:S(2)}, u32[]{:S(2)}) collective-permute-start(f32[128,512]{1,0:T(8,128)S(1)} %get-tuple-element.26), channel_id=1, source_target_pairs={{0,2},{1,3},{2,0},{3,1},{4,6},{5,7},{6,4},{7,5},{8,10},{9,11},{10,... | collective-permute-start | bytes 786440 | tf_op jit(solution)/shard_map/ppermute | solution.py:231
  31.2 5.1 %collective-permute-start.5 = (f32[4,512]{1,0:T(4,128)S(1)}, f32[4,512]{1,0:T(4,128)S(1)}, u32[]{:S(2)}, u32[]{:S(2)}) collective-permute-start(f32[4,512]{1,0:T(4,128)S(1)} %stats.1.stat_ref), channel_id=1, source_target_pairs={{0,9},{2,11},{4,13},{6,15},{8,17},{9,0},{10,19},{11,2},{12,21},{13... | collective-permute-start | bytes 24584 | tf_op jit(solution)/shard_map/ppermute | solution.py:231
  33.1 26.7 %collective-permute-start.8 = (f32[4,512]{1,0:T(4,128)S(1)}, f32[4,512]{1,0:T(4,128)S(1)}, u32[]{:S(2)}, u32[]{:S(2)}) collective-permute-start(f32[4,512]{1,0:T(4,128)S(1)} %stats.1.stat_ref), channel_id=1, source_target_pairs={{0,5},{2,7},{5,0},{7,2},{8,13},{10,15},{13,8},{15,10},{16,21},{18,... | collective-permute-start | bytes 24584 | tf_op jit(solution)/shard_map/ppermute | solution.py:231
  57.8 18.0 %collective-permute-start.10 = (f32[3,256,256]{2,1,0:T(8,128)S(1)}, f32[3,256,256]{2,1,0:T(8,128)S(1)}, u32[]{:S(2)}, u32[]{:S(2)}) collective-permute-start(f32[3,256,256]{2,1,0:T(8,128)S(1)} %get-tuple-element.33), channel_id=1, source_target_pairs={{0,2},{1,3},{2,0},{3,1},{4,6},{5,7},{6,4},{7,5},{8,10},{9,11},{10,... | collective-permute-start | bytes 2359304 | tf_op jit(solution)/shard_map/ppermute | solution.py:231
  67.1 17.1 %collective-permute-start.9 = (bf16[2,3,256,256]{3,2,1,0:T(8,128)(2,1)S(1)}, bf16[2,3,256,256]{3,2,1,0:T(8,128)(2,1)S(1)}, u32[]{:S(2)}, u32[]{:S(2)}) collective-permute-start(bf16[2,3,256,256]{3,2,1,0:T(8,128)(2,1)S(1)} %get-tuple-element.30), channel_id=1, source_target_pairs={{0,2},{2,0},{5,7},{7,5},{8,10},{10,8},{13,15},{15,13},{16,18},{18,... | collective-permute-start | bytes 2359304 | tf_op jit(solution)/shard_map/ppermute | solution.py:231
  76.6 16.5 %collective-permute-start.12 = (f32[256,512]{1,0:T(8,128)S(1)}, f32[256,512]{1,0:T(8,128)S(1)}, u32[]{:S(2)}, u32[]{:S(2)}) collective-permute-start(f32[256,512]{1,0:T(8,128)S(1)} %get-tuple-element.36), channel_id=1, source_target_pairs={{0,9},{2,11},{4,13},{6,15},{8,17},{9,0},{10,19},{11,2},{12,21},{13... | collective-permute-start | bytes 1572872 | tf_op jit(solution)/shard_map/ppermute | solution.py:231
  85.1 10.5 %collective-permute-start.11 = (bf16[2,256,512]{2,1,0:T(8,128)(2,1)S(1)}, bf16[2,256,512]{2,1,0:T(8,128)(2,1)S(1)}, u32[]{:S(2)}, u32[]{:S(2)}) collective-permute-start(bf16[2,256,512]{2,1,0:T(8,128)(2,1)S(1)} %get-tuple-element.35), channel_id=1, source_target_pairs={{0,5},{2,7},{5,0},{7,2},{8,13},{10,15},{13,8},{15,10},{16,21},{18,... | collective-permute-start | bytes 1572872 | tf_op jit(solution)/shard_map/ppermute | solution.py:231
  87.9 5.2 %collective-permute-start.13 = (bf16[256,512]{1,0:T(8,128)(2,1)S(1)}, bf16[256,512]{1,0:T(8,128)(2,1)S(1)}, u32[]{:S(2)}, u32[]{:S(2)}) collective-permute-start(bf16[256,512]{1,0:T(8,128)(2,1)S(1)} %get-tuple-element.37), channel_id=1, source_target_pairs={{0,9},{2,11},{8,17},{10,19},{13,4},{15,6},{16,25},{18,27},{21,12},... | collective-permute-start | bytes 786440 | tf_op jit(solution)/shard_map/ppermute | solution.py:231
  96.3 2.4 %collective-permute-start.14 = (f32[3,128,512]{2,1,0:T(8,128)S(1)}, f32[3,128,512]{2,1,0:T(8,128)S(1)}, u32[]{:S(2)}, u32[]{:S(2)}) collective-permute-start(f32[3,128,512]{2,1,0:T(8,128)S(1)} %get-tuple-element.39), channel_id=1, source_target_pairs={{0,1},{1,0},{2,3},{3,2},{4,5},{5,4},{6,7},{7,6},{8,9},{9,8},{10,11... | collective-permute-start | bytes 2359304 | tf_op jit(solution)/shard_map/ppermute | solution.py:231

commit v4 on v3

--- a/solution.py
+++ b/solution.py
@@ -12,7 +12,6 @@
 VMEM = pl.BlockSpec(memory_space=pltpu.VMEM)
 SMEM = pl.BlockSpec(memory_space=pltpu.SMEM)
 SOME = pltpu.CompilerParams(vmem_limit_bytes=24 << 20)
-C_TYPE, BD_TYPE = F32, BF16
 
 
 def dot(a, b):
@@ -23,10 +22,18 @@
     return ((raw.astype(F32) - stat_ref[0:1, :]) * stat_ref[1:2, :]).astype(BF16)
 
 
-def local_kernel(steps, x_ref, out_ref, center, total, square):
+def cut_kernel(part, x_ref, out_ref):
+    size = out_ref.shape[1] // 2
+    for half in range(2):
+        start = (2 * half + part) * size
+        out_ref[:, half * size:(half + 1) * size] = x_ref[:, start:start + size]
+
+
+def local_kernel(steps, x_ref, chunk_ref, out_ref, center, total, square):
     step = pl.program_id(0)
     rows, width = x_ref.shape
     group = min(64, rows)
+    cut_kernel(1, x_ref, chunk_ref)
 
     @pl.when(step == 0)
     def _():
@@ -53,7 +60,7 @@
         out_ref[1:2, :] = jnp.maximum(around, 0.0)
 
 
-def stat_kernel(pos_ref, live_ref, offsets_ref, own_ref, sib_ref, far_ref, cross_ref, stat_ref):
+def stat_kernel(pos_ref, live_ref, offsets_ref, own_ref, sib_ref, far_ref, cross_ref, stat_ref, chunked_ref):
     width = own_ref.shape[1]
     samples = pos_ref[4].astype(F32)
 
@@ -72,6 +79,8 @@
         for slot in range(1, SLOTS):
             listed = jnp.logical_or(listed, offsets_ref[0, slot] == step)
         stat_ref[1 + step:2 + step, :] = jnp.full((1, width), jnp.where(listed, 1.0, 0.0), F32)
+    for part in range(2):
+        cut_kernel(part, stat_ref, chunked_ref.at[:, part * (width // 2):(part + 1) * (width // 2)])
 
 
 def own_kernel(pos_ref, x_ref, stat_ref, turned_ref, keep_ref, send_ref, acc):
@@ -103,12 +112,12 @@
 
 
 def put_quarters(x, source, keep, send):
-    half = keep.shape[-1]
+    high, wide = keep.shape[1:]
     for out, near in ((keep, x), (send, 1 - x)):
         for index, (row, col) in enumerate(((near, near), (near, 1 - near), (1 - near, near))):
-            rows = pl.ds(pl.multiple_of(row * half, half), half)
-            cols = pl.ds(pl.multiple_of(col * half, half), half)
-            out[index] = source[rows, cols].astype(out.dtype)
+            rows = pl.ds(pl.multiple_of(row * high, high), high)
+            cols = pl.ds(pl.multiple_of(col * wide, wide), wide)
+            out[index] = source[rows, cols]
 
 
 def far_kernel(pos_ref, turned_ref, w_ref, stat_ref, wstat_ref, keep_ref, send_ref, w_out, acc):
@@ -129,66 +138,97 @@
         put_quarters(pos_ref[0], acc, keep_ref, send_ref)
 
 
-def near_kernel(pos_ref, turned_ref, y_ref, w_ref, stat_ref, ystat_ref, wstat_ref, keep_ref, send_ref, acc_b, acc_d):
+def near_kernel(pos_ref, turned_ref, y_ref, stat_ref, ystat_ref, keep_ref, send_ref, y_out, acc):
     step = pl.program_id(0)
 
     @pl.when(pos_ref[1] == 1)
     def _():
         @pl.when(step == 0)
         def _():
-            acc_b[...] = jnp.zeros_like(acc_b)
-            acc_d[...] = jnp.zeros_like(acc_d)
+            acc[...] = jnp.zeros_like(acc)
 
         y = standardized(y_ref[...], ystat_ref)
-        acc_b[...] += dot(turned_ref[...], y)
-        acc_d[...] += dot(y.T, w_ref[...])
+        acc[...] += dot(turned_ref[...], y)
+        y_out[...] = y.T
 
         @pl.when(step == pl.num_programs(0) - 1)
         def _():
-            first = pos_ref[2] == 0
-            share = 1.0 / pos_ref[4].astype(F32)
-            acc_b[...] *= jnp.where(first, stat_ref[2:3, :], ystat_ref[2:3, :]) * share
-            acc_d[...] *= jnp.where(first, ystat_ref[2:3, :], wstat_ref[2:3, :]) * share
-            put_quarters(pos_ref[0], acc_b, keep_ref.at[0], send_ref.at[0])
-            put_quarters(pos_ref[0], acc_d, keep_ref.at[1], send_ref.at[1])
+            listed = jnp.where(pos_ref[2] == 0, stat_ref[2:3, :], ystat_ref[2:3, :])
+            acc[...] *= listed * (1.0 / pos_ref[4].astype(F32))
+            put_quarters(pos_ref[0], acc, keep_ref, send_ref)
+
+
+def cross_kernel(pos_ref, y_ref, w0_ref, w1_ref, ystat_ref, wstat_ref, keep_ref, send_ref, acc_0, acc_1, acc):
+    step = pl.program_id(0)
+
+    @pl.when(pos_ref[1] == 1)
+    def _():
+        @pl.when(step == 0)
+        def _():
+            acc_0[...] = jnp.zeros_like(acc_0)
+            acc_1[...] = jnp.zeros_like(acc_1)
+
+        acc_0[...] += dot(y_ref[...], w0_ref[...])
+        acc_1[...] += dot(y_ref[...], w1_ref[...])
+
+        @pl.when(step == pl.num_programs(0) - 1)
+        def _():
+            listed = jnp.where(pos_ref[2] == 0, ystat_ref[2:3, :], wstat_ref[2:3, :]) * (1.0 / pos_ref[4].astype(F32))
+            size = acc_0.shape[1] // 2
+            for half in range(2):
+                for part, piece in enumerate((acc_0, acc_1)):
+                    start = (2 * half + part) * size
+                    acc[:, start:start + size] = piece[:, half * size:(half + 1) * size] * listed[:, start:start + size]
+            put_quarters(pos_ref[0], acc, keep_ref, send_ref)
 
 
 def add_halves(x, keep, got, rows_out, cols_out):
     half = keep.shape[-1]
     here = pl.ds(pl.multiple_of(x * half, half), half)
     there = pl.ds(pl.multiple_of((1 - x) * half, half), half)
-    corner = keep[0] + got[0].astype(F32)
-    rows_out[:, here] = corner.astype(rows_out.dtype)
-    rows_out[:, there] = (keep[1] + got[1].astype(F32)).astype(rows_out.dtype)
-    cols_out[:, here] = corner.T.astype(cols_out.dtype)
-    cols_out[:, there] = (keep[2] + got[2].astype(F32)).T.astype(cols_out.dtype)
-
-
-def far_strips_kernel(pos_ref, keep, got, held, to_z):
-    add_halves(pos_ref[0], keep, got, held, to_z)
-
-
-def near_strips_kernel(pos_ref, keep, got, held, to_y, to_z):
+    corner = keep[0] + got[0]
+    rows_out[:, here] = corner
+    rows_out[:, there] = keep[1] + got[1]
+    cols_out[:, here] = corner.T
+    cols_out[:, there] = (keep[2] + got[2]).T
+
+
+def far_strips_kernel(part, pos_ref, keep, got, rows_out, cols_out):
+    high, wide = keep.shape[1:]
+    x = pos_ref[0]
+    here = pl.ds(pl.multiple_of(x * high, high), high)
+    there = pl.ds(pl.multiple_of((1 - x) * high, high), high)
+    corner = keep[0] + got[0]
+    rows_out[:, pl.ds(pl.multiple_of(x * wide, wide), wide)] = corner
+    rows_out[:, pl.ds(pl.multiple_of((1 - x) * wide, wide), wide)] = keep[1] + got[1]
+    cols_out[:, here] = corner.T
+    cols_out[:, there] = (keep[2] + got[2]).T
+
+
+def near_strips_kernel(pos_ref, keep, got, rows_out, cols_out):
     @pl.when(pos_ref[1] == 1)
     def _():
-        add_halves(pos_ref[0], keep.at[0], got.at[0], held, to_y.at[0])
-        add_halves(pos_ref[0], keep.at[1], got.at[1], to_y.at[1], to_z)
-
-
-def combine_kernel(pos_ref, held_b, held_c, from_y, from_z_c, from_z_d, mine, sib):
+        add_halves(pos_ref[0], keep, got, rows_out, cols_out)
+
+
+def combine_kernel(pos_ref, held_b, held_c0, held_c1, from_y_b, from_y_d, from_z_c0, from_z_c1, from_z_d, mine, sib):
     rows = mine.shape[1]
     for core, out in ((pos_ref[2], mine), (1 - pos_ref[2], sib)):
         at = pl.ds(pl.multiple_of(core * rows, rows), rows)
-        out[1] = held_c[at, :] + from_z_c[at, :].astype(F32)
+        for part, held in enumerate((held_c0, held_c1)):
+            for half in range(2):
+                start = (2 * half + part) * rows
+                side = jnp.where(core == 0, from_z_c0[:, start:start + rows], from_z_c1[:, start:start + rows])
+                out[1, :, start:start + rows] = held[at, half * rows:(half + 1) * rows] + side
 
         @pl.when(pos_ref[1] == 1)
         def _():
-            out[0] = held_b[at, :] + from_y[0, at, :].astype(F32)
-            out[2] = from_y[1, at, :].astype(F32)
+            out[0] = held_b[at, :] + from_y_b[at, :]
+            out[2] = from_y_d[at, :]
 
         @pl.when(pos_ref[1] == 0)
         def _():
-            out[2] = from_z_d[at, :].astype(F32)
+            out[2] = from_z_d[at, :]
 
 
 def finish_kernel(pos_ref, offsets_ref, diag_mine, diag_got, mine, sib, upper, mirror):
@@ -245,7 +285,7 @@
     across_active = [(at(a, b), at(a, b ^ 2)) for a, b in everyone if active_on(a, b)]
     sibling = [(at(a, b), at(a, b ^ 1)) for a, b in everyone]
 
-    w_raw, y_raw = send(dosage, z_main), send(dosage, y_main)
+    y_raw = send(dosage, y_main)
 
     pos = jnp.stack([x, active, core, odd, jnp.int32(samples_all)]).astype(jnp.int32)
     step_rows = min(1024, depth)
@@ -254,19 +294,28 @@
     flat = pl.BlockSpec((width, step_rows), lambda k: (0, k))
     whole = lambda *dims: pl.BlockSpec(dims, lambda k: (0,) * len(dims))
 
+    bytes_block, tile_flops = 2 * depth * width, 2 * depth * width * width
+
     def call(kernel, name, grid, in_specs, out_specs, out_shape, scratch=(), flops=0, moved=0):
         return pl.pallas_call(
             kernel, grid=grid, in_specs=in_specs, out_specs=out_specs, out_shape=out_shape, scratch_shapes=scratch,
             compiler_params=SOME, name=name,
             cost_estimate=pl.CostEstimate(flops=flops, bytes_accessed=moved, transcendentals=0))
 
-    bytes_block, tile_flops = 2 * depth * width, 2 * depth * width * width
-    local = call(lambda *refs: local_kernel(steps, *refs), "local_stats", (steps,), [wide], whole(2, width), shape(2, width),
-                 [pltpu.VMEM((1, width), F32)] + [pltpu.VMEM((8, width), F32)] * 2, 5 * depth * width, bytes_block)(dosage)
+    part_block = pl.BlockSpec((step_rows, half), lambda k: (k, 0))
+    chunk_0 = call(lambda *refs: cut_kernel(0, *refs), "first_chunk", (steps,), [wide], part_block,
+                   shape(depth, half, dtype=BF16), moved=bytes_block)(dosage)
+    w_raw_0 = send(chunk_0, z_main)
+    chunk_1, local = call(lambda *refs: local_kernel(steps, *refs), "second_chunk_and_local_stats", (steps,), [wide],
+                          [part_block, whole(2, width)], [shape(depth, half, dtype=BF16), shape(2, width)],
+                          [pltpu.VMEM((1, width), F32)] + [pltpu.VMEM((8, width), F32)] * 2,
+                          5 * depth * width, 2 * bytes_block)(lax.optimization_barrier((dosage, chunk_0))[0])
     others = [send(local, [(at(a, b), at(a, b ^ flip)) for a, b in everyone]) for flip in (1, 2, 3)]
-    stat = call(stat_kernel, "stats", (), [SMEM] * 3 + [VMEM] * 4, VMEM, shape(4, width))(
+    stat, chunked = call(stat_kernel, "stats", (), [SMEM] * 3 + [VMEM] * 4, [VMEM] * 2, [shape(4, width)] * 2)(
         pos, live_counts, pair_offsets, local, *others)
-    w_stat, y_stat = send(stat, z_cross), send(stat, y_cross)
+    chunk_1, stat = lax.optimization_barrier((chunk_1, stat))
+    w_raw_1 = send(chunk_1, z_main)
+    w_stat, y_stat = send(chunked, z_cross), send(stat, y_cross)
 
     turned, diag_keep, diag_send = call(
         own_kernel, "own_tile", (steps,), [SMEM, wide, whole(4, width)],
@@ -277,31 +326,51 @@
         pos, diag_keep, send(diag_send, sibling))
     diag_got = send(diag_other, across)
 
-    keep_c, send_c, w = call(
-        far_kernel, "far_tile", (steps,), [SMEM, flat, wide, whole(4, width), whole(4, width)],
-        [whole(3, half, half)] * 2 + [wide],
-        [shape(3, half, half), shape(3, half, half, dtype=C_TYPE), shape(depth, width, dtype=BF16)],
-        [pltpu.VMEM((width, width), F32)], tile_flops, 3 * bytes_block)(pos, turned, w_raw, stat, w_stat)
-    send_c, diag_got = lax.optimization_barrier((send_c, diag_got))
-    got_c = send(send_c, across)
-
-    keep_bd, send_bd = call(
-        near_kernel, "near_tiles", (steps,), [SMEM, flat, wide, wide] + [whole(4, width)] * 3,
-        [whole(2, 3, half, half)] * 2,
-        [shape(2, 3, half, half), shape(2, 3, half, half, dtype=BD_TYPE)],
-        [pltpu.VMEM((width, width), F32)] * 2, 2 * tile_flops, 3 * bytes_block)(pos, turned, y_raw, w, stat, y_stat, w_stat)
-    got_bd = send(send_bd, across_active)
-
-    held_c, to_z_c = call(far_strips_kernel, "far_strips", (), [SMEM] + [VMEM] * 2, [VMEM] * 2,
-                          [shape(half, width), shape(half, width, dtype=C_TYPE)])(pos, keep_c, got_c)
-    from_z_c = send(to_z_c, z_cross)
-    held_b, to_y, to_z_d = call(
-        near_strips_kernel, "near_strips", (), [SMEM] + [VMEM] * 2, [VMEM] * 3,
-        [shape(half, width), shape(2, half, width, dtype=BD_TYPE), shape(half, width, dtype=BD_TYPE)])(pos, keep_bd, got_bd)
-    from_y, from_z_d = send(to_y, y_cross), send(to_z_d, z_cross_active)
-
-    mine, sib = call(combine_kernel, "combine", (), [SMEM] + [VMEM] * 5, [VMEM] * 2, [shape(3, strip, width)] * 2)(
-        pos, held_b, held_c, from_y, from_z_c, from_z_d)
+    def far(part, w_raw):
+        stats = pl.BlockSpec((4, half), lambda k: (0, part))
+        return call(
+            far_kernel, f"far_tile_{part}", (steps,), [SMEM, flat, part_block, stats, stats],
+            [whole(3, half, strip)] * 2 + [part_block],
+            [shape(3, half, strip)] * 2 + [shape(depth, half, dtype=BF16)],
+            [pltpu.VMEM((width, half), F32)], tile_flops // 2, 2 * bytes_block)(pos, turned, w_raw, chunked, w_stat)
+
+    def far_strips(part, keep, got):
+        return call(lambda *refs: far_strips_kernel(part, *refs), f"far_strips_{part}", (), [SMEM] + [VMEM] * 2, [VMEM] * 2,
+                    [shape(half, half), shape(strip, width)])(pos, keep, got)
+
+    def near_strips(name, keep, got):
+        return call(near_strips_kernel, name, (), [SMEM] + [VMEM] * 2, [VMEM] * 2, [shape(half, width)] * 2)(pos, keep, got)
+
+    stats, quarters = whole(4, width), [whole(3, half, half)] * 2
+    keep_c0, send_c0, w_0 = far(0, w_raw_0)
+    send_c0, diag_got = lax.optimization_barrier((send_c0, diag_got))
+    got_c0 = send(send_c0, across)
+    keep_b, send_b, y = call(
+        near_kernel, "near_tile", (steps,), [SMEM, flat, wide, stats, stats], quarters + [flat],
+        [shape(3, half, half)] * 2 + [shape(width, depth, dtype=BF16)],
+        [pltpu.VMEM((width, width), F32)], tile_flops, 3 * bytes_block)(pos, turned, y_raw, stat, y_stat)
+    send_b, got_c0 = lax.optimization_barrier((send_b, got_c0))
+    w_raw_1, send_b = lax.optimization_barrier((w_raw_1, send_b))
+    got_b = send(send_b, across_active)
+    held_c0, to_z_c0 = far_strips(0, keep_c0, got_c0)
+    keep_c1, send_c1, w_1 = far(1, w_raw_1)
+    keep_d, send_d = call(
+        cross_kernel, "cross_tile", (steps,), [SMEM, flat, part_block, part_block, stats, stats], quarters,
+        [shape(3, half, half)] * 2, [pltpu.VMEM((width, half), F32)] * 2 + [pltpu.VMEM((width, width), F32)],
+        tile_flops, 2 * bytes_block)(pos, y, w_0, w_1, y_stat, w_stat)
+    send_d, send_c1, to_z_c0, got_b = lax.optimization_barrier((send_d, send_c1, to_z_c0, got_b))
+    from_z_c0 = send(to_z_c0, z_cross)
+    got_d = send(send_d, across_active)
+    got_c1 = send(send_c1, across)
+    held_b, to_y_b = near_strips("near_strips", keep_b, got_b)
+    from_y_b = send(to_y_b, y_cross)
+    to_y_d, to_z_d = near_strips("cross_strips", keep_d, got_d)
+    from_y_d, from_z_d = send(to_y_d, y_cross), send(to_z_d, z_cross_active)
+    held_c1, to_z_c1 = far_strips(1, keep_c1, got_c1)
+    from_z_c1 = send(to_z_c1, z_cross)
+
+    mine, sib = call(combine_kernel, "combine", (), [SMEM] + [VMEM] * 8, [VMEM] * 2, [shape(3, strip, width)] * 2)(
+        pos, held_b, held_c0, held_c1, from_y_b, from_y_d, from_z_c0, from_z_c1, from_z_d)
     return call(finish_kernel, "finish", (), [SMEM] * 2 + [VMEM] * 4, [VMEM] * 2,
                 [shape(1, SLOTS, strip, width, dtype=BF16), shape(1, 2, strip, width, dtype=BF16)])(
         pos, pair_offsets, diag_mine, diag_got, mine, send(sib, sibling))

time: 101 us -> 111 us (1.099)
  starting transfers between devices: 28.1 us -> 40.9 us
  waiting for transfers between devices: 42.3 us -> 31 us
  Pallas kernels: 23.9 us -> 30.6 us
  local copies, waits for them, and re-layouts: 4.46 us -> 5.83 us
    ppermute x15 -> x20, starting transfers between devices: 28.1 us -> 40.9 us  [send(): return lax.ppermute(value, AXES, pairs)]
    ppermute x15 -> x20, waiting for transfers between devices: 42.3 us -> 31 us  [send(): return lax.ppermute(value, AXES, pairs)]
    pallas_call x7 -> x12, Pallas kernels: 17.4 us -> 24.1 us  [the longest x2 5.93 us: far(): call(far_kernel, f'far_tile_{part}', (steps,), [SMEM, flat, part_block, s...]
    unnamed x6 -> x8, local copies, waits for them, and re-layouts: 4.37 us -> 5.75 us
  transfers between devices with their start and end apart: 15 -> 20, of which waited for: 10 -> 12; matrix products, arithmetic and copies ran while one was open for 0% -> 0% of each run, Pallas kernels for 22% -> 26%
where the time goes in v4:
time: 111 us; the launch traced here: 110 us
  starting transfers between devices  40.9 us (37%)
  waiting for transfers between devices  31 us (28%)
  Pallas kernels  30.6 us (28%)
  local copies, waits for them, and re-layouts  5.83 us (5%)
  between operations  1.55 us (1%)
    ppermute x20, starting transfers between devices, send(): return lax.ppermute(value, AXES, pairs)  40.9 us
    ppermute x20, waiting for transfers between devices, send(): return lax.ppermute(value, AXES, pairs)  31 us
    pallas_call x2, Pallas kernels, far(): call(far_kernel, f'far_tile_{part}', (steps,), [SMEM, flat, part_block, s...  5.93 us
    unnamed x8, local copies, waits for them, and re-layouts  5.75 us
    pallas_call x1, Pallas kernels, body(): call(near_kernel, 'near_tile', (steps,), [SMEM, flat, wide, stats, stats]...  5.58 us
    pallas_call x1, Pallas kernels, body(): call(own_kernel, 'own_tile', (steps,), [SMEM, wide, whole(4, width)], [fl...  4.3 us
    pallas_call x1, Pallas kernels, body(): call(cross_kernel, 'cross_tile', (steps,), [SMEM, flat, part_block, part_...  4.07 us
    pallas_call x1, Pallas kernels, body(): call(lambda *refs: local_kernel(steps, *refs), 'second_chunk_and_local_st...  2.25 us
  transfers between devices with their start and end apart: 20, of which 12 were waited for; matrix products, arithmetic and copies ran while one was open for 0% of the time, Pallas kernels for 26%

profile of v4, /device:TPU:0, one launch (start us, length us, event | category | flops | bytes accessed | tf_op | source)
XLA Modules:
  0.0 110.0 jit_solution(2002058954063409195)
XLA Ops:
  0.6 1.3 %collective-permute-start.7 = (bf16[4096,512]{1,0:T(8,128)(2,1)}, bf16[4096,512]{1,0:T(8,128)(2,1)}, u32[]{:S(2)}, u32[]{:S(2)}) collective-permute-start(bf16[4096,512]{1,0:T(8,128)(2,1)} %x_ref.1), channel_id=1, source_target_pairs={{1,5},{3,7},{4,0},{6,2},{9,13},{11,15},{12,8},{14,10},{17,21},{19,... | collective-permute-start | bytes 12582920 | tf_op jit(solution)/shard_map/ppermute | solution.py:271
  1.9 2.2 %copy-done = bf16[4096,512]{1,0:T(8,128)(2,1)S(1)} copy-done((bf16[4096,512]{1,0:T(8,128)(2,1)S(1)}, bf16[4096,512]{1,0:T(8,128)(2,1)}, u32[]{:S(2)}) %copy-start) | copy-done | bytes 4194328
  4.1 2.1 %first_chunk.1 = bf16[4096,256]{1,0:T(8,128)(2,1)} custom-call(bf16[4096,512]{1,0:T(8,128)(2,1)S(1)} %copy-done), custom_call_target="tpu_custom_call" | custom-call | bytes 4194304 | tf_op jit(solution)/shard_map/first_chunk/pallas_call | solution.py:306
  6.2 1.4 %collective-permute-start.4 = (bf16[4096,256]{1,0:T(8,128)(2,1)}, bf16[4096,256]{1,0:T(8,128)(2,1)S(1)}, u32[]{:S(2)}, u32[]{:S(2)}) collective-permute-start(bf16[4096,256]{1,0:T(8,128)(2,1)} %first_chunk.1), channel_id=1, source_target_pairs={{1,9},{3,11},{5,13},{7,15},{8,0},{9,17},{10,2},{11,19},{12,4},{13,... | collective-permute-start | bytes 6291464 | tf_op jit(solution)/shard_map/ppermute | solution.py:271
  7.6 2.2 %second_chunk_and_local_stats.1 = (bf16[4096,256]{1,0:T(8,128)(2,1)S(1)}, f32[2,512]{1,0:T(2,128)S(1)}) custom-call(bf16[4096,512]{1,0:T(8,128)(2,1)S(1)} %copy-done), custom_call_target="tpu_custom_call" | custom-call | flops 10485760 | bytes 8388608 | tf_op jit(solution)/shard_map/second_chunk_and_local_stats/pallas_call | solution.py:309
  9.9 1.4 %copy-done.3 = bf16[4096,256]{1,0:T(8,128)(2,1)} copy-done((bf16[4096,256]{1,0:T(8,128)(2,1)}, bf16[4096,256]{1,0:T(8,128)(2,1)S(1)}, u32[]{:S(2)}) %copy-start.3) | copy-done | bytes 2097176
  11.3 7.1 %collective-permute-start = (f32[2,512]{1,0:T(2,128)S(1)}, f32[2,512]{1,0:T(2,128)S(1)}, u32[]{:S(2)}, u32[]{:S(2)}) collective-permute-start(f32[2,512]{1,0:T(2,128)S(1)} %get-tuple-element.47.own_ref), channel_id=1, source_target_pairs={{0,1},{1,0},{2,3},{3,2},{4,5},{5,4},{6,7},{7,6},{8,9},{9,8},{10,11... | collective-permute-start | bytes 12296 | tf_op jit(solution)/shard_map/ppermute | solution.py:271
  18.4 1.5 %collective-permute-start.1 = (f32[2,512]{1,0:T(2,128)S(1)}, f32[2,512]{1,0:T(2,128)S(1)}, u32[]{:S(2)}, u32[]{:S(2)}) collective-permute-start(f32[2,512]{1,0:T(2,128)S(1)} %get-tuple-element.47.own_ref), channel_id=1, source_target_pairs={{0,2},{1,3},{2,0},{3,1},{4,6},{5,7},{6,4},{7,5},{8,10},{9,11},{10,... | collective-permute-start | bytes 12296 | tf_op jit(solution)/shard_map/ppermute | solution.py:271
  20.5 0.1 stack.23.pos_ref.refs_0_
  20.6 1.4 %collective-permute-done.1.far_ref = f32[2,512]{1,0:T(2,128)S(1)} collective-permute-done((f32[2,512]{1,0:T(2,128)S(1)}, f32[2,512]{1,0:T(2,128)S(1)}, u32[]{:S(2)}, u32[]{:S(2)}) %collective-permute-start.1) | collective-permute-done | bytes 4128 | tf_op jit(solution)/shard_map/ppermute | solution.py:271
  22.0 0.9 collective-permute-done.2.cross_ref
  22.9 0.6 stats.1
  23.5 1.3 %collective-permute-start.9 = (bf16[4096,256]{1,0:T(8,128)(2,1)}, bf16[4096,256]{1,0:T(8,128)(2,1)S(1)}, u32[]{:S(2)}, u32[]{:S(2)}) collective-permute-start(bf16[4096,256]{1,0:T(8,128)(2,1)} %copy-done.3), channel_id=1, source_target_pairs={{1,9},{3,11},{5,13},{7,15},{8,0},{9,17},{10,2},{11,19},{12,4},{13,... | collective-permute-start | bytes 6291464 | tf_op jit(solution)/shard_map/ppermute | solution.py:271
  24.8 2.2 %copy-done.1 = bf16[4096,512]{1,0:T(8,128)(2,1)S(1)} copy-done((bf16[4096,512]{1,0:T(8,128)(2,1)S(1)}, bf16[4096,512]{1,0:T(8,128)(2,1)}, u32[]{:S(2)}) %copy-start.1) | copy-done | bytes 4194328
  27.0 4.3 %own_tile.1 = (bf16[512,4096]{1,0:T(8,128)(2,1)S(1)}, f32[2,128,512]{2,1,0:T(8,128)S(1)}, f32[2,128,512]{2,1,0:T(8,128)S(1)}) custom-call(s32[5]{0:T(128)S(1)} %stack.23.pos_ref.refs_0_, bf16[4096,512]{1,0:T(8,128)(2,1)S(1)} %copy-done.1, f32[4,512]{1,0:T(4,128)S(1)} %get-tuple-element.49.stat_ref), custom_call_target="tpu_custom_call" | custom-call | flops 2147483648 | bytes 8388608 | tf_op jit(solution)/shard_map/own_tile/pallas_call | solution.py:320
  31.3 2.1 %collective-permute-start.3 = (f32[2,128,512]{2,1,0:T(8,128)S(1)}, f32[2,128,512]{2,1,0:T(8,128)S(1)}, u32[]{:S(2)}, u32[]{:S(2)}) collective-permute-start(f32[2,128,512]{2,1,0:T(8,128)S(1)} %get-tuple-element.51), channel_id=1, source_target_pairs={{0,1},{1,0},{2,3},{3,2},{4,5},{5,4},{6,7},{7,6},{8,9},{9,8},{10,11... | collective-permute-start | bytes 1572872 | tf_op jit(solution)/shard_map/ppermute | solution.py:271
  33.4 1.5 %collective-permute-done.3.got_ref = f32[2,128,512]{2,1,0:T(8,128)S(1)} collective-permute-done((f32[2,128,512]{2,1,0:T(8,128)S(1)}, f32[2,128,512]{2,1,0:T(8,128)S(1)}, u32[]{:S(2)}, u32[]{:S(2)}) %collective-permute-start.3) | collective-permute-done | bytes 524320 | tf_op jit(solution)/shard_map/ppermute | solution.py:271
  34.9 0.6 own_tile_strips.1
  35.5 0.8 collective-permute-start.6
  36.3 3.0 %collective-permute-start.5 = (f32[4,512]{1,0:T(4,128)S(1)}, f32[4,512]{1,0:T(4,128)S(1)}, u32[]{:S(2)}, u32[]{:S(2)}) collective-permute-start(f32[4,512]{1,0:T(4,128)S(1)} %get-tuple-element.54.stat_ref), channel_id=1, source_target_pairs={{0,9},{2,11},{4,13},{6,15},{8,17},{9,0},{10,19},{11,2},{12,21},{13... | collective-permute-start | bytes 24584 | tf_op jit(solution)/shard_map/ppermute | solution.py:271
  39.4 2.1 %collective-permute-done.5.wstat_ref = f32[4,512]{1,0:T(4,128)S(1)} collective-permute-done((f32[4,512]{1,0:T(4,128)S(1)}, f32[4,512]{1,0:T(4,128)S(1)}, u32[]{:S(2)}, u32[]{:S(2)}) %collective-permute-start.5) | collective-permute-done | bytes 8224 | tf_op jit(solution)/shard_map/ppermute | solution.py:271
  41.4 3.0 %far_tile_0.1 = (f32[3,256,128]{2,1,0:T(8,128)S(1)}, f32[3,256,128]{2,1,0:T(8,128)S(1)}, bf16[4096,256]{1,0:T(8,128)(2,1)S(1)}) custom-call(s32[5]{0:T(128)S(1)} %stack.23.pos_ref.refs_0_, bf16[512,4096]{1,0:T(8,128)(2,1)S(1)} %get-tuple-element.53.turned_ref, bf16[4096,256]{1,0:T(8,128)(2,1)S(1)} %collective-permute-done.4.w_ref, ...), custom_call_target="tpu_custom_call" | custom-call | flops 1073741824 | bytes 8388608 | tf_op jit(solution)/shard_map/far_tile_0/pallas_call | solution.py:331
  44.4 1.4 %collective-permute-start.10 = (f32[3,256,128]{2,1,0:T(8,128)S(1)}, f32[3,256,128]{2,1,0:T(8,128)S(1)}, u32[]{:S(2)}, u32[]{:S(2)}) collective-permute-start(f32[3,256,128]{2,1,0:T(8,128)S(1)} %get-tuple-element.63), channel_id=1, source_target_pairs={{0,2},{1,3},{2,0},{3,1},{4,6},{5,7},{6,4},{7,5},{8,10},{9,11},{10,... | collective-permute-start | bytes 1179656 | tf_op jit(solution)/shard_map/ppermute | solution.py:271
  45.8 1.9 %collective-permute-start.8 = (f32[4,512]{1,0:T(4,128)S(1)}, f32[4,512]{1,0:T(4,128)S(1)}, u32[]{:S(2)}, u32[]{:S(2)}) collective-permute-start(f32[4,512]{1,0:T(4,128)S(1)} %get-tuple-element.49.stat_ref), channel_id=1, source_target_pairs={{0,5},{2,7},{5,0},{7,2},{8,13},{10,15},{13,8},{15,10},{16,21},{18,... | collective-permute-start | bytes 24584 | tf_op jit(solution)/shard_map/ppermute | solution.py:271
  47.7 3.2 %collective-permute-done.8.ystat_ref = f32[4,512]{1,0:T(4,128)S(1)} collective-permute-done((f32[4,512]{1,0:T(4,128)S(1)}, f32[4,512]{1,0:T(4,128)S(1)}, u32[]{:S(2)}, u32[]{:S(2)}) %collective-permute-start.8) | collective-permute-done | bytes 8224 | tf_op jit(solution)/shard_map/ppermute | solution.py:271
  50.9 0.9 collective-permute-done.7.y_ref
  51.8 5.6 %near_tile.1 = (f32[3,256,256]{2,1,0:T(8,128)S(1)}, f32[3,256,256]{2,1,0:T(8,128)S(1)}, bf16[512,4096]{1,0:T(8,128)(2,1)S(1)}) custom-call(s32[5]{0:T(128)S(1)} %stack.23.pos_ref.refs_0_, bf16[512,4096]{1,0:T(8,128)(2,1)S(1)} %get-tuple-element.53.turned_ref, bf16[4096,512]{1,0:T(8,128)(2,1)} %collective-permute-done.7.y_ref, ...), custom_call_target="tpu_custom_call" | custom-call | flops 2147483648 | bytes 12582912 | tf_op jit(solution)/shard_map/near_tile/pallas_call | solution.py:348
  57.4 0.7 collective-permute-done.9.w_ref
  58.0 3.9 %collective-permute-start.11 = (f32[3,256,256]{2,1,0:T(8,128)S(1)}, f32[3,256,256]{2,1,0:T(8,128)S(1)}, u32[]{:S(2)}, u32[]{:S(2)}) collective-permute-start(f32[3,256,256]{2,1,0:T(8,128)S(1)} %get-tuple-element.72), channel_id=1, source_target_pairs={{0,2},{2,0},{5,7},{7,5},{8,10},{10,8},{13,15},{15,13},{16,18},{18,... | collective-permute-start | bytes 2359304 | tf_op jit(solution)/shard_map/ppermute | solution.py:271
  61.9 0.7 far_strips_0.1
  62.6 3.0 %far_tile_1.1 = (f32[3,256,128]{2,1,0:T(8,128)S(1)}, f32[3,256,128]{2,1,0:T(8,128)S(1)}, bf16[4096,256]{1,0:T(8,128)(2,1)S(1)}) custom-call(s32[5]{0:T(128)S(1)} %stack.23.pos_ref.refs_0_, bf16[512,4096]{1,0:T(8,128)(2,1)S(1)} %get-tuple-element.53.turned_ref, bf16[4096,256]{1,0:T(8,128)(2,1)S(1)} %collective-permute-done.9.w_ref, ...), custom_call_target="tpu_custom_call" | custom-call | flops 1073741824 | bytes 8388608 | tf_op jit(solution)/shard_map/far_tile_1/pallas_call | solution.py:331
  65.6 4.1 %cross_tile.1 = (f32[3,256,256]{2,1,0:T(8,128)S(1)}, f32[3,256,256]{2,1,0:T(8,128)S(1)}) custom-call(s32[5]{0:T(128)S(1)} %stack.23.pos_ref.refs_0_, bf16[512,4096]{1,0:T(8,128)(2,1)S(1)} %get-tuple-element.59.y_ref, bf16[4096,256]{1,0:T(8,128)(2,1)S(1)} %get-tuple-element.60.w0_ref, bf16[4096,256]{1,0:T(8,128)(2,1)S(1)} %get-tuple-element.66.w1_ref, ...), custom_call_target="tpu_custom_call" | custom-call | flops 2147483648 | bytes 8388608 | tf_op jit(solution)/shard_map/cross_tile/pallas_call | solution.py:357
  69.6 5.0 %collective-permute-done.11.got = f32[3,256,256]{2,1,0:T(8,128)S(1)} collective-permute-done((f32[3,256,256]{2,1,0:T(8,128)S(1)}, f32[3,256,256]{2,1,0:T(8,128)S(1)}, u32[]{:S(2)}, u32[]{:S(2)}) %collective-permute-start.11) | collective-permute-done | bytes 786464 | tf_op jit(solution)/shard_map/ppermute | solution.py:271
  74.6 4.4 %collective-permute-start.14 = (f32[3,256,256]{2,1,0:T(8,128)S(1)}, f32[3,256,256]{2,1,0:T(8,128)S(1)}, u32[]{:S(2)}, u32[]{:S(2)}) collective-permute-start(f32[3,256,256]{2,1,0:T(8,128)S(1)} %get-tuple-element.81), channel_id=1, source_target_pairs={{0,2},{2,0},{5,7},{7,5},{8,10},{10,8},{13,15},{15,13},{16,18},{18,... | collective-permute-start | bytes 2359304 | tf_op jit(solution)/shard_map/ppermute | solution.py:271
  79.1 0.8 near_strips.1
  79.8 1.9 %collective-permute-start.13 = (f32[256,512]{1,0:T(8,128)S(1)}, f32[256,512]{1,0:T(8,128)S(1)}, u32[]{:S(2)}, u32[]{:S(2)}) collective-permute-start(f32[256,512]{1,0:T(8,128)S(1)} %get-tuple-element.79), channel_id=1, source_target_pairs={{0,5},{2,7},{5,0},{7,2},{8,13},{10,15},{13,8},{15,10},{16,21},{18,... | collective-permute-start | bytes 1572872 | tf_op jit(solution)/shard_map/ppermute | solution.py:271
  81.7 7.2 %collective-permute-done.14.got = f32[3,256,256]{2,1,0:T(8,128)S(1)} collective-permute-done((f32[3,256,256]{2,1,0:T(8,128)S(1)}, f32[3,256,256]{2,1,0:T(8,128)S(1)}, u32[]{:S(2)}, u32[]{:S(2)}) %collective-permute-start.14) | collective-permute-done | bytes 786464 | tf_op jit(solution)/shard_map/ppermute | solution.py:271
  88.9 0.7 cross_strips.1
  89.7 1.9 %collective-permute-start.15 = (f32[256,512]{1,0:T(8,128)S(1)}, f32[256,512]{1,0:T(8,128)S(1)}, u32[]{:S(2)}, u32[]{:S(2)}) collective-permute-start(f32[256,512]{1,0:T(8,128)S(1)} %get-tuple-element.82), channel_id=1, source_target_pairs={{0,5},{2,7},{5,0},{7,2},{8,13},{10,15},{13,8},{15,10},{16,21},{18,... | collective-permute-start | bytes 1572872 | tf_op jit(solution)/shard_map/ppermute | solution.py:271
  91.6 1.3 %collective-permute-start.18 = (f32[256,512]{1,0:T(8,128)S(1)}, f32[256,512]{1,0:T(8,128)S(1)}, u32[]{:S(2)}, u32[]{:S(2)}) collective-permute-start(f32[256,512]{1,0:T(8,128)S(1)} %get-tuple-element.85), channel_id=1, source_target_pairs={{0,9},{2,11},{8,17},{10,19},{13,4},{15,6},{16,25},{18,27},{21,12},... | collective-permute-start | bytes 1572872 | tf_op jit(solution)/shard_map/ppermute | solution.py:271
  92.9 1.9 %collective-permute-start.16 = (f32[128,512]{1,0:T(8,128)S(1)}, f32[128,512]{1,0:T(8,128)S(1)}, u32[]{:S(2)}, u32[]{:S(2)}) collective-permute-start(f32[128,512]{1,0:T(8,128)S(1)} %get-tuple-element.83), channel_id=1, source_target_pairs={{0,9},{2,11},{4,13},{6,15},{8,17},{9,0},{10,19},{11,2},{12,21},{13... | collective-permute-start | bytes 786440 | tf_op jit(solution)/shard_map/ppermute | solution.py:271
  94.9 0.7 far_strips_1.1
  95.6 3.6 %collective-permute-start.17 = (f32[128,512]{1,0:T(8,128)S(1)}, f32[128,512]{1,0:T(8,128)S(1)}, u32[]{:S(2)}, u32[]{:S(2)}) collective-permute-start(f32[128,512]{1,0:T(8,128)S(1)} %get-tuple-element.84), channel_id=1, source_target_pairs={{0,9},{2,11},{4,13},{6,15},{8,17},{9,0},{10,19},{11,2},{12,21},{13... | collective-permute-start | bytes 786440 | tf_op jit(solution)/shard_map/ppermute | solution.py:271
  99.2 3.2 %collective-permute-done.16.from_z_c0 = f32[128,512]{1,0:T(8,128)S(1)} collective-permute-done((f32[128,512]{1,0:T(8,128)S(1)}, f32[128,512]{1,0:T(8,128)S(1)}, u32[]{:S(2)}, u32[]{:S(2)}) %collective-permute-start.16) | collective-permute-done | bytes 262176 | tf_op jit(solution)/shard_map/ppermute | solution.py:271
  102.4 2.8 %collective-permute-done.17.from_z_c1 = f32[128,512]{1,0:T(8,128)S(1)} collective-permute-done((f32[128,512]{1,0:T(8,128)S(1)}, f32[128,512]{1,0:T(8,128)S(1)}, u32[]{:S(2)}, u32[]{:S(2)}) %collective-permute-start.17) | collective-permute-done | bytes 262176 | tf_op jit(solution)/shard_map/ppermute | solution.py:271
  105.2 0.7 combine.1
  106.0 2.3 %collective-permute-done.19.sib = f32[3,128,512]{2,1,0:T(8,128)S(1)} collective-permute-done((f32[3,128,512]{2,1,0:T(8,128)S(1)}, f32[3,128,512]{2,1,0:T(8,128)S(1)}, u32[]{:S(2)}, u32[]{:S(2)}) %collective-permute-start.19) | collective-permute-done | bytes 786464 | tf_op jit(solution)/shard_map/ppermute | solution.py:271
  108.3 1.6 %finish.1 = (bf16[1,3,128,512]{3,2,1,0:T(8,128)(2,1)}, bf16[1,2,128,512]{3,2,1,0:T(8,128)(2,1)}) custom-call(s32[5]{0:T(128)S(1)} %stack.23.pos_ref.refs_0_, s32[1,3]{1,0:T(1,128)S(1)} %copy-done.2, f32[128,512]{1,0:T(8,128)S(1)} %get-tuple-element.52.diag_mine, f32[128,512]{1,0:T(8,128)S(1)} %collective-permute-done.6.diag_got, ...), custom_call_target="tpu_custom_call" | custom-call | tf_op jit(solution)/shard_map/finish/pallas_call | solution.py:374
  (16 shorter events, 0.2 us)
Async XLA Ops:
  0.6 51.1 %collective-permute-start.7 = (bf16[4096,512]{1,0:T(8,128)(2,1)}, bf16[4096,512]{1,0:T(8,128)(2,1)}, u32[]{:S(2)}, u32[]{:S(2)}) collective-permute-start(bf16[4096,512]{1,0:T(8,128)(2,1)} %x_ref.1), channel_id=1, source_target_pairs={{1,5},{3,7},{4,0},{6,2},{9,13},{11,15},{12,8},{14,10},{17,21},{19,... | collective-permute-start | bytes 12582920 | tf_op jit(solution)/shard_map/ppermute | solution.py:271
  1.9 2.2 %copy-start = (bf16[4096,512]{1,0:T(8,128)(2,1)S(1)}, bf16[4096,512]{1,0:T(8,128)(2,1)}, u32[]{:S(2)}) copy-start(bf16[4096,512]{1,0:T(8,128)(2,1)} %x_ref.1) | copy-start | bytes 12582916
  6.2 16.7 %copy-start.2 = (s32[1,3]{1,0:T(1,128)S(1)}, s32[1,3]{1,0:T(1,128)}, u32[]{:S(2)}) copy-start(s32[1,3]{1,0:T(1,128)} %offsets_ref.3) | copy-start | bytes 40
  6.2 35.3 %collective-permute-start.4 = (bf16[4096,256]{1,0:T(8,128)(2,1)}, bf16[4096,256]{1,0:T(8,128)(2,1)S(1)}, u32[]{:S(2)}, u32[]{:S(2)}) collective-permute-start(bf16[4096,256]{1,0:T(8,128)(2,1)} %first_chunk.1), channel_id=1, source_target_pairs={{1,9},{3,11},{5,13},{7,15},{8,0},{9,17},{10,2},{11,19},{12,4},{13,... | collective-permute-start | bytes 6291464 | tf_op jit(solution)/shard_map/ppermute | solution.py:271
  9.9 1.4 %copy-start.3 = (bf16[4096,256]{1,0:T(8,128)(2,1)}, bf16[4096,256]{1,0:T(8,128)(2,1)S(1)}, u32[]{:S(2)}) copy-start(bf16[4096,256]{1,0:T(8,128)(2,1)S(1)} %get-tuple-element.61) | copy-start | bytes 6291460
  11.3 9.4 %collective-permute-start = (f32[2,512]{1,0:T(2,128)S(1)}, f32[2,512]{1,0:T(2,128)S(1)}, u32[]{:S(2)}, u32[]{:S(2)}) collective-permute-start(f32[2,512]{1,0:T(2,128)S(1)} %get-tuple-element.47.own_ref), channel_id=1, source_target_pairs={{0,1},{1,0},{2,3},{3,2},{4,5},{5,4},{6,7},{7,6},{8,9},{9,8},{10,11... | collective-permute-start | bytes 12296 | tf_op jit(solution)/shard_map/ppermute | solution.py:271
  18.4 3.6 %collective-permute-start.1 = (f32[2,512]{1,0:T(2,128)S(1)}, f32[2,512]{1,0:T(2,128)S(1)}, u32[]{:S(2)}, u32[]{:S(2)}) collective-permute-start(f32[2,512]{1,0:T(2,128)S(1)} %get-tuple-element.47.own_ref), channel_id=1, source_target_pairs={{0,2},{1,3},{2,0},{3,1},{4,6},{5,7},{6,4},{7,5},{8,10},{9,11},{10,... | collective-permute-start | bytes 12296 | tf_op jit(solution)/shard_map/ppermute | solution.py:271
  19.9 3.0 %collective-permute-start.2 = (f32[2,512]{1,0:T(2,128)S(1)}, f32[2,512]{1,0:T(2,128)S(1)}, u32[]{:S(2)}, u32[]{:S(2)}) collective-permute-start(f32[2,512]{1,0:T(2,128)S(1)} %get-tuple-element.47.own_ref), channel_id=1, source_target_pairs={{0,3},{1,2},{2,1},{3,0},{4,7},{5,6},{6,5},{7,4},{8,11},{9,10},{10,... | collective-permute-start | bytes 12296 | tf_op jit(solution)/shard_map/ppermute | solution.py:271
  23.5 34.5 %collective-permute-start.9 = (bf16[4096,256]{1,0:T(8,128)(2,1)}, bf16[4096,256]{1,0:T(8,128)(2,1)S(1)}, u32[]{:S(2)}, u32[]{:S(2)}) collective-permute-start(bf16[4096,256]{1,0:T(8,128)(2,1)} %copy-done.3), channel_id=1, source_target_pairs={{1,9},{3,11},{5,13},{7,15},{8,0},{9,17},{10,2},{11,19},{12,4},{13,... | collective-permute-start | bytes 6291464 | tf_op jit(solution)/shard_map/ppermute | solution.py:271
  24.8 2.2 %copy-start.1 = (bf16[4096,512]{1,0:T(8,128)(2,1)S(1)}, bf16[4096,512]{1,0:T(8,128)(2,1)}, u32[]{:S(2)}) copy-start(bf16[4096,512]{1,0:T(8,128)(2,1)} %x_ref.1) | copy-start | bytes 12582916
  31.3 3.6 %collective-permute-start.3 = (f32[2,128,512]{2,1,0:T(8,128)S(1)}, f32[2,128,512]{2,1,0:T(8,128)S(1)}, u32[]{:S(2)}, u32[]{:S(2)}) collective-permute-start(f32[2,128,512]{2,1,0:T(8,128)S(1)} %get-tuple-element.51), channel_id=1, source_target_pairs={{0,1},{1,0},{2,3},{3,2},{4,5},{5,4},{6,7},{7,6},{8,9},{9,8},{10,11... | collective-permute-start | bytes 1572872 | tf_op jit(solution)/shard_map/ppermute | solution.py:271
  35.5 8.9 %collective-permute-start.6 = (f32[128,512]{1,0:T(8,128)S(1)}, f32[128,512]{1,0:T(8,128)S(1)}, u32[]{:S(2)}, u32[]{:S(2)}) collective-permute-start(f32[128,512]{1,0:T(8,128)S(1)} %get-tuple-element.56), channel_id=1, source_target_pairs={{0,2},{1,3},{2,0},{3,1},{4,6},{5,7},{6,4},{7,5},{8,10},{9,11},{10,... | collective-permute-start | bytes 786440 | tf_op jit(solution)/shard_map/ppermute | solution.py:271
  36.3 5.1 %collective-permute-start.5 = (f32[4,512]{1,0:T(4,128)S(1)}, f32[4,512]{1,0:T(4,128)S(1)}, u32[]{:S(2)}, u32[]{:S(2)}) collective-permute-start(f32[4,512]{1,0:T(4,128)S(1)} %get-tuple-element.54.stat_ref), channel_id=1, source_target_pairs={{0,9},{2,11},{4,13},{6,15},{8,17},{9,0},{10,19},{11,2},{12,21},{13... | collective-permute-start | bytes 24584 | tf_op jit(solution)/shard_map/ppermute | solution.py:271
  44.4 12.9 %collective-permute-start.10 = (f32[3,256,128]{2,1,0:T(8,128)S(1)}, f32[3,256,128]{2,1,0:T(8,128)S(1)}, u32[]{:S(2)}, u32[]{:S(2)}) collective-permute-start(f32[3,256,128]{2,1,0:T(8,128)S(1)} %get-tuple-element.63), channel_id=1, source_target_pairs={{0,2},{1,3},{2,0},{3,1},{4,6},{5,7},{6,4},{7,5},{8,10},{9,11},{10,... | collective-permute-start | bytes 1179656 | tf_op jit(solution)/shard_map/ppermute | solution.py:271
  45.8 5.1 %collective-permute-start.8 = (f32[4,512]{1,0:T(4,128)S(1)}, f32[4,512]{1,0:T(4,128)S(1)}, u32[]{:S(2)}, u32[]{:S(2)}) collective-permute-start(f32[4,512]{1,0:T(4,128)S(1)} %get-tuple-element.49.stat_ref), channel_id=1, source_target_pairs={{0,5},{2,7},{5,0},{7,2},{8,13},{10,15},{13,8},{15,10},{16,21},{18,... | collective-permute-start | bytes 24584 | tf_op jit(solution)/shard_map/ppermute | solution.py:271
  58.0 16.6 %collective-permute-start.11 = (f32[3,256,256]{2,1,0:T(8,128)S(1)}, f32[3,256,256]{2,1,0:T(8,128)S(1)}, u32[]{:S(2)}, u32[]{:S(2)}) collective-permute-start(f32[3,256,256]{2,1,0:T(8,128)S(1)} %get-tuple-element.72), channel_id=1, source_target_pairs={{0,2},{2,0},{5,7},{7,5},{8,10},{10,8},{13,15},{15,13},{16,18},{18,... | collective-permute-start | bytes 2359304 | tf_op jit(solution)/shard_map/ppermute | solution.py:271
  74.6 14.3 %collective-permute-start.14 = (f32[3,256,256]{2,1,0:T(8,128)S(1)}, f32[3,256,256]{2,1,0:T(8,128)S(1)}, u32[]{:S(2)}, u32[]{:S(2)}) collective-permute-start(f32[3,256,256]{2,1,0:T(8,128)S(1)} %get-tuple-element.81), channel_id=1, source_target_pairs={{0,2},{2,0},{5,7},{7,5},{8,10},{10,8},{13,15},{15,13},{16,18},{18,... | collective-permute-start | bytes 2359304 | tf_op jit(solution)/shard_map/ppermute | solution.py:271
  79.0 15.9 %collective-permute-start.12 = (f32[3,256,128]{2,1,0:T(8,128)S(1)}, f32[3,256,128]{2,1,0:T(8,128)S(1)}, u32[]{:S(2)}, u32[]{:S(2)}) collective-permute-start(f32[3,256,128]{2,1,0:T(8,128)S(1)} %get-tuple-element.77), channel_id=1, source_target_pairs={{0,2},{1,3},{2,0},{3,1},{4,6},{5,7},{6,4},{7,5},{8,10},{9,11},{10,... | collective-permute-start | bytes 1179656 | tf_op jit(solution)/shard_map/ppermute | solution.py:271
  79.8 22.6 %collective-permute-start.13 = (f32[256,512]{1,0:T(8,128)S(1)}, f32[256,512]{1,0:T(8,128)S(1)}, u32[]{:S(2)}, u32[]{:S(2)}) collective-permute-start(f32[256,512]{1,0:T(8,128)S(1)} %get-tuple-element.79), channel_id=1, source_target_pairs={{0,5},{2,7},{5,0},{7,2},{8,13},{10,15},{13,8},{15,10},{16,21},{18,... | collective-permute-start | bytes 1572872 | tf_op jit(solution)/shard_map/ppermute | solution.py:271
  89.7 15.5 %collective-permute-start.15 = (f32[256,512]{1,0:T(8,128)S(1)}, f32[256,512]{1,0:T(8,128)S(1)}, u32[]{:S(2)}, u32[]{:S(2)}) collective-permute-start(f32[256,512]{1,0:T(8,128)S(1)} %get-tuple-element.82), channel_id=1, source_target_pairs={{0,5},{2,7},{5,0},{7,2},{8,13},{10,15},{13,8},{15,10},{16,21},{18,... | collective-permute-start | bytes 1572872 | tf_op jit(solution)/shard_map/ppermute | solution.py:271
  91.6 13.6 %collective-permute-start.18 = (f32[256,512]{1,0:T(8,128)S(1)}, f32[256,512]{1,0:T(8,128)S(1)}, u32[]{:S(2)}, u32[]{:S(2)}) collective-permute-start(f32[256,512]{1,0:T(8,128)S(1)} %get-tuple-element.85), channel_id=1, source_target_pairs={{0,9},{2,11},{8,17},{10,19},{13,4},{15,6},{16,25},{18,27},{21,12},... | collective-permute-start | bytes 1572872 | tf_op jit(solution)/shard_map/ppermute | solution.py:271
  92.9 9.5 %collective-permute-start.16 = (f32[128,512]{1,0:T(8,128)S(1)}, f32[128,512]{1,0:T(8,128)S(1)}, u32[]{:S(2)}, u32[]{:S(2)}) collective-permute-start(f32[128,512]{1,0:T(8,128)S(1)} %get-tuple-element.83), channel_id=1, source_target_pairs={{0,9},{2,11},{4,13},{6,15},{8,17},{9,0},{10,19},{11,2},{12,21},{13... | collective-permute-start | bytes 786440 | tf_op jit(solution)/shard_map/ppermute | solution.py:271
  95.6 9.6 %collective-permute-start.17 = (f32[128,512]{1,0:T(8,128)S(1)}, f32[128,512]{1,0:T(8,128)S(1)}, u32[]{:S(2)}, u32[]{:S(2)}) collective-permute-start(f32[128,512]{1,0:T(8,128)S(1)} %get-tuple-element.84), channel_id=1, source_target_pairs={{0,9},{2,11},{4,13},{6,15},{8,17},{9,0},{10,19},{11,2},{12,21},{13... | collective-permute-start | bytes 786440 | tf_op jit(solution)/shard_map/ppermute | solution.py:271
  106.0 2.4 %collective-permute-start.19 = (f32[3,128,512]{2,1,0:T(8,128)S(1)}, f32[3,128,512]{2,1,0:T(8,128)S(1)}, u32[]{:S(2)}, u32[]{:S(2)}) collective-permute-start(f32[3,128,512]{2,1,0:T(8,128)S(1)} %get-tuple-element.87), channel_id=1, source_target_pairs={{0,1},{1,0},{2,3},{3,2},{4,5},{5,4},{6,7},{7,6},{8,9},{9,8},{10,11... | collective-permute-start | bytes 2359304 | tf_op jit(solution)/shard_map/ppermute | solution.py:271

commit v5 on v3

--- a/solution.py
+++ b/solution.py
@@ -12,7 +12,7 @@
 VMEM = pl.BlockSpec(memory_space=pltpu.VMEM)
 SMEM = pl.BlockSpec(memory_space=pltpu.SMEM)
 SOME = pltpu.CompilerParams(vmem_limit_bytes=24 << 20)
-C_TYPE, BD_TYPE = F32, BF16
+HALVES = BF16
 
 
 def dot(a, b):
@@ -129,7 +129,7 @@
         put_quarters(pos_ref[0], acc, keep_ref, send_ref)
 
 
-def near_kernel(pos_ref, turned_ref, y_ref, w_ref, stat_ref, ystat_ref, wstat_ref, keep_ref, send_ref, acc_b, acc_d):
+def near_kernel(pos_ref, turned_ref, y_ref, w_ref, stat_ref, ystat_ref, wstat_ref, keep_b, send_b, keep_d, send_d, acc_b, acc_d):
     step = pl.program_id(0)
 
     @pl.when(pos_ref[1] == 1)
@@ -149,8 +149,8 @@
             share = 1.0 / pos_ref[4].astype(F32)
             acc_b[...] *= jnp.where(first, stat_ref[2:3, :], ystat_ref[2:3, :]) * share
             acc_d[...] *= jnp.where(first, ystat_ref[2:3, :], wstat_ref[2:3, :]) * share
-            put_quarters(pos_ref[0], acc_b, keep_ref.at[0], send_ref.at[0])
-            put_quarters(pos_ref[0], acc_d, keep_ref.at[1], send_ref.at[1])
+            put_quarters(pos_ref[0], acc_b, keep_b, send_b)
+            put_quarters(pos_ref[0], acc_d, keep_d, send_d)
 
 
 def add_halves(x, keep, got, rows_out, cols_out):
@@ -168,27 +168,26 @@
     add_halves(pos_ref[0], keep, got, held, to_z)
 
 
-def near_strips_kernel(pos_ref, keep, got, held, to_y, to_z):
+def near_strips_kernel(pos_ref, keep, got, rows_out, cols_out):
     @pl.when(pos_ref[1] == 1)
     def _():
-        add_halves(pos_ref[0], keep.at[0], got.at[0], held, to_y.at[0])
-        add_halves(pos_ref[0], keep.at[1], got.at[1], to_y.at[1], to_z)
-
-
-def combine_kernel(pos_ref, held_b, held_c, from_y, from_z_c, from_z_d, mine, sib):
+        add_halves(pos_ref[0], keep, got, rows_out, cols_out)
+
+
+def combine_kernel(pos_ref, held_b, held_c, from_y_b, from_y_d, from_z_c, from_z_d, mine, sib):
     rows = mine.shape[1]
     for core, out in ((pos_ref[2], mine), (1 - pos_ref[2], sib)):
         at = pl.ds(pl.multiple_of(core * rows, rows), rows)
-        out[1] = held_c[at, :] + from_z_c[at, :].astype(F32)
+        out[1] = held_c[at, :] + from_z_c[at, :]
 
         @pl.when(pos_ref[1] == 1)
         def _():
-            out[0] = held_b[at, :] + from_y[0, at, :].astype(F32)
-            out[2] = from_y[1, at, :].astype(F32)
+            out[0] = held_b[at, :] + from_y_b[at, :]
+            out[2] = from_y_d[at, :]
 
         @pl.when(pos_ref[1] == 0)
         def _():
-            out[2] = from_z_d[at, :].astype(F32)
+            out[2] = from_z_d[at, :]
 
 
 def finish_kernel(pos_ref, offsets_ref, diag_mine, diag_got, mine, sib, upper, mirror):
@@ -280,28 +279,34 @@
     keep_c, send_c, w = call(
         far_kernel, "far_tile", (steps,), [SMEM, flat, wide, whole(4, width), whole(4, width)],
         [whole(3, half, half)] * 2 + [wide],
-        [shape(3, half, half), shape(3, half, half, dtype=C_TYPE), shape(depth, width, dtype=BF16)],
+        [shape(3, half, half), shape(3, half, half, dtype=HALVES), shape(depth, width, dtype=BF16)],
         [pltpu.VMEM((width, width), F32)], tile_flops, 3 * bytes_block)(pos, turned, w_raw, stat, w_stat)
     send_c, diag_got = lax.optimization_barrier((send_c, diag_got))
     got_c = send(send_c, across)
 
-    keep_bd, send_bd = call(
+    keep_b, send_b, keep_d, send_d = call(
         near_kernel, "near_tiles", (steps,), [SMEM, flat, wide, wide] + [whole(4, width)] * 3,
-        [whole(2, 3, half, half)] * 2,
-        [shape(2, 3, half, half), shape(2, 3, half, half, dtype=BD_TYPE)],
+        [whole(3, half, half)] * 4, [shape(3, half, half, dtype=kind) for kind in (F32, HALVES)] * 2,
         [pltpu.VMEM((width, width), F32)] * 2, 2 * tile_flops, 3 * bytes_block)(pos, turned, y_raw, w, stat, y_stat, w_stat)
-    got_bd = send(send_bd, across_active)
+    got_b = send(send_b, across_active)
+    send_d, got_c = lax.optimization_barrier((send_d, got_c))
+    got_d = send(send_d, across_active)
 
     held_c, to_z_c = call(far_strips_kernel, "far_strips", (), [SMEM] + [VMEM] * 2, [VMEM] * 2,
-                          [shape(half, width), shape(half, width, dtype=C_TYPE)])(pos, keep_c, got_c)
+                          [shape(half, width)] * 2)(pos, keep_c, got_c)
     from_z_c = send(to_z_c, z_cross)
-    held_b, to_y, to_z_d = call(
-        near_strips_kernel, "near_strips", (), [SMEM] + [VMEM] * 2, [VMEM] * 3,
-        [shape(half, width), shape(2, half, width, dtype=BD_TYPE), shape(half, width, dtype=BD_TYPE)])(pos, keep_bd, got_bd)
-    from_y, from_z_d = send(to_y, y_cross), send(to_z_d, z_cross_active)
-
-    mine, sib = call(combine_kernel, "combine", (), [SMEM] + [VMEM] * 5, [VMEM] * 2, [shape(3, strip, width)] * 2)(
-        pos, held_b, held_c, from_y, from_z_c, from_z_d)
+
+    def near_strips(name, keep, got):
+        return call(near_strips_kernel, name, (), [SMEM] + [VMEM] * 2, [VMEM] * 2, [shape(half, width)] * 2)(pos, keep, got)
+
+    held_b, to_y_b = near_strips("near_strips", keep_b, got_b)
+    from_y_b = send(to_y_b, y_cross)
+    got_d, to_y_b = lax.optimization_barrier((got_d, to_y_b))
+    to_y_d, to_z_d = near_strips("cross_strips", keep_d, got_d)
+    from_y_d, from_z_d = send(to_y_d, y_cross), send(to_z_d, z_cross_active)
+
+    mine, sib = call(combine_kernel, "combine", (), [SMEM] + [VMEM] * 6, [VMEM] * 2, [shape(3, strip, width)] * 2)(
+        pos, held_b, held_c, from_y_b, from_y_d, from_z_c, from_z_d)
     return call(finish_kernel, "finish", (), [SMEM] * 2 + [VMEM] * 4, [VMEM] * 2,
                 [shape(1, SLOTS, strip, width, dtype=BF16), shape(1, 2, strip, width, dtype=BF16)])(
         pos, pair_offsets, diag_mine, diag_got, mine, send(sib, sibling))

time: 101 us -> 100 us (0.990)
  waiting for transfers between devices: 42.3 us -> 34.9 us
  starting transfers between devices: 28.1 us -> 33.8 us
    ppermute x15 -> x17, waiting for transfers between devices: 42.3 us -> 34.9 us  [send(): return lax.ppermute(value, AXES, pairs)]
    ppermute x15 -> x17, starting transfers between devices: 28.1 us -> 33.8 us  [send(): return lax.ppermute(value, AXES, pairs)]
    pallas_call x2 -> x3, Pallas kernels: 1.51 us -> 2.21 us  [the longest x2 1.5 us: near_strips(): call(near_strips_kernel, name, (), [SMEM] + [VMEM] * 2, [VMEM] * 2, [shap...]
  transfers between devices with their start and end apart: 15 -> 17, of which waited for: 10 -> 11; matrix products, arithmetic and copies ran while one was open for 0% -> 0% of each run, Pallas kernels for 22% -> 22%
where the time goes in v5:
time: 100 us; the launch traced here: 99.2 us
  waiting for transfers between devices  34.9 us (35%)
  starting transfers between devices  33.8 us (34%)
  Pallas kernels  24.6 us (25%)
  local copies, waits for them, and re-layouts  4.46 us (4%)
  between operations  1.49 us (1%)
    ppermute x17, waiting for transfers between devices, send(): return lax.ppermute(value, AXES, pairs)  34.9 us
    ppermute x17, starting transfers between devices, send(): return lax.ppermute(value, AXES, pairs)  33.8 us
    pallas_call x1, Pallas kernels, body(): call(near_kernel, 'near_tiles', (steps,), [SMEM, flat, wide, wide] + [who...  7.34 us
    pallas_call x1, Pallas kernels, body(): call(far_kernel, 'far_tile', (steps,), [SMEM, flat, wide, whole(4, width)...  5.33 us
    unnamed x6, local copies, waits for them, and re-layouts  4.37 us
    pallas_call x1, Pallas kernels, body(): call(own_kernel, 'own_tile', (steps,), [SMEM, wide, whole(4, width)], [fl...  4.3 us
  transfers between devices with their start and end apart: 17, of which 11 were waited for; matrix products, arithmetic and copies ran while one was open for 0% of the time, Pallas kernels for 22%

profile of v5, /device:TPU:0, one launch (start us, length us, event | category | flops | bytes accessed | tf_op | source)
XLA Modules:
  0.0 99.2 jit_solution(3014309215647398469)
XLA Ops:
  0.6 1.3 %collective-permute-start.4 = (bf16[4096,512]{1,0:T(8,128)(2,1)}, bf16[4096,512]{1,0:T(8,128)(2,1)}, u32[]{:S(2)}, u32[]{:S(2)}) collective-permute-start(bf16[4096,512]{1,0:T(8,128)(2,1)} %x_ref.1), channel_id=1, source_target_pairs={{1,9},{3,11},{5,13},{7,15},{8,0},{9,17},{10,2},{11,19},{12,4},{13,... | collective-permute-start | bytes 12582920 | tf_op jit(solution)/shard_map/ppermute | solution.py:230
  1.9 1.3 %collective-permute-start.7 = (bf16[4096,512]{1,0:T(8,128)(2,1)}, bf16[4096,512]{1,0:T(8,128)(2,1)}, u32[]{:S(2)}, u32[]{:S(2)}) collective-permute-start(bf16[4096,512]{1,0:T(8,128)(2,1)} %x_ref.1), channel_id=1, source_target_pairs={{1,5},{3,7},{4,0},{6,2},{9,13},{11,15},{12,8},{14,10},{17,21},{19,... | collective-permute-start | bytes 12582920 | tf_op jit(solution)/shard_map/ppermute | solution.py:230
  3.2 0.0 copy-start
  3.2 2.2 %copy-done = bf16[4096,512]{1,0:T(8,128)(2,1)S(1)} copy-done((bf16[4096,512]{1,0:T(8,128)(2,1)S(1)}, bf16[4096,512]{1,0:T(8,128)(2,1)}, u32[]{:S(2)}) %copy-start) | copy-done | bytes 4194328
  5.4 1.9 %local_stats.1.own_ref = f32[2,512]{1,0:T(2,128)S(1)} custom-call(bf16[4096,512]{1,0:T(8,128)(2,1)S(1)} %copy-done), custom_call_target="tpu_custom_call" | custom-call | flops 10485760 | bytes 4194304 | tf_op jit(solution)/shard_map/local_stats/pallas_call | solution.py:263
  7.3 9.1 %collective-permute-start = (f32[2,512]{1,0:T(2,128)S(1)}, f32[2,512]{1,0:T(2,128)S(1)}, u32[]{:S(2)}, u32[]{:S(2)}) collective-permute-start(f32[2,512]{1,0:T(2,128)S(1)} %local_stats.1.own_ref), channel_id=1, source_target_pairs={{0,1},{1,0},{2,3},{3,2},{4,5},{5,4},{6,7},{7,6},{8,9},{9,8},{10,11... | collective-permute-start | bytes 12296 | tf_op jit(solution)/shard_map/ppermute | solution.py:230
  16.4 1.5 %collective-permute-start.1 = (f32[2,512]{1,0:T(2,128)S(1)}, f32[2,512]{1,0:T(2,128)S(1)}, u32[]{:S(2)}, u32[]{:S(2)}) collective-permute-start(f32[2,512]{1,0:T(2,128)S(1)} %local_stats.1.own_ref), channel_id=1, source_target_pairs={{0,2},{1,3},{2,0},{3,1},{4,6},{5,7},{6,4},{7,5},{8,10},{9,11},{10,... | collective-permute-start | bytes 12296 | tf_op jit(solution)/shard_map/ppermute | solution.py:230
  17.9 0.0 collective-permute-start.2
  18.5 0.1 stack.23.pos_ref
  18.6 0.0 collective-permute-done.sib_ref
  18.6 1.4 %collective-permute-done.1.far_ref = f32[2,512]{1,0:T(2,128)S(1)} collective-permute-done((f32[2,512]{1,0:T(2,128)S(1)}, f32[2,512]{1,0:T(2,128)S(1)}, u32[]{:S(2)}, u32[]{:S(2)}) %collective-permute-start.1) | collective-permute-done | bytes 4128 | tf_op jit(solution)/shard_map/ppermute | solution.py:230
  20.0 0.9 collective-permute-done.2.cross_ref
  20.9 0.6 stats.1.stat_ref
  21.5 0.0 copy-start.1
  21.5 2.2 %copy-done.1 = bf16[4096,512]{1,0:T(8,128)(2,1)S(1)} copy-done((bf16[4096,512]{1,0:T(8,128)(2,1)S(1)}, bf16[4096,512]{1,0:T(8,128)(2,1)}, u32[]{:S(2)}) %copy-start.1) | copy-done | bytes 4194328
  23.7 4.3 %own_tile.1 = (bf16[512,4096]{1,0:T(8,128)(2,1)S(1)}, f32[2,128,512]{2,1,0:T(8,128)S(1)}, f32[2,128,512]{2,1,0:T(8,128)S(1)}) custom-call(s32[5]{0:T(128)S(1)} %stack.23.pos_ref, bf16[4096,512]{1,0:T(8,128)(2,1)S(1)} %copy-done.1, f32[4,512]{1,0:T(4,128)S(1)} %stats.1.stat_ref), custom_call_target="tpu_custom_call" | custom-call | flops 2147483648 | bytes 8388608 | tf_op jit(solution)/shard_map/own_tile/pallas_call | solution.py:270
  28.0 0.3 collective-permute-start.3
  28.2 1.7 %collective-permute-done.3.got_ref = f32[2,128,512]{2,1,0:T(8,128)S(1)} collective-permute-done((f32[2,128,512]{2,1,0:T(8,128)S(1)}, f32[2,128,512]{2,1,0:T(8,128)S(1)}, u32[]{:S(2)}, u32[]{:S(2)}) %collective-permute-start.3) | collective-permute-done | bytes 524320 | tf_op jit(solution)/shard_map/ppermute | solution.py:230
  30.0 0.6 own_tile_strips.1
  30.6 0.6 collective-permute-start.6
  31.2 1.9 %collective-permute-start.5 = (f32[4,512]{1,0:T(4,128)S(1)}, f32[4,512]{1,0:T(4,128)S(1)}, u32[]{:S(2)}, u32[]{:S(2)}) collective-permute-start(f32[4,512]{1,0:T(4,128)S(1)} %stats.1.stat_ref), channel_id=1, source_target_pairs={{0,9},{2,11},{4,13},{6,15},{8,17},{9,0},{10,19},{11,2},{12,21},{13... | collective-permute-start | bytes 24584 | tf_op jit(solution)/shard_map/ppermute | solution.py:230
  33.1 1.9 %collective-permute-start.8 = (f32[4,512]{1,0:T(4,128)S(1)}, f32[4,512]{1,0:T(4,128)S(1)}, u32[]{:S(2)}, u32[]{:S(2)}) collective-permute-start(f32[4,512]{1,0:T(4,128)S(1)} %stats.1.stat_ref), channel_id=1, source_target_pairs={{0,5},{2,7},{5,0},{7,2},{8,13},{10,15},{13,8},{15,10},{16,21},{18,... | collective-permute-start | bytes 24584 | tf_op jit(solution)/shard_map/ppermute | solution.py:230
  35.1 1.3 %collective-permute-done.5.wstat_ref = f32[4,512]{1,0:T(4,128)S(1)} collective-permute-done((f32[4,512]{1,0:T(4,128)S(1)}, f32[4,512]{1,0:T(4,128)S(1)}, u32[]{:S(2)}, u32[]{:S(2)}) %collective-permute-start.5) | collective-permute-done | bytes 8224 | tf_op jit(solution)/shard_map/ppermute | solution.py:230
  36.3 16.1 %collective-permute-done.4.w_ref = bf16[4096,512]{1,0:T(8,128)(2,1)} collective-permute-done((bf16[4096,512]{1,0:T(8,128)(2,1)}, bf16[4096,512]{1,0:T(8,128)(2,1)}, u32[]{:S(2)}, u32[]{:S(2)}) %collective-permute-start.4) | collective-permute-done | bytes 4194336 | tf_op jit(solution)/shard_map/ppermute | solution.py:230
  52.4 5.3 %far_tile.1 = (f32[3,256,256]{2,1,0:T(8,128)S(1)}, bf16[3,256,256]{2,1,0:T(8,128)(2,1)S(1)}, bf16[4096,512]{1,0:T(8,128)(2,1)S(1)}) custom-call(s32[5]{0:T(128)S(1)} %stack.23.pos_ref, bf16[512,4096]{1,0:T(8,128)(2,1)S(1)} %get-tuple-element.30.turned_ref, bf16[4096,512]{1,0:T(8,128)(2,1)} %collective-permute-done.4.w_ref, f32[4,512]{1,0:T(4,128)S(1)} %stats.1.stat_ref, ...), custom_call_target="tpu_custom_call" | custom-call | flops 2147483648 | bytes 12582912 | tf_op jit(solution)/shard_map/far_tile/pallas_call | solution.py:279
  57.8 2.0 %collective-permute-start.10 = (bf16[3,256,256]{2,1,0:T(8,128)(2,1)S(1)}, bf16[3,256,256]{2,1,0:T(8,128)(2,1)S(1)}, u32[]{:S(2)}, u32[]{:S(2)}) collective-permute-start(bf16[3,256,256]{2,1,0:T(8,128)(2,1)S(1)} %get-tuple-element.40), channel_id=1, source_target_pairs={{0,2},{1,3},{2,0},{3,1},{4,6},{5,7},{6,4},{7,5},{8,10},{9,11},{10,... | collective-permute-start | bytes 1179656 | tf_op jit(solution)/shard_map/ppermute | solution.py:230
  59.8 0.0 collective-permute-done.8.ystat_ref
  59.8 0.0 collective-permute-done.7.y_ref
  59.8 7.3 %near_tiles.1 = (f32[3,256,256]{2,1,0:T(8,128)S(1)}, bf16[3,256,256]{2,1,0:T(8,128)(2,1)S(1)}, f32[3,256,256]{2,1,0:T(8,128)S(1)}, bf16[3,256,256]{2,1,0:T(8,128)(2,1)S(1)}) custom-call(s32[5]{0:T(128)S(1)} %stack.23.pos_ref, bf16[512,4096]{1,0:T(8,128)(2,1)S(1)} %get-tuple-element.30.turned_ref, bf16[4096,512]{1,0:T(8,128)(2,1)} %collective-permute-done.7.y_ref, ...), custom_call_target="tpu_custom_call" | custom-call | flops 4294967296 | bytes 12582912 | tf_op jit(solution)/shard_map/near_tiles/pallas_call | solution.py:287
  67.1 2.0 %collective-permute-start.9 = (bf16[3,256,256]{2,1,0:T(8,128)(2,1)S(1)}, bf16[3,256,256]{2,1,0:T(8,128)(2,1)S(1)}, u32[]{:S(2)}, u32[]{:S(2)}) collective-permute-start(bf16[3,256,256]{2,1,0:T(8,128)(2,1)S(1)} %get-tuple-element.36), channel_id=1, source_target_pairs={{0,2},{2,0},{5,7},{7,5},{8,10},{10,8},{13,15},{15,13},{16,18},{18,... | collective-permute-start | bytes 1179656 | tf_op jit(solution)/shard_map/ppermute | solution.py:230
  69.2 3.8 %collective-permute-start.12 = (bf16[3,256,256]{2,1,0:T(8,128)(2,1)S(1)}, bf16[3,256,256]{2,1,0:T(8,128)(2,1)S(1)}, u32[]{:S(2)}, u32[]{:S(2)}) collective-permute-start(bf16[3,256,256]{2,1,0:T(8,128)(2,1)S(1)} %get-tuple-element.45), channel_id=1, source_target_pairs={{0,2},{2,0},{5,7},{7,5},{8,10},{10,8},{13,15},{15,13},{16,18},{18,... | collective-permute-start | bytes 1179656 | tf_op jit(solution)/shard_map/ppermute | solution.py:230
  73.0 3.8 %collective-permute-done.9.got = bf16[3,256,256]{2,1,0:T(8,128)(2,1)S(1)} collective-permute-done((bf16[3,256,256]{2,1,0:T(8,128)(2,1)S(1)}, bf16[3,256,256]{2,1,0:T(8,128)(2,1)S(1)}, u32[]{:S(2)}, u32[]{:S(2)}) %collective-permute-start.9) | collective-permute-done | bytes 393248 | tf_op jit(solution)/shard_map/ppermute | solution.py:230
  76.8 0.8 near_strips.1
  77.6 1.9 %collective-permute-start.11 = (f32[256,512]{1,0:T(8,128)S(1)}, f32[256,512]{1,0:T(8,128)S(1)}, u32[]{:S(2)}, u32[]{:S(2)}) collective-permute-start(f32[256,512]{1,0:T(8,128)S(1)} %get-tuple-element.43), channel_id=1, source_target_pairs={{0,5},{2,7},{5,0},{7,2},{8,13},{10,15},{13,8},{15,10},{16,21},{18,... | collective-permute-start | bytes 1572872 | tf_op jit(solution)/shard_map/ppermute | solution.py:230
  79.5 0.7 far_strips.1
  80.3 1.9 %collective-permute-start.14 = (f32[256,512]{1,0:T(8,128)S(1)}, f32[256,512]{1,0:T(8,128)S(1)}, u32[]{:S(2)}, u32[]{:S(2)}) collective-permute-start(f32[256,512]{1,0:T(8,128)S(1)} %get-tuple-element.48), channel_id=1, source_target_pairs={{0,9},{2,11},{4,13},{6,15},{8,17},{9,0},{10,19},{11,2},{12,21},{13... | collective-permute-start | bytes 1572872 | tf_op jit(solution)/shard_map/ppermute | solution.py:230
  82.2 0.0 collective-permute-done.12.got
  82.2 0.7 cross_strips.1
  83.0 2.4 %collective-permute-start.13 = (f32[256,512]{1,0:T(8,128)S(1)}, f32[256,512]{1,0:T(8,128)S(1)}, u32[]{:S(2)}, u32[]{:S(2)}) collective-permute-start(f32[256,512]{1,0:T(8,128)S(1)} %get-tuple-element.47), channel_id=1, source_target_pairs={{0,5},{2,7},{5,0},{7,2},{8,13},{10,15},{13,8},{15,10},{16,21},{18,... | collective-permute-start | bytes 1572872 | tf_op jit(solution)/shard_map/ppermute | solution.py:230
  85.4 1.8 %collective-permute-start.15 = (f32[256,512]{1,0:T(8,128)S(1)}, f32[256,512]{1,0:T(8,128)S(1)}, u32[]{:S(2)}, u32[]{:S(2)}) collective-permute-start(f32[256,512]{1,0:T(8,128)S(1)} %get-tuple-element.49), channel_id=1, source_target_pairs={{0,9},{2,11},{8,17},{10,19},{13,4},{15,6},{16,25},{18,27},{21,12},... | collective-permute-start | bytes 1572872 | tf_op jit(solution)/shard_map/ppermute | solution.py:230
  87.1 0.9 collective-permute-done.11.from_y_b
  88.1 2.7 %collective-permute-done.14.from_z_c = f32[256,512]{1,0:T(8,128)S(1)} collective-permute-done((f32[256,512]{1,0:T(8,128)S(1)}, f32[256,512]{1,0:T(8,128)S(1)}, u32[]{:S(2)}, u32[]{:S(2)}) %collective-permute-start.14) | collective-permute-done | bytes 524320 | tf_op jit(solution)/shard_map/ppermute | solution.py:230
  90.8 2.9 %collective-permute-done.13.from_y_d = f32[256,512]{1,0:T(8,128)S(1)} collective-permute-done((f32[256,512]{1,0:T(8,128)S(1)}, f32[256,512]{1,0:T(8,128)S(1)}, u32[]{:S(2)}, u32[]{:S(2)}) %collective-permute-start.13) | collective-permute-done | bytes 524320 | tf_op jit(solution)/shard_map/ppermute | solution.py:230
  93.7 0.8 collective-permute-done.15.from_z_d
  94.5 0.7 combine.1
  95.2 0.1 collective-permute-start.16
  95.3 2.3 %collective-permute-done.16.sib = f32[3,128,512]{2,1,0:T(8,128)S(1)} collective-permute-done((f32[3,128,512]{2,1,0:T(8,128)S(1)}, f32[3,128,512]{2,1,0:T(8,128)S(1)}, u32[]{:S(2)}, u32[]{:S(2)}) %collective-permute-start.16) | collective-permute-done | bytes 786464 | tf_op jit(solution)/shard_map/ppermute | solution.py:230
  97.5 1.7 %finish.1 = (bf16[1,3,128,512]{3,2,1,0:T(8,128)(2,1)}, bf16[1,2,128,512]{3,2,1,0:T(8,128)(2,1)}) custom-call(s32[5]{0:T(128)S(1)} %stack.23.pos_ref, s32[1,3]{1,0:T(1,128)S(1)} %copy-done.2, f32[128,512]{1,0:T(8,128)S(1)} %get-tuple-element.29.diag_mine, f32[128,512]{1,0:T(8,128)S(1)} %collective-permute-done.6.diag_got, ...), custom_call_target="tpu_custom_call" | custom-call | tf_op jit(solution)/shard_map/finish/pallas_call | solution.py:310
  (4 shorter events, 0.0 us)
Async XLA Ops:
  0.6 51.8 %collective-permute-start.4 = (bf16[4096,512]{1,0:T(8,128)(2,1)}, bf16[4096,512]{1,0:T(8,128)(2,1)}, u32[]{:S(2)}, u32[]{:S(2)}) collective-permute-start(bf16[4096,512]{1,0:T(8,128)(2,1)} %x_ref.1), channel_id=1, source_target_pairs={{1,9},{3,11},{5,13},{7,15},{8,0},{9,17},{10,2},{11,19},{12,4},{13,... | collective-permute-start | bytes 12582920 | tf_op jit(solution)/shard_map/ppermute | solution.py:230
  1.9 57.9 %collective-permute-start.7 = (bf16[4096,512]{1,0:T(8,128)(2,1)}, bf16[4096,512]{1,0:T(8,128)(2,1)}, u32[]{:S(2)}, u32[]{:S(2)}) collective-permute-start(bf16[4096,512]{1,0:T(8,128)(2,1)} %x_ref.1), channel_id=1, source_target_pairs={{1,5},{3,7},{4,0},{6,2},{9,13},{11,15},{12,8},{14,10},{17,21},{19,... | collective-permute-start | bytes 12582920 | tf_op jit(solution)/shard_map/ppermute | solution.py:230
  3.2 2.2 %copy-start = (bf16[4096,512]{1,0:T(8,128)(2,1)S(1)}, bf16[4096,512]{1,0:T(8,128)(2,1)}, u32[]{:S(2)}) copy-start(bf16[4096,512]{1,0:T(8,128)(2,1)} %x_ref.1) | copy-start | bytes 12582916
  5.4 15.5 %copy-start.2 = (s32[1,3]{1,0:T(1,128)S(1)}, s32[1,3]{1,0:T(1,128)}, u32[]{:S(2)}) copy-start(s32[1,3]{1,0:T(1,128)} %offsets_ref.3) | copy-start | bytes 40
  7.3 11.3 %collective-permute-start = (f32[2,512]{1,0:T(2,128)S(1)}, f32[2,512]{1,0:T(2,128)S(1)}, u32[]{:S(2)}, u32[]{:S(2)}) collective-permute-start(f32[2,512]{1,0:T(2,128)S(1)} %local_stats.1.own_ref), channel_id=1, source_target_pairs={{0,1},{1,0},{2,3},{3,2},{4,5},{5,4},{6,7},{7,6},{8,9},{9,8},{10,11... | collective-permute-start | bytes 12296 | tf_op jit(solution)/shard_map/ppermute | solution.py:230
  16.4 3.6 %collective-permute-start.1 = (f32[2,512]{1,0:T(2,128)S(1)}, f32[2,512]{1,0:T(2,128)S(1)}, u32[]{:S(2)}, u32[]{:S(2)}) collective-permute-start(f32[2,512]{1,0:T(2,128)S(1)} %local_stats.1.own_ref), channel_id=1, source_target_pairs={{0,2},{1,3},{2,0},{3,1},{4,6},{5,7},{6,4},{7,5},{8,10},{9,11},{10,... | collective-permute-start | bytes 12296 | tf_op jit(solution)/shard_map/ppermute | solution.py:230
  17.9 3.1 %collective-permute-start.2 = (f32[2,512]{1,0:T(2,128)S(1)}, f32[2,512]{1,0:T(2,128)S(1)}, u32[]{:S(2)}, u32[]{:S(2)}) collective-permute-start(f32[2,512]{1,0:T(2,128)S(1)} %local_stats.1.own_ref), channel_id=1, source_target_pairs={{0,3},{1,2},{2,1},{3,0},{4,7},{5,6},{6,5},{7,4},{8,11},{9,10},{10,... | collective-permute-start | bytes 12296 | tf_op jit(solution)/shard_map/ppermute | solution.py:230
  21.5 2.2 %copy-start.1 = (bf16[4096,512]{1,0:T(8,128)(2,1)S(1)}, bf16[4096,512]{1,0:T(8,128)(2,1)}, u32[]{:S(2)}) copy-start(bf16[4096,512]{1,0:T(8,128)(2,1)} %x_ref.1) | copy-start | bytes 12582916
  28.0 2.0 %collective-permute-start.3 = (f32[2,128,512]{2,1,0:T(8,128)S(1)}, f32[2,128,512]{2,1,0:T(8,128)S(1)}, u32[]{:S(2)}, u32[]{:S(2)}) collective-permute-start(f32[2,128,512]{2,1,0:T(8,128)S(1)} %get-tuple-element.28), channel_id=1, source_target_pairs={{0,1},{1,0},{2,3},{3,2},{4,5},{5,4},{6,7},{7,6},{8,9},{9,8},{10,11... | collective-permute-start | bytes 1572872 | tf_op jit(solution)/shard_map/ppermute | solution.py:230
  30.6 27.2 %collective-permute-start.6 = (f32[128,512]{1,0:T(8,128)S(1)}, f32[128,512]{1,0:T(8,128)S(1)}, u32[]{:S(2)}, u32[]{:S(2)}) collective-permute-start(f32[128,512]{1,0:T(8,128)S(1)} %get-tuple-element.32), channel_id=1, source_target_pairs={{0,2},{1,3},{2,0},{3,1},{4,6},{5,7},{6,4},{7,5},{8,10},{9,11},{10,... | collective-permute-start | bytes 786440 | tf_op jit(solution)/shard_map/ppermute | solution.py:230
  31.2 5.1 %collective-permute-start.5 = (f32[4,512]{1,0:T(4,128)S(1)}, f32[4,512]{1,0:T(4,128)S(1)}, u32[]{:S(2)}, u32[]{:S(2)}) collective-permute-start(f32[4,512]{1,0:T(4,128)S(1)} %stats.1.stat_ref), channel_id=1, source_target_pairs={{0,9},{2,11},{4,13},{6,15},{8,17},{9,0},{10,19},{11,2},{12,21},{13... | collective-permute-start | bytes 24584 | tf_op jit(solution)/shard_map/ppermute | solution.py:230
  33.1 26.7 %collective-permute-start.8 = (f32[4,512]{1,0:T(4,128)S(1)}, f32[4,512]{1,0:T(4,128)S(1)}, u32[]{:S(2)}, u32[]{:S(2)}) collective-permute-start(f32[4,512]{1,0:T(4,128)S(1)} %stats.1.stat_ref), channel_id=1, source_target_pairs={{0,5},{2,7},{5,0},{7,2},{8,13},{10,15},{13,8},{15,10},{16,21},{18,... | collective-permute-start | bytes 24584 | tf_op jit(solution)/shard_map/ppermute | solution.py:230
  57.8 11.4 %collective-permute-start.10 = (bf16[3,256,256]{2,1,0:T(8,128)(2,1)S(1)}, bf16[3,256,256]{2,1,0:T(8,128)(2,1)S(1)}, u32[]{:S(2)}, u32[]{:S(2)}) collective-permute-start(bf16[3,256,256]{2,1,0:T(8,128)(2,1)S(1)} %get-tuple-element.40), channel_id=1, source_target_pairs={{0,2},{1,3},{2,0},{3,1},{4,6},{5,7},{6,4},{7,5},{8,10},{9,11},{10,... | collective-permute-start | bytes 1179656 | tf_op jit(solution)/shard_map/ppermute | solution.py:230
  67.1 9.7 %collective-permute-start.9 = (bf16[3,256,256]{2,1,0:T(8,128)(2,1)S(1)}, bf16[3,256,256]{2,1,0:T(8,128)(2,1)S(1)}, u32[]{:S(2)}, u32[]{:S(2)}) collective-permute-start(bf16[3,256,256]{2,1,0:T(8,128)(2,1)S(1)} %get-tuple-element.36), channel_id=1, source_target_pairs={{0,2},{2,0},{5,7},{7,5},{8,10},{10,8},{13,15},{15,13},{16,18},{18,... | collective-permute-start | bytes 1179656 | tf_op jit(solution)/shard_map/ppermute | solution.py:230
  69.2 13.0 %collective-permute-start.12 = (bf16[3,256,256]{2,1,0:T(8,128)(2,1)S(1)}, bf16[3,256,256]{2,1,0:T(8,128)(2,1)S(1)}, u32[]{:S(2)}, u32[]{:S(2)}) collective-permute-start(bf16[3,256,256]{2,1,0:T(8,128)(2,1)S(1)} %get-tuple-element.45), channel_id=1, source_target_pairs={{0,2},{2,0},{5,7},{7,5},{8,10},{10,8},{13,15},{15,13},{16,18},{18,... | collective-permute-start | bytes 1179656 | tf_op jit(solution)/shard_map/ppermute | solution.py:230
  77.6 10.5 %collective-permute-start.11 = (f32[256,512]{1,0:T(8,128)S(1)}, f32[256,512]{1,0:T(8,128)S(1)}, u32[]{:S(2)}, u32[]{:S(2)}) collective-permute-start(f32[256,512]{1,0:T(8,128)S(1)} %get-tuple-element.43), channel_id=1, source_target_pairs={{0,5},{2,7},{5,0},{7,2},{8,13},{10,15},{13,8},{15,10},{16,21},{18,... | collective-permute-start | bytes 1572872 | tf_op jit(solution)/shard_map/ppermute | solution.py:230
  80.3 10.5 %collective-permute-start.14 = (f32[256,512]{1,0:T(8,128)S(1)}, f32[256,512]{1,0:T(8,128)S(1)}, u32[]{:S(2)}, u32[]{:S(2)}) collective-permute-start(f32[256,512]{1,0:T(8,128)S(1)} %get-tuple-element.48), channel_id=1, source_target_pairs={{0,9},{2,11},{4,13},{6,15},{8,17},{9,0},{10,19},{11,2},{12,21},{13... | collective-permute-start | bytes 1572872 | tf_op jit(solution)/shard_map/ppermute | solution.py:230
  83.0 10.7 %collective-permute-start.13 = (f32[256,512]{1,0:T(8,128)S(1)}, f32[256,512]{1,0:T(8,128)S(1)}, u32[]{:S(2)}, u32[]{:S(2)}) collective-permute-start(f32[256,512]{1,0:T(8,128)S(1)} %get-tuple-element.47), channel_id=1, source_target_pairs={{0,5},{2,7},{5,0},{7,2},{8,13},{10,15},{13,8},{15,10},{16,21},{18,... | collective-permute-start | bytes 1572872 | tf_op jit(solution)/shard_map/ppermute | solution.py:230
  85.4 9.1 %collective-permute-start.15 = (f32[256,512]{1,0:T(8,128)S(1)}, f32[256,512]{1,0:T(8,128)S(1)}, u32[]{:S(2)}, u32[]{:S(2)}) collective-permute-start(f32[256,512]{1,0:T(8,128)S(1)} %get-tuple-element.49), channel_id=1, source_target_pairs={{0,9},{2,11},{8,17},{10,19},{13,4},{15,6},{16,25},{18,27},{21,12},... | collective-permute-start | bytes 1572872 | tf_op jit(solution)/shard_map/ppermute | solution.py:230
  95.2 2.4 %collective-permute-start.16 = (f32[3,128,512]{2,1,0:T(8,128)S(1)}, f32[3,128,512]{2,1,0:T(8,128)S(1)}, u32[]{:S(2)}, u32[]{:S(2)}) collective-permute-start(f32[3,128,512]{2,1,0:T(8,128)S(1)} %get-tuple-element.51), channel_id=1, source_target_pairs={{0,1},{1,0},{2,3},{3,2},{4,5},{5,4},{6,7},{7,6},{8,9},{9,8},{10,11... | collective-permute-start | bytes 2359304 | tf_op jit(solution)/shard_map/ppermute | solution.py:230

commit v6 on v5

--- a/solution.py
+++ b/solution.py
@@ -111,46 +111,43 @@
             out[index] = source[rows, cols].astype(out.dtype)
 
 
-def far_kernel(pos_ref, turned_ref, w_ref, stat_ref, wstat_ref, keep_ref, send_ref, w_out, acc):
-    step = pl.program_id(0)
-
-    @pl.when(step == 0)
-    def _():
-        acc[...] = jnp.zeros_like(acc)
-
-    w = standardized(w_ref[...], wstat_ref)
-    w_out[...] = w
-    acc[...] += dot(turned_ref[...], w)
-
-    @pl.when(step == pl.num_programs(0) - 1)
-    def _():
-        listed = jnp.where(pos_ref[2] == 0, stat_ref[3:4, :], wstat_ref[3:4, :])
-        acc[...] *= listed * (1.0 / pos_ref[4].astype(F32))
-        put_quarters(pos_ref[0], acc, keep_ref, send_ref)
-
-
-def near_kernel(pos_ref, turned_ref, y_ref, w_ref, stat_ref, ystat_ref, wstat_ref, keep_b, send_b, keep_d, send_d, acc_b, acc_d):
-    step = pl.program_id(0)
-
+def fetched(source, parts, sems):
+    rows = parts.shape[1]
+    copies = [pltpu.make_async_copy(source.at[pl.ds(k * rows, rows), :], parts.at[k], sems.at[k])
+              for k in range(parts.shape[0])]
+    for copy in copies:
+        copy.start()
+    return [(slice(k * rows, (k + 1) * rows), copy.wait) for k, copy in enumerate(copies)]
+
+
+def far_kernel(pos_ref, turned_ref, w_ref, stat_ref, wstat_ref, keep_ref, send_ref, w_out, acc, parts, sems):
+    for k, (rows, wait) in enumerate(fetched(w_ref, parts, sems)):
+        wait()
+        w = standardized(parts[k], wstat_ref)
+        w_out[rows, :] = w
+        part = dot(turned_ref[:, rows], w)
+        acc[...] = part if k == 0 else acc[...] + part
+    listed = jnp.where(pos_ref[2] == 0, stat_ref[3:4, :], wstat_ref[3:4, :])
+    acc[...] *= listed * (1.0 / pos_ref[4].astype(F32))
+    put_quarters(pos_ref[0], acc, keep_ref, send_ref)
+
+
+def near_kernel(pos_ref, turned_ref, y_ref, w_ref, stat_ref, ystat_ref, wstat_ref, keep_b, send_b, keep_d, send_d,
+                acc_b, acc_d, parts, sems):
     @pl.when(pos_ref[1] == 1)
     def _():
-        @pl.when(step == 0)
-        def _():
-            acc_b[...] = jnp.zeros_like(acc_b)
-            acc_d[...] = jnp.zeros_like(acc_d)
-
-        y = standardized(y_ref[...], ystat_ref)
-        acc_b[...] += dot(turned_ref[...], y)
-        acc_d[...] += dot(y.T, w_ref[...])
-
-        @pl.when(step == pl.num_programs(0) - 1)
-        def _():
-            first = pos_ref[2] == 0
-            share = 1.0 / pos_ref[4].astype(F32)
-            acc_b[...] *= jnp.where(first, stat_ref[2:3, :], ystat_ref[2:3, :]) * share
-            acc_d[...] *= jnp.where(first, ystat_ref[2:3, :], wstat_ref[2:3, :]) * share
-            put_quarters(pos_ref[0], acc_b, keep_b, send_b)
-            put_quarters(pos_ref[0], acc_d, keep_d, send_d)
+        for k, (rows, wait) in enumerate(fetched(y_ref, parts, sems)):
+            wait()
+            y = standardized(parts[k], ystat_ref)
+            part_b, part_d = dot(turned_ref[:, rows], y), dot(y.T, w_ref[rows, :])
+            acc_b[...] = part_b if k == 0 else acc_b[...] + part_b
+            acc_d[...] = part_d if k == 0 else acc_d[...] + part_d
+        first = pos_ref[2] == 0
+        share = 1.0 / pos_ref[4].astype(F32)
+        acc_b[...] *= jnp.where(first, stat_ref[2:3, :], ystat_ref[2:3, :]) * share
+        acc_d[...] *= jnp.where(first, ystat_ref[2:3, :], wstat_ref[2:3, :]) * share
+        put_quarters(pos_ref[0], acc_b, keep_b, send_b)
+        put_quarters(pos_ref[0], acc_d, keep_d, send_d)
 
 
 def add_halves(x, keep, got, rows_out, cols_out):
@@ -276,18 +273,20 @@
         pos, diag_keep, send(diag_send, sibling))
     diag_got = send(diag_other, across)
 
+    anywhere = pl.BlockSpec(memory_space=pl.ANY)
+    parts = [pltpu.VMEM((steps, step_rows, width), BF16), pltpu.SemaphoreType.DMA((steps,))]
+    sums = pltpu.VMEM((width, width), F32)
+    pair = [shape(3, half, half), shape(3, half, half, dtype=HALVES)]
     keep_c, send_c, w = call(
-        far_kernel, "far_tile", (steps,), [SMEM, flat, wide, whole(4, width), whole(4, width)],
-        [whole(3, half, half)] * 2 + [wide],
-        [shape(3, half, half), shape(3, half, half, dtype=HALVES), shape(depth, width, dtype=BF16)],
-        [pltpu.VMEM((width, width), F32)], tile_flops, 3 * bytes_block)(pos, turned, w_raw, stat, w_stat)
+        far_kernel, "far_tile", (), [SMEM, VMEM, anywhere, VMEM, VMEM], [VMEM] * 3,
+        pair + [shape(depth, width, dtype=BF16)], [sums] + parts, tile_flops, 3 * bytes_block)(
+        pos, turned, w_raw, stat, w_stat)
     send_c, diag_got = lax.optimization_barrier((send_c, diag_got))
     got_c = send(send_c, across)
 
     keep_b, send_b, keep_d, send_d = call(
-        near_kernel, "near_tiles", (steps,), [SMEM, flat, wide, wide] + [whole(4, width)] * 3,
-        [whole(3, half, half)] * 4, [shape(3, half, half, dtype=kind) for kind in (F32, HALVES)] * 2,
-        [pltpu.VMEM((width, width), F32)] * 2, 2 * tile_flops, 3 * bytes_block)(pos, turned, y_raw, w, stat, y_stat, w_stat)
+        near_kernel, "near_tiles", (), [SMEM, VMEM, anywhere] + [VMEM] * 4, [VMEM] * 4, pair * 2, [sums] * 2 + parts,
+        2 * tile_flops, 3 * bytes_block)(pos, turned, y_raw, w, stat, y_stat, w_stat)
     got_b = send(send_b, across_active)
     send_d, got_c = lax.optimization_barrier((send_d, got_c))
     got_d = send(send_d, across_active)
@@ -295,6 +294,7 @@
     held_c, to_z_c = call(far_strips_kernel, "far_strips", (), [SMEM] + [VMEM] * 2, [VMEM] * 2,
                           [shape(half, width)] * 2)(pos, keep_c, got_c)
     from_z_c = send(to_z_c, z_cross)
+    got_b, to_z_c = lax.optimization_barrier((got_b, to_z_c))
 
     def near_strips(name, keep, got):
         return call(near_strips_kernel, name, (), [SMEM] + [VMEM] * 2, [VMEM] * 2, [shape(half, width)] * 2)(pos, keep, got)

time: 100 us -> 97.5 us (0.975)
  Pallas kernels: 24.6 us -> 23.3 us
    pallas_call x2, Pallas kernels: 12.7 us -> 11.3 us  [the longest x1 6.74 us: body(): call(near_kernel, 'near_tiles', (), [SMEM, VMEM, anywhere] + [VMEM] * 4,...]
  transfers between devices with their start and end apart: 17 -> 17, of which waited for: 11 -> 10; matrix products, arithmetic and copies ran while one was open for 0% -> 0% of each run, Pallas kernels for 22% -> 22%
where the time goes in v6:
time: 97.5 us; the launch traced here: 97.1 us
  waiting for transfers between devices  34.8 us (36%)
  starting transfers between devices  33.1 us (34%)
  Pallas kernels  23.3 us (24%)
  local copies, waits for them, and re-layouts  4.46 us (5%)
  between operations  1.48 us (2%)
    ppermute x17, waiting for transfers between devices, send(): return lax.ppermute(value, AXES, pairs)  34.8 us
    ppermute x17, starting transfers between devices, send(): return lax.ppermute(value, AXES, pairs)  33.1 us
    pallas_call x1, Pallas kernels, body(): call(near_kernel, 'near_tiles', (), [SMEM, VMEM, anywhere] + [VMEM] * 4,...  6.74 us
    pallas_call x1, Pallas kernels, body(): call(far_kernel, 'far_tile', (), [SMEM, VMEM, anywhere, VMEM, VMEM], [VME...  4.6 us
    unnamed x6, local copies, waits for them, and re-layouts  4.37 us
    pallas_call x1, Pallas kernels, body(): call(own_kernel, 'own_tile', (steps,), [SMEM, wide, whole(4, width)], [fl...  4.3 us
  transfers between devices with their start and end apart: 17, of which 10 were waited for; matrix products, arithmetic and copies ran while one was open for 0% of the time, Pallas kernels for 22%

profile of v6, /device:TPU:0, one launch (start us, length us, event | category | flops | bytes accessed | tf_op | source)
XLA Modules:
  0.0 97.1 jit_solution(13764776262196107679)
XLA Ops:
  0.6 1.3 %collective-permute-start.4 = (bf16[4096,512]{1,0:T(8,128)(2,1)}, bf16[4096,512]{1,0:T(8,128)(2,1)}, u32[]{:S(2)}, u32[]{:S(2)}) collective-permute-start(bf16[4096,512]{1,0:T(8,128)(2,1)} %x_ref.1), channel_id=1, source_target_pairs={{1,9},{3,11},{5,13},{7,15},{8,0},{9,17},{10,2},{11,19},{12,4},{13,... | collective-permute-start | bytes 12582920 | tf_op jit(solution)/shard_map/ppermute | solution.py:227
  1.9 1.3 %collective-permute-start.7 = (bf16[4096,512]{1,0:T(8,128)(2,1)}, bf16[4096,512]{1,0:T(8,128)(2,1)}, u32[]{:S(2)}, u32[]{:S(2)}) collective-permute-start(bf16[4096,512]{1,0:T(8,128)(2,1)} %x_ref.1), channel_id=1, source_target_pairs={{1,5},{3,7},{4,0},{6,2},{9,13},{11,15},{12,8},{14,10},{17,21},{19,... | collective-permute-start | bytes 12582920 | tf_op jit(solution)/shard_map/ppermute | solution.py:227
  3.2 0.0 copy-start
  3.2 2.2 %copy-done = bf16[4096,512]{1,0:T(8,128)(2,1)S(1)} copy-done((bf16[4096,512]{1,0:T(8,128)(2,1)S(1)}, bf16[4096,512]{1,0:T(8,128)(2,1)}, u32[]{:S(2)}) %copy-start) | copy-done | bytes 4194328
  5.4 1.9 %local_stats.1.own_ref = f32[2,512]{1,0:T(2,128)S(1)} custom-call(bf16[4096,512]{1,0:T(8,128)(2,1)S(1)} %copy-done), custom_call_target="tpu_custom_call" | custom-call | flops 10485760 | bytes 4194304 | tf_op jit(solution)/shard_map/local_stats/pallas_call | solution.py:260
  7.3 9.1 %collective-permute-start = (f32[2,512]{1,0:T(2,128)S(1)}, f32[2,512]{1,0:T(2,128)S(1)}, u32[]{:S(2)}, u32[]{:S(2)}) collective-permute-start(f32[2,512]{1,0:T(2,128)S(1)} %local_stats.1.own_ref), channel_id=1, source_target_pairs={{0,1},{1,0},{2,3},{3,2},{4,5},{5,4},{6,7},{7,6},{8,9},{9,8},{10,11... | collective-permute-start | bytes 12296 | tf_op jit(solution)/shard_map/ppermute | solution.py:227
  16.4 1.5 %collective-permute-start.1 = (f32[2,512]{1,0:T(2,128)S(1)}, f32[2,512]{1,0:T(2,128)S(1)}, u32[]{:S(2)}, u32[]{:S(2)}) collective-permute-start(f32[2,512]{1,0:T(2,128)S(1)} %local_stats.1.own_ref), channel_id=1, source_target_pairs={{0,2},{1,3},{2,0},{3,1},{4,6},{5,7},{6,4},{7,5},{8,10},{9,11},{10,... | collective-permute-start | bytes 12296 | tf_op jit(solution)/shard_map/ppermute | solution.py:227
  17.9 0.0 collective-permute-start.2
  18.5 0.1 stack.23.pos_ref
  18.6 0.0 collective-permute-done.sib_ref
  18.6 1.4 %collective-permute-done.1.far_ref = f32[2,512]{1,0:T(2,128)S(1)} collective-permute-done((f32[2,512]{1,0:T(2,128)S(1)}, f32[2,512]{1,0:T(2,128)S(1)}, u32[]{:S(2)}, u32[]{:S(2)}) %collective-permute-start.1) | collective-permute-done | bytes 4128 | tf_op jit(solution)/shard_map/ppermute | solution.py:227
  20.0 0.9 collective-permute-done.2.cross_ref
  20.9 0.6 stats.1.stat_ref
  21.5 0.0 copy-start.1
  21.5 2.2 %copy-done.1 = bf16[4096,512]{1,0:T(8,128)(2,1)S(1)} copy-done((bf16[4096,512]{1,0:T(8,128)(2,1)S(1)}, bf16[4096,512]{1,0:T(8,128)(2,1)}, u32[]{:S(2)}) %copy-start.1) | copy-done | bytes 4194328
  23.7 4.3 %own_tile.1 = (bf16[512,4096]{1,0:T(8,128)(2,1)S(1)}, f32[2,128,512]{2,1,0:T(8,128)S(1)}, f32[2,128,512]{2,1,0:T(8,128)S(1)}) custom-call(s32[5]{0:T(128)S(1)} %stack.23.pos_ref, bf16[4096,512]{1,0:T(8,128)(2,1)S(1)} %copy-done.1, f32[4,512]{1,0:T(4,128)S(1)} %stats.1.stat_ref), custom_call_target="tpu_custom_call" | custom-call | flops 2147483648 | bytes 8388608 | tf_op jit(solution)/shard_map/own_tile/pallas_call | solution.py:267
  28.0 0.3 collective-permute-start.3
  28.2 1.7 %collective-permute-done.3.got_ref = f32[2,128,512]{2,1,0:T(8,128)S(1)} collective-permute-done((f32[2,128,512]{2,1,0:T(8,128)S(1)}, f32[2,128,512]{2,1,0:T(8,128)S(1)}, u32[]{:S(2)}, u32[]{:S(2)}) %collective-permute-start.3) | collective-permute-done | bytes 524320 | tf_op jit(solution)/shard_map/ppermute | solution.py:227
  30.0 0.6 own_tile_strips.1
  30.6 0.6 collective-permute-start.6
  31.2 1.9 %collective-permute-start.5 = (f32[4,512]{1,0:T(4,128)S(1)}, f32[4,512]{1,0:T(4,128)S(1)}, u32[]{:S(2)}, u32[]{:S(2)}) collective-permute-start(f32[4,512]{1,0:T(4,128)S(1)} %stats.1.stat_ref), channel_id=1, source_target_pairs={{0,9},{2,11},{4,13},{6,15},{8,17},{9,0},{10,19},{11,2},{12,21},{13... | collective-permute-start | bytes 24584 | tf_op jit(solution)/shard_map/ppermute | solution.py:227
  33.1 1.9 %collective-permute-start.8 = (f32[4,512]{1,0:T(4,128)S(1)}, f32[4,512]{1,0:T(4,128)S(1)}, u32[]{:S(2)}, u32[]{:S(2)}) collective-permute-start(f32[4,512]{1,0:T(4,128)S(1)} %stats.1.stat_ref), channel_id=1, source_target_pairs={{0,5},{2,7},{5,0},{7,2},{8,13},{10,15},{13,8},{15,10},{16,21},{18,... | collective-permute-start | bytes 24584 | tf_op jit(solution)/shard_map/ppermute | solution.py:227
  35.1 1.3 %collective-permute-done.5.wstat_ref = f32[4,512]{1,0:T(4,128)S(1)} collective-permute-done((f32[4,512]{1,0:T(4,128)S(1)}, f32[4,512]{1,0:T(4,128)S(1)}, u32[]{:S(2)}, u32[]{:S(2)}) %collective-permute-start.5) | collective-permute-done | bytes 8224 | tf_op jit(solution)/shard_map/ppermute | solution.py:227
  36.3 16.1 %collective-permute-done.4.w_ref = bf16[4096,512]{1,0:T(8,128)(2,1)} collective-permute-done((bf16[4096,512]{1,0:T(8,128)(2,1)}, bf16[4096,512]{1,0:T(8,128)(2,1)}, u32[]{:S(2)}, u32[]{:S(2)}) %collective-permute-start.4) | collective-permute-done | bytes 4194336 | tf_op jit(solution)/shard_map/ppermute | solution.py:227
  52.4 4.6 %far_tile.1 = (f32[3,256,256]{2,1,0:T(8,128)S(1)}, bf16[3,256,256]{2,1,0:T(8,128)(2,1)S(1)}, bf16[4096,512]{1,0:T(8,128)(2,1)S(1)}) custom-call(s32[5]{0:T(128)S(1)} %stack.23.pos_ref, bf16[512,4096]{1,0:T(8,128)(2,1)S(1)} %get-tuple-element.31.turned_ref, bf16[4096,512]{1,0:T(8,128)(2,1)} %collective-permute-done.4.w_ref, f32[4,512]{1,0:T(4,128)S(1)} %stats.1.stat_ref, ...), custom_call_target="tpu_custom_call" | custom-call | flops 2147483648 | bytes 12582912 | tf_op jit(solution)/shard_map/far_tile/pallas_call | solution.py:280
  57.1 0.0 collective-permute-done.6.diag_got
  57.1 2.0 %collective-permute-start.10 = (bf16[3,256,256]{2,1,0:T(8,128)(2,1)S(1)}, bf16[3,256,256]{2,1,0:T(8,128)(2,1)S(1)}, u32[]{:S(2)}, u32[]{:S(2)}) collective-permute-start(bf16[3,256,256]{2,1,0:T(8,128)(2,1)S(1)} %get-tuple-element.40), channel_id=1, source_target_pairs={{0,2},{1,3},{2,0},{3,1},{4,6},{5,7},{6,4},{7,5},{8,10},{9,11},{10,... | collective-permute-start | bytes 1179656 | tf_op jit(solution)/shard_map/ppermute | solution.py:227
  59.1 0.0 collective-permute-done.8.ystat_ref
  59.1 0.0 collective-permute-done.7.y_ref
  59.1 6.7 %near_tiles.1 = (f32[3,256,256]{2,1,0:T(8,128)S(1)}, bf16[3,256,256]{2,1,0:T(8,128)(2,1)S(1)}, f32[3,256,256]{2,1,0:T(8,128)S(1)}, bf16[3,256,256]{2,1,0:T(8,128)(2,1)S(1)}) custom-call(s32[5]{0:T(128)S(1)} %stack.23.pos_ref, bf16[512,4096]{1,0:T(8,128)(2,1)S(1)} %get-tuple-element.31.turned_ref, bf16[4096,512]{1,0:T(8,128)(2,1)} %collective-permute-done.7.y_ref, ...), custom_call_target="tpu_custom_call" | custom-call | flops 4294967296 | bytes 12582912 | tf_op jit(solution)/shard_map/near_tiles/pallas_call | solution.py:287
  65.8 2.0 %collective-permute-start.9 = (bf16[3,256,256]{2,1,0:T(8,128)(2,1)S(1)}, bf16[3,256,256]{2,1,0:T(8,128)(2,1)S(1)}, u32[]{:S(2)}, u32[]{:S(2)}) collective-permute-start(bf16[3,256,256]{2,1,0:T(8,128)(2,1)S(1)} %get-tuple-element.37), channel_id=1, source_target_pairs={{0,2},{2,0},{5,7},{7,5},{8,10},{10,8},{13,15},{15,13},{16,18},{18,... | collective-permute-start | bytes 1179656 | tf_op jit(solution)/shard_map/ppermute | solution.py:227
  67.8 0.0 collective-permute-done.10.got
  67.8 3.8 %collective-permute-start.12 = (bf16[3,256,256]{2,1,0:T(8,128)(2,1)S(1)}, bf16[3,256,256]{2,1,0:T(8,128)(2,1)S(1)}, u32[]{:S(2)}, u32[]{:S(2)}) collective-permute-start(bf16[3,256,256]{2,1,0:T(8,128)(2,1)S(1)} %get-tuple-element.48), channel_id=1, source_target_pairs={{0,2},{2,0},{5,7},{7,5},{8,10},{10,8},{13,15},{15,13},{16,18},{18,... | collective-permute-start | bytes 1179656 | tf_op jit(solution)/shard_map/ppermute | solution.py:227
  71.7 0.7 far_strips.1
  72.4 1.9 %collective-permute-start.14 = (f32[256,512]{1,0:T(8,128)S(1)}, f32[256,512]{1,0:T(8,128)S(1)}, u32[]{:S(2)}, u32[]{:S(2)}) collective-permute-start(f32[256,512]{1,0:T(8,128)S(1)} %get-tuple-element.42), channel_id=1, source_target_pairs={{0,9},{2,11},{4,13},{6,15},{8,17},{9,0},{10,19},{11,2},{12,21},{13... | collective-permute-start | bytes 1572872 | tf_op jit(solution)/shard_map/ppermute | solution.py:227
  74.4 1.1 %collective-permute-done.9.got = bf16[3,256,256]{2,1,0:T(8,128)(2,1)S(1)} collective-permute-done((bf16[3,256,256]{2,1,0:T(8,128)(2,1)S(1)}, bf16[3,256,256]{2,1,0:T(8,128)(2,1)S(1)}, u32[]{:S(2)}, u32[]{:S(2)}) %collective-permute-start.9) | collective-permute-done | bytes 393248 | tf_op jit(solution)/shard_map/ppermute | solution.py:227
  75.5 0.8 near_strips.1
  76.2 1.9 %collective-permute-start.11 = (f32[256,512]{1,0:T(8,128)S(1)}, f32[256,512]{1,0:T(8,128)S(1)}, u32[]{:S(2)}, u32[]{:S(2)}) collective-permute-start(f32[256,512]{1,0:T(8,128)S(1)} %get-tuple-element.46), channel_id=1, source_target_pairs={{0,5},{2,7},{5,0},{7,2},{8,13},{10,15},{13,8},{15,10},{16,21},{18,... | collective-permute-start | bytes 1572872 | tf_op jit(solution)/shard_map/ppermute | solution.py:227
  78.2 1.5 %collective-permute-done.12.got = bf16[3,256,256]{2,1,0:T(8,128)(2,1)S(1)} collective-permute-done((bf16[3,256,256]{2,1,0:T(8,128)(2,1)S(1)}, bf16[3,256,256]{2,1,0:T(8,128)(2,1)S(1)}, u32[]{:S(2)}, u32[]{:S(2)}) %collective-permute-start.12) | collective-permute-done | bytes 393248 | tf_op jit(solution)/shard_map/ppermute | solution.py:227
  79.7 0.7 cross_strips.1
  80.4 2.1 %collective-permute-start.13 = (f32[256,512]{1,0:T(8,128)S(1)}, f32[256,512]{1,0:T(8,128)S(1)}, u32[]{:S(2)}, u32[]{:S(2)}) collective-permute-start(f32[256,512]{1,0:T(8,128)S(1)} %get-tuple-element.50), channel_id=1, source_target_pairs={{0,5},{2,7},{5,0},{7,2},{8,13},{10,15},{13,8},{15,10},{16,21},{18,... | collective-permute-start | bytes 1572872 | tf_op jit(solution)/shard_map/ppermute | solution.py:227
  82.6 1.3 %collective-permute-start.15 = (f32[256,512]{1,0:T(8,128)S(1)}, f32[256,512]{1,0:T(8,128)S(1)}, u32[]{:S(2)}, u32[]{:S(2)}) collective-permute-start(f32[256,512]{1,0:T(8,128)S(1)} %get-tuple-element.51), channel_id=1, source_target_pairs={{0,9},{2,11},{8,17},{10,19},{13,4},{15,6},{16,25},{18,27},{21,12},... | collective-permute-start | bytes 1572872 | tf_op jit(solution)/shard_map/ppermute | solution.py:227
  83.9 2.8 %collective-permute-done.11.from_y_b = f32[256,512]{1,0:T(8,128)S(1)} collective-permute-done((f32[256,512]{1,0:T(8,128)S(1)}, f32[256,512]{1,0:T(8,128)S(1)}, u32[]{:S(2)}, u32[]{:S(2)}) %collective-permute-start.11) | collective-permute-done | bytes 524320 | tf_op jit(solution)/shard_map/ppermute | solution.py:227
  86.7 5.6 %collective-permute-done.13.from_y_d = f32[256,512]{1,0:T(8,128)S(1)} collective-permute-done((f32[256,512]{1,0:T(8,128)S(1)}, f32[256,512]{1,0:T(8,128)S(1)}, u32[]{:S(2)}, u32[]{:S(2)}) %collective-permute-start.13) | collective-permute-done | bytes 524320 | tf_op jit(solution)/shard_map/ppermute | solution.py:227
  92.4 0.7 combine.1
  93.1 0.1 collective-permute-start.16
  93.2 2.3 %collective-permute-done.16.sib = f32[3,128,512]{2,1,0:T(8,128)S(1)} collective-permute-done((f32[3,128,512]{2,1,0:T(8,128)S(1)}, f32[3,128,512]{2,1,0:T(8,128)S(1)}, u32[]{:S(2)}, u32[]{:S(2)}) %collective-permute-start.16) | collective-permute-done | bytes 786464 | tf_op jit(solution)/shard_map/ppermute | solution.py:227
  95.4 1.7 %finish.1 = (bf16[1,3,128,512]{3,2,1,0:T(8,128)(2,1)}, bf16[1,2,128,512]{3,2,1,0:T(8,128)(2,1)}) custom-call(s32[5]{0:T(128)S(1)} %stack.23.pos_ref, s32[1,3]{1,0:T(1,128)S(1)} %copy-done.2, f32[128,512]{1,0:T(8,128)S(1)} %get-tuple-element.30.diag_mine, f32[128,512]{1,0:T(8,128)S(1)} %collective-permute-done.6.diag_got, ...), custom_call_target="tpu_custom_call" | custom-call | tf_op jit(solution)/shard_map/finish/pallas_call | solution.py:310
  (4 shorter events, 0.0 us)
Async XLA Ops:
  0.6 51.8 %collective-permute-start.4 = (bf16[4096,512]{1,0:T(8,128)(2,1)}, bf16[4096,512]{1,0:T(8,128)(2,1)}, u32[]{:S(2)}, u32[]{:S(2)}) collective-permute-start(bf16[4096,512]{1,0:T(8,128)(2,1)} %x_ref.1), channel_id=1, source_target_pairs={{1,9},{3,11},{5,13},{7,15},{8,0},{9,17},{10,2},{11,19},{12,4},{13,... | collective-permute-start | bytes 12582920 | tf_op jit(solution)/shard_map/ppermute | solution.py:227
  1.9 57.1 %collective-permute-start.7 = (bf16[4096,512]{1,0:T(8,128)(2,1)}, bf16[4096,512]{1,0:T(8,128)(2,1)}, u32[]{:S(2)}, u32[]{:S(2)}) collective-permute-start(bf16[4096,512]{1,0:T(8,128)(2,1)} %x_ref.1), channel_id=1, source_target_pairs={{1,5},{3,7},{4,0},{6,2},{9,13},{11,15},{12,8},{14,10},{17,21},{19,... | collective-permute-start | bytes 12582920 | tf_op jit(solution)/shard_map/ppermute | solution.py:227
  3.2 2.2 %copy-start = (bf16[4096,512]{1,0:T(8,128)(2,1)S(1)}, bf16[4096,512]{1,0:T(8,128)(2,1)}, u32[]{:S(2)}) copy-start(bf16[4096,512]{1,0:T(8,128)(2,1)} %x_ref.1) | copy-start | bytes 12582916
  5.4 15.5 %copy-start.2 = (s32[1,3]{1,0:T(1,128)S(1)}, s32[1,3]{1,0:T(1,128)}, u32[]{:S(2)}) copy-start(s32[1,3]{1,0:T(1,128)} %offsets_ref.3) | copy-start | bytes 40
  7.3 11.3 %collective-permute-start = (f32[2,512]{1,0:T(2,128)S(1)}, f32[2,512]{1,0:T(2,128)S(1)}, u32[]{:S(2)}, u32[]{:S(2)}) collective-permute-start(f32[2,512]{1,0:T(2,128)S(1)} %local_stats.1.own_ref), channel_id=1, source_target_pairs={{0,1},{1,0},{2,3},{3,2},{4,5},{5,4},{6,7},{7,6},{8,9},{9,8},{10,11... | collective-permute-start | bytes 12296 | tf_op jit(solution)/shard_map/ppermute | solution.py:227
  16.4 3.6 %collective-permute-start.1 = (f32[2,512]{1,0:T(2,128)S(1)}, f32[2,512]{1,0:T(2,128)S(1)}, u32[]{:S(2)}, u32[]{:S(2)}) collective-permute-start(f32[2,512]{1,0:T(2,128)S(1)} %local_stats.1.own_ref), channel_id=1, source_target_pairs={{0,2},{1,3},{2,0},{3,1},{4,6},{5,7},{6,4},{7,5},{8,10},{9,11},{10,... | collective-permute-start | bytes 12296 | tf_op jit(solution)/shard_map/ppermute | solution.py:227
  17.9 3.1 %collective-permute-start.2 = (f32[2,512]{1,0:T(2,128)S(1)}, f32[2,512]{1,0:T(2,128)S(1)}, u32[]{:S(2)}, u32[]{:S(2)}) collective-permute-start(f32[2,512]{1,0:T(2,128)S(1)} %local_stats.1.own_ref), channel_id=1, source_target_pairs={{0,3},{1,2},{2,1},{3,0},{4,7},{5,6},{6,5},{7,4},{8,11},{9,10},{10,... | collective-permute-start | bytes 12296 | tf_op jit(solution)/shard_map/ppermute | solution.py:227
  21.5 2.2 %copy-start.1 = (bf16[4096,512]{1,0:T(8,128)(2,1)S(1)}, bf16[4096,512]{1,0:T(8,128)(2,1)}, u32[]{:S(2)}) copy-start(bf16[4096,512]{1,0:T(8,128)(2,1)} %x_ref.1) | copy-start | bytes 12582916
  28.0 2.0 %collective-permute-start.3 = (f32[2,128,512]{2,1,0:T(8,128)S(1)}, f32[2,128,512]{2,1,0:T(8,128)S(1)}, u32[]{:S(2)}, u32[]{:S(2)}) collective-permute-start(f32[2,128,512]{2,1,0:T(8,128)S(1)} %get-tuple-element.29), channel_id=1, source_target_pairs={{0,1},{1,0},{2,3},{3,2},{4,5},{5,4},{6,7},{7,6},{8,9},{9,8},{10,11... | collective-permute-start | bytes 1572872 | tf_op jit(solution)/shard_map/ppermute | solution.py:227
  30.6 26.5 %collective-permute-start.6 = (f32[128,512]{1,0:T(8,128)S(1)}, f32[128,512]{1,0:T(8,128)S(1)}, u32[]{:S(2)}, u32[]{:S(2)}) collective-permute-start(f32[128,512]{1,0:T(8,128)S(1)} %get-tuple-element.33), channel_id=1, source_target_pairs={{0,2},{1,3},{2,0},{3,1},{4,6},{5,7},{6,4},{7,5},{8,10},{9,11},{10,... | collective-permute-start | bytes 786440 | tf_op jit(solution)/shard_map/ppermute | solution.py:227
  31.2 5.1 %collective-permute-start.5 = (f32[4,512]{1,0:T(4,128)S(1)}, f32[4,512]{1,0:T(4,128)S(1)}, u32[]{:S(2)}, u32[]{:S(2)}) collective-permute-start(f32[4,512]{1,0:T(4,128)S(1)} %stats.1.stat_ref), channel_id=1, source_target_pairs={{0,9},{2,11},{4,13},{6,15},{8,17},{9,0},{10,19},{11,2},{12,21},{13... | collective-permute-start | bytes 24584 | tf_op jit(solution)/shard_map/ppermute | solution.py:227
  33.1 25.9 %collective-permute-start.8 = (f32[4,512]{1,0:T(4,128)S(1)}, f32[4,512]{1,0:T(4,128)S(1)}, u32[]{:S(2)}, u32[]{:S(2)}) collective-permute-start(f32[4,512]{1,0:T(4,128)S(1)} %stats.1.stat_ref), channel_id=1, source_target_pairs={{0,5},{2,7},{5,0},{7,2},{8,13},{10,15},{13,8},{15,10},{16,21},{18,... | collective-permute-start | bytes 24584 | tf_op jit(solution)/shard_map/ppermute | solution.py:227
  57.1 10.8 %collective-permute-start.10 = (bf16[3,256,256]{2,1,0:T(8,128)(2,1)S(1)}, bf16[3,256,256]{2,1,0:T(8,128)(2,1)S(1)}, u32[]{:S(2)}, u32[]{:S(2)}) collective-permute-start(bf16[3,256,256]{2,1,0:T(8,128)(2,1)S(1)} %get-tuple-element.40), channel_id=1, source_target_pairs={{0,2},{1,3},{2,0},{3,1},{4,6},{5,7},{6,4},{7,5},{8,10},{9,11},{10,... | collective-permute-start | bytes 1179656 | tf_op jit(solution)/shard_map/ppermute | solution.py:227
  65.8 9.7 %collective-permute-start.9 = (bf16[3,256,256]{2,1,0:T(8,128)(2,1)S(1)}, bf16[3,256,256]{2,1,0:T(8,128)(2,1)S(1)}, u32[]{:S(2)}, u32[]{:S(2)}) collective-permute-start(bf16[3,256,256]{2,1,0:T(8,128)(2,1)S(1)} %get-tuple-element.37), channel_id=1, source_target_pairs={{0,2},{2,0},{5,7},{7,5},{8,10},{10,8},{13,15},{15,13},{16,18},{18,... | collective-permute-start | bytes 1179656 | tf_op jit(solution)/shard_map/ppermute | solution.py:227
  67.8 11.9 %collective-permute-start.12 = (bf16[3,256,256]{2,1,0:T(8,128)(2,1)S(1)}, bf16[3,256,256]{2,1,0:T(8,128)(2,1)S(1)}, u32[]{:S(2)}, u32[]{:S(2)}) collective-permute-start(bf16[3,256,256]{2,1,0:T(8,128)(2,1)S(1)} %get-tuple-element.48), channel_id=1, source_target_pairs={{0,2},{2,0},{5,7},{7,5},{8,10},{10,8},{13,15},{15,13},{16,18},{18,... | collective-permute-start | bytes 1179656 | tf_op jit(solution)/shard_map/ppermute | solution.py:227
  72.4 14.3 %collective-permute-start.14 = (f32[256,512]{1,0:T(8,128)S(1)}, f32[256,512]{1,0:T(8,128)S(1)}, u32[]{:S(2)}, u32[]{:S(2)}) collective-permute-start(f32[256,512]{1,0:T(8,128)S(1)} %get-tuple-element.42), channel_id=1, source_target_pairs={{0,9},{2,11},{4,13},{6,15},{8,17},{9,0},{10,19},{11,2},{12,21},{13... | collective-permute-start | bytes 1572872 | tf_op jit(solution)/shard_map/ppermute | solution.py:227
  76.2 10.5 %collective-permute-start.11 = (f32[256,512]{1,0:T(8,128)S(1)}, f32[256,512]{1,0:T(8,128)S(1)}, u32[]{:S(2)}, u32[]{:S(2)}) collective-permute-start(f32[256,512]{1,0:T(8,128)S(1)} %get-tuple-element.46), channel_id=1, source_target_pairs={{0,5},{2,7},{5,0},{7,2},{8,13},{10,15},{13,8},{15,10},{16,21},{18,... | collective-permute-start | bytes 1572872 | tf_op jit(solution)/shard_map/ppermute | solution.py:227
  80.4 11.9 %collective-permute-start.13 = (f32[256,512]{1,0:T(8,128)S(1)}, f32[256,512]{1,0:T(8,128)S(1)}, u32[]{:S(2)}, u32[]{:S(2)}) collective-permute-start(f32[256,512]{1,0:T(8,128)S(1)} %get-tuple-element.50), channel_id=1, source_target_pairs={{0,5},{2,7},{5,0},{7,2},{8,13},{10,15},{13,8},{15,10},{16,21},{18,... | collective-permute-start | bytes 1572872 | tf_op jit(solution)/shard_map/ppermute | solution.py:227
  82.6 9.8 %collective-permute-start.15 = (f32[256,512]{1,0:T(8,128)S(1)}, f32[256,512]{1,0:T(8,128)S(1)}, u32[]{:S(2)}, u32[]{:S(2)}) collective-permute-start(f32[256,512]{1,0:T(8,128)S(1)} %get-tuple-element.51), channel_id=1, source_target_pairs={{0,9},{2,11},{8,17},{10,19},{13,4},{15,6},{16,25},{18,27},{21,12},... | collective-permute-start | bytes 1572872 | tf_op jit(solution)/shard_map/ppermute | solution.py:227
  93.1 2.4 %collective-permute-start.16 = (f32[3,128,512]{2,1,0:T(8,128)S(1)}, f32[3,128,512]{2,1,0:T(8,128)S(1)}, u32[]{:S(2)}, u32[]{:S(2)}) collective-permute-start(f32[3,128,512]{2,1,0:T(8,128)S(1)} %get-tuple-element.53), channel_id=1, source_target_pairs={{0,1},{1,0},{2,3},{3,2},{4,5},{5,4},{6,7},{7,6},{8,9},{9,8},{10,11... | collective-permute-start | bytes 2359304 | tf_op jit(solution)/shard_map/ppermute | solution.py:227

commit v7 on v6

--- a/solution.py
+++ b/solution.py
@@ -120,34 +120,44 @@
     return [(slice(k * rows, (k + 1) * rows), copy.wait) for k, copy in enumerate(copies)]
 
 
-def far_kernel(pos_ref, turned_ref, w_ref, stat_ref, wstat_ref, keep_ref, send_ref, w_out, acc, parts, sems):
-    for k, (rows, wait) in enumerate(fetched(w_ref, parts, sems)):
-        wait()
-        w = standardized(parts[k], wstat_ref)
-        w_out[rows, :] = w
-        part = dot(turned_ref[:, rows], w)
-        acc[...] = part if k == 0 else acc[...] + part
-    listed = jnp.where(pos_ref[2] == 0, stat_ref[3:4, :], wstat_ref[3:4, :])
-    acc[...] *= listed * (1.0 / pos_ref[4].astype(F32))
-    put_quarters(pos_ref[0], acc, keep_ref, send_ref)
-
-
-def near_kernel(pos_ref, turned_ref, y_ref, w_ref, stat_ref, ystat_ref, wstat_ref, keep_b, send_b, keep_d, send_d,
-                acc_b, acc_d, parts, sems):
+def near_kernel(pos_ref, turned_ref, y_ref, stat_ref, ystat_ref, keep_ref, send_ref, y_out, acc, parts, sems):
     @pl.when(pos_ref[1] == 1)
     def _():
         for k, (rows, wait) in enumerate(fetched(y_ref, parts, sems)):
             wait()
             y = standardized(parts[k], ystat_ref)
-            part_b, part_d = dot(turned_ref[:, rows], y), dot(y.T, w_ref[rows, :])
-            acc_b[...] = part_b if k == 0 else acc_b[...] + part_b
-            acc_d[...] = part_d if k == 0 else acc_d[...] + part_d
-        first = pos_ref[2] == 0
-        share = 1.0 / pos_ref[4].astype(F32)
-        acc_b[...] *= jnp.where(first, stat_ref[2:3, :], ystat_ref[2:3, :]) * share
-        acc_d[...] *= jnp.where(first, ystat_ref[2:3, :], wstat_ref[2:3, :]) * share
-        put_quarters(pos_ref[0], acc_b, keep_b, send_b)
-        put_quarters(pos_ref[0], acc_d, keep_d, send_d)
+            y_out[:, rows] = y.T
+            part = dot(turned_ref[:, rows], y)
+            acc[...] = part if k == 0 else acc[...] + part
+        listed = jnp.where(pos_ref[2] == 0, stat_ref[2:3, :], ystat_ref[2:3, :])
+        acc[...] *= listed * (1.0 / pos_ref[4].astype(F32))
+        put_quarters(pos_ref[0], acc, keep_ref, send_ref)
+
+
+def far_kernel(pos_ref, turned_ref, w_ref, y_ref, stat_ref, ystat_ref, wstat_ref, keep_c, send_c, keep_d, send_d,
+               acc_c, acc_d, parts, sems):
+    first = pos_ref[2] == 0
+    share = 1.0 / pos_ref[4].astype(F32)
+
+    def run(with_y):
+        for k, (rows, wait) in enumerate(fetched(w_ref, parts, sems)):
+            wait()
+            w = standardized(parts[k], wstat_ref)
+            part = dot(turned_ref[:, rows], w)
+            acc_c[...] = part if k == 0 else acc_c[...] + part
+            if with_y:
+                part = dot(y_ref[:, rows], w)
+                acc_d[...] = part if k == 0 else acc_d[...] + part
+        acc_c[...] *= jnp.where(first, stat_ref[3:4, :], wstat_ref[3:4, :]) * share
+        put_quarters(pos_ref[0], acc_c, keep_c, send_c)
+        if with_y:
+            acc_d[...] *= jnp.where(first, ystat_ref[2:3, :], wstat_ref[2:3, :]) * share
+            put_quarters(pos_ref[0], acc_d, keep_d, send_d)
+
+    for with_y in (True, False):
+        @pl.when((pos_ref[1] == 1) == with_y)
+        def _():
+            run(with_y)
 
 
 def add_halves(x, keep, got, rows_out, cols_out):
@@ -241,7 +251,7 @@
     across_active = [(at(a, b), at(a, b ^ 2)) for a, b in everyone if active_on(a, b)]
     sibling = [(at(a, b), at(a, b ^ 1)) for a, b in everyone]
 
-    w_raw, y_raw = send(dosage, z_main), send(dosage, y_main)
+    y_raw, w_raw = send(dosage, y_main), send(dosage, z_main)
 
     pos = jnp.stack([x, active, core, odd, jnp.int32(samples_all)]).astype(jnp.int32)
     step_rows = min(1024, depth)
@@ -277,24 +287,17 @@
     parts = [pltpu.VMEM((steps, step_rows, width), BF16), pltpu.SemaphoreType.DMA((steps,))]
     sums = pltpu.VMEM((width, width), F32)
     pair = [shape(3, half, half), shape(3, half, half, dtype=HALVES)]
-    keep_c, send_c, w = call(
-        far_kernel, "far_tile", (), [SMEM, VMEM, anywhere, VMEM, VMEM], [VMEM] * 3,
-        pair + [shape(depth, width, dtype=BF16)], [sums] + parts, tile_flops, 3 * bytes_block)(
-        pos, turned, w_raw, stat, w_stat)
-    send_c, diag_got = lax.optimization_barrier((send_c, diag_got))
-    got_c = send(send_c, across)
-
-    keep_b, send_b, keep_d, send_d = call(
-        near_kernel, "near_tiles", (), [SMEM, VMEM, anywhere] + [VMEM] * 4, [VMEM] * 4, pair * 2, [sums] * 2 + parts,
-        2 * tile_flops, 3 * bytes_block)(pos, turned, y_raw, w, stat, y_stat, w_stat)
+    keep_b, send_b, y = call(
+        near_kernel, "near_tile", (), [SMEM, VMEM, anywhere, VMEM, VMEM], [VMEM] * 3,
+        pair + [shape(width, depth, dtype=BF16)], [sums] + parts, tile_flops, 3 * bytes_block)(
+        pos, turned, y_raw, stat, y_stat)
+    send_b, diag_got = lax.optimization_barrier((send_b, diag_got))
     got_b = send(send_b, across_active)
-    send_d, got_c = lax.optimization_barrier((send_d, got_c))
-    got_d = send(send_d, across_active)
-
-    held_c, to_z_c = call(far_strips_kernel, "far_strips", (), [SMEM] + [VMEM] * 2, [VMEM] * 2,
-                          [shape(half, width)] * 2)(pos, keep_c, got_c)
-    from_z_c = send(to_z_c, z_cross)
-    got_b, to_z_c = lax.optimization_barrier((got_b, to_z_c))
+    keep_c, send_c, keep_d, send_d = call(
+        far_kernel, "far_tiles", (), [SMEM, VMEM, anywhere] + [VMEM] * 4, [VMEM] * 4, pair * 2, [sums] * 2 + parts,
+        2 * tile_flops, 3 * bytes_block)(pos, turned, w_raw, y, stat, y_stat, w_stat)
+    send_d, got_b = lax.optimization_barrier((send_d, got_b))
+    got_d, got_c = send(send_d, across_active), send(send_c, across)
 
     def near_strips(name, keep, got):
         return call(near_strips_kernel, name, (), [SMEM] + [VMEM] * 2, [VMEM] * 2, [shape(half, width)] * 2)(pos, keep, got)
@@ -304,6 +307,11 @@
     got_d, to_y_b = lax.optimization_barrier((got_d, to_y_b))
     to_y_d, to_z_d = near_strips("cross_strips", keep_d, got_d)
     from_y_d, from_z_d = send(to_y_d, y_cross), send(to_z_d, z_cross_active)
+    got_c, to_y_d, to_z_d = lax.optimization_barrier((got_c, to_y_d, to_z_d))
+    held_c, to_z_c = call(far_strips_kernel, "far_strips", (), [SMEM] + [VMEM] * 2, [VMEM] * 2,
+                          [shape(half, width)] * 2)(pos, keep_c, got_c)
+    to_z_c, from_z_d = lax.optimization_barrier((to_z_c, from_z_d))
+    from_z_c = send(to_z_c, z_cross)
 
     mine, sib = call(combine_kernel, "combine", (), [SMEM] + [VMEM] * 6, [VMEM] * 2, [shape(3, strip, width)] * 2)(
         pos, held_b, held_c, from_y_b, from_y_d, from_z_c, from_z_d)

time: 97.5 us -> 104 us (1.067)
  starting transfers between devices: 33.1 us -> 37.8 us
  waiting for transfers between devices: 34.8 us -> 36.6 us
    ppermute x17, starting transfers between devices: 33.1 us -> 37.8 us  [send(): return lax.ppermute(value, AXES, pairs)]
    ppermute x17, waiting for transfers between devices: 34.8 us -> 36.6 us  [send(): return lax.ppermute(value, AXES, pairs)]
  transfers between devices with their start and end apart: 17 -> 17, of which waited for: 10 -> 11; matrix products, arithmetic and copies ran while one was open for 0% -> 0% of each run, Pallas kernels for 22% -> 20%
where the time goes in v7:
time: 104 us
  starting transfers between devices  37.8 us (36%)
  waiting for transfers between devices  36.6 us (35%)
  Pallas kernels  23.5 us (23%)
  local copies, waits for them, and re-layouts  4.46 us (4%)
  between operations  1.51 us (1%)
    ppermute x17, starting transfers between devices, send(): return lax.ppermute(value, AXES, pairs)  37.8 us
    ppermute x17, waiting for transfers between devices, send(): return lax.ppermute(value, AXES, pairs)  36.6 us
    pallas_call x1, Pallas kernels, body(): call(far_kernel, 'far_tiles', (), [SMEM, VMEM, anywhere] + [VMEM] * 4, [V...  6.8 us
    pallas_call x1, Pallas kernels, body(): call(near_kernel, 'near_tile', (), [SMEM, VMEM, anywhere, VMEM, VMEM], [V...  4.74 us
    unnamed x6, local copies, waits for them, and re-layouts  4.37 us
    pallas_call x1, Pallas kernels, body(): call(own_kernel, 'own_tile', (steps,), [SMEM, wide, whole(4, width)], [fl...  4.3 us
  transfers between devices with their start and end apart: 17, of which 11 were waited for; matrix products, arithmetic and copies ran while one was open for 0% of the time, Pallas kernels for 20%

profile of v7, /device:TPU:0, one launch (start us, length us, event | category | flops | bytes accessed | tf_op | source)
XLA Modules:
  0.0 103.8 jit_solution(8622316324025890636)
XLA Ops:
  0.6 1.3 %collective-permute-start.4 = (bf16[4096,512]{1,0:T(8,128)(2,1)}, bf16[4096,512]{1,0:T(8,128)(2,1)}, u32[]{:S(2)}, u32[]{:S(2)}) collective-permute-start(bf16[4096,512]{1,0:T(8,128)(2,1)} %x_ref.1), channel_id=1, source_target_pairs={{1,5},{3,7},{4,0},{6,2},{9,13},{11,15},{12,8},{14,10},{17,21},{19,... | collective-permute-start | bytes 12582920 | tf_op jit(solution)/shard_map/ppermute | solution.py:237
  1.9 1.3 %collective-permute-start.7 = (bf16[4096,512]{1,0:T(8,128)(2,1)}, bf16[4096,512]{1,0:T(8,128)(2,1)}, u32[]{:S(2)}, u32[]{:S(2)}) collective-permute-start(bf16[4096,512]{1,0:T(8,128)(2,1)} %x_ref.1), channel_id=1, source_target_pairs={{1,9},{3,11},{5,13},{7,15},{8,0},{9,17},{10,2},{11,19},{12,4},{13,... | collective-permute-start | bytes 12582920 | tf_op jit(solution)/shard_map/ppermute | solution.py:237
  3.2 0.0 copy-start
  3.2 2.2 %copy-done = bf16[4096,512]{1,0:T(8,128)(2,1)S(1)} copy-done((bf16[4096,512]{1,0:T(8,128)(2,1)S(1)}, bf16[4096,512]{1,0:T(8,128)(2,1)}, u32[]{:S(2)}) %copy-start) | copy-done | bytes 4194328
  5.4 1.9 %local_stats.1.own_ref = f32[2,512]{1,0:T(2,128)S(1)} custom-call(bf16[4096,512]{1,0:T(8,128)(2,1)S(1)} %copy-done), custom_call_target="tpu_custom_call" | custom-call | flops 10485760 | bytes 4194304 | tf_op jit(solution)/shard_map/local_stats/pallas_call | solution.py:270
  7.3 9.1 %collective-permute-start = (f32[2,512]{1,0:T(2,128)S(1)}, f32[2,512]{1,0:T(2,128)S(1)}, u32[]{:S(2)}, u32[]{:S(2)}) collective-permute-start(f32[2,512]{1,0:T(2,128)S(1)} %local_stats.1.own_ref), channel_id=1, source_target_pairs={{0,1},{1,0},{2,3},{3,2},{4,5},{5,4},{6,7},{7,6},{8,9},{9,8},{10,11... | collective-permute-start | bytes 12296 | tf_op jit(solution)/shard_map/ppermute | solution.py:237
  16.4 1.5 %collective-permute-start.1 = (f32[2,512]{1,0:T(2,128)S(1)}, f32[2,512]{1,0:T(2,128)S(1)}, u32[]{:S(2)}, u32[]{:S(2)}) collective-permute-start(f32[2,512]{1,0:T(2,128)S(1)} %local_stats.1.own_ref), channel_id=1, source_target_pairs={{0,2},{1,3},{2,0},{3,1},{4,6},{5,7},{6,4},{7,5},{8,10},{9,11},{10,... | collective-permute-start | bytes 12296 | tf_op jit(solution)/shard_map/ppermute | solution.py:237
  17.9 0.0 collective-permute-start.2
  18.5 0.1 stack.23.pos_ref
  18.6 0.0 collective-permute-done.sib_ref
  18.6 1.4 %collective-permute-done.1.far_ref = f32[2,512]{1,0:T(2,128)S(1)} collective-permute-done((f32[2,512]{1,0:T(2,128)S(1)}, f32[2,512]{1,0:T(2,128)S(1)}, u32[]{:S(2)}, u32[]{:S(2)}) %collective-permute-start.1) | collective-permute-done | bytes 4128 | tf_op jit(solution)/shard_map/ppermute | solution.py:237
  20.0 0.9 collective-permute-done.2.cross_ref
  20.9 0.6 stats.1.stat_ref
  21.5 0.0 copy-start.1
  21.5 2.2 %copy-done.1 = bf16[4096,512]{1,0:T(8,128)(2,1)S(1)} copy-done((bf16[4096,512]{1,0:T(8,128)(2,1)S(1)}, bf16[4096,512]{1,0:T(8,128)(2,1)}, u32[]{:S(2)}) %copy-start.1) | copy-done | bytes 4194328
  23.7 4.3 %own_tile.1 = (bf16[512,4096]{1,0:T(8,128)(2,1)S(1)}, f32[2,128,512]{2,1,0:T(8,128)S(1)}, f32[2,128,512]{2,1,0:T(8,128)S(1)}) custom-call(s32[5]{0:T(128)S(1)} %stack.23.pos_ref, bf16[4096,512]{1,0:T(8,128)(2,1)S(1)} %copy-done.1, f32[4,512]{1,0:T(4,128)S(1)} %stats.1.stat_ref), custom_call_target="tpu_custom_call" | custom-call | flops 2147483648 | bytes 8388608 | tf_op jit(solution)/shard_map/own_tile/pallas_call | solution.py:277
  28.0 0.3 collective-permute-start.3
  28.2 1.7 %collective-permute-done.3.got_ref = f32[2,128,512]{2,1,0:T(8,128)S(1)} collective-permute-done((f32[2,128,512]{2,1,0:T(8,128)S(1)}, f32[2,128,512]{2,1,0:T(8,128)S(1)}, u32[]{:S(2)}, u32[]{:S(2)}) %collective-permute-start.3) | collective-permute-done | bytes 524320 | tf_op jit(solution)/shard_map/ppermute | solution.py:237
  30.0 0.6 own_tile_strips.1
  30.6 0.6 collective-permute-start.6
  31.2 1.9 %collective-permute-start.5 = (f32[4,512]{1,0:T(4,128)S(1)}, f32[4,512]{1,0:T(4,128)S(1)}, u32[]{:S(2)}, u32[]{:S(2)}) collective-permute-start(f32[4,512]{1,0:T(4,128)S(1)} %stats.1.stat_ref), channel_id=1, source_target_pairs={{0,5},{2,7},{5,0},{7,2},{8,13},{10,15},{13,8},{15,10},{16,21},{18,... | collective-permute-start | bytes 24584 | tf_op jit(solution)/shard_map/ppermute | solution.py:237
  33.1 1.9 %collective-permute-start.8 = (f32[4,512]{1,0:T(4,128)S(1)}, f32[4,512]{1,0:T(4,128)S(1)}, u32[]{:S(2)}, u32[]{:S(2)}) collective-permute-start(f32[4,512]{1,0:T(4,128)S(1)} %stats.1.stat_ref), channel_id=1, source_target_pairs={{0,9},{2,11},{4,13},{6,15},{8,17},{9,0},{10,19},{11,2},{12,21},{13... | collective-permute-start | bytes 24584 | tf_op jit(solution)/shard_map/ppermute | solution.py:237
  35.1 1.3 %collective-permute-done.5.ystat_ref = f32[4,512]{1,0:T(4,128)S(1)} collective-permute-done((f32[4,512]{1,0:T(4,128)S(1)}, f32[4,512]{1,0:T(4,128)S(1)}, u32[]{:S(2)}, u32[]{:S(2)}) %collective-permute-start.5) | collective-permute-done | bytes 8224 | tf_op jit(solution)/shard_map/ppermute | solution.py:237
  36.3 15.4 %collective-permute-done.4.y_ref = bf16[4096,512]{1,0:T(8,128)(2,1)} collective-permute-done((bf16[4096,512]{1,0:T(8,128)(2,1)}, bf16[4096,512]{1,0:T(8,128)(2,1)}, u32[]{:S(2)}, u32[]{:S(2)}) %collective-permute-start.4) | collective-permute-done | bytes 4194336 | tf_op jit(solution)/shard_map/ppermute | solution.py:237
  51.8 4.7 %near_tile.1 = (f32[3,256,256]{2,1,0:T(8,128)S(1)}, bf16[3,256,256]{2,1,0:T(8,128)(2,1)S(1)}, bf16[512,4096]{1,0:T(8,128)(2,1)S(1)}) custom-call(s32[5]{0:T(128)S(1)} %stack.23.pos_ref, bf16[512,4096]{1,0:T(8,128)(2,1)S(1)} %get-tuple-element.33.turned_ref, bf16[4096,512]{1,0:T(8,128)(2,1)} %collective-permute-done.4.y_ref, f32[4,512]{1,0:T(4,128)S(1)} %stats.1.stat_ref, ...), custom_call_target="tpu_custom_call" | custom-call | flops 2147483648 | bytes 12582912 | tf_op jit(solution)/shard_map/near_tile/pallas_call | solution.py:290
  56.5 0.0 collective-permute-done.6.diag_got
  56.5 4.5 %collective-permute-start.9 = (bf16[3,256,256]{2,1,0:T(8,128)(2,1)S(1)}, bf16[3,256,256]{2,1,0:T(8,128)(2,1)S(1)}, u32[]{:S(2)}, u32[]{:S(2)}) collective-permute-start(bf16[3,256,256]{2,1,0:T(8,128)(2,1)S(1)} %get-tuple-element.40), channel_id=1, source_target_pairs={{0,2},{2,0},{5,7},{7,5},{8,10},{10,8},{13,15},{15,13},{16,18},{18,... | collective-permute-start | bytes 1179656 | tf_op jit(solution)/shard_map/ppermute | solution.py:237
  61.1 0.0 collective-permute-done.8.wstat_ref
  61.1 6.8 %far_tiles.1 = (f32[3,256,256]{2,1,0:T(8,128)S(1)}, bf16[3,256,256]{2,1,0:T(8,128)(2,1)S(1)}, f32[3,256,256]{2,1,0:T(8,128)S(1)}, bf16[3,256,256]{2,1,0:T(8,128)(2,1)S(1)}) custom-call(s32[5]{0:T(128)S(1)} %stack.23.pos_ref, bf16[512,4096]{1,0:T(8,128)(2,1)S(1)} %get-tuple-element.33.turned_ref, bf16[4096,512]{1,0:T(8,128)(2,1)} %collective-permute-done.7.w_ref, ...), custom_call_target="tpu_custom_call" | custom-call | flops 4294967296 | bytes 12582912 | tf_op jit(solution)/shard_map/far_tiles/pallas_call | solution.py:296
  67.9 4.2 %collective-permute-start.11 = (bf16[3,256,256]{2,1,0:T(8,128)(2,1)S(1)}, bf16[3,256,256]{2,1,0:T(8,128)(2,1)S(1)}, u32[]{:S(2)}, u32[]{:S(2)}) collective-permute-start(bf16[3,256,256]{2,1,0:T(8,128)(2,1)S(1)} %get-tuple-element.46), channel_id=1, source_target_pairs={{0,2},{2,0},{5,7},{7,5},{8,10},{10,8},{13,15},{15,13},{16,18},{18,... | collective-permute-start | bytes 1179656 | tf_op jit(solution)/shard_map/ppermute | solution.py:237
  72.1 0.7 near_strips.1
  72.9 5.0 %collective-permute-done.11.got = bf16[3,256,256]{2,1,0:T(8,128)(2,1)S(1)} collective-permute-done((bf16[3,256,256]{2,1,0:T(8,128)(2,1)S(1)}, bf16[3,256,256]{2,1,0:T(8,128)(2,1)S(1)}, u32[]{:S(2)}, u32[]{:S(2)}) %collective-permute-start.11) | collective-permute-done | bytes 393248 | tf_op jit(solution)/shard_map/ppermute | solution.py:237
  77.9 0.7 cross_strips.1
  78.6 1.3 %collective-permute-start.14 = (f32[256,512]{1,0:T(8,128)S(1)}, f32[256,512]{1,0:T(8,128)S(1)}, u32[]{:S(2)}, u32[]{:S(2)}) collective-permute-start(f32[256,512]{1,0:T(8,128)S(1)} %get-tuple-element.50), channel_id=1, source_target_pairs={{0,9},{2,11},{8,17},{10,19},{13,4},{15,6},{16,25},{18,27},{21,12},... | collective-permute-start | bytes 1572872 | tf_op jit(solution)/shard_map/ppermute | solution.py:237
  79.9 2.1 %collective-permute-start.10 = (bf16[3,256,256]{2,1,0:T(8,128)(2,1)S(1)}, bf16[3,256,256]{2,1,0:T(8,128)(2,1)S(1)}, u32[]{:S(2)}, u32[]{:S(2)}) collective-permute-start(bf16[3,256,256]{2,1,0:T(8,128)(2,1)S(1)} %get-tuple-element.44), channel_id=1, source_target_pairs={{0,2},{1,3},{2,0},{3,1},{4,6},{5,7},{6,4},{7,5},{8,10},{9,11},{10,... | collective-permute-start | bytes 1179656 | tf_op jit(solution)/shard_map/ppermute | solution.py:237
  82.0 1.9 %collective-permute-start.12 = (f32[256,512]{1,0:T(8,128)S(1)}, f32[256,512]{1,0:T(8,128)S(1)}, u32[]{:S(2)}, u32[]{:S(2)}) collective-permute-start(f32[256,512]{1,0:T(8,128)S(1)} %get-tuple-element.47), channel_id=1, source_target_pairs={{0,5},{2,7},{5,0},{7,2},{8,13},{10,15},{13,8},{15,10},{16,21},{18,... | collective-permute-start | bytes 1572872 | tf_op jit(solution)/shard_map/ppermute | solution.py:237
  83.9 3.6 %collective-permute-start.13 = (f32[256,512]{1,0:T(8,128)S(1)}, f32[256,512]{1,0:T(8,128)S(1)}, u32[]{:S(2)}, u32[]{:S(2)}) collective-permute-start(f32[256,512]{1,0:T(8,128)S(1)} %get-tuple-element.49), channel_id=1, source_target_pairs={{0,5},{2,7},{5,0},{7,2},{8,13},{10,15},{13,8},{15,10},{16,21},{18,... | collective-permute-start | bytes 1572872 | tf_op jit(solution)/shard_map/ppermute | solution.py:237
  87.6 0.2 collective-permute-done.10.got
  87.8 0.7 far_strips.1
  88.5 0.0 collective-permute-done.14.from_z_d
  88.6 2.1 %collective-permute-start.15 = (f32[256,512]{1,0:T(8,128)S(1)}, f32[256,512]{1,0:T(8,128)S(1)}, u32[]{:S(2)}, u32[]{:S(2)}) collective-permute-start(f32[256,512]{1,0:T(8,128)S(1)} %get-tuple-element.54), channel_id=1, source_target_pairs={{0,9},{2,11},{4,13},{6,15},{8,17},{9,0},{10,19},{11,2},{12,21},{13... | collective-permute-start | bytes 1572872 | tf_op jit(solution)/shard_map/ppermute | solution.py:237
  90.7 1.8 %collective-permute-done.12.from_y_b = f32[256,512]{1,0:T(8,128)S(1)} collective-permute-done((f32[256,512]{1,0:T(8,128)S(1)}, f32[256,512]{1,0:T(8,128)S(1)}, u32[]{:S(2)}, u32[]{:S(2)}) %collective-permute-start.12) | collective-permute-done | bytes 524320 | tf_op jit(solution)/shard_map/ppermute | solution.py:237
  92.5 5.6 %collective-permute-done.13.from_y_d = f32[256,512]{1,0:T(8,128)S(1)} collective-permute-done((f32[256,512]{1,0:T(8,128)S(1)}, f32[256,512]{1,0:T(8,128)S(1)}, u32[]{:S(2)}, u32[]{:S(2)}) %collective-permute-start.13) | collective-permute-done | bytes 524320 | tf_op jit(solution)/shard_map/ppermute | solution.py:237
  98.1 0.9 collective-permute-done.15.from_z_c
  99.1 0.7 combine.1
  99.8 0.1 collective-permute-start.16
  99.8 2.3 %collective-permute-done.16.sib = f32[3,128,512]{2,1,0:T(8,128)S(1)} collective-permute-done((f32[3,128,512]{2,1,0:T(8,128)S(1)}, f32[3,128,512]{2,1,0:T(8,128)S(1)}, u32[]{:S(2)}, u32[]{:S(2)}) %collective-permute-start.16) | collective-permute-done | bytes 786464 | tf_op jit(solution)/shard_map/ppermute | solution.py:237
  102.1 1.7 %finish.1 = (bf16[1,3,128,512]{3,2,1,0:T(8,128)(2,1)}, bf16[1,2,128,512]{3,2,1,0:T(8,128)(2,1)}) custom-call(s32[5]{0:T(128)S(1)} %stack.23.pos_ref, s32[1,3]{1,0:T(1,128)S(1)} %copy-done.2, f32[128,512]{1,0:T(8,128)S(1)} %get-tuple-element.32.diag_mine, f32[128,512]{1,0:T(8,128)S(1)} %collective-permute-done.6.diag_got, ...), custom_call_target="tpu_custom_call" | custom-call | tf_op jit(solution)/shard_map/finish/pallas_call | solution.py:318
  (4 shorter events, 0.0 us)
Async XLA Ops:
  0.6 51.1 %collective-permute-start.4 = (bf16[4096,512]{1,0:T(8,128)(2,1)}, bf16[4096,512]{1,0:T(8,128)(2,1)}, u32[]{:S(2)}, u32[]{:S(2)}) collective-permute-start(bf16[4096,512]{1,0:T(8,128)(2,1)} %x_ref.1), channel_id=1, source_target_pairs={{1,5},{3,7},{4,0},{6,2},{9,13},{11,15},{12,8},{14,10},{17,21},{19,... | collective-permute-start | bytes 12582920 | tf_op jit(solution)/shard_map/ppermute | solution.py:237
  1.9 59.1 %collective-permute-start.7 = (bf16[4096,512]{1,0:T(8,128)(2,1)}, bf16[4096,512]{1,0:T(8,128)(2,1)}, u32[]{:S(2)}, u32[]{:S(2)}) collective-permute-start(bf16[4096,512]{1,0:T(8,128)(2,1)} %x_ref.1), channel_id=1, source_target_pairs={{1,9},{3,11},{5,13},{7,15},{8,0},{9,17},{10,2},{11,19},{12,4},{13,... | collective-permute-start | bytes 12582920 | tf_op jit(solution)/shard_map/ppermute | solution.py:237
  3.2 2.2 %copy-start = (bf16[4096,512]{1,0:T(8,128)(2,1)S(1)}, bf16[4096,512]{1,0:T(8,128)(2,1)}, u32[]{:S(2)}) copy-start(bf16[4096,512]{1,0:T(8,128)(2,1)} %x_ref.1) | copy-start | bytes 12582916
  5.4 15.5 %copy-start.2 = (s32[1,3]{1,0:T(1,128)S(1)}, s32[1,3]{1,0:T(1,128)}, u32[]{:S(2)}) copy-start(s32[1,3]{1,0:T(1,128)} %offsets_ref.3) | copy-start | bytes 40
  7.3 11.3 %collective-permute-start = (f32[2,512]{1,0:T(2,128)S(1)}, f32[2,512]{1,0:T(2,128)S(1)}, u32[]{:S(2)}, u32[]{:S(2)}) collective-permute-start(f32[2,512]{1,0:T(2,128)S(1)} %local_stats.1.own_ref), channel_id=1, source_target_pairs={{0,1},{1,0},{2,3},{3,2},{4,5},{5,4},{6,7},{7,6},{8,9},{9,8},{10,11... | collective-permute-start | bytes 12296 | tf_op jit(solution)/shard_map/ppermute | solution.py:237
  16.4 3.6 %collective-permute-start.1 = (f32[2,512]{1,0:T(2,128)S(1)}, f32[2,512]{1,0:T(2,128)S(1)}, u32[]{:S(2)}, u32[]{:S(2)}) collective-permute-start(f32[2,512]{1,0:T(2,128)S(1)} %local_stats.1.own_ref), channel_id=1, source_target_pairs={{0,2},{1,3},{2,0},{3,1},{4,6},{5,7},{6,4},{7,5},{8,10},{9,11},{10,... | collective-permute-start | bytes 12296 | tf_op jit(solution)/shard_map/ppermute | solution.py:237
  17.9 3.1 %collective-permute-start.2 = (f32[2,512]{1,0:T(2,128)S(1)}, f32[2,512]{1,0:T(2,128)S(1)}, u32[]{:S(2)}, u32[]{:S(2)}) collective-permute-start(f32[2,512]{1,0:T(2,128)S(1)} %local_stats.1.own_ref), channel_id=1, source_target_pairs={{0,3},{1,2},{2,1},{3,0},{4,7},{5,6},{6,5},{7,4},{8,11},{9,10},{10,... | collective-permute-start | bytes 12296 | tf_op jit(solution)/shard_map/ppermute | solution.py:237
  21.5 2.2 %copy-start.1 = (bf16[4096,512]{1,0:T(8,128)(2,1)S(1)}, bf16[4096,512]{1,0:T(8,128)(2,1)}, u32[]{:S(2)}) copy-start(bf16[4096,512]{1,0:T(8,128)(2,1)} %x_ref.1) | copy-start | bytes 12582916
  28.0 2.0 %collective-permute-start.3 = (f32[2,128,512]{2,1,0:T(8,128)S(1)}, f32[2,128,512]{2,1,0:T(8,128)S(1)}, u32[]{:S(2)}, u32[]{:S(2)}) collective-permute-start(f32[2,128,512]{2,1,0:T(8,128)S(1)} %get-tuple-element.31), channel_id=1, source_target_pairs={{0,1},{1,0},{2,3},{3,2},{4,5},{5,4},{6,7},{7,6},{8,9},{9,8},{10,11... | collective-permute-start | bytes 1572872 | tf_op jit(solution)/shard_map/ppermute | solution.py:237
  30.6 25.9 %collective-permute-start.6 = (f32[128,512]{1,0:T(8,128)S(1)}, f32[128,512]{1,0:T(8,128)S(1)}, u32[]{:S(2)}, u32[]{:S(2)}) collective-permute-start(f32[128,512]{1,0:T(8,128)S(1)} %get-tuple-element.35), channel_id=1, source_target_pairs={{0,2},{1,3},{2,0},{3,1},{4,6},{5,7},{6,4},{7,5},{8,10},{9,11},{10,... | collective-permute-start | bytes 786440 | tf_op jit(solution)/shard_map/ppermute | solution.py:237
  31.2 5.1 %collective-permute-start.5 = (f32[4,512]{1,0:T(4,128)S(1)}, f32[4,512]{1,0:T(4,128)S(1)}, u32[]{:S(2)}, u32[]{:S(2)}) collective-permute-start(f32[4,512]{1,0:T(4,128)S(1)} %stats.1.stat_ref), channel_id=1, source_target_pairs={{0,5},{2,7},{5,0},{7,2},{8,13},{10,15},{13,8},{15,10},{16,21},{18,... | collective-permute-start | bytes 24584 | tf_op jit(solution)/shard_map/ppermute | solution.py:237
  33.1 27.9 %collective-permute-start.8 = (f32[4,512]{1,0:T(4,128)S(1)}, f32[4,512]{1,0:T(4,128)S(1)}, u32[]{:S(2)}, u32[]{:S(2)}) collective-permute-start(f32[4,512]{1,0:T(4,128)S(1)} %stats.1.stat_ref), channel_id=1, source_target_pairs={{0,9},{2,11},{4,13},{6,15},{8,17},{9,0},{10,19},{11,2},{12,21},{13... | collective-permute-start | bytes 24584 | tf_op jit(solution)/shard_map/ppermute | solution.py:237
  56.5 11.4 %collective-permute-start.9 = (bf16[3,256,256]{2,1,0:T(8,128)(2,1)S(1)}, bf16[3,256,256]{2,1,0:T(8,128)(2,1)S(1)}, u32[]{:S(2)}, u32[]{:S(2)}) collective-permute-start(bf16[3,256,256]{2,1,0:T(8,128)(2,1)S(1)} %get-tuple-element.40), channel_id=1, source_target_pairs={{0,2},{2,0},{5,7},{7,5},{8,10},{10,8},{13,15},{15,13},{16,18},{18,... | collective-permute-start | bytes 1179656 | tf_op jit(solution)/shard_map/ppermute | solution.py:237
  67.9 10.0 %collective-permute-start.11 = (bf16[3,256,256]{2,1,0:T(8,128)(2,1)S(1)}, bf16[3,256,256]{2,1,0:T(8,128)(2,1)S(1)}, u32[]{:S(2)}, u32[]{:S(2)}) collective-permute-start(bf16[3,256,256]{2,1,0:T(8,128)(2,1)S(1)} %get-tuple-element.46), channel_id=1, source_target_pairs={{0,2},{2,0},{5,7},{7,5},{8,10},{10,8},{13,15},{15,13},{16,18},{18,... | collective-permute-start | bytes 1179656 | tf_op jit(solution)/shard_map/ppermute | solution.py:237
  78.6 9.9 %collective-permute-start.14 = (f32[256,512]{1,0:T(8,128)S(1)}, f32[256,512]{1,0:T(8,128)S(1)}, u32[]{:S(2)}, u32[]{:S(2)}) collective-permute-start(f32[256,512]{1,0:T(8,128)S(1)} %get-tuple-element.50), channel_id=1, source_target_pairs={{0,9},{2,11},{8,17},{10,19},{13,4},{15,6},{16,25},{18,27},{21,12},... | collective-permute-start | bytes 1572872 | tf_op jit(solution)/shard_map/ppermute | solution.py:237
  79.9 7.8 %collective-permute-start.10 = (bf16[3,256,256]{2,1,0:T(8,128)(2,1)S(1)}, bf16[3,256,256]{2,1,0:T(8,128)(2,1)S(1)}, u32[]{:S(2)}, u32[]{:S(2)}) collective-permute-start(bf16[3,256,256]{2,1,0:T(8,128)(2,1)S(1)} %get-tuple-element.44), channel_id=1, source_target_pairs={{0,2},{1,3},{2,0},{3,1},{4,6},{5,7},{6,4},{7,5},{8,10},{9,11},{10,... | collective-permute-start | bytes 1179656 | tf_op jit(solution)/shard_map/ppermute | solution.py:237
  82.0 10.5 %collective-permute-start.12 = (f32[256,512]{1,0:T(8,128)S(1)}, f32[256,512]{1,0:T(8,128)S(1)}, u32[]{:S(2)}, u32[]{:S(2)}) collective-permute-start(f32[256,512]{1,0:T(8,128)S(1)} %get-tuple-element.47), channel_id=1, source_target_pairs={{0,5},{2,7},{5,0},{7,2},{8,13},{10,15},{13,8},{15,10},{16,21},{18,... | collective-permute-start | bytes 1572872 | tf_op jit(solution)/shard_map/ppermute | solution.py:237
  83.9 14.2 %collective-permute-start.13 = (f32[256,512]{1,0:T(8,128)S(1)}, f32[256,512]{1,0:T(8,128)S(1)}, u32[]{:S(2)}, u32[]{:S(2)}) collective-permute-start(f32[256,512]{1,0:T(8,128)S(1)} %get-tuple-element.49), channel_id=1, source_target_pairs={{0,5},{2,7},{5,0},{7,2},{8,13},{10,15},{13,8},{15,10},{16,21},{18,... | collective-permute-start | bytes 1572872 | tf_op jit(solution)/shard_map/ppermute | solution.py:237
  88.6 10.5 %collective-permute-start.15 = (f32[256,512]{1,0:T(8,128)S(1)}, f32[256,512]{1,0:T(8,128)S(1)}, u32[]{:S(2)}, u32[]{:S(2)}) collective-permute-start(f32[256,512]{1,0:T(8,128)S(1)} %get-tuple-element.54), channel_id=1, source_target_pairs={{0,9},{2,11},{4,13},{6,15},{8,17},{9,0},{10,19},{11,2},{12,21},{13... | collective-permute-start | bytes 1572872 | tf_op jit(solution)/shard_map/ppermute | solution.py:237
  99.8 2.4 %collective-permute-start.16 = (f32[3,128,512]{2,1,0:T(8,128)S(1)}, f32[3,128,512]{2,1,0:T(8,128)S(1)}, u32[]{:S(2)}, u32[]{:S(2)}) collective-permute-start(f32[3,128,512]{2,1,0:T(8,128)S(1)} %get-tuple-element.57), channel_id=1, source_target_pairs={{0,1},{1,0},{2,3},{3,2},{4,5},{5,4},{6,7},{7,6},{8,9},{9,8},{10,11... | collective-permute-start | bytes 2359304 | tf_op jit(solution)/shard_map/ppermute | solution.py:237

commit v8 on v6

--- a/solution.py
+++ b/solution.py
@@ -120,34 +120,54 @@
     return [(slice(k * rows, (k + 1) * rows), copy.wait) for k, copy in enumerate(copies)]
 
 
-def far_kernel(pos_ref, turned_ref, w_ref, stat_ref, wstat_ref, keep_ref, send_ref, w_out, acc, parts, sems):
+def far_kernel(last, pos_ref, turned_ref, w_ref, stat_ref, wstat_ref, *refs):
+    if last:
+        before, keep_ref, send_ref, w_out, acc, parts, sems = refs
+    else:
+        acc, w_out, parts, sems = refs
+    skip = w_ref.shape[0] if last else 0
     for k, (rows, wait) in enumerate(fetched(w_ref, parts, sems)):
         wait()
         w = standardized(parts[k], wstat_ref)
         w_out[rows, :] = w
-        part = dot(turned_ref[:, rows], w)
-        acc[...] = part if k == 0 else acc[...] + part
-    listed = jnp.where(pos_ref[2] == 0, stat_ref[3:4, :], wstat_ref[3:4, :])
-    acc[...] *= listed * (1.0 / pos_ref[4].astype(F32))
-    put_quarters(pos_ref[0], acc, keep_ref, send_ref)
-
-
-def near_kernel(pos_ref, turned_ref, y_ref, w_ref, stat_ref, ystat_ref, wstat_ref, keep_b, send_b, keep_d, send_d,
-                acc_b, acc_d, parts, sems):
+        part = dot(turned_ref[:, skip + rows.start:skip + rows.stop], w)
+        if k == 0:
+            acc[...] = before[...] + part if last else part
+        else:
+            acc[...] += part
+    if last:
+        listed = jnp.where(pos_ref[2] == 0, stat_ref[3:4, :], wstat_ref[3:4, :])
+        acc[...] *= listed * (1.0 / pos_ref[4].astype(F32))
+        put_quarters(pos_ref[0], acc, keep_ref, send_ref)
+
+
+def near_kernel(last, pos_ref, turned_ref, y_ref, w_ref, stat_ref, ystat_ref, wstat_ref, *refs):
+    if last:
+        before_b, before_d, keep_b, send_b, keep_d, send_d, acc_b, acc_d, parts, sems = refs
+    else:
+        acc_b, acc_d, parts, sems = refs
+    skip = y_ref.shape[0] if last else 0
+
     @pl.when(pos_ref[1] == 1)
     def _():
         for k, (rows, wait) in enumerate(fetched(y_ref, parts, sems)):
             wait()
             y = standardized(parts[k], ystat_ref)
-            part_b, part_d = dot(turned_ref[:, rows], y), dot(y.T, w_ref[rows, :])
-            acc_b[...] = part_b if k == 0 else acc_b[...] + part_b
-            acc_d[...] = part_d if k == 0 else acc_d[...] + part_d
-        first = pos_ref[2] == 0
-        share = 1.0 / pos_ref[4].astype(F32)
-        acc_b[...] *= jnp.where(first, stat_ref[2:3, :], ystat_ref[2:3, :]) * share
-        acc_d[...] *= jnp.where(first, ystat_ref[2:3, :], wstat_ref[2:3, :]) * share
-        put_quarters(pos_ref[0], acc_b, keep_b, send_b)
-        put_quarters(pos_ref[0], acc_d, keep_d, send_d)
+            part_b = dot(turned_ref[:, skip + rows.start:skip + rows.stop], y)
+            part_d = dot(y.T, w_ref[rows, :])
+            if k == 0:
+                acc_b[...] = before_b[...] + part_b if last else part_b
+                acc_d[...] = before_d[...] + part_d if last else part_d
+            else:
+                acc_b[...] += part_b
+                acc_d[...] += part_d
+        if last:
+            first = pos_ref[2] == 0
+            share = 1.0 / pos_ref[4].astype(F32)
+            acc_b[...] *= jnp.where(first, stat_ref[2:3, :], ystat_ref[2:3, :]) * share
+            acc_d[...] *= jnp.where(first, ystat_ref[2:3, :], wstat_ref[2:3, :]) * share
+            put_quarters(pos_ref[0], acc_b, keep_b, send_b)
+            put_quarters(pos_ref[0], acc_d, keep_d, send_d)
 
 
 def add_halves(x, keep, got, rows_out, cols_out):
@@ -241,7 +261,8 @@
     across_active = [(at(a, b), at(a, b ^ 2)) for a, b in everyone if active_on(a, b)]
     sibling = [(at(a, b), at(a, b ^ 1)) for a, b in everyone]
 
-    w_raw, y_raw = send(dosage, z_main), send(dosage, y_main)
+    upper_rows = dosage[:depth // 2]
+    w_raw, y_raw = send(upper_rows, z_main), send(upper_rows, y_main)
 
     pos = jnp.stack([x, active, core, odd, jnp.int32(samples_all)]).astype(jnp.int32)
     step_rows = min(1024, depth)
@@ -259,6 +280,9 @@
     bytes_block, tile_flops = 2 * depth * width, 2 * depth * width * width
     local = call(lambda *refs: local_kernel(steps, *refs), "local_stats", (steps,), [wide], whole(2, width), shape(2, width),
                  [pltpu.VMEM((1, width), F32)] + [pltpu.VMEM((8, width), F32)] * 2, 5 * depth * width, bytes_block)(dosage)
+    below, local = lax.optimization_barrier((dosage, local))
+    lower_rows = below[depth // 2:]
+    w_last, y_last = send(lower_rows, z_main), send(lower_rows, y_main)
     others = [send(local, [(at(a, b), at(a, b ^ flip)) for a, b in everyone]) for flip in (1, 2, 3)]
     stat = call(stat_kernel, "stats", (), [SMEM] * 3 + [VMEM] * 4, VMEM, shape(4, width))(
         pos, live_counts, pair_offsets, local, *others)
@@ -274,19 +298,26 @@
     diag_got = send(diag_other, across)
 
     anywhere = pl.BlockSpec(memory_space=pl.ANY)
-    parts = [pltpu.VMEM((steps, step_rows, width), BF16), pltpu.SemaphoreType.DMA((steps,))]
-    sums = pltpu.VMEM((width, width), F32)
+    pieces = max(steps // 2, 1)
+    parts = [pltpu.VMEM((pieces, depth // 2 // pieces, width), BF16), pltpu.SemaphoreType.DMA((pieces,))]
+    sums, total = pltpu.VMEM((width, width), F32), shape(width, width)
+    rows_out = shape(depth // 2, width, dtype=BF16)
     pair = [shape(3, half, half), shape(3, half, half, dtype=HALVES)]
+    far_in, near_in = [SMEM, VMEM, anywhere, VMEM, VMEM], [SMEM, VMEM, anywhere] + [VMEM] * 4
+    sum_c, w = call(lambda *refs: far_kernel(False, *refs), "far_tile_0", (), far_in, [VMEM] * 2, [total, rows_out],
+                    parts, tile_flops // 2, bytes_block)(pos, turned, w_raw, stat, w_stat)
+    sum_b, sum_d = call(lambda *refs: near_kernel(False, *refs), "near_tiles_0", (), near_in, [VMEM] * 2, [total] * 2,
+                        parts, tile_flops, bytes_block)(pos, turned, y_raw, w, stat, y_stat, w_stat)
+    w_last, sum_b = lax.optimization_barrier((w_last, sum_b))
     keep_c, send_c, w = call(
-        far_kernel, "far_tile", (), [SMEM, VMEM, anywhere, VMEM, VMEM], [VMEM] * 3,
-        pair + [shape(depth, width, dtype=BF16)], [sums] + parts, tile_flops, 3 * bytes_block)(
-        pos, turned, w_raw, stat, w_stat)
+        lambda *refs: far_kernel(True, *refs), "far_tile_1", (), far_in + [VMEM], [VMEM] * 3, pair + [rows_out],
+        [sums] + parts, tile_flops // 2, bytes_block)(pos, turned, w_last, stat, w_stat, sum_c)
     send_c, diag_got = lax.optimization_barrier((send_c, diag_got))
     got_c = send(send_c, across)
 
     keep_b, send_b, keep_d, send_d = call(
-        near_kernel, "near_tiles", (), [SMEM, VMEM, anywhere] + [VMEM] * 4, [VMEM] * 4, pair * 2, [sums] * 2 + parts,
-        2 * tile_flops, 3 * bytes_block)(pos, turned, y_raw, w, stat, y_stat, w_stat)
+        lambda *refs: near_kernel(True, *refs), "near_tiles_1", (), near_in + [VMEM] * 2, [VMEM] * 4, pair * 2,
+        [sums] * 2 + parts, tile_flops, bytes_block)(pos, turned, y_last, w, stat, y_stat, w_stat, sum_b, sum_d)
     got_b = send(send_b, across_active)
     send_d, got_c = lax.optimization_barrier((send_d, got_c))
     got_d = send(send_d, across_active)

time: 97.5 us -> 97.3 us (level)
  waiting for transfers between devices: 34.8 us -> 24.4 us
  starting transfers between devices: 33.1 us -> 37.7 us
  Pallas kernels: 23.3 us -> 26.2 us
  local copies, waits for them, and re-layouts: 4.46 us -> 6.96 us
    ppermute x17 -> x19, waiting for transfers between devices: 34.8 us -> 24.4 us  [send(): return lax.ppermute(value, AXES, pairs)]
    slice x0 -> x2, local copies, waits for them, and re-layouts: none -> 4.68 us  [the longest x1 3.19 us: body(): upper_rows = dosage[:depth // 2]]
    ppermute x17 -> x19, starting transfers between devices: 33.1 us -> 37.7 us  [send(): return lax.ppermute(value, AXES, pairs)]
    pallas_call x2 -> x4, Pallas kernels: 11.3 us -> 14.3 us  [the longest x1 4.52 us: body(): call(lambda *refs: near_kernel(True, *refs), 'near_tiles_1', (), near_in...]
    unnamed x6, local copies, waits for them, and re-layouts: 4.37 us -> 2.2 us
  transfers between devices with their start and end apart: 17 -> 19, of which waited for: 10 -> 12; matrix products, arithmetic and copies ran while one was open for 0% -> 2% of each run, Pallas kernels for 22% -> 25%
where the time goes in v8:
time: 97.3 us; the launch traced here: 96.8 us
  starting transfers between devices  37.7 us (39%)
  Pallas kernels  26.2 us (27%)
  waiting for transfers between devices  24.4 us (25%)
  local copies, waits for them, and re-layouts  6.96 us (7%)
  between operations  1.55 us (2%)
    ppermute x19, starting transfers between devices, send(): return lax.ppermute(value, AXES, pairs)  37.7 us
    ppermute x19, waiting for transfers between devices, send(): return lax.ppermute(value, AXES, pairs)  24.4 us
    pallas_call x1, Pallas kernels, body(): call(lambda *refs: near_kernel(True, *refs), 'near_tiles_1', (), near_in...  4.52 us
    pallas_call x1, Pallas kernels, body(): call(own_kernel, 'own_tile', (steps,), [SMEM, wide, whole(4, width)], [fl...  4.3 us
    pallas_call x1, Pallas kernels, body(): call(lambda *refs: far_kernel(True, *refs), 'far_tile_1', (), far_in + [V...  3.36 us
    pallas_call x1, Pallas kernels, body(): call(lambda *refs: far_kernel(False, *refs), 'far_tile_0', (), far_in, [V...  3.2 us
    slice x1, local copies, waits for them, and re-layouts, body(): upper_rows = dosage[:depth // 2]  3.19 us
    pallas_call x1, Pallas kernels, body(): call(lambda *refs: near_kernel(False, *refs), 'near_tiles_0', (), near_in...  3.18 us
  transfers between devices with their start and end apart: 19, of which 12 were waited for; matrix products, arithmetic and copies ran while one was open for 2% of the time, Pallas kernels for 25%

profile of v8, /device:TPU:0, one launch (start us, length us, event | category | flops | bytes accessed | tf_op | source)
XLA Modules:
  0.0 96.8 jit_solution(11206057680482355337)
XLA Ops:
  0.6 3.2 %slice.7 = bf16[2048,512]{1,0:T(8,128)(2,1)} slice(bf16[4096,512]{1,0:T(8,128)(2,1)} %x_ref.1), slice={[0:2048], [0:512]} | slice | bytes 4194304 | tf_op jit(solution)/shard_map/slice | solution.py:264
  3.8 1.3 %collective-permute-start.6 = (bf16[2048,512]{1,0:T(8,128)(2,1)}, bf16[2048,512]{1,0:T(8,128)(2,1)}, u32[]{:S(2)}, u32[]{:S(2)}) collective-permute-start(bf16[2048,512]{1,0:T(8,128)(2,1)} %slice.7), channel_id=1, source_target_pairs={{1,9},{3,11},{5,13},{7,15},{8,0},{9,17},{10,2},{11,19},{12,4},{13,... | collective-permute-start | bytes 6291464 | tf_op jit(solution)/shard_map/ppermute | solution.py:247
  5.1 1.3 %collective-permute-start.5 = (bf16[2048,512]{1,0:T(8,128)(2,1)}, bf16[2048,512]{1,0:T(8,128)(2,1)S(1)}, u32[]{:S(2)}, u32[]{:S(2)}) collective-permute-start(bf16[2048,512]{1,0:T(8,128)(2,1)} %slice.7), channel_id=1, source_target_pairs={{1,5},{3,7},{4,0},{6,2},{9,13},{11,15},{12,8},{14,10},{17,21},{19,... | collective-permute-start | bytes 6291464 | tf_op jit(solution)/shard_map/ppermute | solution.py:247
  6.4 1.9 %local_stats.1.own_ref = f32[2,512]{1,0:T(2,128)S(1)} custom-call(bf16[4096,512]{1,0:T(8,128)(2,1)S(1)} %copy-done), custom_call_target="tpu_custom_call" | custom-call | flops 10485760 | bytes 4194304 | tf_op jit(solution)/shard_map/local_stats/pallas_call | solution.py:281
  8.3 1.5 %slice.6 = bf16[2048,512]{1,0:T(8,128)(2,1)} slice(bf16[4096,512]{1,0:T(8,128)(2,1)S(1)} %copy-done), slice={[2048:4096], [0:512]} | slice | bytes 4194304 | tf_op jit(solution)/shard_map/slice | solution.py:284
  9.8 1.3 %collective-permute-start.4 = (bf16[2048,512]{1,0:T(8,128)(2,1)}, bf16[2048,512]{1,0:T(8,128)(2,1)}, u32[]{:S(2)}, u32[]{:S(2)}) collective-permute-start(bf16[2048,512]{1,0:T(8,128)(2,1)} %slice.6), channel_id=1, source_target_pairs={{1,9},{3,11},{5,13},{7,15},{8,0},{9,17},{10,2},{11,19},{12,4},{13,... | collective-permute-start | bytes 6291464 | tf_op jit(solution)/shard_map/ppermute | solution.py:247
  11.1 1.3 %collective-permute-start.10 = (bf16[2048,512]{1,0:T(8,128)(2,1)}, bf16[2048,512]{1,0:T(8,128)(2,1)}, u32[]{:S(2)}, u32[]{:S(2)}) collective-permute-start(bf16[2048,512]{1,0:T(8,128)(2,1)} %slice.6), channel_id=1, source_target_pairs={{1,5},{3,7},{4,0},{6,2},{9,13},{11,15},{12,8},{14,10},{17,21},{19,... | collective-permute-start | bytes 6291464 | tf_op jit(solution)/shard_map/ppermute | solution.py:247
  12.4 9.8 %collective-permute-start = (f32[2,512]{1,0:T(2,128)S(1)}, f32[2,512]{1,0:T(2,128)S(1)}, u32[]{:S(2)}, u32[]{:S(2)}) collective-permute-start(f32[2,512]{1,0:T(2,128)S(1)} %local_stats.1.own_ref), channel_id=1, source_target_pairs={{0,1},{1,0},{2,3},{3,2},{4,5},{5,4},{6,7},{7,6},{8,9},{9,8},{10,11... | collective-permute-start | bytes 12296 | tf_op jit(solution)/shard_map/ppermute | solution.py:247
  22.2 0.8 collective-permute-done.sib_ref
  23.1 1.5 %collective-permute-start.1 = (f32[2,512]{1,0:T(2,128)S(1)}, f32[2,512]{1,0:T(2,128)S(1)}, u32[]{:S(2)}, u32[]{:S(2)}) collective-permute-start(f32[2,512]{1,0:T(2,128)S(1)} %local_stats.1.own_ref), channel_id=1, source_target_pairs={{0,2},{1,3},{2,0},{3,1},{4,6},{5,7},{6,4},{7,5},{8,10},{9,11},{10,... | collective-permute-start | bytes 12296 | tf_op jit(solution)/shard_map/ppermute | solution.py:247
  24.6 2.1 %collective-permute-done.1.far_ref = f32[2,512]{1,0:T(2,128)S(1)} collective-permute-done((f32[2,512]{1,0:T(2,128)S(1)}, f32[2,512]{1,0:T(2,128)S(1)}, u32[]{:S(2)}, u32[]{:S(2)}) %collective-permute-start.1) | collective-permute-done | bytes 4128 | tf_op jit(solution)/shard_map/ppermute | solution.py:247
  26.7 0.7 collective-permute-start.2
  28.0 0.1 stack.23.pos_ref.refs_0_
  28.1 1.6 %collective-permute-done.2.cross_ref = f32[2,512]{1,0:T(2,128)S(1)} collective-permute-done((f32[2,512]{1,0:T(2,128)S(1)}, f32[2,512]{1,0:T(2,128)S(1)}, u32[]{:S(2)}, u32[]{:S(2)}) %collective-permute-start.2) | collective-permute-done | bytes 4128 | tf_op jit(solution)/shard_map/ppermute | solution.py:247
  29.7 0.6 stats.1.stat_ref.refs_3_.refs_4_
  30.3 2.2 %copy-done.1 = bf16[4096,512]{1,0:T(8,128)(2,1)S(1)} copy-done((bf16[4096,512]{1,0:T(8,128)(2,1)S(1)}, bf16[4096,512]{1,0:T(8,128)(2,1)}, u32[]{:S(2)}) %copy-start.1) | copy-done | bytes 4194328
  32.5 4.3 %own_tile.1 = (bf16[512,4096]{1,0:T(8,128)(2,1)S(1)}, f32[2,128,512]{2,1,0:T(8,128)S(1)}, f32[2,128,512]{2,1,0:T(8,128)S(1)}) custom-call(s32[5]{0:T(128)S(1)} %stack.23.pos_ref.refs_0_, bf16[4096,512]{1,0:T(8,128)(2,1)S(1)} %copy-done.1, f32[4,512]{1,0:T(4,128)S(1)} %stats.1.stat_ref.refs_3_.refs_4_), custom_call_target="tpu_custom_call" | custom-call | flops 2147483648 | bytes 8388608 | tf_op jit(solution)/shard_map/own_tile/pallas_call | solution.py:291
  36.8 0.3 collective-permute-start.3
  37.1 1.6 %collective-permute-done.3.got_ref = f32[2,128,512]{2,1,0:T(8,128)S(1)} collective-permute-done((f32[2,128,512]{2,1,0:T(8,128)S(1)}, f32[2,128,512]{2,1,0:T(8,128)S(1)}, u32[]{:S(2)}, u32[]{:S(2)}) %collective-permute-start.3) | collective-permute-done | bytes 524320 | tf_op jit(solution)/shard_map/ppermute | solution.py:247
  38.8 2.0 %collective-permute-start.7 = (f32[4,512]{1,0:T(4,128)S(1)}, f32[4,512]{1,0:T(4,128)S(1)}, u32[]{:S(2)}, u32[]{:S(2)}) collective-permute-start(f32[4,512]{1,0:T(4,128)S(1)} %stats.1.stat_ref.refs_3_.refs_4_), channel_id=1, source_target_pairs={{0,9},{2,11},{4,13},{6,15},{8,17},{9,0},{10,19},{11,2},{12,21},{13... | collective-permute-start | bytes 24584 | tf_op jit(solution)/shard_map/ppermute | solution.py:247
  40.7 0.6 own_tile_strips.1
  41.4 2.5 %collective-permute-done.7.refs_4_.refs_6_ = f32[4,512]{1,0:T(4,128)S(1)} collective-permute-done((f32[4,512]{1,0:T(4,128)S(1)}, f32[4,512]{1,0:T(4,128)S(1)}, u32[]{:S(2)}, u32[]{:S(2)}) %collective-permute-start.7) | collective-permute-done | bytes 8224 | tf_op jit(solution)/shard_map/ppermute | solution.py:247
  43.9 1.9 %collective-permute-start.8 = (f32[4,512]{1,0:T(4,128)S(1)}, f32[4,512]{1,0:T(4,128)S(1)}, u32[]{:S(2)}, u32[]{:S(2)}) collective-permute-start(f32[4,512]{1,0:T(4,128)S(1)} %stats.1.stat_ref.refs_3_.refs_4_), channel_id=1, source_target_pairs={{0,5},{2,7},{5,0},{7,2},{8,13},{10,15},{13,8},{15,10},{16,21},{18,... | collective-permute-start | bytes 24584 | tf_op jit(solution)/shard_map/ppermute | solution.py:247
  45.8 1.5 %collective-permute-start.9 = (f32[128,512]{1,0:T(8,128)S(1)}, f32[128,512]{1,0:T(8,128)S(1)}, u32[]{:S(2)}, u32[]{:S(2)}) collective-permute-start(f32[128,512]{1,0:T(8,128)S(1)} %get-tuple-element.47), channel_id=1, source_target_pairs={{0,2},{1,3},{2,0},{3,1},{4,6},{5,7},{6,4},{7,5},{8,10},{9,11},{10,... | collective-permute-start | bytes 786440 | tf_op jit(solution)/shard_map/ppermute | solution.py:247
  47.4 3.2 %far_tile_0.1 = (f32[512,512]{1,0:T(8,128)S(1)}, bf16[2048,512]{1,0:T(8,128)(2,1)S(1)}) custom-call(s32[5]{0:T(128)S(1)} %stack.23.pos_ref.refs_0_, bf16[512,4096]{1,0:T(8,128)(2,1)S(1)} %get-tuple-element.40.refs_1_, bf16[2048,512]{1,0:T(8,128)(2,1)} %collective-permute-done.6.refs_2_, f32[4,512]{1,0:T(4,128)S(1)} %stats.1.stat_ref.refs_3_.refs_4_, ...), custom_call_target="tpu_custom_call" | custom-call | flops 1073741824 | bytes 4194304 | tf_op jit(solution)/shard_map/far_tile_0/pallas_call | solution.py:307
  50.6 3.2 %near_tiles_0.1 = (f32[512,512]{1,0:T(8,128)S(1)}, f32[512,512]{1,0:T(8,128)S(1)}) custom-call(s32[5]{0:T(128)S(1)} %stack.23.pos_ref.refs_0_, bf16[512,4096]{1,0:T(8,128)(2,1)S(1)} %get-tuple-element.40.refs_1_, bf16[2048,512]{1,0:T(8,128)(2,1)S(1)} %collective-permute-done.5.refs_2_, bf16[2048,512]{1,0:T(8,128)(2,1)S(1)} %get-tuple-element.42.refs_3_, ...), custom_call_target="tpu_custom_call" | custom-call | flops 2147483648 | bytes 4194304 | tf_op jit(solution)/shard_map/near_tiles_0/pallas_call | solution.py:309
  53.8 1.9 %collective-permute-done.4.refs_2_ = bf16[2048,512]{1,0:T(8,128)(2,1)} collective-permute-done((bf16[2048,512]{1,0:T(8,128)(2,1)}, bf16[2048,512]{1,0:T(8,128)(2,1)}, u32[]{:S(2)}, u32[]{:S(2)}) %collective-permute-start.4) | collective-permute-done | bytes 2097184 | tf_op jit(solution)/shard_map/ppermute | solution.py:247
  55.6 3.4 %far_tile_1.1 = (f32[3,256,256]{2,1,0:T(8,128)S(1)}, bf16[3,256,256]{2,1,0:T(8,128)(2,1)S(1)}, bf16[2048,512]{1,0:T(8,128)(2,1)S(1)}) custom-call(s32[5]{0:T(128)S(1)} %stack.23.pos_ref.refs_0_, bf16[512,4096]{1,0:T(8,128)(2,1)S(1)} %get-tuple-element.40.refs_1_, bf16[2048,512]{1,0:T(8,128)(2,1)} %collective-permute-done.4.refs_2_, ...), custom_call_target="tpu_custom_call" | custom-call | flops 1073741824 | bytes 4194304 | tf_op jit(solution)/shard_map/far_tile_1/pallas_call | solution.py:312
  59.0 2.0 %collective-permute-start.12 = (bf16[3,256,256]{2,1,0:T(8,128)(2,1)S(1)}, bf16[3,256,256]{2,1,0:T(8,128)(2,1)S(1)}, u32[]{:S(2)}, u32[]{:S(2)}) collective-permute-start(bf16[3,256,256]{2,1,0:T(8,128)(2,1)S(1)} %get-tuple-element.56), channel_id=1, source_target_pairs={{0,2},{1,3},{2,0},{3,1},{4,6},{5,7},{6,4},{7,5},{8,10},{9,11},{10,... | collective-permute-start | bytes 1179656 | tf_op jit(solution)/shard_map/ppermute | solution.py:247
  61.0 4.5 %near_tiles_1.1 = (f32[3,256,256]{2,1,0:T(8,128)S(1)}, bf16[3,256,256]{2,1,0:T(8,128)(2,1)S(1)}, f32[3,256,256]{2,1,0:T(8,128)S(1)}, bf16[3,256,256]{2,1,0:T(8,128)(2,1)S(1)}) custom-call(s32[5]{0:T(128)S(1)} %stack.23.pos_ref.refs_0_, bf16[512,4096]{1,0:T(8,128)(2,1)S(1)} %get-tuple-element.40.refs_1_, bf16[2048,512]{1,0:T(8,128)(2,1)} %collective-permute-done.10.refs_2_, ...), custom_call_target="tpu_custom_call" | custom-call | flops 2147483648 | bytes 4194304 | tf_op jit(solution)/shard_map/near_tiles_1/pallas_call | solution.py:318
  65.5 2.0 %collective-permute-start.11 = (bf16[3,256,256]{2,1,0:T(8,128)(2,1)S(1)}, bf16[3,256,256]{2,1,0:T(8,128)(2,1)S(1)}, u32[]{:S(2)}, u32[]{:S(2)}) collective-permute-start(bf16[3,256,256]{2,1,0:T(8,128)(2,1)S(1)} %get-tuple-element.53), channel_id=1, source_target_pairs={{0,2},{2,0},{5,7},{7,5},{8,10},{10,8},{13,15},{15,13},{16,18},{18,... | collective-permute-start | bytes 1179656 | tf_op jit(solution)/shard_map/ppermute | solution.py:247
  67.5 1.1 %collective-permute-done.12.got = bf16[3,256,256]{2,1,0:T(8,128)(2,1)S(1)} collective-permute-done((bf16[3,256,256]{2,1,0:T(8,128)(2,1)S(1)}, bf16[3,256,256]{2,1,0:T(8,128)(2,1)S(1)}, u32[]{:S(2)}, u32[]{:S(2)}) %collective-permute-start.12) | collective-permute-done | bytes 393248 | tf_op jit(solution)/shard_map/ppermute | solution.py:247
  68.6 3.4 %collective-permute-start.14 = (bf16[3,256,256]{2,1,0:T(8,128)(2,1)S(1)}, bf16[3,256,256]{2,1,0:T(8,128)(2,1)S(1)}, u32[]{:S(2)}, u32[]{:S(2)}) collective-permute-start(bf16[3,256,256]{2,1,0:T(8,128)(2,1)S(1)} %get-tuple-element.64), channel_id=1, source_target_pairs={{0,2},{2,0},{5,7},{7,5},{8,10},{10,8},{13,15},{15,13},{16,18},{18,... | collective-permute-start | bytes 1179656 | tf_op jit(solution)/shard_map/ppermute | solution.py:247
  72.0 0.7 far_strips.1
  72.8 1.9 %collective-permute-start.16 = (f32[256,512]{1,0:T(8,128)S(1)}, f32[256,512]{1,0:T(8,128)S(1)}, u32[]{:S(2)}, u32[]{:S(2)}) collective-permute-start(f32[256,512]{1,0:T(8,128)S(1)} %get-tuple-element.58), channel_id=1, source_target_pairs={{0,9},{2,11},{4,13},{6,15},{8,17},{9,0},{10,19},{11,2},{12,21},{13... | collective-permute-start | bytes 1572872 | tf_op jit(solution)/shard_map/ppermute | solution.py:247
  74.7 0.5 collective-permute-done.11.got
  75.2 0.8 near_strips.1
  76.0 1.9 %collective-permute-start.13 = (f32[256,512]{1,0:T(8,128)S(1)}, f32[256,512]{1,0:T(8,128)S(1)}, u32[]{:S(2)}, u32[]{:S(2)}) collective-permute-start(f32[256,512]{1,0:T(8,128)S(1)} %get-tuple-element.62), channel_id=1, source_target_pairs={{0,5},{2,7},{5,0},{7,2},{8,13},{10,15},{13,8},{15,10},{16,21},{18,... | collective-permute-start | bytes 1572872 | tf_op jit(solution)/shard_map/ppermute | solution.py:247
  77.9 1.5 %collective-permute-done.14.got = bf16[3,256,256]{2,1,0:T(8,128)(2,1)S(1)} collective-permute-done((bf16[3,256,256]{2,1,0:T(8,128)(2,1)S(1)}, bf16[3,256,256]{2,1,0:T(8,128)(2,1)S(1)}, u32[]{:S(2)}, u32[]{:S(2)}) %collective-permute-start.14) | collective-permute-done | bytes 393248 | tf_op jit(solution)/shard_map/ppermute | solution.py:247
  79.4 0.7 cross_strips.1
  80.2 2.1 %collective-permute-start.15 = (f32[256,512]{1,0:T(8,128)S(1)}, f32[256,512]{1,0:T(8,128)S(1)}, u32[]{:S(2)}, u32[]{:S(2)}) collective-permute-start(f32[256,512]{1,0:T(8,128)S(1)} %get-tuple-element.66), channel_id=1, source_target_pairs={{0,5},{2,7},{5,0},{7,2},{8,13},{10,15},{13,8},{15,10},{16,21},{18,... | collective-permute-start | bytes 1572872 | tf_op jit(solution)/shard_map/ppermute | solution.py:247
  82.3 1.3 %collective-permute-start.17 = (f32[256,512]{1,0:T(8,128)S(1)}, f32[256,512]{1,0:T(8,128)S(1)}, u32[]{:S(2)}, u32[]{:S(2)}) collective-permute-start(f32[256,512]{1,0:T(8,128)S(1)} %get-tuple-element.67), channel_id=1, source_target_pairs={{0,9},{2,11},{8,17},{10,19},{13,4},{15,6},{16,25},{18,27},{21,12},... | collective-permute-start | bytes 1572872 | tf_op jit(solution)/shard_map/ppermute | solution.py:247
  83.6 2.8 %collective-permute-done.13.from_y_b = f32[256,512]{1,0:T(8,128)S(1)} collective-permute-done((f32[256,512]{1,0:T(8,128)S(1)}, f32[256,512]{1,0:T(8,128)S(1)}, u32[]{:S(2)}, u32[]{:S(2)}) %collective-permute-start.13) | collective-permute-done | bytes 524320 | tf_op jit(solution)/shard_map/ppermute | solution.py:247
  86.5 5.6 %collective-permute-done.15.from_y_d = f32[256,512]{1,0:T(8,128)S(1)} collective-permute-done((f32[256,512]{1,0:T(8,128)S(1)}, f32[256,512]{1,0:T(8,128)S(1)}, u32[]{:S(2)}, u32[]{:S(2)}) %collective-permute-start.15) | collective-permute-done | bytes 524320 | tf_op jit(solution)/shard_map/ppermute | solution.py:247
  92.1 0.7 combine.1
  92.8 0.1 collective-permute-start.18
  92.9 2.3 %collective-permute-done.18.sib = f32[3,128,512]{2,1,0:T(8,128)S(1)} collective-permute-done((f32[3,128,512]{2,1,0:T(8,128)S(1)}, f32[3,128,512]{2,1,0:T(8,128)S(1)}, u32[]{:S(2)}, u32[]{:S(2)}) %collective-permute-start.18) | collective-permute-done | bytes 786464 | tf_op jit(solution)/shard_map/ppermute | solution.py:247
  95.2 1.7 %finish.1 = (bf16[1,3,128,512]{3,2,1,0:T(8,128)(2,1)}, bf16[1,2,128,512]{3,2,1,0:T(8,128)(2,1)}) custom-call(s32[5]{0:T(128)S(1)} %stack.23.pos_ref.refs_0_, s32[1,3]{1,0:T(1,128)S(1)} %copy-done.2, f32[128,512]{1,0:T(8,128)S(1)} %get-tuple-element.39.diag_mine, f32[128,512]{1,0:T(8,128)S(1)} %collective-permute-done.9.diag_got, ...), custom_call_target="tpu_custom_call" | custom-call | tf_op jit(solution)/shard_map/finish/pallas_call | solution.py:341
  (12 shorter events, 0.0 us)
Async XLA Ops:
  0.6 5.8 %copy-start = (bf16[4096,512]{1,0:T(8,128)(2,1)S(1)}, bf16[4096,512]{1,0:T(8,128)(2,1)}, u32[]{:S(2)}) copy-start(bf16[4096,512]{1,0:T(8,128)(2,1)} %x_ref.1) | copy-start | bytes 12582916
  3.8 42.0 %collective-permute-start.6 = (bf16[2048,512]{1,0:T(8,128)(2,1)}, bf16[2048,512]{1,0:T(8,128)(2,1)}, u32[]{:S(2)}, u32[]{:S(2)}) collective-permute-start(bf16[2048,512]{1,0:T(8,128)(2,1)} %slice.7), channel_id=1, source_target_pairs={{1,9},{3,11},{5,13},{7,15},{8,0},{9,17},{10,2},{11,19},{12,4},{13,... | collective-permute-start | bytes 6291464 | tf_op jit(solution)/shard_map/ppermute | solution.py:247
  5.1 45.5 %collective-permute-start.5 = (bf16[2048,512]{1,0:T(8,128)(2,1)}, bf16[2048,512]{1,0:T(8,128)(2,1)S(1)}, u32[]{:S(2)}, u32[]{:S(2)}) collective-permute-start(bf16[2048,512]{1,0:T(8,128)(2,1)} %slice.7), channel_id=1, source_target_pairs={{1,5},{3,7},{4,0},{6,2},{9,13},{11,15},{12,8},{14,10},{17,21},{19,... | collective-permute-start | bytes 6291464 | tf_op jit(solution)/shard_map/ppermute | solution.py:247
  8.3 21.4 %copy-start.2 = (s32[1,3]{1,0:T(1,128)S(1)}, s32[1,3]{1,0:T(1,128)}, u32[]{:S(2)}) copy-start(s32[1,3]{1,0:T(1,128)} %offsets_ref.3) | copy-start | bytes 40
  9.8 45.8 %collective-permute-start.4 = (bf16[2048,512]{1,0:T(8,128)(2,1)}, bf16[2048,512]{1,0:T(8,128)(2,1)}, u32[]{:S(2)}, u32[]{:S(2)}) collective-permute-start(bf16[2048,512]{1,0:T(8,128)(2,1)} %slice.6), channel_id=1, source_target_pairs={{1,9},{3,11},{5,13},{7,15},{8,0},{9,17},{10,2},{11,19},{12,4},{13,... | collective-permute-start | bytes 6291464 | tf_op jit(solution)/shard_map/ppermute | solution.py:247
  11.1 49.9 %collective-permute-start.10 = (bf16[2048,512]{1,0:T(8,128)(2,1)}, bf16[2048,512]{1,0:T(8,128)(2,1)}, u32[]{:S(2)}, u32[]{:S(2)}) collective-permute-start(bf16[2048,512]{1,0:T(8,128)(2,1)} %slice.6), channel_id=1, source_target_pairs={{1,5},{3,7},{4,0},{6,2},{9,13},{11,15},{12,8},{14,10},{17,21},{19,... | collective-permute-start | bytes 6291464 | tf_op jit(solution)/shard_map/ppermute | solution.py:247
  12.4 10.7 %collective-permute-start = (f32[2,512]{1,0:T(2,128)S(1)}, f32[2,512]{1,0:T(2,128)S(1)}, u32[]{:S(2)}, u32[]{:S(2)}) collective-permute-start(f32[2,512]{1,0:T(2,128)S(1)} %local_stats.1.own_ref), channel_id=1, source_target_pairs={{0,1},{1,0},{2,3},{3,2},{4,5},{5,4},{6,7},{7,6},{8,9},{9,8},{10,11... | collective-permute-start | bytes 12296 | tf_op jit(solution)/shard_map/ppermute | solution.py:247
  23.1 3.6 %collective-permute-start.1 = (f32[2,512]{1,0:T(2,128)S(1)}, f32[2,512]{1,0:T(2,128)S(1)}, u32[]{:S(2)}, u32[]{:S(2)}) collective-permute-start(f32[2,512]{1,0:T(2,128)S(1)} %local_stats.1.own_ref), channel_id=1, source_target_pairs={{0,2},{1,3},{2,0},{3,1},{4,6},{5,7},{6,4},{7,5},{8,10},{9,11},{10,... | collective-permute-start | bytes 12296 | tf_op jit(solution)/shard_map/ppermute | solution.py:247
  26.7 3.0 %collective-permute-start.2 = (f32[2,512]{1,0:T(2,128)S(1)}, f32[2,512]{1,0:T(2,128)S(1)}, u32[]{:S(2)}, u32[]{:S(2)}) collective-permute-start(f32[2,512]{1,0:T(2,128)S(1)} %local_stats.1.own_ref), channel_id=1, source_target_pairs={{0,3},{1,2},{2,1},{3,0},{4,7},{5,6},{6,5},{7,4},{8,11},{9,10},{10,... | collective-permute-start | bytes 12296 | tf_op jit(solution)/shard_map/ppermute | solution.py:247
  30.3 2.2 %copy-start.1 = (bf16[4096,512]{1,0:T(8,128)(2,1)S(1)}, bf16[4096,512]{1,0:T(8,128)(2,1)}, u32[]{:S(2)}) copy-start(bf16[4096,512]{1,0:T(8,128)(2,1)} %x_ref.1) | copy-start | bytes 12582916
  36.8 2.0 %collective-permute-start.3 = (f32[2,128,512]{2,1,0:T(8,128)S(1)}, f32[2,128,512]{2,1,0:T(8,128)S(1)}, u32[]{:S(2)}, u32[]{:S(2)}) collective-permute-start(f32[2,128,512]{2,1,0:T(8,128)S(1)} %get-tuple-element.38), channel_id=1, source_target_pairs={{0,1},{1,0},{2,3},{3,2},{4,5},{5,4},{6,7},{7,6},{8,9},{9,8},{10,11... | collective-permute-start | bytes 1572872 | tf_op jit(solution)/shard_map/ppermute | solution.py:247
  38.8 5.1 %collective-permute-start.7 = (f32[4,512]{1,0:T(4,128)S(1)}, f32[4,512]{1,0:T(4,128)S(1)}, u32[]{:S(2)}, u32[]{:S(2)}) collective-permute-start(f32[4,512]{1,0:T(4,128)S(1)} %stats.1.stat_ref.refs_3_.refs_4_), channel_id=1, source_target_pairs={{0,9},{2,11},{4,13},{6,15},{8,17},{9,0},{10,19},{11,2},{12,21},{13... | collective-permute-start | bytes 24584 | tf_op jit(solution)/shard_map/ppermute | solution.py:247
  43.9 6.7 %collective-permute-start.8 = (f32[4,512]{1,0:T(4,128)S(1)}, f32[4,512]{1,0:T(4,128)S(1)}, u32[]{:S(2)}, u32[]{:S(2)}) collective-permute-start(f32[4,512]{1,0:T(4,128)S(1)} %stats.1.stat_ref.refs_3_.refs_4_), channel_id=1, source_target_pairs={{0,5},{2,7},{5,0},{7,2},{8,13},{10,15},{13,8},{15,10},{16,21},{18,... | collective-permute-start | bytes 24584 | tf_op jit(solution)/shard_map/ppermute | solution.py:247
  45.8 13.2 %collective-permute-start.9 = (f32[128,512]{1,0:T(8,128)S(1)}, f32[128,512]{1,0:T(8,128)S(1)}, u32[]{:S(2)}, u32[]{:S(2)}) collective-permute-start(f32[128,512]{1,0:T(8,128)S(1)} %get-tuple-element.47), channel_id=1, source_target_pairs={{0,2},{1,3},{2,0},{3,1},{4,6},{5,7},{6,4},{7,5},{8,10},{9,11},{10,... | collective-permute-start | bytes 786440 | tf_op jit(solution)/shard_map/ppermute | solution.py:247
  59.0 9.6 %collective-permute-start.12 = (bf16[3,256,256]{2,1,0:T(8,128)(2,1)S(1)}, bf16[3,256,256]{2,1,0:T(8,128)(2,1)S(1)}, u32[]{:S(2)}, u32[]{:S(2)}) collective-permute-start(bf16[3,256,256]{2,1,0:T(8,128)(2,1)S(1)} %get-tuple-element.56), channel_id=1, source_target_pairs={{0,2},{1,3},{2,0},{3,1},{4,6},{5,7},{6,4},{7,5},{8,10},{9,11},{10,... | collective-permute-start | bytes 1179656 | tf_op jit(solution)/shard_map/ppermute | solution.py:247
  65.5 9.7 %collective-permute-start.11 = (bf16[3,256,256]{2,1,0:T(8,128)(2,1)S(1)}, bf16[3,256,256]{2,1,0:T(8,128)(2,1)S(1)}, u32[]{:S(2)}, u32[]{:S(2)}) collective-permute-start(bf16[3,256,256]{2,1,0:T(8,128)(2,1)S(1)} %get-tuple-element.53), channel_id=1, source_target_pairs={{0,2},{2,0},{5,7},{7,5},{8,10},{10,8},{13,15},{15,13},{16,18},{18,... | collective-permute-start | bytes 1179656 | tf_op jit(solution)/shard_map/ppermute | solution.py:247
  68.6 10.8 %collective-permute-start.14 = (bf16[3,256,256]{2,1,0:T(8,128)(2,1)S(1)}, bf16[3,256,256]{2,1,0:T(8,128)(2,1)S(1)}, u32[]{:S(2)}, u32[]{:S(2)}) collective-permute-start(bf16[3,256,256]{2,1,0:T(8,128)(2,1)S(1)} %get-tuple-element.64), channel_id=1, source_target_pairs={{0,2},{2,0},{5,7},{7,5},{8,10},{10,8},{13,15},{15,13},{16,18},{18,... | collective-permute-start | bytes 1179656 | tf_op jit(solution)/shard_map/ppermute | solution.py:247
  72.8 13.7 %collective-permute-start.16 = (f32[256,512]{1,0:T(8,128)S(1)}, f32[256,512]{1,0:T(8,128)S(1)}, u32[]{:S(2)}, u32[]{:S(2)}) collective-permute-start(f32[256,512]{1,0:T(8,128)S(1)} %get-tuple-element.58), channel_id=1, source_target_pairs={{0,9},{2,11},{4,13},{6,15},{8,17},{9,0},{10,19},{11,2},{12,21},{13... | collective-permute-start | bytes 1572872 | tf_op jit(solution)/shard_map/ppermute | solution.py:247
  76.0 10.5 %collective-permute-start.13 = (f32[256,512]{1,0:T(8,128)S(1)}, f32[256,512]{1,0:T(8,128)S(1)}, u32[]{:S(2)}, u32[]{:S(2)}) collective-permute-start(f32[256,512]{1,0:T(8,128)S(1)} %get-tuple-element.62), channel_id=1, source_target_pairs={{0,5},{2,7},{5,0},{7,2},{8,13},{10,15},{13,8},{15,10},{16,21},{18,... | collective-permute-start | bytes 1572872 | tf_op jit(solution)/shard_map/ppermute | solution.py:247
  80.2 11.9 %collective-permute-start.15 = (f32[256,512]{1,0:T(8,128)S(1)}, f32[256,512]{1,0:T(8,128)S(1)}, u32[]{:S(2)}, u32[]{:S(2)}) collective-permute-start(f32[256,512]{1,0:T(8,128)S(1)} %get-tuple-element.66), channel_id=1, source_target_pairs={{0,5},{2,7},{5,0},{7,2},{8,13},{10,15},{13,8},{15,10},{16,21},{18,... | collective-permute-start | bytes 1572872 | tf_op jit(solution)/shard_map/ppermute | solution.py:247
  82.3 9.8 %collective-permute-start.17 = (f32[256,512]{1,0:T(8,128)S(1)}, f32[256,512]{1,0:T(8,128)S(1)}, u32[]{:S(2)}, u32[]{:S(2)}) collective-permute-start(f32[256,512]{1,0:T(8,128)S(1)} %get-tuple-element.67), channel_id=1, source_target_pairs={{0,9},{2,11},{8,17},{10,19},{13,4},{15,6},{16,25},{18,27},{21,12},... | collective-permute-start | bytes 1572872 | tf_op jit(solution)/shard_map/ppermute | solution.py:247
  92.8 2.4 %collective-permute-start.18 = (f32[3,128,512]{2,1,0:T(8,128)S(1)}, f32[3,128,512]{2,1,0:T(8,128)S(1)}, u32[]{:S(2)}, u32[]{:S(2)}) collective-permute-start(f32[3,128,512]{2,1,0:T(8,128)S(1)} %get-tuple-element.69), channel_id=1, source_target_pairs={{0,1},{1,0},{2,3},{3,2},{4,5},{5,4},{6,7},{7,6},{8,9},{9,8},{10,11... | collective-permute-start | bytes 2359304 | tf_op jit(solution)/shard_map/ppermute | solution.py:247

commit v9 on v6

--- a/solution.py
+++ b/solution.py
@@ -12,7 +12,7 @@
 VMEM = pl.BlockSpec(memory_space=pltpu.VMEM)
 SMEM = pl.BlockSpec(memory_space=pltpu.SMEM)
 SOME = pltpu.CompilerParams(vmem_limit_bytes=24 << 20)
-HALVES = BF16
+HALVES, CROSS = BF16, BF16
 
 
 def dot(a, b):
@@ -180,11 +180,11 @@
         @pl.when(pos_ref[1] == 1)
         def _():
             out[0] = held_b[at, :] + from_y_b[at, :]
-            out[2] = from_y_d[at, :]
+            out[2] = from_y_d[at, :].astype(F32)
 
         @pl.when(pos_ref[1] == 0)
         def _():
-            out[2] = from_z_d[at, :]
+            out[2] = from_z_d[at, :].astype(F32)
 
 
 def finish_kernel(pos_ref, offsets_ref, diag_mine, diag_got, mine, sib, upper, mirror):
@@ -296,13 +296,14 @@
     from_z_c = send(to_z_c, z_cross)
     got_b, to_z_c = lax.optimization_barrier((got_b, to_z_c))
 
-    def near_strips(name, keep, got):
-        return call(near_strips_kernel, name, (), [SMEM] + [VMEM] * 2, [VMEM] * 2, [shape(half, width)] * 2)(pos, keep, got)
-
-    held_b, to_y_b = near_strips("near_strips", keep_b, got_b)
+    def near_strips(name, kind, keep, got):
+        return call(near_strips_kernel, name, (), [SMEM] + [VMEM] * 2, [VMEM] * 2, [shape(half, width, dtype=kind)] * 2)(
+            pos, keep, got)
+
+    held_b, to_y_b = near_strips("near_strips", F32, keep_b, got_b)
     from_y_b = send(to_y_b, y_cross)
     got_d, to_y_b = lax.optimization_barrier((got_d, to_y_b))
-    to_y_d, to_z_d = near_strips("cross_strips", keep_d, got_d)
+    to_y_d, to_z_d = near_strips("cross_strips", CROSS, keep_d, got_d)
     from_y_d, from_z_d = send(to_y_d, y_cross), send(to_z_d, z_cross_active)
 
     mine, sib = call(combine_kernel, "combine", (), [SMEM] + [VMEM] * 6, [VMEM] * 2, [shape(3, strip, width)] * 2)(

time: 97.5 us -> 95.5 us (0.979)
  waiting for transfers between devices: 34.8 us -> 31.3 us
    ppermute x17, waiting for transfers between devices: 34.8 us -> 31.3 us  [send(): return lax.ppermute(value, AXES, pairs)]
where the time goes in v9:
time: 95.5 us; the launch traced here: 94.3 us
  starting transfers between devices  33.8 us (35%)
  waiting for transfers between devices  31.3 us (33%)
  Pallas kernels  23.2 us (24%)
  local copies, waits for them, and re-layouts  4.46 us (5%)
  between operations  1.49 us (2%)
    ppermute x17, starting transfers between devices, send(): return lax.ppermute(value, AXES, pairs)  33.8 us
    ppermute x17, waiting for transfers between devices, send(): return lax.ppermute(value, AXES, pairs)  31.3 us
    pallas_call x1, Pallas kernels, body(): call(near_kernel, 'near_tiles', (), [SMEM, VMEM, anywhere] + [VMEM] * 4,...  6.74 us
    pallas_call x1, Pallas kernels, body(): call(far_kernel, 'far_tile', (), [SMEM, VMEM, anywhere, VMEM, VMEM], [VME...  4.6 us
    unnamed x6, local copies, waits for them, and re-layouts  4.37 us
    pallas_call x1, Pallas kernels, body(): call(own_kernel, 'own_tile', (steps,), [SMEM, wide, whole(4, width)], [fl...  4.3 us
  transfers between devices with their start and end apart: 17, of which 10 were waited for; matrix products, arithmetic and copies ran while one was open for 0% of the time, Pallas kernels for 22%

profile of v9, /device:TPU:0, one launch (start us, length us, event | category | flops | bytes accessed | tf_op | source)
XLA Modules:
  0.0 94.3 jit_solution(7166463716112022243)
XLA Ops:
  0.6 1.3 %collective-permute-start.4 = (bf16[4096,512]{1,0:T(8,128)(2,1)}, bf16[4096,512]{1,0:T(8,128)(2,1)}, u32[]{:S(2)}, u32[]{:S(2)}) collective-permute-start(bf16[4096,512]{1,0:T(8,128)(2,1)} %x_ref.1), channel_id=1, source_target_pairs={{1,9},{3,11},{5,13},{7,15},{8,0},{9,17},{10,2},{11,19},{12,4},{13,... | collective-permute-start | bytes 12582920 | tf_op jit(solution)/shard_map/ppermute | solution.py:227
  1.9 1.3 %collective-permute-start.7 = (bf16[4096,512]{1,0:T(8,128)(2,1)}, bf16[4096,512]{1,0:T(8,128)(2,1)}, u32[]{:S(2)}, u32[]{:S(2)}) collective-permute-start(bf16[4096,512]{1,0:T(8,128)(2,1)} %x_ref.1), channel_id=1, source_target_pairs={{1,5},{3,7},{4,0},{6,2},{9,13},{11,15},{12,8},{14,10},{17,21},{19,... | collective-permute-start | bytes 12582920 | tf_op jit(solution)/shard_map/ppermute | solution.py:227
  3.2 0.0 copy-start
  3.2 2.2 %copy-done = bf16[4096,512]{1,0:T(8,128)(2,1)S(1)} copy-done((bf16[4096,512]{1,0:T(8,128)(2,1)S(1)}, bf16[4096,512]{1,0:T(8,128)(2,1)}, u32[]{:S(2)}) %copy-start) | copy-done | bytes 4194328
  5.4 1.9 %local_stats.1.own_ref = f32[2,512]{1,0:T(2,128)S(1)} custom-call(bf16[4096,512]{1,0:T(8,128)(2,1)S(1)} %copy-done), custom_call_target="tpu_custom_call" | custom-call | flops 10485760 | bytes 4194304 | tf_op jit(solution)/shard_map/local_stats/pallas_call | solution.py:260
  7.3 9.1 %collective-permute-start = (f32[2,512]{1,0:T(2,128)S(1)}, f32[2,512]{1,0:T(2,128)S(1)}, u32[]{:S(2)}, u32[]{:S(2)}) collective-permute-start(f32[2,512]{1,0:T(2,128)S(1)} %local_stats.1.own_ref), channel_id=1, source_target_pairs={{0,1},{1,0},{2,3},{3,2},{4,5},{5,4},{6,7},{7,6},{8,9},{9,8},{10,11... | collective-permute-start | bytes 12296 | tf_op jit(solution)/shard_map/ppermute | solution.py:227
  16.4 1.5 %collective-permute-start.1 = (f32[2,512]{1,0:T(2,128)S(1)}, f32[2,512]{1,0:T(2,128)S(1)}, u32[]{:S(2)}, u32[]{:S(2)}) collective-permute-start(f32[2,512]{1,0:T(2,128)S(1)} %local_stats.1.own_ref), channel_id=1, source_target_pairs={{0,2},{1,3},{2,0},{3,1},{4,6},{5,7},{6,4},{7,5},{8,10},{9,11},{10,... | collective-permute-start | bytes 12296 | tf_op jit(solution)/shard_map/ppermute | solution.py:227
  17.9 0.0 collective-permute-start.2
  18.5 0.1 stack.23.pos_ref
  18.6 0.0 collective-permute-done.sib_ref
  18.6 1.4 %collective-permute-done.1.far_ref = f32[2,512]{1,0:T(2,128)S(1)} collective-permute-done((f32[2,512]{1,0:T(2,128)S(1)}, f32[2,512]{1,0:T(2,128)S(1)}, u32[]{:S(2)}, u32[]{:S(2)}) %collective-permute-start.1) | collective-permute-done | bytes 4128 | tf_op jit(solution)/shard_map/ppermute | solution.py:227
  20.0 0.9 collective-permute-done.2.cross_ref
  20.9 0.6 stats.1.stat_ref
  21.5 0.0 copy-start.1
  21.5 2.2 %copy-done.1 = bf16[4096,512]{1,0:T(8,128)(2,1)S(1)} copy-done((bf16[4096,512]{1,0:T(8,128)(2,1)S(1)}, bf16[4096,512]{1,0:T(8,128)(2,1)}, u32[]{:S(2)}) %copy-start.1) | copy-done | bytes 4194328
  23.7 4.3 %own_tile.1 = (bf16[512,4096]{1,0:T(8,128)(2,1)S(1)}, f32[2,128,512]{2,1,0:T(8,128)S(1)}, f32[2,128,512]{2,1,0:T(8,128)S(1)}) custom-call(s32[5]{0:T(128)S(1)} %stack.23.pos_ref, bf16[4096,512]{1,0:T(8,128)(2,1)S(1)} %copy-done.1, f32[4,512]{1,0:T(4,128)S(1)} %stats.1.stat_ref), custom_call_target="tpu_custom_call" | custom-call | flops 2147483648 | bytes 8388608 | tf_op jit(solution)/shard_map/own_tile/pallas_call | solution.py:267
  28.0 0.3 collective-permute-start.3
  28.2 1.7 %collective-permute-done.3.got_ref = f32[2,128,512]{2,1,0:T(8,128)S(1)} collective-permute-done((f32[2,128,512]{2,1,0:T(8,128)S(1)}, f32[2,128,512]{2,1,0:T(8,128)S(1)}, u32[]{:S(2)}, u32[]{:S(2)}) %collective-permute-start.3) | collective-permute-done | bytes 524320 | tf_op jit(solution)/shard_map/ppermute | solution.py:227
  30.0 0.6 own_tile_strips.1
  30.6 0.6 collective-permute-start.6
  31.2 1.9 %collective-permute-start.5 = (f32[4,512]{1,0:T(4,128)S(1)}, f32[4,512]{1,0:T(4,128)S(1)}, u32[]{:S(2)}, u32[]{:S(2)}) collective-permute-start(f32[4,512]{1,0:T(4,128)S(1)} %stats.1.stat_ref), channel_id=1, source_target_pairs={{0,9},{2,11},{4,13},{6,15},{8,17},{9,0},{10,19},{11,2},{12,21},{13... | collective-permute-start | bytes 24584 | tf_op jit(solution)/shard_map/ppermute | solution.py:227
  33.1 1.9 %collective-permute-start.8 = (f32[4,512]{1,0:T(4,128)S(1)}, f32[4,512]{1,0:T(4,128)S(1)}, u32[]{:S(2)}, u32[]{:S(2)}) collective-permute-start(f32[4,512]{1,0:T(4,128)S(1)} %stats.1.stat_ref), channel_id=1, source_target_pairs={{0,5},{2,7},{5,0},{7,2},{8,13},{10,15},{13,8},{15,10},{16,21},{18,... | collective-permute-start | bytes 24584 | tf_op jit(solution)/shard_map/ppermute | solution.py:227
  35.1 1.3 %collective-permute-done.5.wstat_ref = f32[4,512]{1,0:T(4,128)S(1)} collective-permute-done((f32[4,512]{1,0:T(4,128)S(1)}, f32[4,512]{1,0:T(4,128)S(1)}, u32[]{:S(2)}, u32[]{:S(2)}) %collective-permute-start.5) | collective-permute-done | bytes 8224 | tf_op jit(solution)/shard_map/ppermute | solution.py:227
  36.3 16.1 %collective-permute-done.4.w_ref = bf16[4096,512]{1,0:T(8,128)(2,1)} collective-permute-done((bf16[4096,512]{1,0:T(8,128)(2,1)}, bf16[4096,512]{1,0:T(8,128)(2,1)}, u32[]{:S(2)}, u32[]{:S(2)}) %collective-permute-start.4) | collective-permute-done | bytes 4194336 | tf_op jit(solution)/shard_map/ppermute | solution.py:227
  52.4 4.6 %far_tile.1 = (f32[3,256,256]{2,1,0:T(8,128)S(1)}, bf16[3,256,256]{2,1,0:T(8,128)(2,1)S(1)}, bf16[4096,512]{1,0:T(8,128)(2,1)S(1)}) custom-call(s32[5]{0:T(128)S(1)} %stack.23.pos_ref, bf16[512,4096]{1,0:T(8,128)(2,1)S(1)} %get-tuple-element.31.turned_ref, bf16[4096,512]{1,0:T(8,128)(2,1)} %collective-permute-done.4.w_ref, f32[4,512]{1,0:T(4,128)S(1)} %stats.1.stat_ref, ...), custom_call_target="tpu_custom_call" | custom-call | flops 2147483648 | bytes 12582912 | tf_op jit(solution)/shard_map/far_tile/pallas_call | solution.py:280
  57.1 0.0 collective-permute-done.6.diag_got
  57.1 2.0 %collective-permute-start.10 = (bf16[3,256,256]{2,1,0:T(8,128)(2,1)S(1)}, bf16[3,256,256]{2,1,0:T(8,128)(2,1)S(1)}, u32[]{:S(2)}, u32[]{:S(2)}) collective-permute-start(bf16[3,256,256]{2,1,0:T(8,128)(2,1)S(1)} %get-tuple-element.40), channel_id=1, source_target_pairs={{0,2},{1,3},{2,0},{3,1},{4,6},{5,7},{6,4},{7,5},{8,10},{9,11},{10,... | collective-permute-start | bytes 1179656 | tf_op jit(solution)/shard_map/ppermute | solution.py:227
  59.1 0.0 collective-permute-done.8.ystat_ref
  59.1 0.0 collective-permute-done.7.y_ref
  59.1 6.7 %near_tiles.1 = (f32[3,256,256]{2,1,0:T(8,128)S(1)}, bf16[3,256,256]{2,1,0:T(8,128)(2,1)S(1)}, f32[3,256,256]{2,1,0:T(8,128)S(1)}, bf16[3,256,256]{2,1,0:T(8,128)(2,1)S(1)}) custom-call(s32[5]{0:T(128)S(1)} %stack.23.pos_ref, bf16[512,4096]{1,0:T(8,128)(2,1)S(1)} %get-tuple-element.31.turned_ref, bf16[4096,512]{1,0:T(8,128)(2,1)} %collective-permute-done.7.y_ref, ...), custom_call_target="tpu_custom_call" | custom-call | flops 4294967296 | bytes 12582912 | tf_op jit(solution)/shard_map/near_tiles/pallas_call | solution.py:287
  65.8 2.0 %collective-permute-start.9 = (bf16[3,256,256]{2,1,0:T(8,128)(2,1)S(1)}, bf16[3,256,256]{2,1,0:T(8,128)(2,1)S(1)}, u32[]{:S(2)}, u32[]{:S(2)}) collective-permute-start(bf16[3,256,256]{2,1,0:T(8,128)(2,1)S(1)} %get-tuple-element.37), channel_id=1, source_target_pairs={{0,2},{2,0},{5,7},{7,5},{8,10},{10,8},{13,15},{15,13},{16,18},{18,... | collective-permute-start | bytes 1179656 | tf_op jit(solution)/shard_map/ppermute | solution.py:227
  67.8 3.8 %collective-permute-start.12 = (bf16[3,256,256]{2,1,0:T(8,128)(2,1)S(1)}, bf16[3,256,256]{2,1,0:T(8,128)(2,1)S(1)}, u32[]{:S(2)}, u32[]{:S(2)}) collective-permute-start(bf16[3,256,256]{2,1,0:T(8,128)(2,1)S(1)} %get-tuple-element.48), channel_id=1, source_target_pairs={{0,2},{2,0},{5,7},{7,5},{8,10},{10,8},{13,15},{15,13},{16,18},{18,... | collective-permute-start | bytes 1179656 | tf_op jit(solution)/shard_map/ppermute | solution.py:227
  71.7 0.7 far_strips.1
  72.4 3.1 %collective-permute-done.9.got = bf16[3,256,256]{2,1,0:T(8,128)(2,1)S(1)} collective-permute-done((bf16[3,256,256]{2,1,0:T(8,128)(2,1)S(1)}, bf16[3,256,256]{2,1,0:T(8,128)(2,1)S(1)}, u32[]{:S(2)}, u32[]{:S(2)}) %collective-permute-start.9) | collective-permute-done | bytes 393248 | tf_op jit(solution)/shard_map/ppermute | solution.py:227
  75.5 0.8 near_strips.1
  76.2 1.9 %collective-permute-start.11 = (f32[256,512]{1,0:T(8,128)S(1)}, f32[256,512]{1,0:T(8,128)S(1)}, u32[]{:S(2)}, u32[]{:S(2)}) collective-permute-start(f32[256,512]{1,0:T(8,128)S(1)} %get-tuple-element.46), channel_id=1, source_target_pairs={{0,5},{2,7},{5,0},{7,2},{8,13},{10,15},{13,8},{15,10},{16,21},{18,... | collective-permute-start | bytes 1572872 | tf_op jit(solution)/shard_map/ppermute | solution.py:227
  78.2 1.9 %collective-permute-start.14 = (f32[256,512]{1,0:T(8,128)S(1)}, f32[256,512]{1,0:T(8,128)S(1)}, u32[]{:S(2)}, u32[]{:S(2)}) collective-permute-start(f32[256,512]{1,0:T(8,128)S(1)} %get-tuple-element.42), channel_id=1, source_target_pairs={{0,9},{2,11},{4,13},{6,15},{8,17},{9,0},{10,19},{11,2},{12,21},{13... | collective-permute-start | bytes 1572872 | tf_op jit(solution)/shard_map/ppermute | solution.py:227
  80.1 0.7 cross_strips.1
  80.8 2.4 %collective-permute-start.13 = (bf16[256,512]{1,0:T(8,128)(2,1)S(1)}, bf16[256,512]{1,0:T(8,128)(2,1)S(1)}, u32[]{:S(2)}, u32[]{:S(2)}) collective-permute-start(bf16[256,512]{1,0:T(8,128)(2,1)S(1)} %get-tuple-element.50), channel_id=1, source_target_pairs={{0,5},{2,7},{5,0},{7,2},{8,13},{10,15},{13,8},{15,10},{16,21},{18,... | collective-permute-start | bytes 786440 | tf_op jit(solution)/shard_map/ppermute | solution.py:227
  83.2 1.8 %collective-permute-start.15 = (bf16[256,512]{1,0:T(8,128)(2,1)S(1)}, bf16[256,512]{1,0:T(8,128)(2,1)S(1)}, u32[]{:S(2)}, u32[]{:S(2)}) collective-permute-start(bf16[256,512]{1,0:T(8,128)(2,1)S(1)} %get-tuple-element.51), channel_id=1, source_target_pairs={{0,9},{2,11},{8,17},{10,19},{13,4},{15,6},{16,25},{18,27},{21,12},... | collective-permute-start | bytes 786440 | tf_op jit(solution)/shard_map/ppermute | solution.py:227
  85.0 1.7 %collective-permute-done.11.from_y_b = f32[256,512]{1,0:T(8,128)S(1)} collective-permute-done((f32[256,512]{1,0:T(8,128)S(1)}, f32[256,512]{1,0:T(8,128)S(1)}, u32[]{:S(2)}, u32[]{:S(2)}) %collective-permute-start.11) | collective-permute-done | bytes 524320 | tf_op jit(solution)/shard_map/ppermute | solution.py:227
  86.7 1.9 %collective-permute-done.14.from_z_c = f32[256,512]{1,0:T(8,128)S(1)} collective-permute-done((f32[256,512]{1,0:T(8,128)S(1)}, f32[256,512]{1,0:T(8,128)S(1)}, u32[]{:S(2)}, u32[]{:S(2)}) %collective-permute-start.14) | collective-permute-done | bytes 524320 | tf_op jit(solution)/shard_map/ppermute | solution.py:227
  88.7 0.9 collective-permute-done.13.from_y_d
  89.5 0.0 collective-permute-done.15.from_z_d
  89.6 0.7 combine.1
  90.3 0.1 collective-permute-start.16
  90.4 2.3 %collective-permute-done.16.sib = f32[3,128,512]{2,1,0:T(8,128)S(1)} collective-permute-done((f32[3,128,512]{2,1,0:T(8,128)S(1)}, f32[3,128,512]{2,1,0:T(8,128)S(1)}, u32[]{:S(2)}, u32[]{:S(2)}) %collective-permute-start.16) | collective-permute-done | bytes 786464 | tf_op jit(solution)/shard_map/ppermute | solution.py:227
  92.6 1.7 %finish.1 = (bf16[1,3,128,512]{3,2,1,0:T(8,128)(2,1)}, bf16[1,2,128,512]{3,2,1,0:T(8,128)(2,1)}) custom-call(s32[5]{0:T(128)S(1)} %stack.23.pos_ref, s32[1,3]{1,0:T(1,128)S(1)} %copy-done.2, f32[128,512]{1,0:T(8,128)S(1)} %get-tuple-element.30.diag_mine, f32[128,512]{1,0:T(8,128)S(1)} %collective-permute-done.6.diag_got, ...), custom_call_target="tpu_custom_call" | custom-call | tf_op jit(solution)/shard_map/finish/pallas_call | solution.py:311
  (4 shorter events, 0.0 us)
Async XLA Ops:
  0.6 51.8 %collective-permute-start.4 = (bf16[4096,512]{1,0:T(8,128)(2,1)}, bf16[4096,512]{1,0:T(8,128)(2,1)}, u32[]{:S(2)}, u32[]{:S(2)}) collective-permute-start(bf16[4096,512]{1,0:T(8,128)(2,1)} %x_ref.1), channel_id=1, source_target_pairs={{1,9},{3,11},{5,13},{7,15},{8,0},{9,17},{10,2},{11,19},{12,4},{13,... | collective-permute-start | bytes 12582920 | tf_op jit(solution)/shard_map/ppermute | solution.py:227
  1.9 57.1 %collective-permute-start.7 = (bf16[4096,512]{1,0:T(8,128)(2,1)}, bf16[4096,512]{1,0:T(8,128)(2,1)}, u32[]{:S(2)}, u32[]{:S(2)}) collective-permute-start(bf16[4096,512]{1,0:T(8,128)(2,1)} %x_ref.1), channel_id=1, source_target_pairs={{1,5},{3,7},{4,0},{6,2},{9,13},{11,15},{12,8},{14,10},{17,21},{19,... | collective-permute-start | bytes 12582920 | tf_op jit(solution)/shard_map/ppermute | solution.py:227
  3.2 2.2 %copy-start = (bf16[4096,512]{1,0:T(8,128)(2,1)S(1)}, bf16[4096,512]{1,0:T(8,128)(2,1)}, u32[]{:S(2)}) copy-start(bf16[4096,512]{1,0:T(8,128)(2,1)} %x_ref.1) | copy-start | bytes 12582916
  5.4 15.5 %copy-start.2 = (s32[1,3]{1,0:T(1,128)S(1)}, s32[1,3]{1,0:T(1,128)}, u32[]{:S(2)}) copy-start(s32[1,3]{1,0:T(1,128)} %offsets_ref.3) | copy-start | bytes 40
  7.3 11.3 %collective-permute-start = (f32[2,512]{1,0:T(2,128)S(1)}, f32[2,512]{1,0:T(2,128)S(1)}, u32[]{:S(2)}, u32[]{:S(2)}) collective-permute-start(f32[2,512]{1,0:T(2,128)S(1)} %local_stats.1.own_ref), channel_id=1, source_target_pairs={{0,1},{1,0},{2,3},{3,2},{4,5},{5,4},{6,7},{7,6},{8,9},{9,8},{10,11... | collective-permute-start | bytes 12296 | tf_op jit(solution)/shard_map/ppermute | solution.py:227
  16.4 3.6 %collective-permute-start.1 = (f32[2,512]{1,0:T(2,128)S(1)}, f32[2,512]{1,0:T(2,128)S(1)}, u32[]{:S(2)}, u32[]{:S(2)}) collective-permute-start(f32[2,512]{1,0:T(2,128)S(1)} %local_stats.1.own_ref), channel_id=1, source_target_pairs={{0,2},{1,3},{2,0},{3,1},{4,6},{5,7},{6,4},{7,5},{8,10},{9,11},{10,... | collective-permute-start | bytes 12296 | tf_op jit(solution)/shard_map/ppermute | solution.py:227
  17.9 3.1 %collective-permute-start.2 = (f32[2,512]{1,0:T(2,128)S(1)}, f32[2,512]{1,0:T(2,128)S(1)}, u32[]{:S(2)}, u32[]{:S(2)}) collective-permute-start(f32[2,512]{1,0:T(2,128)S(1)} %local_stats.1.own_ref), channel_id=1, source_target_pairs={{0,3},{1,2},{2,1},{3,0},{4,7},{5,6},{6,5},{7,4},{8,11},{9,10},{10,... | collective-permute-start | bytes 12296 | tf_op jit(solution)/shard_map/ppermute | solution.py:227
  21.5 2.2 %copy-start.1 = (bf16[4096,512]{1,0:T(8,128)(2,1)S(1)}, bf16[4096,512]{1,0:T(8,128)(2,1)}, u32[]{:S(2)}) copy-start(bf16[4096,512]{1,0:T(8,128)(2,1)} %x_ref.1) | copy-start | bytes 12582916
  28.0 2.0 %collective-permute-start.3 = (f32[2,128,512]{2,1,0:T(8,128)S(1)}, f32[2,128,512]{2,1,0:T(8,128)S(1)}, u32[]{:S(2)}, u32[]{:S(2)}) collective-permute-start(f32[2,128,512]{2,1,0:T(8,128)S(1)} %get-tuple-element.29), channel_id=1, source_target_pairs={{0,1},{1,0},{2,3},{3,2},{4,5},{5,4},{6,7},{7,6},{8,9},{9,8},{10,11... | collective-permute-start | bytes 1572872 | tf_op jit(solution)/shard_map/ppermute | solution.py:227
  30.6 26.5 %collective-permute-start.6 = (f32[128,512]{1,0:T(8,128)S(1)}, f32[128,512]{1,0:T(8,128)S(1)}, u32[]{:S(2)}, u32[]{:S(2)}) collective-permute-start(f32[128,512]{1,0:T(8,128)S(1)} %get-tuple-element.33), channel_id=1, source_target_pairs={{0,2},{1,3},{2,0},{3,1},{4,6},{5,7},{6,4},{7,5},{8,10},{9,11},{10,... | collective-permute-start | bytes 786440 | tf_op jit(solution)/shard_map/ppermute | solution.py:227
  31.2 5.1 %collective-permute-start.5 = (f32[4,512]{1,0:T(4,128)S(1)}, f32[4,512]{1,0:T(4,128)S(1)}, u32[]{:S(2)}, u32[]{:S(2)}) collective-permute-start(f32[4,512]{1,0:T(4,128)S(1)} %stats.1.stat_ref), channel_id=1, source_target_pairs={{0,9},{2,11},{4,13},{6,15},{8,17},{9,0},{10,19},{11,2},{12,21},{13... | collective-permute-start | bytes 24584 | tf_op jit(solution)/shard_map/ppermute | solution.py:227
  33.1 25.9 %collective-permute-start.8 = (f32[4,512]{1,0:T(4,128)S(1)}, f32[4,512]{1,0:T(4,128)S(1)}, u32[]{:S(2)}, u32[]{:S(2)}) collective-permute-start(f32[4,512]{1,0:T(4,128)S(1)} %stats.1.stat_ref), channel_id=1, source_target_pairs={{0,5},{2,7},{5,0},{7,2},{8,13},{10,15},{13,8},{15,10},{16,21},{18,... | collective-permute-start | bytes 24584 | tf_op jit(solution)/shard_map/ppermute | solution.py:227
  57.1 10.8 %collective-permute-start.10 = (bf16[3,256,256]{2,1,0:T(8,128)(2,1)S(1)}, bf16[3,256,256]{2,1,0:T(8,128)(2,1)S(1)}, u32[]{:S(2)}, u32[]{:S(2)}) collective-permute-start(bf16[3,256,256]{2,1,0:T(8,128)(2,1)S(1)} %get-tuple-element.40), channel_id=1, source_target_pairs={{0,2},{1,3},{2,0},{3,1},{4,6},{5,7},{6,4},{7,5},{8,10},{9,11},{10,... | collective-permute-start | bytes 1179656 | tf_op jit(solution)/shard_map/ppermute | solution.py:227
  65.8 9.7 %collective-permute-start.9 = (bf16[3,256,256]{2,1,0:T(8,128)(2,1)S(1)}, bf16[3,256,256]{2,1,0:T(8,128)(2,1)S(1)}, u32[]{:S(2)}, u32[]{:S(2)}) collective-permute-start(bf16[3,256,256]{2,1,0:T(8,128)(2,1)S(1)} %get-tuple-element.37), channel_id=1, source_target_pairs={{0,2},{2,0},{5,7},{7,5},{8,10},{10,8},{13,15},{15,13},{16,18},{18,... | collective-permute-start | bytes 1179656 | tf_op jit(solution)/shard_map/ppermute | solution.py:227
  67.8 12.3 %collective-permute-start.12 = (bf16[3,256,256]{2,1,0:T(8,128)(2,1)S(1)}, bf16[3,256,256]{2,1,0:T(8,128)(2,1)S(1)}, u32[]{:S(2)}, u32[]{:S(2)}) collective-permute-start(bf16[3,256,256]{2,1,0:T(8,128)(2,1)S(1)} %get-tuple-element.48), channel_id=1, source_target_pairs={{0,2},{2,0},{5,7},{7,5},{8,10},{10,8},{13,15},{15,13},{16,18},{18,... | collective-permute-start | bytes 1179656 | tf_op jit(solution)/shard_map/ppermute | solution.py:227
  76.2 10.5 %collective-permute-start.11 = (f32[256,512]{1,0:T(8,128)S(1)}, f32[256,512]{1,0:T(8,128)S(1)}, u32[]{:S(2)}, u32[]{:S(2)}) collective-permute-start(f32[256,512]{1,0:T(8,128)S(1)} %get-tuple-element.46), channel_id=1, source_target_pairs={{0,5},{2,7},{5,0},{7,2},{8,13},{10,15},{13,8},{15,10},{16,21},{18,... | collective-permute-start | bytes 1572872 | tf_op jit(solution)/shard_map/ppermute | solution.py:227
  78.2 10.5 %collective-permute-start.14 = (f32[256,512]{1,0:T(8,128)S(1)}, f32[256,512]{1,0:T(8,128)S(1)}, u32[]{:S(2)}, u32[]{:S(2)}) collective-permute-start(f32[256,512]{1,0:T(8,128)S(1)} %get-tuple-element.42), channel_id=1, source_target_pairs={{0,9},{2,11},{4,13},{6,15},{8,17},{9,0},{10,19},{11,2},{12,21},{13... | collective-permute-start | bytes 1572872 | tf_op jit(solution)/shard_map/ppermute | solution.py:227
  80.8 8.7 %collective-permute-start.13 = (bf16[256,512]{1,0:T(8,128)(2,1)S(1)}, bf16[256,512]{1,0:T(8,128)(2,1)S(1)}, u32[]{:S(2)}, u32[]{:S(2)}) collective-permute-start(bf16[256,512]{1,0:T(8,128)(2,1)S(1)} %get-tuple-element.50), channel_id=1, source_target_pairs={{0,5},{2,7},{5,0},{7,2},{8,13},{10,15},{13,8},{15,10},{16,21},{18,... | collective-permute-start | bytes 786440 | tf_op jit(solution)/shard_map/ppermute | solution.py:227
  83.2 6.3 %collective-permute-start.15 = (bf16[256,512]{1,0:T(8,128)(2,1)S(1)}, bf16[256,512]{1,0:T(8,128)(2,1)S(1)}, u32[]{:S(2)}, u32[]{:S(2)}) collective-permute-start(bf16[256,512]{1,0:T(8,128)(2,1)S(1)} %get-tuple-element.51), channel_id=1, source_target_pairs={{0,9},{2,11},{8,17},{10,19},{13,4},{15,6},{16,25},{18,27},{21,12},... | collective-permute-start | bytes 786440 | tf_op jit(solution)/shard_map/ppermute | solution.py:227
  90.3 2.4 %collective-permute-start.16 = (f32[3,128,512]{2,1,0:T(8,128)S(1)}, f32[3,128,512]{2,1,0:T(8,128)S(1)}, u32[]{:S(2)}, u32[]{:S(2)}) collective-permute-start(f32[3,128,512]{2,1,0:T(8,128)S(1)} %get-tuple-element.53), channel_id=1, source_target_pairs={{0,1},{1,0},{2,3},{3,2},{4,5},{5,4},{6,7},{7,6},{8,9},{9,8},{10,11... | collective-permute-start | bytes 2359304 | tf_op jit(solution)/shard_map/ppermute | solution.py:227

commit v10 on v9

--- a/solution.py
+++ b/solution.py
@@ -102,13 +102,14 @@
     send_ref[...] = keep_ref[1 - pos_ref[0]] + got_ref[1 - pos_ref[0]]
 
 
-def put_quarters(x, source, keep, send):
+def put_quarters(x, source, scale, keep, send):
     half = keep.shape[-1]
+    scale = scale[:, :half]
     for out, near in ((keep, x), (send, 1 - x)):
         for index, (row, col) in enumerate(((near, near), (near, 1 - near), (1 - near, near))):
             rows = pl.ds(pl.multiple_of(row * half, half), half)
             cols = pl.ds(pl.multiple_of(col * half, half), half)
-            out[index] = source[rows, cols].astype(out.dtype)
+            out[index] = (source[rows, cols] * scale).astype(out.dtype)
 
 
 def fetched(source, parts, sems):
@@ -128,8 +129,7 @@
         part = dot(turned_ref[:, rows], w)
         acc[...] = part if k == 0 else acc[...] + part
     listed = jnp.where(pos_ref[2] == 0, stat_ref[3:4, :], wstat_ref[3:4, :])
-    acc[...] *= listed * (1.0 / pos_ref[4].astype(F32))
-    put_quarters(pos_ref[0], acc, keep_ref, send_ref)
+    put_quarters(pos_ref[0], acc, listed * (1.0 / pos_ref[4].astype(F32)), keep_ref, send_ref)
 
 
 def near_kernel(pos_ref, turned_ref, y_ref, w_ref, stat_ref, ystat_ref, wstat_ref, keep_b, send_b, keep_d, send_d,
@@ -144,10 +144,8 @@
             acc_d[...] = part_d if k == 0 else acc_d[...] + part_d
         first = pos_ref[2] == 0
         share = 1.0 / pos_ref[4].astype(F32)
-        acc_b[...] *= jnp.where(first, stat_ref[2:3, :], ystat_ref[2:3, :]) * share
-        acc_d[...] *= jnp.where(first, ystat_ref[2:3, :], wstat_ref[2:3, :]) * share
-        put_quarters(pos_ref[0], acc_b, keep_b, send_b)
-        put_quarters(pos_ref[0], acc_d, keep_d, send_d)
+        put_quarters(pos_ref[0], acc_b, jnp.where(first, stat_ref[2:3, :], ystat_ref[2:3, :]) * share, keep_b, send_b)
+        put_quarters(pos_ref[0], acc_d, jnp.where(first, ystat_ref[2:3, :], wstat_ref[2:3, :]) * share, keep_d, send_d)
 
 
 def add_halves(x, keep, got, rows_out, cols_out):
@@ -304,6 +302,7 @@
     from_y_b = send(to_y_b, y_cross)
     got_d, to_y_b = lax.optimization_barrier((got_d, to_y_b))
     to_y_d, to_z_d = near_strips("cross_strips", CROSS, keep_d, got_d)
+    to_z_d, from_z_c = lax.optimization_barrier((to_z_d, from_z_c))
     from_y_d, from_z_d = send(to_y_d, y_cross), send(to_z_d, z_cross_active)
 
     mine, sib = call(combine_kernel, "combine", (), [SMEM] + [VMEM] * 6, [VMEM] * 2, [shape(3, strip, width)] * 2)(

time: 95.5 us -> 94.9 us (level)
  starting transfers between devices: 33.8 us -> 32.8 us
where the time goes in v10:
time: 94.9 us; the launch traced here: 94.4 us
  starting transfers between devices  32.8 us (35%)
  waiting for transfers between devices  32.2 us (34%)
  Pallas kernels  23.3 us (25%)
  local copies, waits for them, and re-layouts  4.46 us (5%)
  between operations  1.49 us (2%)
    ppermute x17, starting transfers between devices, send(): return lax.ppermute(value, AXES, pairs)  32.8 us
    ppermute x17, waiting for transfers between devices, send(): return lax.ppermute(value, AXES, pairs)  32.2 us
    pallas_call x1, Pallas kernels, body(): call(near_kernel, 'near_tiles', (), [SMEM, VMEM, anywhere] + [VMEM] * 4,...  6.82 us
    pallas_call x1, Pallas kernels, body(): call(far_kernel, 'far_tile', (), [SMEM, VMEM, anywhere, VMEM, VMEM], [VME...  4.61 us
    unnamed x6, local copies, waits for them, and re-layouts  4.37 us
    pallas_call x1, Pallas kernels, body(): call(own_kernel, 'own_tile', (steps,), [SMEM, wide, whole(4, width)], [fl...  4.3 us
  transfers between devices with their start and end apart: 17, of which 10 were waited for; matrix products, arithmetic and copies ran while one was open for 0% of the time, Pallas kernels for 22%

profile of v10, /device:TPU:0, one launch (start us, length us, event | category | flops | bytes accessed | tf_op | source)
XLA Modules:
  0.0 94.4 jit_solution(5732039100378119903)
XLA Ops:
  0.6 1.3 %collective-permute-start.4 = (bf16[4096,512]{1,0:T(8,128)(2,1)}, bf16[4096,512]{1,0:T(8,128)(2,1)}, u32[]{:S(2)}, u32[]{:S(2)}) collective-permute-start(bf16[4096,512]{1,0:T(8,128)(2,1)} %x_ref.1), channel_id=1, source_target_pairs={{1,9},{3,11},{5,13},{7,15},{8,0},{9,17},{10,2},{11,19},{12,4},{13,... | collective-permute-start | bytes 12582920 | tf_op jit(solution)/shard_map/ppermute | solution.py:225
  1.9 1.3 %collective-permute-start.7 = (bf16[4096,512]{1,0:T(8,128)(2,1)}, bf16[4096,512]{1,0:T(8,128)(2,1)}, u32[]{:S(2)}, u32[]{:S(2)}) collective-permute-start(bf16[4096,512]{1,0:T(8,128)(2,1)} %x_ref.1), channel_id=1, source_target_pairs={{1,5},{3,7},{4,0},{6,2},{9,13},{11,15},{12,8},{14,10},{17,21},{19,... | collective-permute-start | bytes 12582920 | tf_op jit(solution)/shard_map/ppermute | solution.py:225
  3.2 0.0 copy-start
  3.2 2.2 %copy-done = bf16[4096,512]{1,0:T(8,128)(2,1)S(1)} copy-done((bf16[4096,512]{1,0:T(8,128)(2,1)S(1)}, bf16[4096,512]{1,0:T(8,128)(2,1)}, u32[]{:S(2)}) %copy-start) | copy-done | bytes 4194328
  5.4 1.9 %local_stats.1.own_ref = f32[2,512]{1,0:T(2,128)S(1)} custom-call(bf16[4096,512]{1,0:T(8,128)(2,1)S(1)} %copy-done), custom_call_target="tpu_custom_call" | custom-call | flops 10485760 | bytes 4194304 | tf_op jit(solution)/shard_map/local_stats/pallas_call | solution.py:258
  7.3 9.1 %collective-permute-start = (f32[2,512]{1,0:T(2,128)S(1)}, f32[2,512]{1,0:T(2,128)S(1)}, u32[]{:S(2)}, u32[]{:S(2)}) collective-permute-start(f32[2,512]{1,0:T(2,128)S(1)} %local_stats.1.own_ref), channel_id=1, source_target_pairs={{0,1},{1,0},{2,3},{3,2},{4,5},{5,4},{6,7},{7,6},{8,9},{9,8},{10,11... | collective-permute-start | bytes 12296 | tf_op jit(solution)/shard_map/ppermute | solution.py:225
  16.4 1.5 %collective-permute-start.1 = (f32[2,512]{1,0:T(2,128)S(1)}, f32[2,512]{1,0:T(2,128)S(1)}, u32[]{:S(2)}, u32[]{:S(2)}) collective-permute-start(f32[2,512]{1,0:T(2,128)S(1)} %local_stats.1.own_ref), channel_id=1, source_target_pairs={{0,2},{1,3},{2,0},{3,1},{4,6},{5,7},{6,4},{7,5},{8,10},{9,11},{10,... | collective-permute-start | bytes 12296 | tf_op jit(solution)/shard_map/ppermute | solution.py:225
  17.9 0.0 collective-permute-start.2
  18.5 0.1 stack.23.pos_ref
  18.6 0.0 collective-permute-done.sib_ref
  18.6 1.4 %collective-permute-done.1.far_ref = f32[2,512]{1,0:T(2,128)S(1)} collective-permute-done((f32[2,512]{1,0:T(2,128)S(1)}, f32[2,512]{1,0:T(2,128)S(1)}, u32[]{:S(2)}, u32[]{:S(2)}) %collective-permute-start.1) | collective-permute-done | bytes 4128 | tf_op jit(solution)/shard_map/ppermute | solution.py:225
  20.0 0.9 collective-permute-done.2.cross_ref
  20.9 0.6 stats.1.stat_ref
  21.5 0.0 copy-start.1
  21.5 2.2 %copy-done.1 = bf16[4096,512]{1,0:T(8,128)(2,1)S(1)} copy-done((bf16[4096,512]{1,0:T(8,128)(2,1)S(1)}, bf16[4096,512]{1,0:T(8,128)(2,1)}, u32[]{:S(2)}) %copy-start.1) | copy-done | bytes 4194328
  23.7 4.3 %own_tile.1 = (bf16[512,4096]{1,0:T(8,128)(2,1)S(1)}, f32[2,128,512]{2,1,0:T(8,128)S(1)}, f32[2,128,512]{2,1,0:T(8,128)S(1)}) custom-call(s32[5]{0:T(128)S(1)} %stack.23.pos_ref, bf16[4096,512]{1,0:T(8,128)(2,1)S(1)} %copy-done.1, f32[4,512]{1,0:T(4,128)S(1)} %stats.1.stat_ref), custom_call_target="tpu_custom_call" | custom-call | flops 2147483648 | bytes 8388608 | tf_op jit(solution)/shard_map/own_tile/pallas_call | solution.py:265
  28.0 0.3 collective-permute-start.3
  28.2 1.7 %collective-permute-done.3.got_ref = f32[2,128,512]{2,1,0:T(8,128)S(1)} collective-permute-done((f32[2,128,512]{2,1,0:T(8,128)S(1)}, f32[2,128,512]{2,1,0:T(8,128)S(1)}, u32[]{:S(2)}, u32[]{:S(2)}) %collective-permute-start.3) | collective-permute-done | bytes 524320 | tf_op jit(solution)/shard_map/ppermute | solution.py:225
  30.0 0.6 own_tile_strips.1
  30.6 0.6 collective-permute-start.6
  31.2 1.9 %collective-permute-start.5 = (f32[4,512]{1,0:T(4,128)S(1)}, f32[4,512]{1,0:T(4,128)S(1)}, u32[]{:S(2)}, u32[]{:S(2)}) collective-permute-start(f32[4,512]{1,0:T(4,128)S(1)} %stats.1.stat_ref), channel_id=1, source_target_pairs={{0,9},{2,11},{4,13},{6,15},{8,17},{9,0},{10,19},{11,2},{12,21},{13... | collective-permute-start | bytes 24584 | tf_op jit(solution)/shard_map/ppermute | solution.py:225
  33.1 1.9 %collective-permute-start.8 = (f32[4,512]{1,0:T(4,128)S(1)}, f32[4,512]{1,0:T(4,128)S(1)}, u32[]{:S(2)}, u32[]{:S(2)}) collective-permute-start(f32[4,512]{1,0:T(4,128)S(1)} %stats.1.stat_ref), channel_id=1, source_target_pairs={{0,5},{2,7},{5,0},{7,2},{8,13},{10,15},{13,8},{15,10},{16,21},{18,... | collective-permute-start | bytes 24584 | tf_op jit(solution)/shard_map/ppermute | solution.py:225
  35.1 1.3 %collective-permute-done.5.wstat_ref = f32[4,512]{1,0:T(4,128)S(1)} collective-permute-done((f32[4,512]{1,0:T(4,128)S(1)}, f32[4,512]{1,0:T(4,128)S(1)}, u32[]{:S(2)}, u32[]{:S(2)}) %collective-permute-start.5) | collective-permute-done | bytes 8224 | tf_op jit(solution)/shard_map/ppermute | solution.py:225
  36.3 16.1 %collective-permute-done.4.w_ref = bf16[4096,512]{1,0:T(8,128)(2,1)} collective-permute-done((bf16[4096,512]{1,0:T(8,128)(2,1)}, bf16[4096,512]{1,0:T(8,128)(2,1)}, u32[]{:S(2)}, u32[]{:S(2)}) %collective-permute-start.4) | collective-permute-done | bytes 4194336 | tf_op jit(solution)/shard_map/ppermute | solution.py:225
  52.4 4.6 %far_tile.1 = (f32[3,256,256]{2,1,0:T(8,128)S(1)}, bf16[3,256,256]{2,1,0:T(8,128)(2,1)S(1)}, bf16[4096,512]{1,0:T(8,128)(2,1)S(1)}) custom-call(s32[5]{0:T(128)S(1)} %stack.23.pos_ref, bf16[512,4096]{1,0:T(8,128)(2,1)S(1)} %get-tuple-element.33.turned_ref, bf16[4096,512]{1,0:T(8,128)(2,1)} %collective-permute-done.4.w_ref, f32[4,512]{1,0:T(4,128)S(1)} %stats.1.stat_ref, ...), custom_call_target="tpu_custom_call" | custom-call | flops 2147483648 | bytes 12582912 | tf_op jit(solution)/shard_map/far_tile/pallas_call | solution.py:278
  57.1 0.0 collective-permute-done.6.diag_got
  57.1 2.0 %collective-permute-start.10 = (bf16[3,256,256]{2,1,0:T(8,128)(2,1)S(1)}, bf16[3,256,256]{2,1,0:T(8,128)(2,1)S(1)}, u32[]{:S(2)}, u32[]{:S(2)}) collective-permute-start(bf16[3,256,256]{2,1,0:T(8,128)(2,1)S(1)} %get-tuple-element.42), channel_id=1, source_target_pairs={{0,2},{1,3},{2,0},{3,1},{4,6},{5,7},{6,4},{7,5},{8,10},{9,11},{10,... | collective-permute-start | bytes 1179656 | tf_op jit(solution)/shard_map/ppermute | solution.py:225
  59.1 0.0 collective-permute-done.8.ystat_ref
  59.1 6.8 %near_tiles.1 = (f32[3,256,256]{2,1,0:T(8,128)S(1)}, bf16[3,256,256]{2,1,0:T(8,128)(2,1)S(1)}, f32[3,256,256]{2,1,0:T(8,128)S(1)}, bf16[3,256,256]{2,1,0:T(8,128)(2,1)S(1)}) custom-call(s32[5]{0:T(128)S(1)} %stack.23.pos_ref, bf16[512,4096]{1,0:T(8,128)(2,1)S(1)} %get-tuple-element.33.turned_ref, bf16[4096,512]{1,0:T(8,128)(2,1)} %collective-permute-done.7.y_ref, ...), custom_call_target="tpu_custom_call" | custom-call | flops 4294967296 | bytes 12582912 | tf_op jit(solution)/shard_map/near_tiles/pallas_call | solution.py:285
  65.9 2.0 %collective-permute-start.9 = (bf16[3,256,256]{2,1,0:T(8,128)(2,1)S(1)}, bf16[3,256,256]{2,1,0:T(8,128)(2,1)S(1)}, u32[]{:S(2)}, u32[]{:S(2)}) collective-permute-start(bf16[3,256,256]{2,1,0:T(8,128)(2,1)S(1)} %get-tuple-element.39), channel_id=1, source_target_pairs={{0,2},{2,0},{5,7},{7,5},{8,10},{10,8},{13,15},{15,13},{16,18},{18,... | collective-permute-start | bytes 1179656 | tf_op jit(solution)/shard_map/ppermute | solution.py:225
  67.9 0.7 far_strips.1
  68.7 1.9 %collective-permute-start.14 = (f32[256,512]{1,0:T(8,128)S(1)}, f32[256,512]{1,0:T(8,128)S(1)}, u32[]{:S(2)}, u32[]{:S(2)}) collective-permute-start(f32[256,512]{1,0:T(8,128)S(1)} %get-tuple-element.44), channel_id=1, source_target_pairs={{0,9},{2,11},{4,13},{6,15},{8,17},{9,0},{10,19},{11,2},{12,21},{13... | collective-permute-start | bytes 1572872 | tf_op jit(solution)/shard_map/ppermute | solution.py:225
  70.6 3.8 %collective-permute-start.12 = (bf16[3,256,256]{2,1,0:T(8,128)(2,1)S(1)}, bf16[3,256,256]{2,1,0:T(8,128)(2,1)S(1)}, u32[]{:S(2)}, u32[]{:S(2)}) collective-permute-start(bf16[3,256,256]{2,1,0:T(8,128)(2,1)S(1)} %get-tuple-element.50), channel_id=1, source_target_pairs={{0,2},{2,0},{5,7},{7,5},{8,10},{10,8},{13,15},{15,13},{16,18},{18,... | collective-permute-start | bytes 1179656 | tf_op jit(solution)/shard_map/ppermute | solution.py:225
  74.4 1.1 %collective-permute-done.9.got = bf16[3,256,256]{2,1,0:T(8,128)(2,1)S(1)} collective-permute-done((bf16[3,256,256]{2,1,0:T(8,128)(2,1)S(1)}, bf16[3,256,256]{2,1,0:T(8,128)(2,1)S(1)}, u32[]{:S(2)}, u32[]{:S(2)}) %collective-permute-start.9) | collective-permute-done | bytes 393248 | tf_op jit(solution)/shard_map/ppermute | solution.py:225
  75.6 0.7 near_strips.1
  76.3 1.9 %collective-permute-start.11 = (f32[256,512]{1,0:T(8,128)S(1)}, f32[256,512]{1,0:T(8,128)S(1)}, u32[]{:S(2)}, u32[]{:S(2)}) collective-permute-start(f32[256,512]{1,0:T(8,128)S(1)} %get-tuple-element.48), channel_id=1, source_target_pairs={{0,5},{2,7},{5,0},{7,2},{8,13},{10,15},{13,8},{15,10},{16,21},{18,... | collective-permute-start | bytes 1572872 | tf_op jit(solution)/shard_map/ppermute | solution.py:225
  78.2 2.0 %collective-permute-done.12.got = bf16[3,256,256]{2,1,0:T(8,128)(2,1)S(1)} collective-permute-done((bf16[3,256,256]{2,1,0:T(8,128)(2,1)S(1)}, bf16[3,256,256]{2,1,0:T(8,128)(2,1)S(1)}, u32[]{:S(2)}, u32[]{:S(2)}) %collective-permute-start.12) | collective-permute-done | bytes 393248 | tf_op jit(solution)/shard_map/ppermute | solution.py:225
  80.3 0.7 cross_strips.1
  81.0 1.9 %collective-permute-start.13 = (bf16[256,512]{1,0:T(8,128)(2,1)S(1)}, bf16[256,512]{1,0:T(8,128)(2,1)S(1)}, u32[]{:S(2)}, u32[]{:S(2)}) collective-permute-start(bf16[256,512]{1,0:T(8,128)(2,1)S(1)} %get-tuple-element.52), channel_id=1, source_target_pairs={{0,5},{2,7},{5,0},{7,2},{8,13},{10,15},{13,8},{15,10},{16,21},{18,... | collective-permute-start | bytes 786440 | tf_op jit(solution)/shard_map/ppermute | solution.py:225
  82.9 0.0 collective-permute-done.14.from_z_c
  82.9 1.3 %collective-permute-start.15 = (bf16[256,512]{1,0:T(8,128)(2,1)S(1)}, bf16[256,512]{1,0:T(8,128)(2,1)S(1)}, u32[]{:S(2)}, u32[]{:S(2)}) collective-permute-start(bf16[256,512]{1,0:T(8,128)(2,1)S(1)} %get-tuple-element.55), channel_id=1, source_target_pairs={{0,9},{2,11},{8,17},{10,19},{13,4},{15,6},{16,25},{18,27},{21,12},... | collective-permute-start | bytes 786440 | tf_op jit(solution)/shard_map/ppermute | solution.py:225
  84.2 2.6 %collective-permute-done.11.from_y_b = f32[256,512]{1,0:T(8,128)S(1)} collective-permute-done((f32[256,512]{1,0:T(8,128)S(1)}, f32[256,512]{1,0:T(8,128)S(1)}, u32[]{:S(2)}, u32[]{:S(2)}) %collective-permute-start.11) | collective-permute-done | bytes 524320 | tf_op jit(solution)/shard_map/ppermute | solution.py:225
  86.8 2.8 %collective-permute-done.13.from_y_d = bf16[256,512]{1,0:T(8,128)(2,1)S(1)} collective-permute-done((bf16[256,512]{1,0:T(8,128)(2,1)S(1)}, bf16[256,512]{1,0:T(8,128)(2,1)S(1)}, u32[]{:S(2)}, u32[]{:S(2)}) %collective-permute-start.13) | collective-permute-done | bytes 262176 | tf_op jit(solution)/shard_map/ppermute | solution.py:225
  89.6 0.0 collective-permute-done.15.from_z_d
  89.6 0.7 combine.1
  90.3 0.1 collective-permute-start.16
  90.4 2.3 %collective-permute-done.16.sib = f32[3,128,512]{2,1,0:T(8,128)S(1)} collective-permute-done((f32[3,128,512]{2,1,0:T(8,128)S(1)}, f32[3,128,512]{2,1,0:T(8,128)S(1)}, u32[]{:S(2)}, u32[]{:S(2)}) %collective-permute-start.16) | collective-permute-done | bytes 786464 | tf_op jit(solution)/shard_map/ppermute | solution.py:225
  92.7 1.7 %finish.1 = (bf16[1,3,128,512]{3,2,1,0:T(8,128)(2,1)}, bf16[1,2,128,512]{3,2,1,0:T(8,128)(2,1)}) custom-call(s32[5]{0:T(128)S(1)} %stack.23.pos_ref, s32[1,3]{1,0:T(1,128)S(1)} %copy-done.2, f32[128,512]{1,0:T(8,128)S(1)} %get-tuple-element.32.diag_mine, f32[128,512]{1,0:T(8,128)S(1)} %collective-permute-done.6.diag_got, ...), custom_call_target="tpu_custom_call" | custom-call | tf_op jit(solution)/shard_map/finish/pallas_call | solution.py:310
  (4 shorter events, 0.0 us)
Async XLA Ops:
  0.6 51.8 %collective-permute-start.4 = (bf16[4096,512]{1,0:T(8,128)(2,1)}, bf16[4096,512]{1,0:T(8,128)(2,1)}, u32[]{:S(2)}, u32[]{:S(2)}) collective-permute-start(bf16[4096,512]{1,0:T(8,128)(2,1)} %x_ref.1), channel_id=1, source_target_pairs={{1,9},{3,11},{5,13},{7,15},{8,0},{9,17},{10,2},{11,19},{12,4},{13,... | collective-permute-start | bytes 12582920 | tf_op jit(solution)/shard_map/ppermute | solution.py:225
  1.9 57.1 %collective-permute-start.7 = (bf16[4096,512]{1,0:T(8,128)(2,1)}, bf16[4096,512]{1,0:T(8,128)(2,1)}, u32[]{:S(2)}, u32[]{:S(2)}) collective-permute-start(bf16[4096,512]{1,0:T(8,128)(2,1)} %x_ref.1), channel_id=1, source_target_pairs={{1,5},{3,7},{4,0},{6,2},{9,13},{11,15},{12,8},{14,10},{17,21},{19,... | collective-permute-start | bytes 12582920 | tf_op jit(solution)/shard_map/ppermute | solution.py:225
  3.2 2.2 %copy-start = (bf16[4096,512]{1,0:T(8,128)(2,1)S(1)}, bf16[4096,512]{1,0:T(8,128)(2,1)}, u32[]{:S(2)}) copy-start(bf16[4096,512]{1,0:T(8,128)(2,1)} %x_ref.1) | copy-start | bytes 12582916
  5.4 15.5 %copy-start.2 = (s32[1,3]{1,0:T(1,128)S(1)}, s32[1,3]{1,0:T(1,128)}, u32[]{:S(2)}) copy-start(s32[1,3]{1,0:T(1,128)} %offsets_ref.3) | copy-start | bytes 40
  7.3 11.3 %collective-permute-start = (f32[2,512]{1,0:T(2,128)S(1)}, f32[2,512]{1,0:T(2,128)S(1)}, u32[]{:S(2)}, u32[]{:S(2)}) collective-permute-start(f32[2,512]{1,0:T(2,128)S(1)} %local_stats.1.own_ref), channel_id=1, source_target_pairs={{0,1},{1,0},{2,3},{3,2},{4,5},{5,4},{6,7},{7,6},{8,9},{9,8},{10,11... | collective-permute-start | bytes 12296 | tf_op jit(solution)/shard_map/ppermute | solution.py:225
  16.4 3.6 %collective-permute-start.1 = (f32[2,512]{1,0:T(2,128)S(1)}, f32[2,512]{1,0:T(2,128)S(1)}, u32[]{:S(2)}, u32[]{:S(2)}) collective-permute-start(f32[2,512]{1,0:T(2,128)S(1)} %local_stats.1.own_ref), channel_id=1, source_target_pairs={{0,2},{1,3},{2,0},{3,1},{4,6},{5,7},{6,4},{7,5},{8,10},{9,11},{10,... | collective-permute-start | bytes 12296 | tf_op jit(solution)/shard_map/ppermute | solution.py:225
  17.9 3.1 %collective-permute-start.2 = (f32[2,512]{1,0:T(2,128)S(1)}, f32[2,512]{1,0:T(2,128)S(1)}, u32[]{:S(2)}, u32[]{:S(2)}) collective-permute-start(f32[2,512]{1,0:T(2,128)S(1)} %local_stats.1.own_ref), channel_id=1, source_target_pairs={{0,3},{1,2},{2,1},{3,0},{4,7},{5,6},{6,5},{7,4},{8,11},{9,10},{10,... | collective-permute-start | bytes 12296 | tf_op jit(solution)/shard_map/ppermute | solution.py:225
  21.5 2.2 %copy-start.1 = (bf16[4096,512]{1,0:T(8,128)(2,1)S(1)}, bf16[4096,512]{1,0:T(8,128)(2,1)}, u32[]{:S(2)}) copy-start(bf16[4096,512]{1,0:T(8,128)(2,1)} %x_ref.1) | copy-start | bytes 12582916
  28.0 2.0 %collective-permute-start.3 = (f32[2,128,512]{2,1,0:T(8,128)S(1)}, f32[2,128,512]{2,1,0:T(8,128)S(1)}, u32[]{:S(2)}, u32[]{:S(2)}) collective-permute-start(f32[2,128,512]{2,1,0:T(8,128)S(1)} %get-tuple-element.31), channel_id=1, source_target_pairs={{0,1},{1,0},{2,3},{3,2},{4,5},{5,4},{6,7},{7,6},{8,9},{9,8},{10,11... | collective-permute-start | bytes 1572872 | tf_op jit(solution)/shard_map/ppermute | solution.py:225
  30.6 26.5 %collective-permute-start.6 = (f32[128,512]{1,0:T(8,128)S(1)}, f32[128,512]{1,0:T(8,128)S(1)}, u32[]{:S(2)}, u32[]{:S(2)}) collective-permute-start(f32[128,512]{1,0:T(8,128)S(1)} %get-tuple-element.35), channel_id=1, source_target_pairs={{0,2},{1,3},{2,0},{3,1},{4,6},{5,7},{6,4},{7,5},{8,10},{9,11},{10,... | collective-permute-start | bytes 786440 | tf_op jit(solution)/shard_map/ppermute | solution.py:225
  31.2 5.1 %collective-permute-start.5 = (f32[4,512]{1,0:T(4,128)S(1)}, f32[4,512]{1,0:T(4,128)S(1)}, u32[]{:S(2)}, u32[]{:S(2)}) collective-permute-start(f32[4,512]{1,0:T(4,128)S(1)} %stats.1.stat_ref), channel_id=1, source_target_pairs={{0,9},{2,11},{4,13},{6,15},{8,17},{9,0},{10,19},{11,2},{12,21},{13... | collective-permute-start | bytes 24584 | tf_op jit(solution)/shard_map/ppermute | solution.py:225
  33.1 25.9 %collective-permute-start.8 = (f32[4,512]{1,0:T(4,128)S(1)}, f32[4,512]{1,0:T(4,128)S(1)}, u32[]{:S(2)}, u32[]{:S(2)}) collective-permute-start(f32[4,512]{1,0:T(4,128)S(1)} %stats.1.stat_ref), channel_id=1, source_target_pairs={{0,5},{2,7},{5,0},{7,2},{8,13},{10,15},{13,8},{15,10},{16,21},{18,... | collective-permute-start | bytes 24584 | tf_op jit(solution)/shard_map/ppermute | solution.py:225
  57.1 10.8 %collective-permute-start.10 = (bf16[3,256,256]{2,1,0:T(8,128)(2,1)S(1)}, bf16[3,256,256]{2,1,0:T(8,128)(2,1)S(1)}, u32[]{:S(2)}, u32[]{:S(2)}) collective-permute-start(bf16[3,256,256]{2,1,0:T(8,128)(2,1)S(1)} %get-tuple-element.42), channel_id=1, source_target_pairs={{0,2},{1,3},{2,0},{3,1},{4,6},{5,7},{6,4},{7,5},{8,10},{9,11},{10,... | collective-permute-start | bytes 1179656 | tf_op jit(solution)/shard_map/ppermute | solution.py:225
  65.9 9.7 %collective-permute-start.9 = (bf16[3,256,256]{2,1,0:T(8,128)(2,1)S(1)}, bf16[3,256,256]{2,1,0:T(8,128)(2,1)S(1)}, u32[]{:S(2)}, u32[]{:S(2)}) collective-permute-start(bf16[3,256,256]{2,1,0:T(8,128)(2,1)S(1)} %get-tuple-element.39), channel_id=1, source_target_pairs={{0,2},{2,0},{5,7},{7,5},{8,10},{10,8},{13,15},{15,13},{16,18},{18,... | collective-permute-start | bytes 1179656 | tf_op jit(solution)/shard_map/ppermute | solution.py:225
  68.7 14.3 %collective-permute-start.14 = (f32[256,512]{1,0:T(8,128)S(1)}, f32[256,512]{1,0:T(8,128)S(1)}, u32[]{:S(2)}, u32[]{:S(2)}) collective-permute-start(f32[256,512]{1,0:T(8,128)S(1)} %get-tuple-element.44), channel_id=1, source_target_pairs={{0,9},{2,11},{4,13},{6,15},{8,17},{9,0},{10,19},{11,2},{12,21},{13... | collective-permute-start | bytes 1572872 | tf_op jit(solution)/shard_map/ppermute | solution.py:225
  70.6 9.7 %collective-permute-start.12 = (bf16[3,256,256]{2,1,0:T(8,128)(2,1)S(1)}, bf16[3,256,256]{2,1,0:T(8,128)(2,1)S(1)}, u32[]{:S(2)}, u32[]{:S(2)}) collective-permute-start(bf16[3,256,256]{2,1,0:T(8,128)(2,1)S(1)} %get-tuple-element.50), channel_id=1, source_target_pairs={{0,2},{2,0},{5,7},{7,5},{8,10},{10,8},{13,15},{15,13},{16,18},{18,... | collective-permute-start | bytes 1179656 | tf_op jit(solution)/shard_map/ppermute | solution.py:225
  76.3 10.5 %collective-permute-start.11 = (f32[256,512]{1,0:T(8,128)S(1)}, f32[256,512]{1,0:T(8,128)S(1)}, u32[]{:S(2)}, u32[]{:S(2)}) collective-permute-start(f32[256,512]{1,0:T(8,128)S(1)} %get-tuple-element.48), channel_id=1, source_target_pairs={{0,5},{2,7},{5,0},{7,2},{8,13},{10,15},{13,8},{15,10},{16,21},{18,... | collective-permute-start | bytes 1572872 | tf_op jit(solution)/shard_map/ppermute | solution.py:225
  81.0 8.6 %collective-permute-start.13 = (bf16[256,512]{1,0:T(8,128)(2,1)S(1)}, bf16[256,512]{1,0:T(8,128)(2,1)S(1)}, u32[]{:S(2)}, u32[]{:S(2)}) collective-permute-start(bf16[256,512]{1,0:T(8,128)(2,1)S(1)} %get-tuple-element.52), channel_id=1, source_target_pairs={{0,5},{2,7},{5,0},{7,2},{8,13},{10,15},{13,8},{15,10},{16,21},{18,... | collective-permute-start | bytes 786440 | tf_op jit(solution)/shard_map/ppermute | solution.py:225
  82.9 6.7 %collective-permute-start.15 = (bf16[256,512]{1,0:T(8,128)(2,1)S(1)}, bf16[256,512]{1,0:T(8,128)(2,1)S(1)}, u32[]{:S(2)}, u32[]{:S(2)}) collective-permute-start(bf16[256,512]{1,0:T(8,128)(2,1)S(1)} %get-tuple-element.55), channel_id=1, source_target_pairs={{0,9},{2,11},{8,17},{10,19},{13,4},{15,6},{16,25},{18,27},{21,12},... | collective-permute-start | bytes 786440 | tf_op jit(solution)/shard_map/ppermute | solution.py:225
  90.3 2.4 %collective-permute-start.16 = (f32[3,128,512]{2,1,0:T(8,128)S(1)}, f32[3,128,512]{2,1,0:T(8,128)S(1)}, u32[]{:S(2)}, u32[]{:S(2)}) collective-permute-start(f32[3,128,512]{2,1,0:T(8,128)S(1)} %get-tuple-element.57), channel_id=1, source_target_pairs={{0,1},{1,0},{2,3},{3,2},{4,5},{5,4},{6,7},{7,6},{8,9},{9,8},{10,11... | collective-permute-start | bytes 2359304 | tf_op jit(solution)/shard_map/ppermute | solution.py:225

commit v11 on v10

--- a/solution.py
+++ b/solution.py
@@ -132,20 +132,29 @@
     put_quarters(pos_ref[0], acc, listed * (1.0 / pos_ref[4].astype(F32)), keep_ref, send_ref)
 
 
-def near_kernel(pos_ref, turned_ref, y_ref, w_ref, stat_ref, ystat_ref, wstat_ref, keep_b, send_b, keep_d, send_d,
-                acc_b, acc_d, parts, sems):
+def near_kernel(pos_ref, turned_ref, y_ref, stat_ref, ystat_ref, keep_ref, send_ref, y_out, acc, parts, sems):
     @pl.when(pos_ref[1] == 1)
     def _():
         for k, (rows, wait) in enumerate(fetched(y_ref, parts, sems)):
             wait()
             y = standardized(parts[k], ystat_ref)
-            part_b, part_d = dot(turned_ref[:, rows], y), dot(y.T, w_ref[rows, :])
-            acc_b[...] = part_b if k == 0 else acc_b[...] + part_b
-            acc_d[...] = part_d if k == 0 else acc_d[...] + part_d
-        first = pos_ref[2] == 0
-        share = 1.0 / pos_ref[4].astype(F32)
-        put_quarters(pos_ref[0], acc_b, jnp.where(first, stat_ref[2:3, :], ystat_ref[2:3, :]) * share, keep_b, send_b)
-        put_quarters(pos_ref[0], acc_d, jnp.where(first, ystat_ref[2:3, :], wstat_ref[2:3, :]) * share, keep_d, send_d)
+            y_out[:, rows] = y.T
+            part = dot(turned_ref[:, rows], y)
+            acc[...] = part if k == 0 else acc[...] + part
+        listed = jnp.where(pos_ref[2] == 0, stat_ref[2:3, :], ystat_ref[2:3, :])
+        put_quarters(pos_ref[0], acc, listed * (1.0 / pos_ref[4].astype(F32)), keep_ref, send_ref)
+
+
+def cross_kernel(steps, pos_ref, y_ref, w_ref, ystat_ref, wstat_ref, keep_ref, send_ref, acc):
+    @pl.when(pos_ref[1] == 1)
+    def _():
+        size = w_ref.shape[0] // steps
+        for k in range(steps):
+            rows = slice(k * size, (k + 1) * size)
+            part = dot(y_ref[:, rows], w_ref[rows, :])
+            acc[...] = part if k == 0 else acc[...] + part
+        listed = jnp.where(pos_ref[2] == 0, ystat_ref[2:3, :], wstat_ref[2:3, :])
+        put_quarters(pos_ref[0], acc, listed * (1.0 / pos_ref[4].astype(F32)), keep_ref, send_ref)
 
 
 def add_halves(x, keep, got, rows_out, cols_out):
@@ -282,10 +291,14 @@
     send_c, diag_got = lax.optimization_barrier((send_c, diag_got))
     got_c = send(send_c, across)
 
-    keep_b, send_b, keep_d, send_d = call(
-        near_kernel, "near_tiles", (), [SMEM, VMEM, anywhere] + [VMEM] * 4, [VMEM] * 4, pair * 2, [sums] * 2 + parts,
-        2 * tile_flops, 3 * bytes_block)(pos, turned, y_raw, w, stat, y_stat, w_stat)
+    keep_b, send_b, y = call(
+        near_kernel, "near_tile", (), [SMEM, VMEM, anywhere, VMEM, VMEM], [VMEM] * 3,
+        pair + [shape(width, depth, dtype=BF16)], [sums] + parts, tile_flops, 3 * bytes_block)(
+        pos, turned, y_raw, stat, y_stat)
     got_b = send(send_b, across_active)
+    keep_d, send_d = call(
+        lambda *refs: cross_kernel(steps, *refs), "cross_tile", (), [SMEM] + [VMEM] * 4, [VMEM] * 2, pair, [sums],
+        tile_flops, 2 * bytes_block)(pos, y, w, y_stat, w_stat)
     send_d, got_c = lax.optimization_barrier((send_d, got_c))
     got_d = send(send_d, across_active)
 

time: 94.9 us -> 95.2 us (level)
    pallas_call x1 -> x2, Pallas kernels: 6.82 us -> 7.6 us  [the longest x1 4.64 us: body(): call(near_kernel, 'near_tile', (), [SMEM, VMEM, anywhere, VMEM, VMEM], [V...]
  transfers between devices with their start and end apart: 17 -> 17, of which waited for: 10 -> 8; matrix products, arithmetic and copies ran while one was open for 0% -> 0% of each run, Pallas kernels for 22% -> 23%
where the time goes in v11:
time: 95.2 us; the launch traced here: 94.2 us
  starting transfers between devices  32.8 us (34%)
  waiting for transfers between devices  31.3 us (33%)
  Pallas kernels  24.1 us (25%)
  local copies, waits for them, and re-layouts  4.46 us (5%)
  between operations  1.51 us (2%)
    ppermute x17, starting transfers between devices, send(): return lax.ppermute(value, AXES, pairs)  32.8 us
    ppermute x17, waiting for transfers between devices, send(): return lax.ppermute(value, AXES, pairs)  31.3 us
    pallas_call x1, Pallas kernels, body(): call(near_kernel, 'near_tile', (), [SMEM, VMEM, anywhere, VMEM, VMEM], [V...  4.64 us
    pallas_call x1, Pallas kernels, body(): call(far_kernel, 'far_tile', (), [SMEM, VMEM, anywhere, VMEM, VMEM], [VME...  4.59 us
    unnamed x6, local copies, waits for them, and re-layouts  4.37 us
    pallas_call x1, Pallas kernels, body(): call(own_kernel, 'own_tile', (steps,), [SMEM, wide, whole(4, width)], [fl...  4.31 us
    pallas_call x1, Pallas kernels, body(): call(lambda *refs: cross_kernel(steps, *refs), 'cross_tile', (), [SMEM] +...  2.96 us
  transfers between devices with their start and end apart: 17, of which 8 were waited for; matrix products, arithmetic and copies ran while one was open for 0% of the time, Pallas kernels for 23%

profile of v11, /device:TPU:0, one launch (start us, length us, event | category | flops | bytes accessed | tf_op | source)
XLA Modules:
  0.0 94.2 jit_solution(244252497523766245)
XLA Ops:
  0.6 1.3 %collective-permute-start.4 = (bf16[4096,512]{1,0:T(8,128)(2,1)}, bf16[4096,512]{1,0:T(8,128)(2,1)}, u32[]{:S(2)}, u32[]{:S(2)}) collective-permute-start(bf16[4096,512]{1,0:T(8,128)(2,1)} %x_ref.1), channel_id=1, source_target_pairs={{1,9},{3,11},{5,13},{7,15},{8,0},{9,17},{10,2},{11,19},{12,4},{13,... | collective-permute-start | bytes 12582920 | tf_op jit(solution)/shard_map/ppermute | solution.py:234
  1.9 1.3 %collective-permute-start.7 = (bf16[4096,512]{1,0:T(8,128)(2,1)}, bf16[4096,512]{1,0:T(8,128)(2,1)}, u32[]{:S(2)}, u32[]{:S(2)}) collective-permute-start(bf16[4096,512]{1,0:T(8,128)(2,1)} %x_ref.1), channel_id=1, source_target_pairs={{1,5},{3,7},{4,0},{6,2},{9,13},{11,15},{12,8},{14,10},{17,21},{19,... | collective-permute-start | bytes 12582920 | tf_op jit(solution)/shard_map/ppermute | solution.py:234
  3.2 0.0 copy-start
  3.2 2.2 %copy-done = bf16[4096,512]{1,0:T(8,128)(2,1)S(1)} copy-done((bf16[4096,512]{1,0:T(8,128)(2,1)S(1)}, bf16[4096,512]{1,0:T(8,128)(2,1)}, u32[]{:S(2)}) %copy-start) | copy-done | bytes 4194328
  5.4 1.9 %local_stats.1.own_ref = f32[2,512]{1,0:T(2,128)S(1)} custom-call(bf16[4096,512]{1,0:T(8,128)(2,1)S(1)} %copy-done), custom_call_target="tpu_custom_call" | custom-call | flops 10485760 | bytes 4194304 | tf_op jit(solution)/shard_map/local_stats/pallas_call | solution.py:267
  7.3 10.2 %collective-permute-start.2 = (f32[2,512]{1,0:T(2,128)S(1)}, f32[2,512]{1,0:T(2,128)S(1)}, u32[]{:S(2)}, u32[]{:S(2)}) collective-permute-start(f32[2,512]{1,0:T(2,128)S(1)} %local_stats.1.own_ref), channel_id=1, source_target_pairs={{0,3},{1,2},{2,1},{3,0},{4,7},{5,6},{6,5},{7,4},{8,11},{9,10},{10,... | collective-permute-start | bytes 12296 | tf_op jit(solution)/shard_map/ppermute | solution.py:234
  17.5 0.5 collective-permute-start.1
  18.7 0.1 stack.23.pos_ref.refs_0_
  18.7 0.0 collective-permute-done.2.cross_ref
  18.8 2.3 %collective-permute-done.1.far_ref = f32[2,512]{1,0:T(2,128)S(1)} collective-permute-done((f32[2,512]{1,0:T(2,128)S(1)}, f32[2,512]{1,0:T(2,128)S(1)}, u32[]{:S(2)}, u32[]{:S(2)}) %collective-permute-start.1) | collective-permute-done | bytes 4128 | tf_op jit(solution)/shard_map/ppermute | solution.py:234
  21.1 0.0 collective-permute-done.sib_ref
  21.1 0.6 stats.1.stat_ref
  21.7 0.0 copy-start.1
  21.7 2.2 %copy-done.1 = bf16[4096,512]{1,0:T(8,128)(2,1)S(1)} copy-done((bf16[4096,512]{1,0:T(8,128)(2,1)S(1)}, bf16[4096,512]{1,0:T(8,128)(2,1)}, u32[]{:S(2)}) %copy-start.1) | copy-done | bytes 4194328
  23.8 4.3 %own_tile.1 = (bf16[512,4096]{1,0:T(8,128)(2,1)S(1)}, f32[2,128,512]{2,1,0:T(8,128)S(1)}, f32[2,128,512]{2,1,0:T(8,128)S(1)}) custom-call(s32[5]{0:T(128)S(1)} %stack.23.pos_ref.refs_0_, bf16[4096,512]{1,0:T(8,128)(2,1)S(1)} %copy-done.1, f32[4,512]{1,0:T(4,128)S(1)} %stats.1.stat_ref), custom_call_target="tpu_custom_call" | custom-call | flops 2147483648 | bytes 8388608 | tf_op jit(solution)/shard_map/own_tile/pallas_call | solution.py:274
  28.2 0.1 collective-permute-start.3
  28.2 1.9 %collective-permute-done.3.got_ref = f32[2,128,512]{2,1,0:T(8,128)S(1)} collective-permute-done((f32[2,128,512]{2,1,0:T(8,128)S(1)}, f32[2,128,512]{2,1,0:T(8,128)S(1)}, u32[]{:S(2)}, u32[]{:S(2)}) %collective-permute-start.3) | collective-permute-done | bytes 524320 | tf_op jit(solution)/shard_map/ppermute | solution.py:234
  30.1 0.6 own_tile_strips.1
  30.8 0.6 collective-permute-start.6
  31.3 1.9 %collective-permute-start.5 = (f32[4,512]{1,0:T(4,128)S(1)}, f32[4,512]{1,0:T(4,128)S(1)}, u32[]{:S(2)}, u32[]{:S(2)}) collective-permute-start(f32[4,512]{1,0:T(4,128)S(1)} %stats.1.stat_ref), channel_id=1, source_target_pairs={{0,9},{2,11},{4,13},{6,15},{8,17},{9,0},{10,19},{11,2},{12,21},{13... | collective-permute-start | bytes 24584 | tf_op jit(solution)/shard_map/ppermute | solution.py:234
  33.3 1.9 %collective-permute-start.8 = (f32[4,512]{1,0:T(4,128)S(1)}, f32[4,512]{1,0:T(4,128)S(1)}, u32[]{:S(2)}, u32[]{:S(2)}) collective-permute-start(f32[4,512]{1,0:T(4,128)S(1)} %stats.1.stat_ref), channel_id=1, source_target_pairs={{0,5},{2,7},{5,0},{7,2},{8,13},{10,15},{13,8},{15,10},{16,21},{18,... | collective-permute-start | bytes 24584 | tf_op jit(solution)/shard_map/ppermute | solution.py:234
  35.2 1.3 %collective-permute-done.5.wstat_ref.refs_4_ = f32[4,512]{1,0:T(4,128)S(1)} collective-permute-done((f32[4,512]{1,0:T(4,128)S(1)}, f32[4,512]{1,0:T(4,128)S(1)}, u32[]{:S(2)}, u32[]{:S(2)}) %collective-permute-start.5) | collective-permute-done | bytes 8224 | tf_op jit(solution)/shard_map/ppermute | solution.py:234
  36.4 16.0 %collective-permute-done.4.w_ref = bf16[4096,512]{1,0:T(8,128)(2,1)} collective-permute-done((bf16[4096,512]{1,0:T(8,128)(2,1)}, bf16[4096,512]{1,0:T(8,128)(2,1)}, u32[]{:S(2)}, u32[]{:S(2)}) %collective-permute-start.4) | collective-permute-done | bytes 4194336 | tf_op jit(solution)/shard_map/ppermute | solution.py:234
  52.4 4.6 %far_tile.1 = (f32[3,256,256]{2,1,0:T(8,128)S(1)}, bf16[3,256,256]{2,1,0:T(8,128)(2,1)S(1)}, bf16[4096,512]{1,0:T(8,128)(2,1)S(1)}) custom-call(s32[5]{0:T(128)S(1)} %stack.23.pos_ref.refs_0_, bf16[512,4096]{1,0:T(8,128)(2,1)S(1)} %get-tuple-element.34.turned_ref, bf16[4096,512]{1,0:T(8,128)(2,1)} %collective-permute-done.4.w_ref, ...), custom_call_target="tpu_custom_call" | custom-call | flops 2147483648 | bytes 12582912 | tf_op jit(solution)/shard_map/far_tile/pallas_call | solution.py:287
  57.0 0.0 collective-permute-done.6.diag_got
  57.1 2.0 %collective-permute-start.10 = (bf16[3,256,256]{2,1,0:T(8,128)(2,1)S(1)}, bf16[3,256,256]{2,1,0:T(8,128)(2,1)S(1)}, u32[]{:S(2)}, u32[]{:S(2)}) collective-permute-start(bf16[3,256,256]{2,1,0:T(8,128)(2,1)S(1)} %get-tuple-element.44), channel_id=1, source_target_pairs={{0,2},{1,3},{2,0},{3,1},{4,6},{5,7},{6,4},{7,5},{8,10},{9,11},{10,... | collective-permute-start | bytes 1179656 | tf_op jit(solution)/shard_map/ppermute | solution.py:234
  59.1 0.0 collective-permute-done.7.y_ref
  59.1 4.6 %near_tile.1 = (f32[3,256,256]{2,1,0:T(8,128)S(1)}, bf16[3,256,256]{2,1,0:T(8,128)(2,1)S(1)}, bf16[512,4096]{1,0:T(8,128)(2,1)S(1)}) custom-call(s32[5]{0:T(128)S(1)} %stack.23.pos_ref.refs_0_, bf16[512,4096]{1,0:T(8,128)(2,1)S(1)} %get-tuple-element.34.turned_ref, bf16[4096,512]{1,0:T(8,128)(2,1)} %collective-permute-done.7.y_ref, ...), custom_call_target="tpu_custom_call" | custom-call | flops 2147483648 | bytes 12582912 | tf_op jit(solution)/shard_map/near_tile/pallas_call | solution.py:294
  63.7 2.0 %collective-permute-start.9 = (bf16[3,256,256]{2,1,0:T(8,128)(2,1)S(1)}, bf16[3,256,256]{2,1,0:T(8,128)(2,1)S(1)}, u32[]{:S(2)}, u32[]{:S(2)}) collective-permute-start(bf16[3,256,256]{2,1,0:T(8,128)(2,1)S(1)} %get-tuple-element.39), channel_id=1, source_target_pairs={{0,2},{2,0},{5,7},{7,5},{8,10},{10,8},{13,15},{15,13},{16,18},{18,... | collective-permute-start | bytes 1179656 | tf_op jit(solution)/shard_map/ppermute | solution.py:234
  65.7 3.0 %cross_tile.1 = (f32[3,256,256]{2,1,0:T(8,128)S(1)}, bf16[3,256,256]{2,1,0:T(8,128)(2,1)S(1)}) custom-call(s32[5]{0:T(128)S(1)} %stack.23.pos_ref.refs_0_, bf16[512,4096]{1,0:T(8,128)(2,1)S(1)} %get-tuple-element.41.refs_1_, bf16[4096,512]{1,0:T(8,128)(2,1)S(1)} %get-tuple-element.42.refs_2_, f32[4,512]{1,0:T(4,128)S(1)} %collective-permute-done.8.ystat_ref.refs_3_, ...), custom_call_target="tpu_custom_call" | custom-call | flops 2147483648 | bytes 8388608 | tf_op jit(solution)/shard_map/cross_tile/pallas_call | solution.py:299
  68.7 0.7 far_strips.1
  69.4 1.9 %collective-permute-start.14 = (f32[256,512]{1,0:T(8,128)S(1)}, f32[256,512]{1,0:T(8,128)S(1)}, u32[]{:S(2)}, u32[]{:S(2)}) collective-permute-start(f32[256,512]{1,0:T(8,128)S(1)} %get-tuple-element.46), channel_id=1, source_target_pairs={{0,9},{2,11},{4,13},{6,15},{8,17},{9,0},{10,19},{11,2},{12,21},{13... | collective-permute-start | bytes 1572872 | tf_op jit(solution)/shard_map/ppermute | solution.py:234
  71.4 3.8 %collective-permute-start.12 = (bf16[3,256,256]{2,1,0:T(8,128)(2,1)S(1)}, bf16[3,256,256]{2,1,0:T(8,128)(2,1)S(1)}, u32[]{:S(2)}, u32[]{:S(2)}) collective-permute-start(bf16[3,256,256]{2,1,0:T(8,128)(2,1)S(1)} %get-tuple-element.52), channel_id=1, source_target_pairs={{0,2},{2,0},{5,7},{7,5},{8,10},{10,8},{13,15},{15,13},{16,18},{18,... | collective-permute-start | bytes 1179656 | tf_op jit(solution)/shard_map/ppermute | solution.py:234
  75.2 0.0 collective-permute-done.9.got
  75.2 0.7 near_strips.1
  76.0 1.9 %collective-permute-start.11 = (f32[256,512]{1,0:T(8,128)S(1)}, f32[256,512]{1,0:T(8,128)S(1)}, u32[]{:S(2)}, u32[]{:S(2)}) collective-permute-start(f32[256,512]{1,0:T(8,128)S(1)} %get-tuple-element.50), channel_id=1, source_target_pairs={{0,5},{2,7},{5,0},{7,2},{8,13},{10,15},{13,8},{15,10},{16,21},{18,... | collective-permute-start | bytes 1572872 | tf_op jit(solution)/shard_map/ppermute | solution.py:234
  77.9 3.1 %collective-permute-done.12.got = bf16[3,256,256]{2,1,0:T(8,128)(2,1)S(1)} collective-permute-done((bf16[3,256,256]{2,1,0:T(8,128)(2,1)S(1)}, bf16[3,256,256]{2,1,0:T(8,128)(2,1)S(1)}, u32[]{:S(2)}, u32[]{:S(2)}) %collective-permute-start.12) | collective-permute-done | bytes 393248 | tf_op jit(solution)/shard_map/ppermute | solution.py:234
  81.0 0.7 cross_strips.1
  81.7 1.9 %collective-permute-start.13 = (bf16[256,512]{1,0:T(8,128)(2,1)S(1)}, bf16[256,512]{1,0:T(8,128)(2,1)S(1)}, u32[]{:S(2)}, u32[]{:S(2)}) collective-permute-start(bf16[256,512]{1,0:T(8,128)(2,1)S(1)} %get-tuple-element.54), channel_id=1, source_target_pairs={{0,5},{2,7},{5,0},{7,2},{8,13},{10,15},{13,8},{15,10},{16,21},{18,... | collective-permute-start | bytes 786440 | tf_op jit(solution)/shard_map/ppermute | solution.py:234
  83.7 0.0 collective-permute-done.14.from_z_c
  83.7 1.3 %collective-permute-start.15 = (bf16[256,512]{1,0:T(8,128)(2,1)S(1)}, bf16[256,512]{1,0:T(8,128)(2,1)S(1)}, u32[]{:S(2)}, u32[]{:S(2)}) collective-permute-start(bf16[256,512]{1,0:T(8,128)(2,1)S(1)} %get-tuple-element.57), channel_id=1, source_target_pairs={{0,9},{2,11},{8,17},{10,19},{13,4},{15,6},{16,25},{18,27},{21,12},... | collective-permute-start | bytes 786440 | tf_op jit(solution)/shard_map/ppermute | solution.py:234
  85.0 1.5 %collective-permute-done.11.from_y_b = f32[256,512]{1,0:T(8,128)S(1)} collective-permute-done((f32[256,512]{1,0:T(8,128)S(1)}, f32[256,512]{1,0:T(8,128)S(1)}, u32[]{:S(2)}, u32[]{:S(2)}) %collective-permute-start.11) | collective-permute-done | bytes 524320 | tf_op jit(solution)/shard_map/ppermute | solution.py:234
  86.5 3.0 %collective-permute-done.13.from_y_d = bf16[256,512]{1,0:T(8,128)(2,1)S(1)} collective-permute-done((bf16[256,512]{1,0:T(8,128)(2,1)S(1)}, bf16[256,512]{1,0:T(8,128)(2,1)S(1)}, u32[]{:S(2)}, u32[]{:S(2)}) %collective-permute-start.13) | collective-permute-done | bytes 262176 | tf_op jit(solution)/shard_map/ppermute | solution.py:234
  89.4 0.0 collective-permute-done.15.from_z_d
  89.4 0.7 combine.1
  90.2 0.1 collective-permute-start.16
  90.2 2.3 %collective-permute-done.16.sib = f32[3,128,512]{2,1,0:T(8,128)S(1)} collective-permute-done((f32[3,128,512]{2,1,0:T(8,128)S(1)}, f32[3,128,512]{2,1,0:T(8,128)S(1)}, u32[]{:S(2)}, u32[]{:S(2)}) %collective-permute-start.16) | collective-permute-done | bytes 786464 | tf_op jit(solution)/shard_map/ppermute | solution.py:234
  92.5 1.7 %finish.1 = (bf16[1,3,128,512]{3,2,1,0:T(8,128)(2,1)}, bf16[1,2,128,512]{3,2,1,0:T(8,128)(2,1)}) custom-call(s32[5]{0:T(128)S(1)} %stack.23.pos_ref.refs_0_, s32[1,3]{1,0:T(1,128)S(1)} %copy-done.2, f32[128,512]{1,0:T(8,128)S(1)} %get-tuple-element.33.diag_mine, f32[128,512]{1,0:T(8,128)S(1)} %collective-permute-done.6.diag_got, ...), custom_call_target="tpu_custom_call" | custom-call | tf_op jit(solution)/shard_map/finish/pallas_call | solution.py:323
  (5 shorter events, 0.0 us)
Async XLA Ops:
  0.6 51.8 %collective-permute-start.4 = (bf16[4096,512]{1,0:T(8,128)(2,1)}, bf16[4096,512]{1,0:T(8,128)(2,1)}, u32[]{:S(2)}, u32[]{:S(2)}) collective-permute-start(bf16[4096,512]{1,0:T(8,128)(2,1)} %x_ref.1), channel_id=1, source_target_pairs={{1,9},{3,11},{5,13},{7,15},{8,0},{9,17},{10,2},{11,19},{12,4},{13,... | collective-permute-start | bytes 12582920 | tf_op jit(solution)/shard_map/ppermute | solution.py:234
  1.9 57.1 %collective-permute-start.7 = (bf16[4096,512]{1,0:T(8,128)(2,1)}, bf16[4096,512]{1,0:T(8,128)(2,1)}, u32[]{:S(2)}, u32[]{:S(2)}) collective-permute-start(bf16[4096,512]{1,0:T(8,128)(2,1)} %x_ref.1), channel_id=1, source_target_pairs={{1,5},{3,7},{4,0},{6,2},{9,13},{11,15},{12,8},{14,10},{17,21},{19,... | collective-permute-start | bytes 12582920 | tf_op jit(solution)/shard_map/ppermute | solution.py:234
  3.2 2.2 %copy-start = (bf16[4096,512]{1,0:T(8,128)(2,1)S(1)}, bf16[4096,512]{1,0:T(8,128)(2,1)}, u32[]{:S(2)}) copy-start(bf16[4096,512]{1,0:T(8,128)(2,1)} %x_ref.1) | copy-start | bytes 12582916
  5.4 15.7 %copy-start.2 = (s32[1,3]{1,0:T(1,128)S(1)}, s32[1,3]{1,0:T(1,128)}, u32[]{:S(2)}) copy-start(s32[1,3]{1,0:T(1,128)} %offsets_ref.3) | copy-start | bytes 40
  7.3 11.5 %collective-permute-start.2 = (f32[2,512]{1,0:T(2,128)S(1)}, f32[2,512]{1,0:T(2,128)S(1)}, u32[]{:S(2)}, u32[]{:S(2)}) collective-permute-start(f32[2,512]{1,0:T(2,128)S(1)} %local_stats.1.own_ref), channel_id=1, source_target_pairs={{0,3},{1,2},{2,1},{3,0},{4,7},{5,6},{6,5},{7,4},{8,11},{9,10},{10,... | collective-permute-start | bytes 12296 | tf_op jit(solution)/shard_map/ppermute | solution.py:234
  17.5 3.6 %collective-permute-start.1 = (f32[2,512]{1,0:T(2,128)S(1)}, f32[2,512]{1,0:T(2,128)S(1)}, u32[]{:S(2)}, u32[]{:S(2)}) collective-permute-start(f32[2,512]{1,0:T(2,128)S(1)} %local_stats.1.own_ref), channel_id=1, source_target_pairs={{0,2},{1,3},{2,0},{3,1},{4,6},{5,7},{6,4},{7,5},{8,10},{9,11},{10,... | collective-permute-start | bytes 12296 | tf_op jit(solution)/shard_map/ppermute | solution.py:234
  18.0 3.1 %collective-permute-start = (f32[2,512]{1,0:T(2,128)S(1)}, f32[2,512]{1,0:T(2,128)S(1)}, u32[]{:S(2)}, u32[]{:S(2)}) collective-permute-start(f32[2,512]{1,0:T(2,128)S(1)} %local_stats.1.own_ref), channel_id=1, source_target_pairs={{0,1},{1,0},{2,3},{3,2},{4,5},{5,4},{6,7},{7,6},{8,9},{9,8},{10,11... | collective-permute-start | bytes 12296 | tf_op jit(solution)/shard_map/ppermute | solution.py:234
  21.7 2.2 %copy-start.1 = (bf16[4096,512]{1,0:T(8,128)(2,1)S(1)}, bf16[4096,512]{1,0:T(8,128)(2,1)}, u32[]{:S(2)}) copy-start(bf16[4096,512]{1,0:T(8,128)(2,1)} %x_ref.1) | copy-start | bytes 12582916
  28.2 2.0 %collective-permute-start.3 = (f32[2,128,512]{2,1,0:T(8,128)S(1)}, f32[2,128,512]{2,1,0:T(8,128)S(1)}, u32[]{:S(2)}, u32[]{:S(2)}) collective-permute-start(f32[2,128,512]{2,1,0:T(8,128)S(1)} %get-tuple-element.32), channel_id=1, source_target_pairs={{0,1},{1,0},{2,3},{3,2},{4,5},{5,4},{6,7},{7,6},{8,9},{9,8},{10,11... | collective-permute-start | bytes 1572872 | tf_op jit(solution)/shard_map/ppermute | solution.py:234
  30.8 26.3 %collective-permute-start.6 = (f32[128,512]{1,0:T(8,128)S(1)}, f32[128,512]{1,0:T(8,128)S(1)}, u32[]{:S(2)}, u32[]{:S(2)}) collective-permute-start(f32[128,512]{1,0:T(8,128)S(1)} %get-tuple-element.36), channel_id=1, source_target_pairs={{0,2},{1,3},{2,0},{3,1},{4,6},{5,7},{6,4},{7,5},{8,10},{9,11},{10,... | collective-permute-start | bytes 786440 | tf_op jit(solution)/shard_map/ppermute | solution.py:234
  31.3 5.1 %collective-permute-start.5 = (f32[4,512]{1,0:T(4,128)S(1)}, f32[4,512]{1,0:T(4,128)S(1)}, u32[]{:S(2)}, u32[]{:S(2)}) collective-permute-start(f32[4,512]{1,0:T(4,128)S(1)} %stats.1.stat_ref), channel_id=1, source_target_pairs={{0,9},{2,11},{4,13},{6,15},{8,17},{9,0},{10,19},{11,2},{12,21},{13... | collective-permute-start | bytes 24584 | tf_op jit(solution)/shard_map/ppermute | solution.py:234
  33.3 25.8 %collective-permute-start.8 = (f32[4,512]{1,0:T(4,128)S(1)}, f32[4,512]{1,0:T(4,128)S(1)}, u32[]{:S(2)}, u32[]{:S(2)}) collective-permute-start(f32[4,512]{1,0:T(4,128)S(1)} %stats.1.stat_ref), channel_id=1, source_target_pairs={{0,5},{2,7},{5,0},{7,2},{8,13},{10,15},{13,8},{15,10},{16,21},{18,... | collective-permute-start | bytes 24584 | tf_op jit(solution)/shard_map/ppermute | solution.py:234
  57.1 11.6 %collective-permute-start.10 = (bf16[3,256,256]{2,1,0:T(8,128)(2,1)S(1)}, bf16[3,256,256]{2,1,0:T(8,128)(2,1)S(1)}, u32[]{:S(2)}, u32[]{:S(2)}) collective-permute-start(bf16[3,256,256]{2,1,0:T(8,128)(2,1)S(1)} %get-tuple-element.44), channel_id=1, source_target_pairs={{0,2},{1,3},{2,0},{3,1},{4,6},{5,7},{6,4},{7,5},{8,10},{9,11},{10,... | collective-permute-start | bytes 1179656 | tf_op jit(solution)/shard_map/ppermute | solution.py:234
  63.7 11.5 %collective-permute-start.9 = (bf16[3,256,256]{2,1,0:T(8,128)(2,1)S(1)}, bf16[3,256,256]{2,1,0:T(8,128)(2,1)S(1)}, u32[]{:S(2)}, u32[]{:S(2)}) collective-permute-start(bf16[3,256,256]{2,1,0:T(8,128)(2,1)S(1)} %get-tuple-element.39), channel_id=1, source_target_pairs={{0,2},{2,0},{5,7},{7,5},{8,10},{10,8},{13,15},{15,13},{16,18},{18,... | collective-permute-start | bytes 1179656 | tf_op jit(solution)/shard_map/ppermute | solution.py:234
  69.4 14.2 %collective-permute-start.14 = (f32[256,512]{1,0:T(8,128)S(1)}, f32[256,512]{1,0:T(8,128)S(1)}, u32[]{:S(2)}, u32[]{:S(2)}) collective-permute-start(f32[256,512]{1,0:T(8,128)S(1)} %get-tuple-element.46), channel_id=1, source_target_pairs={{0,9},{2,11},{4,13},{6,15},{8,17},{9,0},{10,19},{11,2},{12,21},{13... | collective-permute-start | bytes 1572872 | tf_op jit(solution)/shard_map/ppermute | solution.py:234
  71.4 9.7 %collective-permute-start.12 = (bf16[3,256,256]{2,1,0:T(8,128)(2,1)S(1)}, bf16[3,256,256]{2,1,0:T(8,128)(2,1)S(1)}, u32[]{:S(2)}, u32[]{:S(2)}) collective-permute-start(bf16[3,256,256]{2,1,0:T(8,128)(2,1)S(1)} %get-tuple-element.52), channel_id=1, source_target_pairs={{0,2},{2,0},{5,7},{7,5},{8,10},{10,8},{13,15},{15,13},{16,18},{18,... | collective-permute-start | bytes 1179656 | tf_op jit(solution)/shard_map/ppermute | solution.py:234
  76.0 10.5 %collective-permute-start.11 = (f32[256,512]{1,0:T(8,128)S(1)}, f32[256,512]{1,0:T(8,128)S(1)}, u32[]{:S(2)}, u32[]{:S(2)}) collective-permute-start(f32[256,512]{1,0:T(8,128)S(1)} %get-tuple-element.50), channel_id=1, source_target_pairs={{0,5},{2,7},{5,0},{7,2},{8,13},{10,15},{13,8},{15,10},{16,21},{18,... | collective-permute-start | bytes 1572872 | tf_op jit(solution)/shard_map/ppermute | solution.py:234
  81.7 7.7 %collective-permute-start.13 = (bf16[256,512]{1,0:T(8,128)(2,1)S(1)}, bf16[256,512]{1,0:T(8,128)(2,1)S(1)}, u32[]{:S(2)}, u32[]{:S(2)}) collective-permute-start(bf16[256,512]{1,0:T(8,128)(2,1)S(1)} %get-tuple-element.54), channel_id=1, source_target_pairs={{0,5},{2,7},{5,0},{7,2},{8,13},{10,15},{13,8},{15,10},{16,21},{18,... | collective-permute-start | bytes 786440 | tf_op jit(solution)/shard_map/ppermute | solution.py:234
  83.7 5.8 %collective-permute-start.15 = (bf16[256,512]{1,0:T(8,128)(2,1)S(1)}, bf16[256,512]{1,0:T(8,128)(2,1)S(1)}, u32[]{:S(2)}, u32[]{:S(2)}) collective-permute-start(bf16[256,512]{1,0:T(8,128)(2,1)S(1)} %get-tuple-element.57), channel_id=1, source_target_pairs={{0,9},{2,11},{8,17},{10,19},{13,4},{15,6},{16,25},{18,27},{21,12},... | collective-permute-start | bytes 786440 | tf_op jit(solution)/shard_map/ppermute | solution.py:234
  90.2 2.4 %collective-permute-start.16 = (f32[3,128,512]{2,1,0:T(8,128)S(1)}, f32[3,128,512]{2,1,0:T(8,128)S(1)}, u32[]{:S(2)}, u32[]{:S(2)}) collective-permute-start(f32[3,128,512]{2,1,0:T(8,128)S(1)} %get-tuple-element.59), channel_id=1, source_target_pairs={{0,1},{1,0},{2,3},{3,2},{4,5},{5,4},{6,7},{7,6},{8,9},{9,8},{10,11... | collective-permute-start | bytes 2359304 | tf_op jit(solution)/shard_map/ppermute | solution.py:234

commit v12 on v11

--- a/solution.py
+++ b/solution.py
@@ -315,7 +315,6 @@
     from_y_b = send(to_y_b, y_cross)
     got_d, to_y_b = lax.optimization_barrier((got_d, to_y_b))
     to_y_d, to_z_d = near_strips("cross_strips", CROSS, keep_d, got_d)
-    to_z_d, from_z_c = lax.optimization_barrier((to_z_d, from_z_c))
     from_y_d, from_z_d = send(to_y_d, y_cross), send(to_z_d, z_cross_active)
 
     mine, sib = call(combine_kernel, "combine", (), [SMEM] + [VMEM] * 6, [VMEM] * 2, [shape(3, strip, width)] * 2)(

time: 95.2 us -> 93.4 us (0.981)
  waiting for transfers between devices: 31.3 us -> 28.8 us
    ppermute x17, waiting for transfers between devices: 31.3 us -> 28.8 us  [send(): return lax.ppermute(value, AXES, pairs)]
  transfers between devices with their start and end apart: 17 -> 17, of which waited for: 8 -> 10; matrix products, arithmetic and copies ran while one was open for 0% -> 0% of each run, Pallas kernels for 23% -> 24%
where the time goes in v12:
time: 93.4 us; the launch traced here: 92.2 us
  starting transfers between devices  33.4 us (36%)
  waiting for transfers between devices  28.8 us (31%)
  Pallas kernels  24.1 us (26%)
  local copies, waits for them, and re-layouts  4.46 us (5%)
  between operations  1.49 us (2%)
    ppermute x17, starting transfers between devices, send(): return lax.ppermute(value, AXES, pairs)  33.4 us
    ppermute x17, waiting for transfers between devices, send(): return lax.ppermute(value, AXES, pairs)  28.8 us
    pallas_call x1, Pallas kernels, body(): call(near_kernel, 'near_tile', (), [SMEM, VMEM, anywhere, VMEM, VMEM], [V...  4.64 us
    pallas_call x1, Pallas kernels, body(): call(far_kernel, 'far_tile', (), [SMEM, VMEM, anywhere, VMEM, VMEM], [VME...  4.59 us
    unnamed x6, local copies, waits for them, and re-layouts  4.37 us
    pallas_call x1, Pallas kernels, body(): call(own_kernel, 'own_tile', (steps,), [SMEM, wide, whole(4, width)], [fl...  4.31 us
    pallas_call x1, Pallas kernels, body(): call(lambda *refs: cross_kernel(steps, *refs), 'cross_tile', (), [SMEM] +...  2.96 us
  transfers between devices with their start and end apart: 17, of which 10 were waited for; matrix products, arithmetic and copies ran while one was open for 0% of the time, Pallas kernels for 24%

profile of v12, /device:TPU:0, one launch (start us, length us, event | category | flops | bytes accessed | tf_op | source)
XLA Modules:
  0.0 92.2 jit_solution(11735642847943228701)
XLA Ops:
  0.6 1.3 %collective-permute-start.4 = (bf16[4096,512]{1,0:T(8,128)(2,1)}, bf16[4096,512]{1,0:T(8,128)(2,1)}, u32[]{:S(2)}, u32[]{:S(2)}) collective-permute-start(bf16[4096,512]{1,0:T(8,128)(2,1)} %x_ref.1), channel_id=1, source_target_pairs={{1,9},{3,11},{5,13},{7,15},{8,0},{9,17},{10,2},{11,19},{12,4},{13,... | collective-permute-start | bytes 12582920 | tf_op jit(solution)/shard_map/ppermute | solution.py:234
  1.9 1.3 %collective-permute-start.7 = (bf16[4096,512]{1,0:T(8,128)(2,1)}, bf16[4096,512]{1,0:T(8,128)(2,1)}, u32[]{:S(2)}, u32[]{:S(2)}) collective-permute-start(bf16[4096,512]{1,0:T(8,128)(2,1)} %x_ref.1), channel_id=1, source_target_pairs={{1,5},{3,7},{4,0},{6,2},{9,13},{11,15},{12,8},{14,10},{17,21},{19,... | collective-permute-start | bytes 12582920 | tf_op jit(solution)/shard_map/ppermute | solution.py:234
  3.2 0.0 copy-start
  3.2 2.2 %copy-done = bf16[4096,512]{1,0:T(8,128)(2,1)S(1)} copy-done((bf16[4096,512]{1,0:T(8,128)(2,1)S(1)}, bf16[4096,512]{1,0:T(8,128)(2,1)}, u32[]{:S(2)}) %copy-start) | copy-done | bytes 4194328
  5.4 1.9 %local_stats.1.own_ref = f32[2,512]{1,0:T(2,128)S(1)} custom-call(bf16[4096,512]{1,0:T(8,128)(2,1)S(1)} %copy-done), custom_call_target="tpu_custom_call" | custom-call | flops 10485760 | bytes 4194304 | tf_op jit(solution)/shard_map/local_stats/pallas_call | solution.py:267
  7.3 10.2 %collective-permute-start.2 = (f32[2,512]{1,0:T(2,128)S(1)}, f32[2,512]{1,0:T(2,128)S(1)}, u32[]{:S(2)}, u32[]{:S(2)}) collective-permute-start(f32[2,512]{1,0:T(2,128)S(1)} %local_stats.1.own_ref), channel_id=1, source_target_pairs={{0,3},{1,2},{2,1},{3,0},{4,7},{5,6},{6,5},{7,4},{8,11},{9,10},{10,... | collective-permute-start | bytes 12296 | tf_op jit(solution)/shard_map/ppermute | solution.py:234
  17.5 0.5 collective-permute-start.1
  18.7 0.1 stack.23.pos_ref.refs_0_
  18.7 0.0 collective-permute-done.2.cross_ref
  18.8 2.3 %collective-permute-done.1.far_ref = f32[2,512]{1,0:T(2,128)S(1)} collective-permute-done((f32[2,512]{1,0:T(2,128)S(1)}, f32[2,512]{1,0:T(2,128)S(1)}, u32[]{:S(2)}, u32[]{:S(2)}) %collective-permute-start.1) | collective-permute-done | bytes 4128 | tf_op jit(solution)/shard_map/ppermute | solution.py:234
  21.1 0.0 collective-permute-done.sib_ref
  21.1 0.6 stats.1.stat_ref
  21.7 0.0 copy-start.1
  21.7 2.2 %copy-done.1 = bf16[4096,512]{1,0:T(8,128)(2,1)S(1)} copy-done((bf16[4096,512]{1,0:T(8,128)(2,1)S(1)}, bf16[4096,512]{1,0:T(8,128)(2,1)}, u32[]{:S(2)}) %copy-start.1) | copy-done | bytes 4194328
  23.8 4.3 %own_tile.1 = (bf16[512,4096]{1,0:T(8,128)(2,1)S(1)}, f32[2,128,512]{2,1,0:T(8,128)S(1)}, f32[2,128,512]{2,1,0:T(8,128)S(1)}) custom-call(s32[5]{0:T(128)S(1)} %stack.23.pos_ref.refs_0_, bf16[4096,512]{1,0:T(8,128)(2,1)S(1)} %copy-done.1, f32[4,512]{1,0:T(4,128)S(1)} %stats.1.stat_ref), custom_call_target="tpu_custom_call" | custom-call | flops 2147483648 | bytes 8388608 | tf_op jit(solution)/shard_map/own_tile/pallas_call | solution.py:274
  28.2 0.1 collective-permute-start.3
  28.2 1.9 %collective-permute-done.3.got_ref = f32[2,128,512]{2,1,0:T(8,128)S(1)} collective-permute-done((f32[2,128,512]{2,1,0:T(8,128)S(1)}, f32[2,128,512]{2,1,0:T(8,128)S(1)}, u32[]{:S(2)}, u32[]{:S(2)}) %collective-permute-start.3) | collective-permute-done | bytes 524320 | tf_op jit(solution)/shard_map/ppermute | solution.py:234
  30.1 0.6 own_tile_strips.1
  30.8 0.6 collective-permute-start.6
  31.3 1.9 %collective-permute-start.5 = (f32[4,512]{1,0:T(4,128)S(1)}, f32[4,512]{1,0:T(4,128)S(1)}, u32[]{:S(2)}, u32[]{:S(2)}) collective-permute-start(f32[4,512]{1,0:T(4,128)S(1)} %stats.1.stat_ref), channel_id=1, source_target_pairs={{0,9},{2,11},{4,13},{6,15},{8,17},{9,0},{10,19},{11,2},{12,21},{13... | collective-permute-start | bytes 24584 | tf_op jit(solution)/shard_map/ppermute | solution.py:234
  33.3 1.9 %collective-permute-start.8 = (f32[4,512]{1,0:T(4,128)S(1)}, f32[4,512]{1,0:T(4,128)S(1)}, u32[]{:S(2)}, u32[]{:S(2)}) collective-permute-start(f32[4,512]{1,0:T(4,128)S(1)} %stats.1.stat_ref), channel_id=1, source_target_pairs={{0,5},{2,7},{5,0},{7,2},{8,13},{10,15},{13,8},{15,10},{16,21},{18,... | collective-permute-start | bytes 24584 | tf_op jit(solution)/shard_map/ppermute | solution.py:234
  35.2 1.3 %collective-permute-done.5.wstat_ref.refs_4_ = f32[4,512]{1,0:T(4,128)S(1)} collective-permute-done((f32[4,512]{1,0:T(4,128)S(1)}, f32[4,512]{1,0:T(4,128)S(1)}, u32[]{:S(2)}, u32[]{:S(2)}) %collective-permute-start.5) | collective-permute-done | bytes 8224 | tf_op jit(solution)/shard_map/ppermute | solution.py:234
  36.4 16.0 %collective-permute-done.4.w_ref = bf16[4096,512]{1,0:T(8,128)(2,1)} collective-permute-done((bf16[4096,512]{1,0:T(8,128)(2,1)}, bf16[4096,512]{1,0:T(8,128)(2,1)}, u32[]{:S(2)}, u32[]{:S(2)}) %collective-permute-start.4) | collective-permute-done | bytes 4194336 | tf_op jit(solution)/shard_map/ppermute | solution.py:234
  52.4 4.6 %far_tile.1 = (f32[3,256,256]{2,1,0:T(8,128)S(1)}, bf16[3,256,256]{2,1,0:T(8,128)(2,1)S(1)}, bf16[4096,512]{1,0:T(8,128)(2,1)S(1)}) custom-call(s32[5]{0:T(128)S(1)} %stack.23.pos_ref.refs_0_, bf16[512,4096]{1,0:T(8,128)(2,1)S(1)} %get-tuple-element.32.turned_ref, bf16[4096,512]{1,0:T(8,128)(2,1)} %collective-permute-done.4.w_ref, ...), custom_call_target="tpu_custom_call" | custom-call | flops 2147483648 | bytes 12582912 | tf_op jit(solution)/shard_map/far_tile/pallas_call | solution.py:287
  57.1 2.0 %collective-permute-start.10 = (bf16[3,256,256]{2,1,0:T(8,128)(2,1)S(1)}, bf16[3,256,256]{2,1,0:T(8,128)(2,1)S(1)}, u32[]{:S(2)}, u32[]{:S(2)}) collective-permute-start(bf16[3,256,256]{2,1,0:T(8,128)(2,1)S(1)} %get-tuple-element.42), channel_id=1, source_target_pairs={{0,2},{1,3},{2,0},{3,1},{4,6},{5,7},{6,4},{7,5},{8,10},{9,11},{10,... | collective-permute-start | bytes 1179656 | tf_op jit(solution)/shard_map/ppermute | solution.py:234
  59.1 0.0 collective-permute-done.8.ystat_ref.refs_3_
  59.1 0.0 collective-permute-done.7.y_ref
  59.1 4.6 %near_tile.1 = (f32[3,256,256]{2,1,0:T(8,128)S(1)}, bf16[3,256,256]{2,1,0:T(8,128)(2,1)S(1)}, bf16[512,4096]{1,0:T(8,128)(2,1)S(1)}) custom-call(s32[5]{0:T(128)S(1)} %stack.23.pos_ref.refs_0_, bf16[512,4096]{1,0:T(8,128)(2,1)S(1)} %get-tuple-element.32.turned_ref, bf16[4096,512]{1,0:T(8,128)(2,1)} %collective-permute-done.7.y_ref, ...), custom_call_target="tpu_custom_call" | custom-call | flops 2147483648 | bytes 12582912 | tf_op jit(solution)/shard_map/near_tile/pallas_call | solution.py:294
  63.7 2.0 %collective-permute-start.9 = (bf16[3,256,256]{2,1,0:T(8,128)(2,1)S(1)}, bf16[3,256,256]{2,1,0:T(8,128)(2,1)S(1)}, u32[]{:S(2)}, u32[]{:S(2)}) collective-permute-start(bf16[3,256,256]{2,1,0:T(8,128)(2,1)S(1)} %get-tuple-element.37), channel_id=1, source_target_pairs={{0,2},{2,0},{5,7},{7,5},{8,10},{10,8},{13,15},{15,13},{16,18},{18,... | collective-permute-start | bytes 1179656 | tf_op jit(solution)/shard_map/ppermute | solution.py:234
  65.7 3.0 %cross_tile.1 = (f32[3,256,256]{2,1,0:T(8,128)S(1)}, bf16[3,256,256]{2,1,0:T(8,128)(2,1)S(1)}) custom-call(s32[5]{0:T(128)S(1)} %stack.23.pos_ref.refs_0_, bf16[512,4096]{1,0:T(8,128)(2,1)S(1)} %get-tuple-element.39.refs_1_, bf16[4096,512]{1,0:T(8,128)(2,1)S(1)} %get-tuple-element.40.refs_2_, f32[4,512]{1,0:T(4,128)S(1)} %collective-permute-done.8.ystat_ref.refs_3_, ...), custom_call_target="tpu_custom_call" | custom-call | flops 2147483648 | bytes 8388608 | tf_op jit(solution)/shard_map/cross_tile/pallas_call | solution.py:299
  68.7 3.8 %collective-permute-start.12 = (bf16[3,256,256]{2,1,0:T(8,128)(2,1)S(1)}, bf16[3,256,256]{2,1,0:T(8,128)(2,1)S(1)}, u32[]{:S(2)}, u32[]{:S(2)}) collective-permute-start(bf16[3,256,256]{2,1,0:T(8,128)(2,1)S(1)} %get-tuple-element.50), channel_id=1, source_target_pairs={{0,2},{2,0},{5,7},{7,5},{8,10},{10,8},{13,15},{15,13},{16,18},{18,... | collective-permute-start | bytes 1179656 | tf_op jit(solution)/shard_map/ppermute | solution.py:234
  72.5 0.7 far_strips.1
  73.3 0.1 collective-permute-done.9.got
  73.4 0.7 near_strips.1
  74.1 1.9 %collective-permute-start.11 = (f32[256,512]{1,0:T(8,128)S(1)}, f32[256,512]{1,0:T(8,128)S(1)}, u32[]{:S(2)}, u32[]{:S(2)}) collective-permute-start(f32[256,512]{1,0:T(8,128)S(1)} %get-tuple-element.48), channel_id=1, source_target_pairs={{0,5},{2,7},{5,0},{7,2},{8,13},{10,15},{13,8},{15,10},{16,21},{18,... | collective-permute-start | bytes 1572872 | tf_op jit(solution)/shard_map/ppermute | solution.py:234
  76.1 1.9 %collective-permute-start.14 = (f32[256,512]{1,0:T(8,128)S(1)}, f32[256,512]{1,0:T(8,128)S(1)}, u32[]{:S(2)}, u32[]{:S(2)}) collective-permute-start(f32[256,512]{1,0:T(8,128)S(1)} %get-tuple-element.44), channel_id=1, source_target_pairs={{0,9},{2,11},{4,13},{6,15},{8,17},{9,0},{10,19},{11,2},{12,21},{13... | collective-permute-start | bytes 1572872 | tf_op jit(solution)/shard_map/ppermute | solution.py:234
  78.0 0.4 collective-permute-done.12.got
  78.4 0.7 cross_strips.1
  79.1 2.1 %collective-permute-start.13 = (bf16[256,512]{1,0:T(8,128)(2,1)S(1)}, bf16[256,512]{1,0:T(8,128)(2,1)S(1)}, u32[]{:S(2)}, u32[]{:S(2)}) collective-permute-start(bf16[256,512]{1,0:T(8,128)(2,1)S(1)} %get-tuple-element.52), channel_id=1, source_target_pairs={{0,5},{2,7},{5,0},{7,2},{8,13},{10,15},{13,8},{15,10},{16,21},{18,... | collective-permute-start | bytes 786440 | tf_op jit(solution)/shard_map/ppermute | solution.py:234
  81.1 1.8 %collective-permute-start.15 = (bf16[256,512]{1,0:T(8,128)(2,1)S(1)}, bf16[256,512]{1,0:T(8,128)(2,1)S(1)}, u32[]{:S(2)}, u32[]{:S(2)}) collective-permute-start(bf16[256,512]{1,0:T(8,128)(2,1)S(1)} %get-tuple-element.53), channel_id=1, source_target_pairs={{0,9},{2,11},{8,17},{10,19},{13,4},{15,6},{16,25},{18,27},{21,12},... | collective-permute-start | bytes 786440 | tf_op jit(solution)/shard_map/ppermute | solution.py:234
  82.9 1.7 %collective-permute-done.11.from_y_b = f32[256,512]{1,0:T(8,128)S(1)} collective-permute-done((f32[256,512]{1,0:T(8,128)S(1)}, f32[256,512]{1,0:T(8,128)S(1)}, u32[]{:S(2)}, u32[]{:S(2)}) %collective-permute-start.11) | collective-permute-done | bytes 524320 | tf_op jit(solution)/shard_map/ppermute | solution.py:234
  84.6 1.9 %collective-permute-done.14.from_z_c = f32[256,512]{1,0:T(8,128)S(1)} collective-permute-done((f32[256,512]{1,0:T(8,128)S(1)}, f32[256,512]{1,0:T(8,128)S(1)}, u32[]{:S(2)}, u32[]{:S(2)}) %collective-permute-start.14) | collective-permute-done | bytes 524320 | tf_op jit(solution)/shard_map/ppermute | solution.py:234
  86.6 0.9 collective-permute-done.13.from_y_d
  87.4 0.0 collective-permute-done.15.from_z_d
  87.5 0.7 combine.1
  88.2 0.1 collective-permute-start.16
  88.3 2.3 %collective-permute-done.16.sib = f32[3,128,512]{2,1,0:T(8,128)S(1)} collective-permute-done((f32[3,128,512]{2,1,0:T(8,128)S(1)}, f32[3,128,512]{2,1,0:T(8,128)S(1)}, u32[]{:S(2)}, u32[]{:S(2)}) %collective-permute-start.16) | collective-permute-done | bytes 786464 | tf_op jit(solution)/shard_map/ppermute | solution.py:234
  90.5 1.7 %finish.1 = (bf16[1,3,128,512]{3,2,1,0:T(8,128)(2,1)}, bf16[1,2,128,512]{3,2,1,0:T(8,128)(2,1)}) custom-call(s32[5]{0:T(128)S(1)} %stack.23.pos_ref.refs_0_, s32[1,3]{1,0:T(1,128)S(1)} %copy-done.2, f32[128,512]{1,0:T(8,128)S(1)} %get-tuple-element.31.diag_mine, f32[128,512]{1,0:T(8,128)S(1)} %collective-permute-done.6.diag_got, ...), custom_call_target="tpu_custom_call" | custom-call | tf_op jit(solution)/shard_map/finish/pallas_call | solution.py:322
  (5 shorter events, 0.0 us)
Async XLA Ops:
  0.6 51.8 %collective-permute-start.4 = (bf16[4096,512]{1,0:T(8,128)(2,1)}, bf16[4096,512]{1,0:T(8,128)(2,1)}, u32[]{:S(2)}, u32[]{:S(2)}) collective-permute-start(bf16[4096,512]{1,0:T(8,128)(2,1)} %x_ref.1), channel_id=1, source_target_pairs={{1,9},{3,11},{5,13},{7,15},{8,0},{9,17},{10,2},{11,19},{12,4},{13,... | collective-permute-start | bytes 12582920 | tf_op jit(solution)/shard_map/ppermute | solution.py:234
  1.9 57.1 %collective-permute-start.7 = (bf16[4096,512]{1,0:T(8,128)(2,1)}, bf16[4096,512]{1,0:T(8,128)(2,1)}, u32[]{:S(2)}, u32[]{:S(2)}) collective-permute-start(bf16[4096,512]{1,0:T(8,128)(2,1)} %x_ref.1), channel_id=1, source_target_pairs={{1,5},{3,7},{4,0},{6,2},{9,13},{11,15},{12,8},{14,10},{17,21},{19,... | collective-permute-start | bytes 12582920 | tf_op jit(solution)/shard_map/ppermute | solution.py:234
  3.2 2.2 %copy-start = (bf16[4096,512]{1,0:T(8,128)(2,1)S(1)}, bf16[4096,512]{1,0:T(8,128)(2,1)}, u32[]{:S(2)}) copy-start(bf16[4096,512]{1,0:T(8,128)(2,1)} %x_ref.1) | copy-start | bytes 12582916
  5.4 15.7 %copy-start.2 = (s32[1,3]{1,0:T(1,128)S(1)}, s32[1,3]{1,0:T(1,128)}, u32[]{:S(2)}) copy-start(s32[1,3]{1,0:T(1,128)} %offsets_ref.3) | copy-start | bytes 40
  7.3 11.5 %collective-permute-start.2 = (f32[2,512]{1,0:T(2,128)S(1)}, f32[2,512]{1,0:T(2,128)S(1)}, u32[]{:S(2)}, u32[]{:S(2)}) collective-permute-start(f32[2,512]{1,0:T(2,128)S(1)} %local_stats.1.own_ref), channel_id=1, source_target_pairs={{0,3},{1,2},{2,1},{3,0},{4,7},{5,6},{6,5},{7,4},{8,11},{9,10},{10,... | collective-permute-start | bytes 12296 | tf_op jit(solution)/shard_map/ppermute | solution.py:234
  17.5 3.6 %collective-permute-start.1 = (f32[2,512]{1,0:T(2,128)S(1)}, f32[2,512]{1,0:T(2,128)S(1)}, u32[]{:S(2)}, u32[]{:S(2)}) collective-permute-start(f32[2,512]{1,0:T(2,128)S(1)} %local_stats.1.own_ref), channel_id=1, source_target_pairs={{0,2},{1,3},{2,0},{3,1},{4,6},{5,7},{6,4},{7,5},{8,10},{9,11},{10,... | collective-permute-start | bytes 12296 | tf_op jit(solution)/shard_map/ppermute | solution.py:234
  18.0 3.1 %collective-permute-start = (f32[2,512]{1,0:T(2,128)S(1)}, f32[2,512]{1,0:T(2,128)S(1)}, u32[]{:S(2)}, u32[]{:S(2)}) collective-permute-start(f32[2,512]{1,0:T(2,128)S(1)} %local_stats.1.own_ref), channel_id=1, source_target_pairs={{0,1},{1,0},{2,3},{3,2},{4,5},{5,4},{6,7},{7,6},{8,9},{9,8},{10,11... | collective-permute-start | bytes 12296 | tf_op jit(solution)/shard_map/ppermute | solution.py:234
  21.7 2.2 %copy-start.1 = (bf16[4096,512]{1,0:T(8,128)(2,1)S(1)}, bf16[4096,512]{1,0:T(8,128)(2,1)}, u32[]{:S(2)}) copy-start(bf16[4096,512]{1,0:T(8,128)(2,1)} %x_ref.1) | copy-start | bytes 12582916
  28.2 2.0 %collective-permute-start.3 = (f32[2,128,512]{2,1,0:T(8,128)S(1)}, f32[2,128,512]{2,1,0:T(8,128)S(1)}, u32[]{:S(2)}, u32[]{:S(2)}) collective-permute-start(f32[2,128,512]{2,1,0:T(8,128)S(1)} %get-tuple-element.30), channel_id=1, source_target_pairs={{0,1},{1,0},{2,3},{3,2},{4,5},{5,4},{6,7},{7,6},{8,9},{9,8},{10,11... | collective-permute-start | bytes 1572872 | tf_op jit(solution)/shard_map/ppermute | solution.py:234
  30.8 26.3 %collective-permute-start.6 = (f32[128,512]{1,0:T(8,128)S(1)}, f32[128,512]{1,0:T(8,128)S(1)}, u32[]{:S(2)}, u32[]{:S(2)}) collective-permute-start(f32[128,512]{1,0:T(8,128)S(1)} %get-tuple-element.34), channel_id=1, source_target_pairs={{0,2},{1,3},{2,0},{3,1},{4,6},{5,7},{6,4},{7,5},{8,10},{9,11},{10,... | collective-permute-start | bytes 786440 | tf_op jit(solution)/shard_map/ppermute | solution.py:234
  31.3 5.1 %collective-permute-start.5 = (f32[4,512]{1,0:T(4,128)S(1)}, f32[4,512]{1,0:T(4,128)S(1)}, u32[]{:S(2)}, u32[]{:S(2)}) collective-permute-start(f32[4,512]{1,0:T(4,128)S(1)} %stats.1.stat_ref), channel_id=1, source_target_pairs={{0,9},{2,11},{4,13},{6,15},{8,17},{9,0},{10,19},{11,2},{12,21},{13... | collective-permute-start | bytes 24584 | tf_op jit(solution)/shard_map/ppermute | solution.py:234
  33.3 25.8 %collective-permute-start.8 = (f32[4,512]{1,0:T(4,128)S(1)}, f32[4,512]{1,0:T(4,128)S(1)}, u32[]{:S(2)}, u32[]{:S(2)}) collective-permute-start(f32[4,512]{1,0:T(4,128)S(1)} %stats.1.stat_ref), channel_id=1, source_target_pairs={{0,5},{2,7},{5,0},{7,2},{8,13},{10,15},{13,8},{15,10},{16,21},{18,... | collective-permute-start | bytes 24584 | tf_op jit(solution)/shard_map/ppermute | solution.py:234
  57.1 11.6 %collective-permute-start.10 = (bf16[3,256,256]{2,1,0:T(8,128)(2,1)S(1)}, bf16[3,256,256]{2,1,0:T(8,128)(2,1)S(1)}, u32[]{:S(2)}, u32[]{:S(2)}) collective-permute-start(bf16[3,256,256]{2,1,0:T(8,128)(2,1)S(1)} %get-tuple-element.42), channel_id=1, source_target_pairs={{0,2},{1,3},{2,0},{3,1},{4,6},{5,7},{6,4},{7,5},{8,10},{9,11},{10,... | collective-permute-start | bytes 1179656 | tf_op jit(solution)/shard_map/ppermute | solution.py:234
  63.7 9.7 %collective-permute-start.9 = (bf16[3,256,256]{2,1,0:T(8,128)(2,1)S(1)}, bf16[3,256,256]{2,1,0:T(8,128)(2,1)S(1)}, u32[]{:S(2)}, u32[]{:S(2)}) collective-permute-start(bf16[3,256,256]{2,1,0:T(8,128)(2,1)S(1)} %get-tuple-element.37), channel_id=1, source_target_pairs={{0,2},{2,0},{5,7},{7,5},{8,10},{10,8},{13,15},{15,13},{16,18},{18,... | collective-permute-start | bytes 1179656 | tf_op jit(solution)/shard_map/ppermute | solution.py:234
  68.7 9.7 %collective-permute-start.12 = (bf16[3,256,256]{2,1,0:T(8,128)(2,1)S(1)}, bf16[3,256,256]{2,1,0:T(8,128)(2,1)S(1)}, u32[]{:S(2)}, u32[]{:S(2)}) collective-permute-start(bf16[3,256,256]{2,1,0:T(8,128)(2,1)S(1)} %get-tuple-element.50), channel_id=1, source_target_pairs={{0,2},{2,0},{5,7},{7,5},{8,10},{10,8},{13,15},{15,13},{16,18},{18,... | collective-permute-start | bytes 1179656 | tf_op jit(solution)/shard_map/ppermute | solution.py:234
  74.1 10.5 %collective-permute-start.11 = (f32[256,512]{1,0:T(8,128)S(1)}, f32[256,512]{1,0:T(8,128)S(1)}, u32[]{:S(2)}, u32[]{:S(2)}) collective-permute-start(f32[256,512]{1,0:T(8,128)S(1)} %get-tuple-element.48), channel_id=1, source_target_pairs={{0,5},{2,7},{5,0},{7,2},{8,13},{10,15},{13,8},{15,10},{16,21},{18,... | collective-permute-start | bytes 1572872 | tf_op jit(solution)/shard_map/ppermute | solution.py:234
  76.1 10.5 %collective-permute-start.14 = (f32[256,512]{1,0:T(8,128)S(1)}, f32[256,512]{1,0:T(8,128)S(1)}, u32[]{:S(2)}, u32[]{:S(2)}) collective-permute-start(f32[256,512]{1,0:T(8,128)S(1)} %get-tuple-element.44), channel_id=1, source_target_pairs={{0,9},{2,11},{4,13},{6,15},{8,17},{9,0},{10,19},{11,2},{12,21},{13... | collective-permute-start | bytes 1572872 | tf_op jit(solution)/shard_map/ppermute | solution.py:234
  79.1 8.4 %collective-permute-start.13 = (bf16[256,512]{1,0:T(8,128)(2,1)S(1)}, bf16[256,512]{1,0:T(8,128)(2,1)S(1)}, u32[]{:S(2)}, u32[]{:S(2)}) collective-permute-start(bf16[256,512]{1,0:T(8,128)(2,1)S(1)} %get-tuple-element.52), channel_id=1, source_target_pairs={{0,5},{2,7},{5,0},{7,2},{8,13},{10,15},{13,8},{15,10},{16,21},{18,... | collective-permute-start | bytes 786440 | tf_op jit(solution)/shard_map/ppermute | solution.py:234
  81.1 6.3 %collective-permute-start.15 = (bf16[256,512]{1,0:T(8,128)(2,1)S(1)}, bf16[256,512]{1,0:T(8,128)(2,1)S(1)}, u32[]{:S(2)}, u32[]{:S(2)}) collective-permute-start(bf16[256,512]{1,0:T(8,128)(2,1)S(1)} %get-tuple-element.53), channel_id=1, source_target_pairs={{0,9},{2,11},{8,17},{10,19},{13,4},{15,6},{16,25},{18,27},{21,12},... | collective-permute-start | bytes 786440 | tf_op jit(solution)/shard_map/ppermute | solution.py:234
  88.2 2.4 %collective-permute-start.16 = (f32[3,128,512]{2,1,0:T(8,128)S(1)}, f32[3,128,512]{2,1,0:T(8,128)S(1)}, u32[]{:S(2)}, u32[]{:S(2)}) collective-permute-start(f32[3,128,512]{2,1,0:T(8,128)S(1)} %get-tuple-element.55), channel_id=1, source_target_pairs={{0,1},{1,0},{2,3},{3,2},{4,5},{5,4},{6,7},{7,6},{8,9},{9,8},{10,11... | collective-permute-start | bytes 2359304 | tf_op jit(solution)/shard_map/ppermute | solution.py:234

commit v13 on v12

--- a/solution.py
+++ b/solution.py
@@ -299,7 +299,7 @@
     keep_d, send_d = call(
         lambda *refs: cross_kernel(steps, *refs), "cross_tile", (), [SMEM] + [VMEM] * 4, [VMEM] * 2, pair, [sums],
         tile_flops, 2 * bytes_block)(pos, y, w, y_stat, w_stat)
-    send_d, got_c = lax.optimization_barrier((send_d, got_c))
+    _, got_c = lax.optimization_barrier((send_d, got_c))
     got_d = send(send_d, across_active)
 
     held_c, to_z_c = call(far_strips_kernel, "far_strips", (), [SMEM] + [VMEM] * 2, [VMEM] * 2,
@@ -317,6 +317,7 @@
     to_y_d, to_z_d = near_strips("cross_strips", CROSS, keep_d, got_d)
     from_y_d, from_z_d = send(to_y_d, y_cross), send(to_z_d, z_cross_active)
 
+    from_z_c, from_y_d = lax.optimization_barrier((from_z_c, from_y_d))
     mine, sib = call(combine_kernel, "combine", (), [SMEM] + [VMEM] * 6, [VMEM] * 2, [shape(3, strip, width)] * 2)(
         pos, held_b, held_c, from_y_b, from_y_d, from_z_c, from_z_d)
     return call(finish_kernel, "finish", (), [SMEM] * 2 + [VMEM] * 4, [VMEM] * 2,

time: 93.4 us -> 94.5 us (1.012)
  waiting for transfers between devices: 28.8 us -> 29.9 us
    ppermute x17, waiting for transfers between devices: 28.8 us -> 29.9 us  [send(): return lax.ppermute(value, AXES, pairs)]
  transfers between devices with their start and end apart: 17 -> 17, of which waited for: 10 -> 7; matrix products, arithmetic and copies ran while one was open for 0% -> 0% of each run, Pallas kernels for 24% -> 23%
where the time goes in v13:
time: 94.5 us; the launch traced here: 94 us
  starting transfers between devices  34.1 us (36%)
  waiting for transfers between devices  29.9 us (32%)
  Pallas kernels  24.1 us (26%)
  local copies, waits for them, and re-layouts  4.46 us (5%)
  between operations  1.5 us (2%)
    ppermute x17, starting transfers between devices, send(): return lax.ppermute(value, AXES, pairs)  34.1 us
    ppermute x17, waiting for transfers between devices, send(): return lax.ppermute(value, AXES, pairs)  29.9 us
    pallas_call x1, Pallas kernels, body(): call(near_kernel, 'near_tile', (), [SMEM, VMEM, anywhere, VMEM, VMEM], [V...  4.64 us
    pallas_call x1, Pallas kernels, body(): call(far_kernel, 'far_tile', (), [SMEM, VMEM, anywhere, VMEM, VMEM], [VME...  4.59 us
    unnamed x6, local copies, waits for them, and re-layouts  4.37 us
    pallas_call x1, Pallas kernels, body(): call(own_kernel, 'own_tile', (steps,), [SMEM, wide, whole(4, width)], [fl...  4.31 us
    pallas_call x1, Pallas kernels, body(): call(lambda *refs: cross_kernel(steps, *refs), 'cross_tile', (), [SMEM] +...  2.96 us
  transfers between devices with their start and end apart: 17, of which 7 were waited for; matrix products, arithmetic and copies ran while one was open for 0% of the time, Pallas kernels for 23%

profile of v13, /device:TPU:0, one launch (start us, length us, event | category | flops | bytes accessed | tf_op | source)
XLA Modules:
  0.0 94.0 jit_solution(1824429437000062032)
XLA Ops:
  0.6 1.3 %collective-permute-start.4 = (bf16[4096,512]{1,0:T(8,128)(2,1)}, bf16[4096,512]{1,0:T(8,128)(2,1)}, u32[]{:S(2)}, u32[]{:S(2)}) collective-permute-start(bf16[4096,512]{1,0:T(8,128)(2,1)} %x_ref.1), channel_id=1, source_target_pairs={{1,9},{3,11},{5,13},{7,15},{8,0},{9,17},{10,2},{11,19},{12,4},{13,... | collective-permute-start | bytes 12582920 | tf_op jit(solution)/shard_map/ppermute | solution.py:234
  1.9 1.3 %collective-permute-start.7 = (bf16[4096,512]{1,0:T(8,128)(2,1)}, bf16[4096,512]{1,0:T(8,128)(2,1)}, u32[]{:S(2)}, u32[]{:S(2)}) collective-permute-start(bf16[4096,512]{1,0:T(8,128)(2,1)} %x_ref.1), channel_id=1, source_target_pairs={{1,5},{3,7},{4,0},{6,2},{9,13},{11,15},{12,8},{14,10},{17,21},{19,... | collective-permute-start | bytes 12582920 | tf_op jit(solution)/shard_map/ppermute | solution.py:234
  3.2 0.0 copy-start
  3.2 2.2 %copy-done = bf16[4096,512]{1,0:T(8,128)(2,1)S(1)} copy-done((bf16[4096,512]{1,0:T(8,128)(2,1)S(1)}, bf16[4096,512]{1,0:T(8,128)(2,1)}, u32[]{:S(2)}) %copy-start) | copy-done | bytes 4194328
  5.4 1.9 %local_stats.1.own_ref = f32[2,512]{1,0:T(2,128)S(1)} custom-call(bf16[4096,512]{1,0:T(8,128)(2,1)S(1)} %copy-done), custom_call_target="tpu_custom_call" | custom-call | flops 10485760 | bytes 4194304 | tf_op jit(solution)/shard_map/local_stats/pallas_call | solution.py:267
  7.3 10.2 %collective-permute-start.2 = (f32[2,512]{1,0:T(2,128)S(1)}, f32[2,512]{1,0:T(2,128)S(1)}, u32[]{:S(2)}, u32[]{:S(2)}) collective-permute-start(f32[2,512]{1,0:T(2,128)S(1)} %local_stats.1.own_ref), channel_id=1, source_target_pairs={{0,3},{1,2},{2,1},{3,0},{4,7},{5,6},{6,5},{7,4},{8,11},{9,10},{10,... | collective-permute-start | bytes 12296 | tf_op jit(solution)/shard_map/ppermute | solution.py:234
  17.5 0.5 collective-permute-start.1
  18.0 0.0 collective-permute-start
  18.7 0.1 stack.23.pos_ref.refs_0_
  18.7 0.0 collective-permute-done.2.cross_ref
  18.8 2.3 %collective-permute-done.1.far_ref = f32[2,512]{1,0:T(2,128)S(1)} collective-permute-done((f32[2,512]{1,0:T(2,128)S(1)}, f32[2,512]{1,0:T(2,128)S(1)}, u32[]{:S(2)}, u32[]{:S(2)}) %collective-permute-start.1) | collective-permute-done | bytes 4128 | tf_op jit(solution)/shard_map/ppermute | solution.py:234
  21.1 0.0 collective-permute-done.sib_ref
  21.1 0.6 stats.1.stat_ref
  21.7 0.0 copy-start.1
  21.7 2.2 %copy-done.1 = bf16[4096,512]{1,0:T(8,128)(2,1)S(1)} copy-done((bf16[4096,512]{1,0:T(8,128)(2,1)S(1)}, bf16[4096,512]{1,0:T(8,128)(2,1)}, u32[]{:S(2)}) %copy-start.1) | copy-done | bytes 4194328
  23.8 4.3 %own_tile.1 = (bf16[512,4096]{1,0:T(8,128)(2,1)S(1)}, f32[2,128,512]{2,1,0:T(8,128)S(1)}, f32[2,128,512]{2,1,0:T(8,128)S(1)}) custom-call(s32[5]{0:T(128)S(1)} %stack.23.pos_ref.refs_0_, bf16[4096,512]{1,0:T(8,128)(2,1)S(1)} %copy-done.1, f32[4,512]{1,0:T(4,128)S(1)} %stats.1.stat_ref), custom_call_target="tpu_custom_call" | custom-call | flops 2147483648 | bytes 8388608 | tf_op jit(solution)/shard_map/own_tile/pallas_call | solution.py:274
  28.2 0.1 collective-permute-start.3
  28.2 1.9 %collective-permute-done.3.got_ref = f32[2,128,512]{2,1,0:T(8,128)S(1)} collective-permute-done((f32[2,128,512]{2,1,0:T(8,128)S(1)}, f32[2,128,512]{2,1,0:T(8,128)S(1)}, u32[]{:S(2)}, u32[]{:S(2)}) %collective-permute-start.3) | collective-permute-done | bytes 524320 | tf_op jit(solution)/shard_map/ppermute | solution.py:234
  30.1 0.6 own_tile_strips.1
  30.8 0.6 collective-permute-start.6
  31.3 1.9 %collective-permute-start.5 = (f32[4,512]{1,0:T(4,128)S(1)}, f32[4,512]{1,0:T(4,128)S(1)}, u32[]{:S(2)}, u32[]{:S(2)}) collective-permute-start(f32[4,512]{1,0:T(4,128)S(1)} %stats.1.stat_ref), channel_id=1, source_target_pairs={{0,9},{2,11},{4,13},{6,15},{8,17},{9,0},{10,19},{11,2},{12,21},{13... | collective-permute-start | bytes 24584 | tf_op jit(solution)/shard_map/ppermute | solution.py:234
  33.3 1.9 %collective-permute-start.8 = (f32[4,512]{1,0:T(4,128)S(1)}, f32[4,512]{1,0:T(4,128)S(1)}, u32[]{:S(2)}, u32[]{:S(2)}) collective-permute-start(f32[4,512]{1,0:T(4,128)S(1)} %stats.1.stat_ref), channel_id=1, source_target_pairs={{0,5},{2,7},{5,0},{7,2},{8,13},{10,15},{13,8},{15,10},{16,21},{18,... | collective-permute-start | bytes 24584 | tf_op jit(solution)/shard_map/ppermute | solution.py:234
  35.2 1.3 %collective-permute-done.5.wstat_ref.refs_4_ = f32[4,512]{1,0:T(4,128)S(1)} collective-permute-done((f32[4,512]{1,0:T(4,128)S(1)}, f32[4,512]{1,0:T(4,128)S(1)}, u32[]{:S(2)}, u32[]{:S(2)}) %collective-permute-start.5) | collective-permute-done | bytes 8224 | tf_op jit(solution)/shard_map/ppermute | solution.py:234
  36.4 16.0 %collective-permute-done.4.w_ref = bf16[4096,512]{1,0:T(8,128)(2,1)} collective-permute-done((bf16[4096,512]{1,0:T(8,128)(2,1)}, bf16[4096,512]{1,0:T(8,128)(2,1)}, u32[]{:S(2)}, u32[]{:S(2)}) %collective-permute-start.4) | collective-permute-done | bytes 4194336 | tf_op jit(solution)/shard_map/ppermute | solution.py:234
  52.4 4.6 %far_tile.1 = (f32[3,256,256]{2,1,0:T(8,128)S(1)}, bf16[3,256,256]{2,1,0:T(8,128)(2,1)S(1)}, bf16[4096,512]{1,0:T(8,128)(2,1)S(1)}) custom-call(s32[5]{0:T(128)S(1)} %stack.23.pos_ref.refs_0_, bf16[512,4096]{1,0:T(8,128)(2,1)S(1)} %get-tuple-element.33.turned_ref, bf16[4096,512]{1,0:T(8,128)(2,1)} %collective-permute-done.4.w_ref, ...), custom_call_target="tpu_custom_call" | custom-call | flops 2147483648 | bytes 12582912 | tf_op jit(solution)/shard_map/far_tile/pallas_call | solution.py:287
  57.0 0.0 collective-permute-done.6.diag_got
  57.1 2.0 %collective-permute-start.10 = (bf16[3,256,256]{2,1,0:T(8,128)(2,1)S(1)}, bf16[3,256,256]{2,1,0:T(8,128)(2,1)S(1)}, u32[]{:S(2)}, u32[]{:S(2)}) collective-permute-start(bf16[3,256,256]{2,1,0:T(8,128)(2,1)S(1)} %get-tuple-element.43), channel_id=1, source_target_pairs={{0,2},{1,3},{2,0},{3,1},{4,6},{5,7},{6,4},{7,5},{8,10},{9,11},{10,... | collective-permute-start | bytes 1179656 | tf_op jit(solution)/shard_map/ppermute | solution.py:234
  59.1 0.0 collective-permute-done.8.ystat_ref.refs_3_
  59.1 0.0 collective-permute-done.7.y_ref
  59.1 4.6 %near_tile.1 = (f32[3,256,256]{2,1,0:T(8,128)S(1)}, bf16[3,256,256]{2,1,0:T(8,128)(2,1)S(1)}, bf16[512,4096]{1,0:T(8,128)(2,1)S(1)}) custom-call(s32[5]{0:T(128)S(1)} %stack.23.pos_ref.refs_0_, bf16[512,4096]{1,0:T(8,128)(2,1)S(1)} %get-tuple-element.33.turned_ref, bf16[4096,512]{1,0:T(8,128)(2,1)} %collective-permute-done.7.y_ref, ...), custom_call_target="tpu_custom_call" | custom-call | flops 2147483648 | bytes 12582912 | tf_op jit(solution)/shard_map/near_tile/pallas_call | solution.py:294
  63.7 2.0 %collective-permute-start.9 = (bf16[3,256,256]{2,1,0:T(8,128)(2,1)S(1)}, bf16[3,256,256]{2,1,0:T(8,128)(2,1)S(1)}, u32[]{:S(2)}, u32[]{:S(2)}) collective-permute-start(bf16[3,256,256]{2,1,0:T(8,128)(2,1)S(1)} %get-tuple-element.38), channel_id=1, source_target_pairs={{0,2},{2,0},{5,7},{7,5},{8,10},{10,8},{13,15},{15,13},{16,18},{18,... | collective-permute-start | bytes 1179656 | tf_op jit(solution)/shard_map/ppermute | solution.py:234
  65.7 3.0 %cross_tile.1 = (f32[3,256,256]{2,1,0:T(8,128)S(1)}, bf16[3,256,256]{2,1,0:T(8,128)(2,1)S(1)}) custom-call(s32[5]{0:T(128)S(1)} %stack.23.pos_ref.refs_0_, bf16[512,4096]{1,0:T(8,128)(2,1)S(1)} %get-tuple-element.40.refs_1_, bf16[4096,512]{1,0:T(8,128)(2,1)S(1)} %get-tuple-element.41.refs_2_, f32[4,512]{1,0:T(4,128)S(1)} %collective-permute-done.8.ystat_ref.refs_3_, ...), custom_call_target="tpu_custom_call" | custom-call | flops 2147483648 | bytes 8388608 | tf_op jit(solution)/shard_map/cross_tile/pallas_call | solution.py:299
  68.7 3.8 %collective-permute-start.13 = (bf16[3,256,256]{2,1,0:T(8,128)(2,1)S(1)}, bf16[3,256,256]{2,1,0:T(8,128)(2,1)S(1)}, u32[]{:S(2)}, u32[]{:S(2)}) collective-permute-start(bf16[3,256,256]{2,1,0:T(8,128)(2,1)S(1)} %get-tuple-element.42), channel_id=1, source_target_pairs={{0,2},{2,0},{5,7},{7,5},{8,10},{10,8},{13,15},{15,13},{16,18},{18,... | collective-permute-start | bytes 1179656 | tf_op jit(solution)/shard_map/ppermute | solution.py:234
  72.5 0.7 far_strips.1
  73.3 1.9 %collective-permute-start.12 = (f32[256,512]{1,0:T(8,128)S(1)}, f32[256,512]{1,0:T(8,128)S(1)}, u32[]{:S(2)}, u32[]{:S(2)}) collective-permute-start(f32[256,512]{1,0:T(8,128)S(1)} %get-tuple-element.45), channel_id=1, source_target_pairs={{0,9},{2,11},{4,13},{6,15},{8,17},{9,0},{10,19},{11,2},{12,21},{13... | collective-permute-start | bytes 1572872 | tf_op jit(solution)/shard_map/ppermute | solution.py:234
  75.2 0.7 near_strips.1
  76.0 1.9 %collective-permute-start.11 = (f32[256,512]{1,0:T(8,128)S(1)}, f32[256,512]{1,0:T(8,128)S(1)}, u32[]{:S(2)}, u32[]{:S(2)}) collective-permute-start(f32[256,512]{1,0:T(8,128)S(1)} %get-tuple-element.49), channel_id=1, source_target_pairs={{0,5},{2,7},{5,0},{7,2},{8,13},{10,15},{13,8},{15,10},{16,21},{18,... | collective-permute-start | bytes 1572872 | tf_op jit(solution)/shard_map/ppermute | solution.py:234
  77.9 0.4 collective-permute-done.13.got
  78.3 0.7 cross_strips.1
  79.1 3.2 %collective-permute-start.14 = (bf16[256,512]{1,0:T(8,128)(2,1)S(1)}, bf16[256,512]{1,0:T(8,128)(2,1)S(1)}, u32[]{:S(2)}, u32[]{:S(2)}) collective-permute-start(bf16[256,512]{1,0:T(8,128)(2,1)S(1)} %get-tuple-element.52), channel_id=1, source_target_pairs={{0,5},{2,7},{5,0},{7,2},{8,13},{10,15},{13,8},{15,10},{16,21},{18,... | collective-permute-start | bytes 786440 | tf_op jit(solution)/shard_map/ppermute | solution.py:234
  82.3 1.3 %collective-permute-start.15 = (bf16[256,512]{1,0:T(8,128)(2,1)S(1)}, bf16[256,512]{1,0:T(8,128)(2,1)S(1)}, u32[]{:S(2)}, u32[]{:S(2)}) collective-permute-start(bf16[256,512]{1,0:T(8,128)(2,1)S(1)} %get-tuple-element.55), channel_id=1, source_target_pairs={{0,9},{2,11},{8,17},{10,19},{13,4},{15,6},{16,25},{18,27},{21,12},... | collective-permute-start | bytes 786440 | tf_op jit(solution)/shard_map/ppermute | solution.py:234
  83.6 5.7 %collective-permute-done.14.from_y_d = bf16[256,512]{1,0:T(8,128)(2,1)S(1)} collective-permute-done((bf16[256,512]{1,0:T(8,128)(2,1)S(1)}, bf16[256,512]{1,0:T(8,128)(2,1)S(1)}, u32[]{:S(2)}, u32[]{:S(2)}) %collective-permute-start.14) | collective-permute-done | bytes 262176 | tf_op jit(solution)/shard_map/ppermute | solution.py:234
  89.3 0.0 collective-permute-done.15.from_z_d
  89.3 0.0 collective-permute-done.11.from_y_b
  89.3 0.7 combine.1
  90.0 0.1 collective-permute-start.16
  90.1 2.3 %collective-permute-done.16.sib = f32[3,128,512]{2,1,0:T(8,128)S(1)} collective-permute-done((f32[3,128,512]{2,1,0:T(8,128)S(1)}, f32[3,128,512]{2,1,0:T(8,128)S(1)}, u32[]{:S(2)}, u32[]{:S(2)}) %collective-permute-start.16) | collective-permute-done | bytes 786464 | tf_op jit(solution)/shard_map/ppermute | solution.py:234
  92.4 1.7 %finish.1 = (bf16[1,3,128,512]{3,2,1,0:T(8,128)(2,1)}, bf16[1,2,128,512]{3,2,1,0:T(8,128)(2,1)}) custom-call(s32[5]{0:T(128)S(1)} %stack.23.pos_ref.refs_0_, s32[1,3]{1,0:T(1,128)S(1)} %copy-done.2, f32[128,512]{1,0:T(8,128)S(1)} %get-tuple-element.32.diag_mine, f32[128,512]{1,0:T(8,128)S(1)} %collective-permute-done.6.diag_got, ...), custom_call_target="tpu_custom_call" | custom-call | tf_op jit(solution)/shard_map/finish/pallas_call | solution.py:323
  (5 shorter events, 0.0 us)
Async XLA Ops:
  0.6 51.8 %collective-permute-start.4 = (bf16[4096,512]{1,0:T(8,128)(2,1)}, bf16[4096,512]{1,0:T(8,128)(2,1)}, u32[]{:S(2)}, u32[]{:S(2)}) collective-permute-start(bf16[4096,512]{1,0:T(8,128)(2,1)} %x_ref.1), channel_id=1, source_target_pairs={{1,9},{3,11},{5,13},{7,15},{8,0},{9,17},{10,2},{11,19},{12,4},{13,... | collective-permute-start | bytes 12582920 | tf_op jit(solution)/shard_map/ppermute | solution.py:234
  1.9 57.1 %collective-permute-start.7 = (bf16[4096,512]{1,0:T(8,128)(2,1)}, bf16[4096,512]{1,0:T(8,128)(2,1)}, u32[]{:S(2)}, u32[]{:S(2)}) collective-permute-start(bf16[4096,512]{1,0:T(8,128)(2,1)} %x_ref.1), channel_id=1, source_target_pairs={{1,5},{3,7},{4,0},{6,2},{9,13},{11,15},{12,8},{14,10},{17,21},{19,... | collective-permute-start | bytes 12582920 | tf_op jit(solution)/shard_map/ppermute | solution.py:234
  3.2 2.2 %copy-start = (bf16[4096,512]{1,0:T(8,128)(2,1)S(1)}, bf16[4096,512]{1,0:T(8,128)(2,1)}, u32[]{:S(2)}) copy-start(bf16[4096,512]{1,0:T(8,128)(2,1)} %x_ref.1) | copy-start | bytes 12582916
  5.4 15.7 %copy-start.2 = (s32[1,3]{1,0:T(1,128)S(1)}, s32[1,3]{1,0:T(1,128)}, u32[]{:S(2)}) copy-start(s32[1,3]{1,0:T(1,128)} %offsets_ref.3) | copy-start | bytes 40
  7.3 11.5 %collective-permute-start.2 = (f32[2,512]{1,0:T(2,128)S(1)}, f32[2,512]{1,0:T(2,128)S(1)}, u32[]{:S(2)}, u32[]{:S(2)}) collective-permute-start(f32[2,512]{1,0:T(2,128)S(1)} %local_stats.1.own_ref), channel_id=1, source_target_pairs={{0,3},{1,2},{2,1},{3,0},{4,7},{5,6},{6,5},{7,4},{8,11},{9,10},{10,... | collective-permute-start | bytes 12296 | tf_op jit(solution)/shard_map/ppermute | solution.py:234
  17.5 3.6 %collective-permute-start.1 = (f32[2,512]{1,0:T(2,128)S(1)}, f32[2,512]{1,0:T(2,128)S(1)}, u32[]{:S(2)}, u32[]{:S(2)}) collective-permute-start(f32[2,512]{1,0:T(2,128)S(1)} %local_stats.1.own_ref), channel_id=1, source_target_pairs={{0,2},{1,3},{2,0},{3,1},{4,6},{5,7},{6,4},{7,5},{8,10},{9,11},{10,... | collective-permute-start | bytes 12296 | tf_op jit(solution)/shard_map/ppermute | solution.py:234
  18.0 3.1 %collective-permute-start = (f32[2,512]{1,0:T(2,128)S(1)}, f32[2,512]{1,0:T(2,128)S(1)}, u32[]{:S(2)}, u32[]{:S(2)}) collective-permute-start(f32[2,512]{1,0:T(2,128)S(1)} %local_stats.1.own_ref), channel_id=1, source_target_pairs={{0,1},{1,0},{2,3},{3,2},{4,5},{5,4},{6,7},{7,6},{8,9},{9,8},{10,11... | collective-permute-start | bytes 12296 | tf_op jit(solution)/shard_map/ppermute | solution.py:234
  21.7 2.2 %copy-start.1 = (bf16[4096,512]{1,0:T(8,128)(2,1)S(1)}, bf16[4096,512]{1,0:T(8,128)(2,1)}, u32[]{:S(2)}) copy-start(bf16[4096,512]{1,0:T(8,128)(2,1)} %x_ref.1) | copy-start | bytes 12582916
  28.2 2.0 %collective-permute-start.3 = (f32[2,128,512]{2,1,0:T(8,128)S(1)}, f32[2,128,512]{2,1,0:T(8,128)S(1)}, u32[]{:S(2)}, u32[]{:S(2)}) collective-permute-start(f32[2,128,512]{2,1,0:T(8,128)S(1)} %get-tuple-element.31), channel_id=1, source_target_pairs={{0,1},{1,0},{2,3},{3,2},{4,5},{5,4},{6,7},{7,6},{8,9},{9,8},{10,11... | collective-permute-start | bytes 1572872 | tf_op jit(solution)/shard_map/ppermute | solution.py:234
  30.8 26.3 %collective-permute-start.6 = (f32[128,512]{1,0:T(8,128)S(1)}, f32[128,512]{1,0:T(8,128)S(1)}, u32[]{:S(2)}, u32[]{:S(2)}) collective-permute-start(f32[128,512]{1,0:T(8,128)S(1)} %get-tuple-element.35), channel_id=1, source_target_pairs={{0,2},{1,3},{2,0},{3,1},{4,6},{5,7},{6,4},{7,5},{8,10},{9,11},{10,... | collective-permute-start | bytes 786440 | tf_op jit(solution)/shard_map/ppermute | solution.py:234
  31.3 5.1 %collective-permute-start.5 = (f32[4,512]{1,0:T(4,128)S(1)}, f32[4,512]{1,0:T(4,128)S(1)}, u32[]{:S(2)}, u32[]{:S(2)}) collective-permute-start(f32[4,512]{1,0:T(4,128)S(1)} %stats.1.stat_ref), channel_id=1, source_target_pairs={{0,9},{2,11},{4,13},{6,15},{8,17},{9,0},{10,19},{11,2},{12,21},{13... | collective-permute-start | bytes 24584 | tf_op jit(solution)/shard_map/ppermute | solution.py:234
  33.3 25.8 %collective-permute-start.8 = (f32[4,512]{1,0:T(4,128)S(1)}, f32[4,512]{1,0:T(4,128)S(1)}, u32[]{:S(2)}, u32[]{:S(2)}) collective-permute-start(f32[4,512]{1,0:T(4,128)S(1)} %stats.1.stat_ref), channel_id=1, source_target_pairs={{0,5},{2,7},{5,0},{7,2},{8,13},{10,15},{13,8},{15,10},{16,21},{18,... | collective-permute-start | bytes 24584 | tf_op jit(solution)/shard_map/ppermute | solution.py:234
  57.1 15.5 %collective-permute-start.10 = (bf16[3,256,256]{2,1,0:T(8,128)(2,1)S(1)}, bf16[3,256,256]{2,1,0:T(8,128)(2,1)S(1)}, u32[]{:S(2)}, u32[]{:S(2)}) collective-permute-start(bf16[3,256,256]{2,1,0:T(8,128)(2,1)S(1)} %get-tuple-element.43), channel_id=1, source_target_pairs={{0,2},{1,3},{2,0},{3,1},{4,6},{5,7},{6,4},{7,5},{8,10},{9,11},{10,... | collective-permute-start | bytes 1179656 | tf_op jit(solution)/shard_map/ppermute | solution.py:234
  63.7 11.5 %collective-permute-start.9 = (bf16[3,256,256]{2,1,0:T(8,128)(2,1)S(1)}, bf16[3,256,256]{2,1,0:T(8,128)(2,1)S(1)}, u32[]{:S(2)}, u32[]{:S(2)}) collective-permute-start(bf16[3,256,256]{2,1,0:T(8,128)(2,1)S(1)} %get-tuple-element.38), channel_id=1, source_target_pairs={{0,2},{2,0},{5,7},{7,5},{8,10},{10,8},{13,15},{15,13},{16,18},{18,... | collective-permute-start | bytes 1179656 | tf_op jit(solution)/shard_map/ppermute | solution.py:234
  68.7 9.7 %collective-permute-start.13 = (bf16[3,256,256]{2,1,0:T(8,128)(2,1)S(1)}, bf16[3,256,256]{2,1,0:T(8,128)(2,1)S(1)}, u32[]{:S(2)}, u32[]{:S(2)}) collective-permute-start(bf16[3,256,256]{2,1,0:T(8,128)(2,1)S(1)} %get-tuple-element.42), channel_id=1, source_target_pairs={{0,2},{2,0},{5,7},{7,5},{8,10},{10,8},{13,15},{15,13},{16,18},{18,... | collective-permute-start | bytes 1179656 | tf_op jit(solution)/shard_map/ppermute | solution.py:234
  73.3 16.0 %collective-permute-start.12 = (f32[256,512]{1,0:T(8,128)S(1)}, f32[256,512]{1,0:T(8,128)S(1)}, u32[]{:S(2)}, u32[]{:S(2)}) collective-permute-start(f32[256,512]{1,0:T(8,128)S(1)} %get-tuple-element.45), channel_id=1, source_target_pairs={{0,9},{2,11},{4,13},{6,15},{8,17},{9,0},{10,19},{11,2},{12,21},{13... | collective-permute-start | bytes 1572872 | tf_op jit(solution)/shard_map/ppermute | solution.py:234
  76.0 13.3 %collective-permute-start.11 = (f32[256,512]{1,0:T(8,128)S(1)}, f32[256,512]{1,0:T(8,128)S(1)}, u32[]{:S(2)}, u32[]{:S(2)}) collective-permute-start(f32[256,512]{1,0:T(8,128)S(1)} %get-tuple-element.49), channel_id=1, source_target_pairs={{0,5},{2,7},{5,0},{7,2},{8,13},{10,15},{13,8},{15,10},{16,21},{18,... | collective-permute-start | bytes 1572872 | tf_op jit(solution)/shard_map/ppermute | solution.py:234
  79.1 10.2 %collective-permute-start.14 = (bf16[256,512]{1,0:T(8,128)(2,1)S(1)}, bf16[256,512]{1,0:T(8,128)(2,1)S(1)}, u32[]{:S(2)}, u32[]{:S(2)}) collective-permute-start(bf16[256,512]{1,0:T(8,128)(2,1)S(1)} %get-tuple-element.52), channel_id=1, source_target_pairs={{0,5},{2,7},{5,0},{7,2},{8,13},{10,15},{13,8},{15,10},{16,21},{18,... | collective-permute-start | bytes 786440 | tf_op jit(solution)/shard_map/ppermute | solution.py:234
  82.3 7.0 %collective-permute-start.15 = (bf16[256,512]{1,0:T(8,128)(2,1)S(1)}, bf16[256,512]{1,0:T(8,128)(2,1)S(1)}, u32[]{:S(2)}, u32[]{:S(2)}) collective-permute-start(bf16[256,512]{1,0:T(8,128)(2,1)S(1)} %get-tuple-element.55), channel_id=1, source_target_pairs={{0,9},{2,11},{8,17},{10,19},{13,4},{15,6},{16,25},{18,27},{21,12},... | collective-permute-start | bytes 786440 | tf_op jit(solution)/shard_map/ppermute | solution.py:234
  90.0 2.4 %collective-permute-start.16 = (f32[3,128,512]{2,1,0:T(8,128)S(1)}, f32[3,128,512]{2,1,0:T(8,128)S(1)}, u32[]{:S(2)}, u32[]{:S(2)}) collective-permute-start(f32[3,128,512]{2,1,0:T(8,128)S(1)} %get-tuple-element.57), channel_id=1, source_target_pairs={{0,1},{1,0},{2,3},{3,2},{4,5},{5,4},{6,7},{7,6},{8,9},{9,8},{10,11... | collective-permute-start | bytes 2359304 | tf_op jit(solution)/shard_map/ppermute | solution.py:234

commit v14 on v13

--- a/solution.py
+++ b/solution.py
@@ -122,11 +122,18 @@
 
 
 def far_kernel(pos_ref, turned_ref, w_ref, stat_ref, wstat_ref, keep_ref, send_ref, w_out, acc, parts, sems):
-    for k, (rows, wait) in enumerate(fetched(w_ref, parts, sems)):
+    chunks = fetched(w_ref, parts, sems)
+
+    def ready(k):
+        rows, wait = chunks[k]
         wait()
-        w = standardized(parts[k], wstat_ref)
-        w_out[rows, :] = w
-        part = dot(turned_ref[:, rows], w)
+        w_out[rows, :] = standardized(parts[k], wstat_ref)
+
+    ready(0)
+    for k, (rows, _) in enumerate(chunks):
+        if k + 1 < len(chunks):
+            ready(k + 1)
+        part = dot(turned_ref[:, rows], w_out[rows, :])
         acc[...] = part if k == 0 else acc[...] + part
     listed = jnp.where(pos_ref[2] == 0, stat_ref[3:4, :], wstat_ref[3:4, :])
     put_quarters(pos_ref[0], acc, listed * (1.0 / pos_ref[4].astype(F32)), keep_ref, send_ref)
@@ -135,11 +142,19 @@
 def near_kernel(pos_ref, turned_ref, y_ref, stat_ref, ystat_ref, keep_ref, send_ref, y_out, acc, parts, sems):
     @pl.when(pos_ref[1] == 1)
     def _():
-        for k, (rows, wait) in enumerate(fetched(y_ref, parts, sems)):
+        chunks = fetched(y_ref, parts, sems)
+
+        def ready(k):
+            rows, wait = chunks[k]
             wait()
-            y = standardized(parts[k], ystat_ref)
-            y_out[:, rows] = y.T
-            part = dot(turned_ref[:, rows], y)
+            parts[k] = standardized(parts[k], ystat_ref)
+            y_out[:, rows] = parts[k].T
+
+        ready(0)
+        for k, (rows, _) in enumerate(chunks):
+            if k + 1 < len(chunks):
+                ready(k + 1)
+            part = dot(turned_ref[:, rows], parts[k])
             acc[...] = part if k == 0 else acc[...] + part
         listed = jnp.where(pos_ref[2] == 0, stat_ref[2:3, :], ystat_ref[2:3, :])
         put_quarters(pos_ref[0], acc, listed * (1.0 / pos_ref[4].astype(F32)), keep_ref, send_ref)
@@ -317,7 +332,6 @@
     to_y_d, to_z_d = near_strips("cross_strips", CROSS, keep_d, got_d)
     from_y_d, from_z_d = send(to_y_d, y_cross), send(to_z_d, z_cross_active)
 
-    from_z_c, from_y_d = lax.optimization_barrier((from_z_c, from_y_d))
     mine, sib = call(combine_kernel, "combine", (), [SMEM] + [VMEM] * 6, [VMEM] * 2, [shape(3, strip, width)] * 2)(
         pos, held_b, held_c, from_y_b, from_y_d, from_z_c, from_z_d)
     return call(finish_kernel, "finish", (), [SMEM] * 2 + [VMEM] * 4, [VMEM] * 2,

time: 94.5 us -> 94.6 us (level)
  Pallas kernels: 24.1 us -> 25.3 us
  waiting for transfers between devices: 29.9 us -> 28.8 us
    ppermute x17, waiting for transfers between devices: 29.9 us -> 28.8 us  [send(): return lax.ppermute(value, AXES, pairs)]
    pallas_call x1, Pallas kernels: 4.59 us -> 5.59 us  [body(): call(far_kernel, 'far_tile', (), [SMEM, VMEM, anywhere, VMEM, VMEM], [VME...]
  transfers between devices with their start and end apart: 17 -> 17, of which waited for: 7 -> 8; matrix products, arithmetic and copies ran while one was open for 0% -> 0% of each run, Pallas kernels for 23% -> 25%
where the time goes in v14:
time: 94.6 us; the launch traced here: 93.4 us
  starting transfers between devices  33.3 us (35%)
  waiting for transfers between devices  28.8 us (30%)
  Pallas kernels  25.3 us (27%)
  local copies, waits for them, and re-layouts  4.46 us (5%)
  between operations  1.49 us (2%)
    ppermute x17, starting transfers between devices, send(): return lax.ppermute(value, AXES, pairs)  33.3 us
    ppermute x17, waiting for transfers between devices, send(): return lax.ppermute(value, AXES, pairs)  28.8 us
    pallas_call x1, Pallas kernels, body(): call(far_kernel, 'far_tile', (), [SMEM, VMEM, anywhere, VMEM, VMEM], [VME...  5.59 us
    pallas_call x1, Pallas kernels, body(): call(near_kernel, 'near_tile', (), [SMEM, VMEM, anywhere, VMEM, VMEM], [V...  4.85 us
    unnamed x6, local copies, waits for them, and re-layouts  4.37 us
    pallas_call x1, Pallas kernels, body(): call(own_kernel, 'own_tile', (steps,), [SMEM, wide, whole(4, width)], [fl...  4.31 us
    pallas_call x1, Pallas kernels, body(): call(lambda *refs: cross_kernel(steps, *refs), 'cross_tile', (), [SMEM] +...  2.96 us
  transfers between devices with their start and end apart: 17, of which 8 were waited for; matrix products, arithmetic and copies ran while one was open for 0% of the time, Pallas kernels for 25%

profile of v14, /device:TPU:0, one launch (start us, length us, event | category | flops | bytes accessed | tf_op | source)
XLA Modules:
  0.0 93.4 jit_solution(15455075475596169613)
XLA Ops:
  0.6 1.3 %collective-permute-start.4 = (bf16[4096,512]{1,0:T(8,128)(2,1)}, bf16[4096,512]{1,0:T(8,128)(2,1)}, u32[]{:S(2)}, u32[]{:S(2)}) collective-permute-start(bf16[4096,512]{1,0:T(8,128)(2,1)} %x_ref.1), channel_id=1, source_target_pairs={{1,9},{3,11},{5,13},{7,15},{8,0},{9,17},{10,2},{11,19},{12,4},{13,... | collective-permute-start | bytes 12582920 | tf_op jit(solution)/shard_map/ppermute | solution.py:249
  1.9 1.3 %collective-permute-start.7 = (bf16[4096,512]{1,0:T(8,128)(2,1)}, bf16[4096,512]{1,0:T(8,128)(2,1)}, u32[]{:S(2)}, u32[]{:S(2)}) collective-permute-start(bf16[4096,512]{1,0:T(8,128)(2,1)} %x_ref.1), channel_id=1, source_target_pairs={{1,5},{3,7},{4,0},{6,2},{9,13},{11,15},{12,8},{14,10},{17,21},{19,... | collective-permute-start | bytes 12582920 | tf_op jit(solution)/shard_map/ppermute | solution.py:249
  3.2 0.0 copy-start
  3.2 2.2 %copy-done = bf16[4096,512]{1,0:T(8,128)(2,1)S(1)} copy-done((bf16[4096,512]{1,0:T(8,128)(2,1)S(1)}, bf16[4096,512]{1,0:T(8,128)(2,1)}, u32[]{:S(2)}) %copy-start) | copy-done | bytes 4194328
  5.4 1.9 %local_stats.1.own_ref = f32[2,512]{1,0:T(2,128)S(1)} custom-call(bf16[4096,512]{1,0:T(8,128)(2,1)S(1)} %copy-done), custom_call_target="tpu_custom_call" | custom-call | flops 10485760 | bytes 4194304 | tf_op jit(solution)/shard_map/local_stats/pallas_call | solution.py:282
  7.3 10.2 %collective-permute-start.2 = (f32[2,512]{1,0:T(2,128)S(1)}, f32[2,512]{1,0:T(2,128)S(1)}, u32[]{:S(2)}, u32[]{:S(2)}) collective-permute-start(f32[2,512]{1,0:T(2,128)S(1)} %local_stats.1.own_ref), channel_id=1, source_target_pairs={{0,3},{1,2},{2,1},{3,0},{4,7},{5,6},{6,5},{7,4},{8,11},{9,10},{10,... | collective-permute-start | bytes 12296 | tf_op jit(solution)/shard_map/ppermute | solution.py:249
  17.5 0.5 collective-permute-start.1
  18.0 0.0 collective-permute-start
  18.7 0.1 stack.23.pos_ref.refs_0_
  18.7 0.0 collective-permute-done.2.cross_ref
  18.8 2.3 %collective-permute-done.1.far_ref = f32[2,512]{1,0:T(2,128)S(1)} collective-permute-done((f32[2,512]{1,0:T(2,128)S(1)}, f32[2,512]{1,0:T(2,128)S(1)}, u32[]{:S(2)}, u32[]{:S(2)}) %collective-permute-start.1) | collective-permute-done | bytes 4128 | tf_op jit(solution)/shard_map/ppermute | solution.py:249
  21.1 0.0 collective-permute-done.sib_ref
  21.1 0.6 stats.1.stat_ref
  21.7 0.0 copy-start.1
  21.7 2.2 %copy-done.1 = bf16[4096,512]{1,0:T(8,128)(2,1)S(1)} copy-done((bf16[4096,512]{1,0:T(8,128)(2,1)S(1)}, bf16[4096,512]{1,0:T(8,128)(2,1)}, u32[]{:S(2)}) %copy-start.1) | copy-done | bytes 4194328
  23.8 4.3 %own_tile.1 = (bf16[512,4096]{1,0:T(8,128)(2,1)S(1)}, f32[2,128,512]{2,1,0:T(8,128)S(1)}, f32[2,128,512]{2,1,0:T(8,128)S(1)}) custom-call(s32[5]{0:T(128)S(1)} %stack.23.pos_ref.refs_0_, bf16[4096,512]{1,0:T(8,128)(2,1)S(1)} %copy-done.1, f32[4,512]{1,0:T(4,128)S(1)} %stats.1.stat_ref), custom_call_target="tpu_custom_call" | custom-call | flops 2147483648 | bytes 8388608 | tf_op jit(solution)/shard_map/own_tile/pallas_call | solution.py:289
  28.2 0.1 collective-permute-start.3
  28.2 1.9 %collective-permute-done.3.got_ref = f32[2,128,512]{2,1,0:T(8,128)S(1)} collective-permute-done((f32[2,128,512]{2,1,0:T(8,128)S(1)}, f32[2,128,512]{2,1,0:T(8,128)S(1)}, u32[]{:S(2)}, u32[]{:S(2)}) %collective-permute-start.3) | collective-permute-done | bytes 524320 | tf_op jit(solution)/shard_map/ppermute | solution.py:249
  30.1 0.6 own_tile_strips.1
  30.8 0.6 collective-permute-start.6
  31.3 1.9 %collective-permute-start.5 = (f32[4,512]{1,0:T(4,128)S(1)}, f32[4,512]{1,0:T(4,128)S(1)}, u32[]{:S(2)}, u32[]{:S(2)}) collective-permute-start(f32[4,512]{1,0:T(4,128)S(1)} %stats.1.stat_ref), channel_id=1, source_target_pairs={{0,9},{2,11},{4,13},{6,15},{8,17},{9,0},{10,19},{11,2},{12,21},{13... | collective-permute-start | bytes 24584 | tf_op jit(solution)/shard_map/ppermute | solution.py:249
  33.3 1.9 %collective-permute-start.8 = (f32[4,512]{1,0:T(4,128)S(1)}, f32[4,512]{1,0:T(4,128)S(1)}, u32[]{:S(2)}, u32[]{:S(2)}) collective-permute-start(f32[4,512]{1,0:T(4,128)S(1)} %stats.1.stat_ref), channel_id=1, source_target_pairs={{0,5},{2,7},{5,0},{7,2},{8,13},{10,15},{13,8},{15,10},{16,21},{18,... | collective-permute-start | bytes 24584 | tf_op jit(solution)/shard_map/ppermute | solution.py:249
  35.2 1.3 %collective-permute-done.5.wstat_ref.refs_4_ = f32[4,512]{1,0:T(4,128)S(1)} collective-permute-done((f32[4,512]{1,0:T(4,128)S(1)}, f32[4,512]{1,0:T(4,128)S(1)}, u32[]{:S(2)}, u32[]{:S(2)}) %collective-permute-start.5) | collective-permute-done | bytes 8224 | tf_op jit(solution)/shard_map/ppermute | solution.py:249
  36.4 16.0 %collective-permute-done.4.w_ref = bf16[4096,512]{1,0:T(8,128)(2,1)} collective-permute-done((bf16[4096,512]{1,0:T(8,128)(2,1)}, bf16[4096,512]{1,0:T(8,128)(2,1)}, u32[]{:S(2)}, u32[]{:S(2)}) %collective-permute-start.4) | collective-permute-done | bytes 4194336 | tf_op jit(solution)/shard_map/ppermute | solution.py:249
  52.4 5.6 %far_tile.1 = (f32[3,256,256]{2,1,0:T(8,128)S(1)}, bf16[3,256,256]{2,1,0:T(8,128)(2,1)S(1)}, bf16[4096,512]{1,0:T(8,128)(2,1)S(1)}) custom-call(s32[5]{0:T(128)S(1)} %stack.23.pos_ref.refs_0_, bf16[512,4096]{1,0:T(8,128)(2,1)S(1)} %get-tuple-element.31.turned_ref, bf16[4096,512]{1,0:T(8,128)(2,1)} %collective-permute-done.4.w_ref, ...), custom_call_target="tpu_custom_call" | custom-call | flops 2147483648 | bytes 12582912 | tf_op jit(solution)/shard_map/far_tile/pallas_call | solution.py:302
  58.0 0.0 collective-permute-done.6.diag_got
  58.1 2.0 %collective-permute-start.10 = (bf16[3,256,256]{2,1,0:T(8,128)(2,1)S(1)}, bf16[3,256,256]{2,1,0:T(8,128)(2,1)S(1)}, u32[]{:S(2)}, u32[]{:S(2)}) collective-permute-start(bf16[3,256,256]{2,1,0:T(8,128)(2,1)S(1)} %get-tuple-element.41), channel_id=1, source_target_pairs={{0,2},{1,3},{2,0},{3,1},{4,6},{5,7},{6,4},{7,5},{8,10},{9,11},{10,... | collective-permute-start | bytes 1179656 | tf_op jit(solution)/shard_map/ppermute | solution.py:249
  60.0 4.8 %near_tile.1 = (f32[3,256,256]{2,1,0:T(8,128)S(1)}, bf16[3,256,256]{2,1,0:T(8,128)(2,1)S(1)}, bf16[512,4096]{1,0:T(8,128)(2,1)S(1)}) custom-call(s32[5]{0:T(128)S(1)} %stack.23.pos_ref.refs_0_, bf16[512,4096]{1,0:T(8,128)(2,1)S(1)} %get-tuple-element.31.turned_ref, bf16[4096,512]{1,0:T(8,128)(2,1)} %collective-permute-done.7.y_ref, ...), custom_call_target="tpu_custom_call" | custom-call | flops 2147483648 | bytes 12582912 | tf_op jit(solution)/shard_map/near_tile/pallas_call | solution.py:309
  64.9 2.0 %collective-permute-start.9 = (bf16[3,256,256]{2,1,0:T(8,128)(2,1)S(1)}, bf16[3,256,256]{2,1,0:T(8,128)(2,1)S(1)}, u32[]{:S(2)}, u32[]{:S(2)}) collective-permute-start(bf16[3,256,256]{2,1,0:T(8,128)(2,1)S(1)} %get-tuple-element.36), channel_id=1, source_target_pairs={{0,2},{2,0},{5,7},{7,5},{8,10},{10,8},{13,15},{15,13},{16,18},{18,... | collective-permute-start | bytes 1179656 | tf_op jit(solution)/shard_map/ppermute | solution.py:249
  66.9 3.0 %cross_tile.1 = (f32[3,256,256]{2,1,0:T(8,128)S(1)}, bf16[3,256,256]{2,1,0:T(8,128)(2,1)S(1)}) custom-call(s32[5]{0:T(128)S(1)} %stack.23.pos_ref.refs_0_, bf16[512,4096]{1,0:T(8,128)(2,1)S(1)} %get-tuple-element.38.refs_1_, bf16[4096,512]{1,0:T(8,128)(2,1)S(1)} %get-tuple-element.39.refs_2_, f32[4,512]{1,0:T(4,128)S(1)} %collective-permute-done.8.ystat_ref.refs_3_, ...), custom_call_target="tpu_custom_call" | custom-call | flops 2147483648 | bytes 8388608 | tf_op jit(solution)/shard_map/cross_tile/pallas_call | solution.py:314
  69.9 3.8 %collective-permute-start.12 = (bf16[3,256,256]{2,1,0:T(8,128)(2,1)S(1)}, bf16[3,256,256]{2,1,0:T(8,128)(2,1)S(1)}, u32[]{:S(2)}, u32[]{:S(2)}) collective-permute-start(bf16[3,256,256]{2,1,0:T(8,128)(2,1)S(1)} %get-tuple-element.40), channel_id=1, source_target_pairs={{0,2},{2,0},{5,7},{7,5},{8,10},{10,8},{13,15},{15,13},{16,18},{18,... | collective-permute-start | bytes 1179656 | tf_op jit(solution)/shard_map/ppermute | solution.py:249
  73.7 0.7 far_strips.1
  74.5 0.1 collective-permute-done.9.got
  74.6 0.7 near_strips.1
  75.3 1.9 %collective-permute-start.11 = (f32[256,512]{1,0:T(8,128)S(1)}, f32[256,512]{1,0:T(8,128)S(1)}, u32[]{:S(2)}, u32[]{:S(2)}) collective-permute-start(f32[256,512]{1,0:T(8,128)S(1)} %get-tuple-element.47), channel_id=1, source_target_pairs={{0,5},{2,7},{5,0},{7,2},{8,13},{10,15},{13,8},{15,10},{16,21},{18,... | collective-permute-start | bytes 1572872 | tf_op jit(solution)/shard_map/ppermute | solution.py:249
  77.3 1.9 %collective-permute-start.14 = (f32[256,512]{1,0:T(8,128)S(1)}, f32[256,512]{1,0:T(8,128)S(1)}, u32[]{:S(2)}, u32[]{:S(2)}) collective-permute-start(f32[256,512]{1,0:T(8,128)S(1)} %get-tuple-element.43), channel_id=1, source_target_pairs={{0,9},{2,11},{4,13},{6,15},{8,17},{9,0},{10,19},{11,2},{12,21},{13... | collective-permute-start | bytes 1572872 | tf_op jit(solution)/shard_map/ppermute | solution.py:249
  79.2 0.4 collective-permute-done.12.got
  79.6 0.7 cross_strips.1
  80.3 2.1 %collective-permute-start.13 = (bf16[256,512]{1,0:T(8,128)(2,1)S(1)}, bf16[256,512]{1,0:T(8,128)(2,1)S(1)}, u32[]{:S(2)}, u32[]{:S(2)}) collective-permute-start(bf16[256,512]{1,0:T(8,128)(2,1)S(1)} %get-tuple-element.50), channel_id=1, source_target_pairs={{0,5},{2,7},{5,0},{7,2},{8,13},{10,15},{13,8},{15,10},{16,21},{18,... | collective-permute-start | bytes 786440 | tf_op jit(solution)/shard_map/ppermute | solution.py:249
  82.3 1.8 %collective-permute-start.15 = (bf16[256,512]{1,0:T(8,128)(2,1)S(1)}, bf16[256,512]{1,0:T(8,128)(2,1)S(1)}, u32[]{:S(2)}, u32[]{:S(2)}) collective-permute-start(bf16[256,512]{1,0:T(8,128)(2,1)S(1)} %get-tuple-element.51), channel_id=1, source_target_pairs={{0,9},{2,11},{8,17},{10,19},{13,4},{15,6},{16,25},{18,27},{21,12},... | collective-permute-start | bytes 786440 | tf_op jit(solution)/shard_map/ppermute | solution.py:249
  84.1 4.5 %collective-permute-done.13.from_y_d = bf16[256,512]{1,0:T(8,128)(2,1)S(1)} collective-permute-done((bf16[256,512]{1,0:T(8,128)(2,1)S(1)}, bf16[256,512]{1,0:T(8,128)(2,1)S(1)}, u32[]{:S(2)}, u32[]{:S(2)}) %collective-permute-start.13) | collective-permute-done | bytes 262176 | tf_op jit(solution)/shard_map/ppermute | solution.py:249
  88.6 0.0 collective-permute-done.15.from_z_d
  88.7 0.0 collective-permute-done.11.from_y_b
  88.7 0.0 collective-permute-done.14.from_z_c
  88.7 0.7 combine.1
  89.4 0.1 collective-permute-start.16
  89.5 2.3 %collective-permute-done.16.sib = f32[3,128,512]{2,1,0:T(8,128)S(1)} collective-permute-done((f32[3,128,512]{2,1,0:T(8,128)S(1)}, f32[3,128,512]{2,1,0:T(8,128)S(1)}, u32[]{:S(2)}, u32[]{:S(2)}) %collective-permute-start.16) | collective-permute-done | bytes 786464 | tf_op jit(solution)/shard_map/ppermute | solution.py:249
  91.7 1.7 %finish.1 = (bf16[1,3,128,512]{3,2,1,0:T(8,128)(2,1)}, bf16[1,2,128,512]{3,2,1,0:T(8,128)(2,1)}) custom-call(s32[5]{0:T(128)S(1)} %stack.23.pos_ref.refs_0_, s32[1,3]{1,0:T(1,128)S(1)} %copy-done.2, f32[128,512]{1,0:T(8,128)S(1)} %get-tuple-element.30.diag_mine, f32[128,512]{1,0:T(8,128)S(1)} %collective-permute-done.6.diag_got, ...), custom_call_target="tpu_custom_call" | custom-call | tf_op jit(solution)/shard_map/finish/pallas_call | solution.py:337
  (5 shorter events, 0.0 us)
Async XLA Ops:
  0.6 51.8 %collective-permute-start.4 = (bf16[4096,512]{1,0:T(8,128)(2,1)}, bf16[4096,512]{1,0:T(8,128)(2,1)}, u32[]{:S(2)}, u32[]{:S(2)}) collective-permute-start(bf16[4096,512]{1,0:T(8,128)(2,1)} %x_ref.1), channel_id=1, source_target_pairs={{1,9},{3,11},{5,13},{7,15},{8,0},{9,17},{10,2},{11,19},{12,4},{13,... | collective-permute-start | bytes 12582920 | tf_op jit(solution)/shard_map/ppermute | solution.py:249
  1.9 58.1 %collective-permute-start.7 = (bf16[4096,512]{1,0:T(8,128)(2,1)}, bf16[4096,512]{1,0:T(8,128)(2,1)}, u32[]{:S(2)}, u32[]{:S(2)}) collective-permute-start(bf16[4096,512]{1,0:T(8,128)(2,1)} %x_ref.1), channel_id=1, source_target_pairs={{1,5},{3,7},{4,0},{6,2},{9,13},{11,15},{12,8},{14,10},{17,21},{19,... | collective-permute-start | bytes 12582920 | tf_op jit(solution)/shard_map/ppermute | solution.py:249
  3.2 2.2 %copy-start = (bf16[4096,512]{1,0:T(8,128)(2,1)S(1)}, bf16[4096,512]{1,0:T(8,128)(2,1)}, u32[]{:S(2)}) copy-start(bf16[4096,512]{1,0:T(8,128)(2,1)} %x_ref.1) | copy-start | bytes 12582916
  5.4 15.7 %copy-start.2 = (s32[1,3]{1,0:T(1,128)S(1)}, s32[1,3]{1,0:T(1,128)}, u32[]{:S(2)}) copy-start(s32[1,3]{1,0:T(1,128)} %offsets_ref.3) | copy-start | bytes 40
  7.3 11.5 %collective-permute-start.2 = (f32[2,512]{1,0:T(2,128)S(1)}, f32[2,512]{1,0:T(2,128)S(1)}, u32[]{:S(2)}, u32[]{:S(2)}) collective-permute-start(f32[2,512]{1,0:T(2,128)S(1)} %local_stats.1.own_ref), channel_id=1, source_target_pairs={{0,3},{1,2},{2,1},{3,0},{4,7},{5,6},{6,5},{7,4},{8,11},{9,10},{10,... | collective-permute-start | bytes 12296 | tf_op jit(solution)/shard_map/ppermute | solution.py:249
  17.5 3.6 %collective-permute-start.1 = (f32[2,512]{1,0:T(2,128)S(1)}, f32[2,512]{1,0:T(2,128)S(1)}, u32[]{:S(2)}, u32[]{:S(2)}) collective-permute-start(f32[2,512]{1,0:T(2,128)S(1)} %local_stats.1.own_ref), channel_id=1, source_target_pairs={{0,2},{1,3},{2,0},{3,1},{4,6},{5,7},{6,4},{7,5},{8,10},{9,11},{10,... | collective-permute-start | bytes 12296 | tf_op jit(solution)/shard_map/ppermute | solution.py:249
  18.0 3.1 %collective-permute-start = (f32[2,512]{1,0:T(2,128)S(1)}, f32[2,512]{1,0:T(2,128)S(1)}, u32[]{:S(2)}, u32[]{:S(2)}) collective-permute-start(f32[2,512]{1,0:T(2,128)S(1)} %local_stats.1.own_ref), channel_id=1, source_target_pairs={{0,1},{1,0},{2,3},{3,2},{4,5},{5,4},{6,7},{7,6},{8,9},{9,8},{10,11... | collective-permute-start | bytes 12296 | tf_op jit(solution)/shard_map/ppermute | solution.py:249
  21.7 2.2 %copy-start.1 = (bf16[4096,512]{1,0:T(8,128)(2,1)S(1)}, bf16[4096,512]{1,0:T(8,128)(2,1)}, u32[]{:S(2)}) copy-start(bf16[4096,512]{1,0:T(8,128)(2,1)} %x_ref.1) | copy-start | bytes 12582916
  28.2 2.0 %collective-permute-start.3 = (f32[2,128,512]{2,1,0:T(8,128)S(1)}, f32[2,128,512]{2,1,0:T(8,128)S(1)}, u32[]{:S(2)}, u32[]{:S(2)}) collective-permute-start(f32[2,128,512]{2,1,0:T(8,128)S(1)} %get-tuple-element.29), channel_id=1, source_target_pairs={{0,1},{1,0},{2,3},{3,2},{4,5},{5,4},{6,7},{7,6},{8,9},{9,8},{10,11... | collective-permute-start | bytes 1572872 | tf_op jit(solution)/shard_map/ppermute | solution.py:249
  30.8 27.3 %collective-permute-start.6 = (f32[128,512]{1,0:T(8,128)S(1)}, f32[128,512]{1,0:T(8,128)S(1)}, u32[]{:S(2)}, u32[]{:S(2)}) collective-permute-start(f32[128,512]{1,0:T(8,128)S(1)} %get-tuple-element.33), channel_id=1, source_target_pairs={{0,2},{1,3},{2,0},{3,1},{4,6},{5,7},{6,4},{7,5},{8,10},{9,11},{10,... | collective-permute-start | bytes 786440 | tf_op jit(solution)/shard_map/ppermute | solution.py:249
  31.3 5.1 %collective-permute-start.5 = (f32[4,512]{1,0:T(4,128)S(1)}, f32[4,512]{1,0:T(4,128)S(1)}, u32[]{:S(2)}, u32[]{:S(2)}) collective-permute-start(f32[4,512]{1,0:T(4,128)S(1)} %stats.1.stat_ref), channel_id=1, source_target_pairs={{0,9},{2,11},{4,13},{6,15},{8,17},{9,0},{10,19},{11,2},{12,21},{13... | collective-permute-start | bytes 24584 | tf_op jit(solution)/shard_map/ppermute | solution.py:249
  33.3 26.8 %collective-permute-start.8 = (f32[4,512]{1,0:T(4,128)S(1)}, f32[4,512]{1,0:T(4,128)S(1)}, u32[]{:S(2)}, u32[]{:S(2)}) collective-permute-start(f32[4,512]{1,0:T(4,128)S(1)} %stats.1.stat_ref), channel_id=1, source_target_pairs={{0,5},{2,7},{5,0},{7,2},{8,13},{10,15},{13,8},{15,10},{16,21},{18,... | collective-permute-start | bytes 24584 | tf_op jit(solution)/shard_map/ppermute | solution.py:249
  58.1 15.7 %collective-permute-start.10 = (bf16[3,256,256]{2,1,0:T(8,128)(2,1)S(1)}, bf16[3,256,256]{2,1,0:T(8,128)(2,1)S(1)}, u32[]{:S(2)}, u32[]{:S(2)}) collective-permute-start(bf16[3,256,256]{2,1,0:T(8,128)(2,1)S(1)} %get-tuple-element.41), channel_id=1, source_target_pairs={{0,2},{1,3},{2,0},{3,1},{4,6},{5,7},{6,4},{7,5},{8,10},{9,11},{10,... | collective-permute-start | bytes 1179656 | tf_op jit(solution)/shard_map/ppermute | solution.py:249
  64.9 9.7 %collective-permute-start.9 = (bf16[3,256,256]{2,1,0:T(8,128)(2,1)S(1)}, bf16[3,256,256]{2,1,0:T(8,128)(2,1)S(1)}, u32[]{:S(2)}, u32[]{:S(2)}) collective-permute-start(bf16[3,256,256]{2,1,0:T(8,128)(2,1)S(1)} %get-tuple-element.36), channel_id=1, source_target_pairs={{0,2},{2,0},{5,7},{7,5},{8,10},{10,8},{13,15},{15,13},{16,18},{18,... | collective-permute-start | bytes 1179656 | tf_op jit(solution)/shard_map/ppermute | solution.py:249
  69.9 9.7 %collective-permute-start.12 = (bf16[3,256,256]{2,1,0:T(8,128)(2,1)S(1)}, bf16[3,256,256]{2,1,0:T(8,128)(2,1)S(1)}, u32[]{:S(2)}, u32[]{:S(2)}) collective-permute-start(bf16[3,256,256]{2,1,0:T(8,128)(2,1)S(1)} %get-tuple-element.40), channel_id=1, source_target_pairs={{0,2},{2,0},{5,7},{7,5},{8,10},{10,8},{13,15},{15,13},{16,18},{18,... | collective-permute-start | bytes 1179656 | tf_op jit(solution)/shard_map/ppermute | solution.py:249
  75.3 13.3 %collective-permute-start.11 = (f32[256,512]{1,0:T(8,128)S(1)}, f32[256,512]{1,0:T(8,128)S(1)}, u32[]{:S(2)}, u32[]{:S(2)}) collective-permute-start(f32[256,512]{1,0:T(8,128)S(1)} %get-tuple-element.47), channel_id=1, source_target_pairs={{0,5},{2,7},{5,0},{7,2},{8,13},{10,15},{13,8},{15,10},{16,21},{18,... | collective-permute-start | bytes 1572872 | tf_op jit(solution)/shard_map/ppermute | solution.py:249
  77.3 11.4 %collective-permute-start.14 = (f32[256,512]{1,0:T(8,128)S(1)}, f32[256,512]{1,0:T(8,128)S(1)}, u32[]{:S(2)}, u32[]{:S(2)}) collective-permute-start(f32[256,512]{1,0:T(8,128)S(1)} %get-tuple-element.43), channel_id=1, source_target_pairs={{0,9},{2,11},{4,13},{6,15},{8,17},{9,0},{10,19},{11,2},{12,21},{13... | collective-permute-start | bytes 1572872 | tf_op jit(solution)/shard_map/ppermute | solution.py:249
  80.3 8.4 %collective-permute-start.13 = (bf16[256,512]{1,0:T(8,128)(2,1)S(1)}, bf16[256,512]{1,0:T(8,128)(2,1)S(1)}, u32[]{:S(2)}, u32[]{:S(2)}) collective-permute-start(bf16[256,512]{1,0:T(8,128)(2,1)S(1)} %get-tuple-element.50), channel_id=1, source_target_pairs={{0,5},{2,7},{5,0},{7,2},{8,13},{10,15},{13,8},{15,10},{16,21},{18,... | collective-permute-start | bytes 786440 | tf_op jit(solution)/shard_map/ppermute | solution.py:249
  82.3 6.3 %collective-permute-start.15 = (bf16[256,512]{1,0:T(8,128)(2,1)S(1)}, bf16[256,512]{1,0:T(8,128)(2,1)S(1)}, u32[]{:S(2)}, u32[]{:S(2)}) collective-permute-start(bf16[256,512]{1,0:T(8,128)(2,1)S(1)} %get-tuple-element.51), channel_id=1, source_target_pairs={{0,9},{2,11},{8,17},{10,19},{13,4},{15,6},{16,25},{18,27},{21,12},... | collective-permute-start | bytes 786440 | tf_op jit(solution)/shard_map/ppermute | solution.py:249
  89.4 2.4 %collective-permute-start.16 = (f32[3,128,512]{2,1,0:T(8,128)S(1)}, f32[3,128,512]{2,1,0:T(8,128)S(1)}, u32[]{:S(2)}, u32[]{:S(2)}) collective-permute-start(f32[3,128,512]{2,1,0:T(8,128)S(1)} %get-tuple-element.53), channel_id=1, source_target_pairs={{0,1},{1,0},{2,3},{3,2},{4,5},{5,4},{6,7},{7,6},{8,9},{9,8},{10,11... | collective-permute-start | bytes 2359304 | tf_op jit(solution)/shard_map/ppermute | solution.py:249

commit v15 on v12

--- a/solution.py
+++ b/solution.py
@@ -12,7 +12,7 @@
 VMEM = pl.BlockSpec(memory_space=pltpu.VMEM)
 SMEM = pl.BlockSpec(memory_space=pltpu.SMEM)
 SOME = pltpu.CompilerParams(vmem_limit_bytes=24 << 20)
-HALVES, CROSS = BF16, BF16
+HALVES, STRIPS = BF16, BF16
 
 
 def dot(a, b):
@@ -182,7 +182,7 @@
     rows = mine.shape[1]
     for core, out in ((pos_ref[2], mine), (1 - pos_ref[2], sib)):
         at = pl.ds(pl.multiple_of(core * rows, rows), rows)
-        out[1] = held_c[at, :] + from_z_c[at, :]
+        out[1] = held_c[at, :] + from_z_c[at, :].astype(F32)
 
         @pl.when(pos_ref[1] == 1)
         def _():
@@ -303,7 +303,7 @@
     got_d = send(send_d, across_active)
 
     held_c, to_z_c = call(far_strips_kernel, "far_strips", (), [SMEM] + [VMEM] * 2, [VMEM] * 2,
-                          [shape(half, width)] * 2)(pos, keep_c, got_c)
+                          [shape(half, width), shape(half, width, dtype=STRIPS)])(pos, keep_c, got_c)
     from_z_c = send(to_z_c, z_cross)
     got_b, to_z_c = lax.optimization_barrier((got_b, to_z_c))
 
@@ -314,7 +314,7 @@
     held_b, to_y_b = near_strips("near_strips", F32, keep_b, got_b)
     from_y_b = send(to_y_b, y_cross)
     got_d, to_y_b = lax.optimization_barrier((got_d, to_y_b))
-    to_y_d, to_z_d = near_strips("cross_strips", CROSS, keep_d, got_d)
+    to_y_d, to_z_d = near_strips("cross_strips", STRIPS, keep_d, got_d)
     from_y_d, from_z_d = send(to_y_d, y_cross), send(to_z_d, z_cross_active)
 
     mine, sib = call(combine_kernel, "combine", (), [SMEM] + [VMEM] * 6, [VMEM] * 2, [shape(3, strip, width)] * 2)(

time: 93.4 us -> 92.7 us (level)
  no operation moved by 1% of the time
where the time goes in v15:
time: 92.7 us; the launch traced here: 92.2 us
  starting transfers between devices  33.4 us (36%)
  waiting for transfers between devices  28.8 us (31%)
  Pallas kernels  24 us (26%)
  local copies, waits for them, and re-layouts  4.46 us (5%)
  between operations  1.49 us (2%)
    ppermute x17, starting transfers between devices, send(): return lax.ppermute(value, AXES, pairs)  33.4 us
    ppermute x17, waiting for transfers between devices, send(): return lax.ppermute(value, AXES, pairs)  28.8 us
    pallas_call x1, Pallas kernels, body(): call(near_kernel, 'near_tile', (), [SMEM, VMEM, anywhere, VMEM, VMEM], [V...  4.64 us
    pallas_call x1, Pallas kernels, body(): call(far_kernel, 'far_tile', (), [SMEM, VMEM, anywhere, VMEM, VMEM], [VME...  4.59 us
    unnamed x6, local copies, waits for them, and re-layouts  4.37 us
    pallas_call x1, Pallas kernels, body(): call(own_kernel, 'own_tile', (steps,), [SMEM, wide, whole(4, width)], [fl...  4.31 us
    pallas_call x1, Pallas kernels, body(): call(lambda *refs: cross_kernel(steps, *refs), 'cross_tile', (), [SMEM] +...  2.96 us
    pallas_call x1, Pallas kernels, body(): call(lambda *refs: local_kernel(steps, *refs), 'local_stats', (steps,), [...  1.87 us
  transfers between devices with their start and end apart: 17, of which 10 were waited for; matrix products, arithmetic and copies ran while one was open for 0% of the time, Pallas kernels for 24%

profile of v15, /device:TPU:0, one launch (start us, length us, event | category | flops | bytes accessed | tf_op | source)
XLA Modules:
  0.0 92.2 jit_solution(11267922191645828166)
XLA Ops:
  0.6 1.3 %collective-permute-start.4 = (bf16[4096,512]{1,0:T(8,128)(2,1)}, bf16[4096,512]{1,0:T(8,128)(2,1)}, u32[]{:S(2)}, u32[]{:S(2)}) collective-permute-start(bf16[4096,512]{1,0:T(8,128)(2,1)} %x_ref.1), channel_id=1, source_target_pairs={{1,9},{3,11},{5,13},{7,15},{8,0},{9,17},{10,2},{11,19},{12,4},{13,... | collective-permute-start | bytes 12582920 | tf_op jit(solution)/shard_map/ppermute | solution.py:234
  1.9 1.3 %collective-permute-start.7 = (bf16[4096,512]{1,0:T(8,128)(2,1)}, bf16[4096,512]{1,0:T(8,128)(2,1)}, u32[]{:S(2)}, u32[]{:S(2)}) collective-permute-start(bf16[4096,512]{1,0:T(8,128)(2,1)} %x_ref.1), channel_id=1, source_target_pairs={{1,5},{3,7},{4,0},{6,2},{9,13},{11,15},{12,8},{14,10},{17,21},{19,... | collective-permute-start | bytes 12582920 | tf_op jit(solution)/shard_map/ppermute | solution.py:234
  3.2 0.0 copy-start
  3.2 2.2 %copy-done = bf16[4096,512]{1,0:T(8,128)(2,1)S(1)} copy-done((bf16[4096,512]{1,0:T(8,128)(2,1)S(1)}, bf16[4096,512]{1,0:T(8,128)(2,1)}, u32[]{:S(2)}) %copy-start) | copy-done | bytes 4194328
  5.4 1.9 %local_stats.1.own_ref = f32[2,512]{1,0:T(2,128)S(1)} custom-call(bf16[4096,512]{1,0:T(8,128)(2,1)S(1)} %copy-done), custom_call_target="tpu_custom_call" | custom-call | flops 10485760 | bytes 4194304 | tf_op jit(solution)/shard_map/local_stats/pallas_call | solution.py:267
  7.3 10.2 %collective-permute-start.2 = (f32[2,512]{1,0:T(2,128)S(1)}, f32[2,512]{1,0:T(2,128)S(1)}, u32[]{:S(2)}, u32[]{:S(2)}) collective-permute-start(f32[2,512]{1,0:T(2,128)S(1)} %local_stats.1.own_ref), channel_id=1, source_target_pairs={{0,3},{1,2},{2,1},{3,0},{4,7},{5,6},{6,5},{7,4},{8,11},{9,10},{10,... | collective-permute-start | bytes 12296 | tf_op jit(solution)/shard_map/ppermute | solution.py:234
  17.5 0.5 collective-permute-start.1
  18.7 0.1 stack.23.pos_ref.refs_0_
  18.7 0.0 collective-permute-done.2.cross_ref
  18.8 2.3 %collective-permute-done.1.far_ref = f32[2,512]{1,0:T(2,128)S(1)} collective-permute-done((f32[2,512]{1,0:T(2,128)S(1)}, f32[2,512]{1,0:T(2,128)S(1)}, u32[]{:S(2)}, u32[]{:S(2)}) %collective-permute-start.1) | collective-permute-done | bytes 4128 | tf_op jit(solution)/shard_map/ppermute | solution.py:234
  21.1 0.0 collective-permute-done.sib_ref
  21.1 0.6 stats.1.stat_ref
  21.7 0.0 copy-start.1
  21.7 2.2 %copy-done.1 = bf16[4096,512]{1,0:T(8,128)(2,1)S(1)} copy-done((bf16[4096,512]{1,0:T(8,128)(2,1)S(1)}, bf16[4096,512]{1,0:T(8,128)(2,1)}, u32[]{:S(2)}) %copy-start.1) | copy-done | bytes 4194328
  23.8 4.3 %own_tile.1 = (bf16[512,4096]{1,0:T(8,128)(2,1)S(1)}, f32[2,128,512]{2,1,0:T(8,128)S(1)}, f32[2,128,512]{2,1,0:T(8,128)S(1)}) custom-call(s32[5]{0:T(128)S(1)} %stack.23.pos_ref.refs_0_, bf16[4096,512]{1,0:T(8,128)(2,1)S(1)} %copy-done.1, f32[4,512]{1,0:T(4,128)S(1)} %stats.1.stat_ref), custom_call_target="tpu_custom_call" | custom-call | flops 2147483648 | bytes 8388608 | tf_op jit(solution)/shard_map/own_tile/pallas_call | solution.py:274
  28.2 0.1 collective-permute-start.3
  28.2 1.9 %collective-permute-done.3.got_ref = f32[2,128,512]{2,1,0:T(8,128)S(1)} collective-permute-done((f32[2,128,512]{2,1,0:T(8,128)S(1)}, f32[2,128,512]{2,1,0:T(8,128)S(1)}, u32[]{:S(2)}, u32[]{:S(2)}) %collective-permute-start.3) | collective-permute-done | bytes 524320 | tf_op jit(solution)/shard_map/ppermute | solution.py:234
  30.1 0.6 own_tile_strips.1
  30.8 0.6 collective-permute-start.6
  31.3 1.9 %collective-permute-start.5 = (f32[4,512]{1,0:T(4,128)S(1)}, f32[4,512]{1,0:T(4,128)S(1)}, u32[]{:S(2)}, u32[]{:S(2)}) collective-permute-start(f32[4,512]{1,0:T(4,128)S(1)} %stats.1.stat_ref), channel_id=1, source_target_pairs={{0,9},{2,11},{4,13},{6,15},{8,17},{9,0},{10,19},{11,2},{12,21},{13... | collective-permute-start | bytes 24584 | tf_op jit(solution)/shard_map/ppermute | solution.py:234
  33.3 1.9 %collective-permute-start.8 = (f32[4,512]{1,0:T(4,128)S(1)}, f32[4,512]{1,0:T(4,128)S(1)}, u32[]{:S(2)}, u32[]{:S(2)}) collective-permute-start(f32[4,512]{1,0:T(4,128)S(1)} %stats.1.stat_ref), channel_id=1, source_target_pairs={{0,5},{2,7},{5,0},{7,2},{8,13},{10,15},{13,8},{15,10},{16,21},{18,... | collective-permute-start | bytes 24584 | tf_op jit(solution)/shard_map/ppermute | solution.py:234
  35.2 1.3 %collective-permute-done.5.wstat_ref.refs_4_ = f32[4,512]{1,0:T(4,128)S(1)} collective-permute-done((f32[4,512]{1,0:T(4,128)S(1)}, f32[4,512]{1,0:T(4,128)S(1)}, u32[]{:S(2)}, u32[]{:S(2)}) %collective-permute-start.5) | collective-permute-done | bytes 8224 | tf_op jit(solution)/shard_map/ppermute | solution.py:234
  36.4 16.0 %collective-permute-done.4.w_ref = bf16[4096,512]{1,0:T(8,128)(2,1)} collective-permute-done((bf16[4096,512]{1,0:T(8,128)(2,1)}, bf16[4096,512]{1,0:T(8,128)(2,1)}, u32[]{:S(2)}, u32[]{:S(2)}) %collective-permute-start.4) | collective-permute-done | bytes 4194336 | tf_op jit(solution)/shard_map/ppermute | solution.py:234
  52.4 4.6 %far_tile.1 = (f32[3,256,256]{2,1,0:T(8,128)S(1)}, bf16[3,256,256]{2,1,0:T(8,128)(2,1)S(1)}, bf16[4096,512]{1,0:T(8,128)(2,1)S(1)}) custom-call(s32[5]{0:T(128)S(1)} %stack.23.pos_ref.refs_0_, bf16[512,4096]{1,0:T(8,128)(2,1)S(1)} %get-tuple-element.32.turned_ref, bf16[4096,512]{1,0:T(8,128)(2,1)} %collective-permute-done.4.w_ref, ...), custom_call_target="tpu_custom_call" | custom-call | flops 2147483648 | bytes 12582912 | tf_op jit(solution)/shard_map/far_tile/pallas_call | solution.py:287
  57.1 2.0 %collective-permute-start.10 = (bf16[3,256,256]{2,1,0:T(8,128)(2,1)S(1)}, bf16[3,256,256]{2,1,0:T(8,128)(2,1)S(1)}, u32[]{:S(2)}, u32[]{:S(2)}) collective-permute-start(bf16[3,256,256]{2,1,0:T(8,128)(2,1)S(1)} %get-tuple-element.42), channel_id=1, source_target_pairs={{0,2},{1,3},{2,0},{3,1},{4,6},{5,7},{6,4},{7,5},{8,10},{9,11},{10,... | collective-permute-start | bytes 1179656 | tf_op jit(solution)/shard_map/ppermute | solution.py:234
  59.1 0.0 collective-permute-done.8.ystat_ref.refs_3_
  59.1 0.0 collective-permute-done.7.y_ref
  59.1 4.6 %near_tile.1 = (f32[3,256,256]{2,1,0:T(8,128)S(1)}, bf16[3,256,256]{2,1,0:T(8,128)(2,1)S(1)}, bf16[512,4096]{1,0:T(8,128)(2,1)S(1)}) custom-call(s32[5]{0:T(128)S(1)} %stack.23.pos_ref.refs_0_, bf16[512,4096]{1,0:T(8,128)(2,1)S(1)} %get-tuple-element.32.turned_ref, bf16[4096,512]{1,0:T(8,128)(2,1)} %collective-permute-done.7.y_ref, ...), custom_call_target="tpu_custom_call" | custom-call | flops 2147483648 | bytes 12582912 | tf_op jit(solution)/shard_map/near_tile/pallas_call | solution.py:294
  63.7 2.0 %collective-permute-start.9 = (bf16[3,256,256]{2,1,0:T(8,128)(2,1)S(1)}, bf16[3,256,256]{2,1,0:T(8,128)(2,1)S(1)}, u32[]{:S(2)}, u32[]{:S(2)}) collective-permute-start(bf16[3,256,256]{2,1,0:T(8,128)(2,1)S(1)} %get-tuple-element.37), channel_id=1, source_target_pairs={{0,2},{2,0},{5,7},{7,5},{8,10},{10,8},{13,15},{15,13},{16,18},{18,... | collective-permute-start | bytes 1179656 | tf_op jit(solution)/shard_map/ppermute | solution.py:234
  65.7 3.0 %cross_tile.1 = (f32[3,256,256]{2,1,0:T(8,128)S(1)}, bf16[3,256,256]{2,1,0:T(8,128)(2,1)S(1)}) custom-call(s32[5]{0:T(128)S(1)} %stack.23.pos_ref.refs_0_, bf16[512,4096]{1,0:T(8,128)(2,1)S(1)} %get-tuple-element.39.refs_1_, bf16[4096,512]{1,0:T(8,128)(2,1)S(1)} %get-tuple-element.40.refs_2_, f32[4,512]{1,0:T(4,128)S(1)} %collective-permute-done.8.ystat_ref.refs_3_, ...), custom_call_target="tpu_custom_call" | custom-call | flops 2147483648 | bytes 8388608 | tf_op jit(solution)/shard_map/cross_tile/pallas_call | solution.py:299
  68.7 0.0 collective-permute-done.10.got
  68.7 3.8 %collective-permute-start.12 = (bf16[3,256,256]{2,1,0:T(8,128)(2,1)S(1)}, bf16[3,256,256]{2,1,0:T(8,128)(2,1)S(1)}, u32[]{:S(2)}, u32[]{:S(2)}) collective-permute-start(bf16[3,256,256]{2,1,0:T(8,128)(2,1)S(1)} %get-tuple-element.50), channel_id=1, source_target_pairs={{0,2},{2,0},{5,7},{7,5},{8,10},{10,8},{13,15},{15,13},{16,18},{18,... | collective-permute-start | bytes 1179656 | tf_op jit(solution)/shard_map/ppermute | solution.py:234
  72.5 0.7 far_strips.1
  73.2 0.1 collective-permute-done.9.got
  73.4 0.7 near_strips.1
  74.1 1.9 %collective-permute-start.11 = (f32[256,512]{1,0:T(8,128)S(1)}, f32[256,512]{1,0:T(8,128)S(1)}, u32[]{:S(2)}, u32[]{:S(2)}) collective-permute-start(f32[256,512]{1,0:T(8,128)S(1)} %get-tuple-element.48), channel_id=1, source_target_pairs={{0,5},{2,7},{5,0},{7,2},{8,13},{10,15},{13,8},{15,10},{16,21},{18,... | collective-permute-start | bytes 1572872 | tf_op jit(solution)/shard_map/ppermute | solution.py:234
  76.1 1.9 %collective-permute-start.14 = (bf16[256,512]{1,0:T(8,128)(2,1)S(1)}, bf16[256,512]{1,0:T(8,128)(2,1)S(1)}, u32[]{:S(2)}, u32[]{:S(2)}) collective-permute-start(bf16[256,512]{1,0:T(8,128)(2,1)S(1)} %get-tuple-element.44), channel_id=1, source_target_pairs={{0,9},{2,11},{4,13},{6,15},{8,17},{9,0},{10,19},{11,2},{12,21},{13... | collective-permute-start | bytes 786440 | tf_op jit(solution)/shard_map/ppermute | solution.py:234
  78.0 0.4 collective-permute-done.12.got
  78.4 0.7 cross_strips.1
  79.1 2.0 %collective-permute-start.13 = (bf16[256,512]{1,0:T(8,128)(2,1)S(1)}, bf16[256,512]{1,0:T(8,128)(2,1)S(1)}, u32[]{:S(2)}, u32[]{:S(2)}) collective-permute-start(bf16[256,512]{1,0:T(8,128)(2,1)S(1)} %get-tuple-element.52), channel_id=1, source_target_pairs={{0,5},{2,7},{5,0},{7,2},{8,13},{10,15},{13,8},{15,10},{16,21},{18,... | collective-permute-start | bytes 786440 | tf_op jit(solution)/shard_map/ppermute | solution.py:234
  81.1 1.8 %collective-permute-start.15 = (bf16[256,512]{1,0:T(8,128)(2,1)S(1)}, bf16[256,512]{1,0:T(8,128)(2,1)S(1)}, u32[]{:S(2)}, u32[]{:S(2)}) collective-permute-start(bf16[256,512]{1,0:T(8,128)(2,1)S(1)} %get-tuple-element.53), channel_id=1, source_target_pairs={{0,9},{2,11},{8,17},{10,19},{13,4},{15,6},{16,25},{18,27},{21,12},... | collective-permute-start | bytes 786440 | tf_op jit(solution)/shard_map/ppermute | solution.py:234
  82.9 0.8 collective-permute-done.14.from_z_c
  83.7 0.9 collective-permute-done.11.from_y_b
  84.6 2.8 %collective-permute-done.13.from_y_d = bf16[256,512]{1,0:T(8,128)(2,1)S(1)} collective-permute-done((bf16[256,512]{1,0:T(8,128)(2,1)S(1)}, bf16[256,512]{1,0:T(8,128)(2,1)S(1)}, u32[]{:S(2)}, u32[]{:S(2)}) %collective-permute-start.13) | collective-permute-done | bytes 262176 | tf_op jit(solution)/shard_map/ppermute | solution.py:234
  87.4 0.7 combine.1
  88.1 0.1 collective-permute-start.16
  88.2 2.3 %collective-permute-done.16.sib = f32[3,128,512]{2,1,0:T(8,128)S(1)} collective-permute-done((f32[3,128,512]{2,1,0:T(8,128)S(1)}, f32[3,128,512]{2,1,0:T(8,128)S(1)}, u32[]{:S(2)}, u32[]{:S(2)}) %collective-permute-start.16) | collective-permute-done | bytes 786464 | tf_op jit(solution)/shard_map/ppermute | solution.py:234
  90.5 1.7 %finish.1 = (bf16[1,3,128,512]{3,2,1,0:T(8,128)(2,1)}, bf16[1,2,128,512]{3,2,1,0:T(8,128)(2,1)}) custom-call(s32[5]{0:T(128)S(1)} %stack.23.pos_ref.refs_0_, s32[1,3]{1,0:T(1,128)S(1)} %copy-done.2, f32[128,512]{1,0:T(8,128)S(1)} %get-tuple-element.31.diag_mine, f32[128,512]{1,0:T(8,128)S(1)} %collective-permute-done.6.diag_got, ...), custom_call_target="tpu_custom_call" | custom-call | tf_op jit(solution)/shard_map/finish/pallas_call | solution.py:322
  (5 shorter events, 0.0 us)
Async XLA Ops:
  0.6 51.8 %collective-permute-start.4 = (bf16[4096,512]{1,0:T(8,128)(2,1)}, bf16[4096,512]{1,0:T(8,128)(2,1)}, u32[]{:S(2)}, u32[]{:S(2)}) collective-permute-start(bf16[4096,512]{1,0:T(8,128)(2,1)} %x_ref.1), channel_id=1, source_target_pairs={{1,9},{3,11},{5,13},{7,15},{8,0},{9,17},{10,2},{11,19},{12,4},{13,... | collective-permute-start | bytes 12582920 | tf_op jit(solution)/shard_map/ppermute | solution.py:234
  1.9 57.1 %collective-permute-start.7 = (bf16[4096,512]{1,0:T(8,128)(2,1)}, bf16[4096,512]{1,0:T(8,128)(2,1)}, u32[]{:S(2)}, u32[]{:S(2)}) collective-permute-start(bf16[4096,512]{1,0:T(8,128)(2,1)} %x_ref.1), channel_id=1, source_target_pairs={{1,5},{3,7},{4,0},{6,2},{9,13},{11,15},{12,8},{14,10},{17,21},{19,... | collective-permute-start | bytes 12582920 | tf_op jit(solution)/shard_map/ppermute | solution.py:234
  3.2 2.2 %copy-start = (bf16[4096,512]{1,0:T(8,128)(2,1)S(1)}, bf16[4096,512]{1,0:T(8,128)(2,1)}, u32[]{:S(2)}) copy-start(bf16[4096,512]{1,0:T(8,128)(2,1)} %x_ref.1) | copy-start | bytes 12582916
  5.4 15.7 %copy-start.2 = (s32[1,3]{1,0:T(1,128)S(1)}, s32[1,3]{1,0:T(1,128)}, u32[]{:S(2)}) copy-start(s32[1,3]{1,0:T(1,128)} %offsets_ref.3) | copy-start | bytes 40
  7.3 11.5 %collective-permute-start.2 = (f32[2,512]{1,0:T(2,128)S(1)}, f32[2,512]{1,0:T(2,128)S(1)}, u32[]{:S(2)}, u32[]{:S(2)}) collective-permute-start(f32[2,512]{1,0:T(2,128)S(1)} %local_stats.1.own_ref), channel_id=1, source_target_pairs={{0,3},{1,2},{2,1},{3,0},{4,7},{5,6},{6,5},{7,4},{8,11},{9,10},{10,... | collective-permute-start | bytes 12296 | tf_op jit(solution)/shard_map/ppermute | solution.py:234
  17.5 3.6 %collective-permute-start.1 = (f32[2,512]{1,0:T(2,128)S(1)}, f32[2,512]{1,0:T(2,128)S(1)}, u32[]{:S(2)}, u32[]{:S(2)}) collective-permute-start(f32[2,512]{1,0:T(2,128)S(1)} %local_stats.1.own_ref), channel_id=1, source_target_pairs={{0,2},{1,3},{2,0},{3,1},{4,6},{5,7},{6,4},{7,5},{8,10},{9,11},{10,... | collective-permute-start | bytes 12296 | tf_op jit(solution)/shard_map/ppermute | solution.py:234
  18.0 3.1 %collective-permute-start = (f32[2,512]{1,0:T(2,128)S(1)}, f32[2,512]{1,0:T(2,128)S(1)}, u32[]{:S(2)}, u32[]{:S(2)}) collective-permute-start(f32[2,512]{1,0:T(2,128)S(1)} %local_stats.1.own_ref), channel_id=1, source_target_pairs={{0,1},{1,0},{2,3},{3,2},{4,5},{5,4},{6,7},{7,6},{8,9},{9,8},{10,11... | collective-permute-start | bytes 12296 | tf_op jit(solution)/shard_map/ppermute | solution.py:234
  21.7 2.2 %copy-start.1 = (bf16[4096,512]{1,0:T(8,128)(2,1)S(1)}, bf16[4096,512]{1,0:T(8,128)(2,1)}, u32[]{:S(2)}) copy-start(bf16[4096,512]{1,0:T(8,128)(2,1)} %x_ref.1) | copy-start | bytes 12582916
  28.2 2.0 %collective-permute-start.3 = (f32[2,128,512]{2,1,0:T(8,128)S(1)}, f32[2,128,512]{2,1,0:T(8,128)S(1)}, u32[]{:S(2)}, u32[]{:S(2)}) collective-permute-start(f32[2,128,512]{2,1,0:T(8,128)S(1)} %get-tuple-element.30), channel_id=1, source_target_pairs={{0,1},{1,0},{2,3},{3,2},{4,5},{5,4},{6,7},{7,6},{8,9},{9,8},{10,11... | collective-permute-start | bytes 1572872 | tf_op jit(solution)/shard_map/ppermute | solution.py:234
  30.8 26.3 %collective-permute-start.6 = (f32[128,512]{1,0:T(8,128)S(1)}, f32[128,512]{1,0:T(8,128)S(1)}, u32[]{:S(2)}, u32[]{:S(2)}) collective-permute-start(f32[128,512]{1,0:T(8,128)S(1)} %get-tuple-element.34), channel_id=1, source_target_pairs={{0,2},{1,3},{2,0},{3,1},{4,6},{5,7},{6,4},{7,5},{8,10},{9,11},{10,... | collective-permute-start | bytes 786440 | tf_op jit(solution)/shard_map/ppermute | solution.py:234
  31.3 5.1 %collective-permute-start.5 = (f32[4,512]{1,0:T(4,128)S(1)}, f32[4,512]{1,0:T(4,128)S(1)}, u32[]{:S(2)}, u32[]{:S(2)}) collective-permute-start(f32[4,512]{1,0:T(4,128)S(1)} %stats.1.stat_ref), channel_id=1, source_target_pairs={{0,9},{2,11},{4,13},{6,15},{8,17},{9,0},{10,19},{11,2},{12,21},{13... | collective-permute-start | bytes 24584 | tf_op jit(solution)/shard_map/ppermute | solution.py:234
  33.3 25.8 %collective-permute-start.8 = (f32[4,512]{1,0:T(4,128)S(1)}, f32[4,512]{1,0:T(4,128)S(1)}, u32[]{:S(2)}, u32[]{:S(2)}) collective-permute-start(f32[4,512]{1,0:T(4,128)S(1)} %stats.1.stat_ref), channel_id=1, source_target_pairs={{0,5},{2,7},{5,0},{7,2},{8,13},{10,15},{13,8},{15,10},{16,21},{18,... | collective-permute-start | bytes 24584 | tf_op jit(solution)/shard_map/ppermute | solution.py:234
  57.1 11.6 %collective-permute-start.10 = (bf16[3,256,256]{2,1,0:T(8,128)(2,1)S(1)}, bf16[3,256,256]{2,1,0:T(8,128)(2,1)S(1)}, u32[]{:S(2)}, u32[]{:S(2)}) collective-permute-start(bf16[3,256,256]{2,1,0:T(8,128)(2,1)S(1)} %get-tuple-element.42), channel_id=1, source_target_pairs={{0,2},{1,3},{2,0},{3,1},{4,6},{5,7},{6,4},{7,5},{8,10},{9,11},{10,... | collective-permute-start | bytes 1179656 | tf_op jit(solution)/shard_map/ppermute | solution.py:234
  63.7 9.7 %collective-permute-start.9 = (bf16[3,256,256]{2,1,0:T(8,128)(2,1)S(1)}, bf16[3,256,256]{2,1,0:T(8,128)(2,1)S(1)}, u32[]{:S(2)}, u32[]{:S(2)}) collective-permute-start(bf16[3,256,256]{2,1,0:T(8,128)(2,1)S(1)} %get-tuple-element.37), channel_id=1, source_target_pairs={{0,2},{2,0},{5,7},{7,5},{8,10},{10,8},{13,15},{15,13},{16,18},{18,... | collective-permute-start | bytes 1179656 | tf_op jit(solution)/shard_map/ppermute | solution.py:234
  68.7 9.7 %collective-permute-start.12 = (bf16[3,256,256]{2,1,0:T(8,128)(2,1)S(1)}, bf16[3,256,256]{2,1,0:T(8,128)(2,1)S(1)}, u32[]{:S(2)}, u32[]{:S(2)}) collective-permute-start(bf16[3,256,256]{2,1,0:T(8,128)(2,1)S(1)} %get-tuple-element.50), channel_id=1, source_target_pairs={{0,2},{2,0},{5,7},{7,5},{8,10},{10,8},{13,15},{15,13},{16,18},{18,... | collective-permute-start | bytes 1179656 | tf_op jit(solution)/shard_map/ppermute | solution.py:234
  74.1 10.5 %collective-permute-start.11 = (f32[256,512]{1,0:T(8,128)S(1)}, f32[256,512]{1,0:T(8,128)S(1)}, u32[]{:S(2)}, u32[]{:S(2)}) collective-permute-start(f32[256,512]{1,0:T(8,128)S(1)} %get-tuple-element.48), channel_id=1, source_target_pairs={{0,5},{2,7},{5,0},{7,2},{8,13},{10,15},{13,8},{15,10},{16,21},{18,... | collective-permute-start | bytes 1572872 | tf_op jit(solution)/shard_map/ppermute | solution.py:234
  76.1 7.7 %collective-permute-start.14 = (bf16[256,512]{1,0:T(8,128)(2,1)S(1)}, bf16[256,512]{1,0:T(8,128)(2,1)S(1)}, u32[]{:S(2)}, u32[]{:S(2)}) collective-permute-start(bf16[256,512]{1,0:T(8,128)(2,1)S(1)} %get-tuple-element.44), channel_id=1, source_target_pairs={{0,9},{2,11},{4,13},{6,15},{8,17},{9,0},{10,19},{11,2},{12,21},{13... | collective-permute-start | bytes 786440 | tf_op jit(solution)/shard_map/ppermute | solution.py:234
  79.1 8.4 %collective-permute-start.13 = (bf16[256,512]{1,0:T(8,128)(2,1)S(1)}, bf16[256,512]{1,0:T(8,128)(2,1)S(1)}, u32[]{:S(2)}, u32[]{:S(2)}) collective-permute-start(bf16[256,512]{1,0:T(8,128)(2,1)S(1)} %get-tuple-element.52), channel_id=1, source_target_pairs={{0,5},{2,7},{5,0},{7,2},{8,13},{10,15},{13,8},{15,10},{16,21},{18,... | collective-permute-start | bytes 786440 | tf_op jit(solution)/shard_map/ppermute | solution.py:234
  81.1 6.3 %collective-permute-start.15 = (bf16[256,512]{1,0:T(8,128)(2,1)S(1)}, bf16[256,512]{1,0:T(8,128)(2,1)S(1)}, u32[]{:S(2)}, u32[]{:S(2)}) collective-permute-start(bf16[256,512]{1,0:T(8,128)(2,1)S(1)} %get-tuple-element.53), channel_id=1, source_target_pairs={{0,9},{2,11},{8,17},{10,19},{13,4},{15,6},{16,25},{18,27},{21,12},... | collective-permute-start | bytes 786440 | tf_op jit(solution)/shard_map/ppermute | solution.py:234
  88.1 2.4 %collective-permute-start.16 = (f32[3,128,512]{2,1,0:T(8,128)S(1)}, f32[3,128,512]{2,1,0:T(8,128)S(1)}, u32[]{:S(2)}, u32[]{:S(2)}) collective-permute-start(f32[3,128,512]{2,1,0:T(8,128)S(1)} %get-tuple-element.55), channel_id=1, source_target_pairs={{0,1},{1,0},{2,3},{3,2},{4,5},{5,4},{6,7},{7,6},{8,9},{9,8},{10,11... | collective-permute-start | bytes 2359304 | tf_op jit(solution)/shard_map/ppermute | solution.py:234

commit v16 on v15

--- a/solution.py
+++ b/solution.py
@@ -317,6 +317,7 @@
     to_y_d, to_z_d = near_strips("cross_strips", STRIPS, keep_d, got_d)
     from_y_d, from_z_d = send(to_y_d, y_cross), send(to_z_d, z_cross_active)
 
+    from_z_d, from_z_c = lax.optimization_barrier((from_z_d, from_z_c))
     mine, sib = call(combine_kernel, "combine", (), [SMEM] + [VMEM] * 6, [VMEM] * 2, [shape(3, strip, width)] * 2)(
         pos, held_b, held_c, from_y_b, from_y_d, from_z_c, from_z_d)
     return call(finish_kernel, "finish", (), [SMEM] * 2 + [VMEM] * 4, [VMEM] * 2,

time: 92.7 us -> 95.1 us (1.026)
  starting transfers between devices: 33.4 us -> 34.6 us
  waiting for transfers between devices: 28.8 us -> 30 us
    ppermute x17, starting transfers between devices: 33.4 us -> 34.6 us  [send(): return lax.ppermute(value, AXES, pairs)]
    ppermute x17, waiting for transfers between devices: 28.8 us -> 30 us  [send(): return lax.ppermute(value, AXES, pairs)]
  transfers between devices with their start and end apart: 17 -> 17, of which waited for: 10 -> 9; matrix products, arithmetic and copies ran while one was open for 0% -> 0% of each run, Pallas kernels for 24% -> 23%
where the time goes in v16:
time: 95.1 us; the launch traced here: 94.6 us
  starting transfers between devices  34.6 us (36%)
  waiting for transfers between devices  30 us (32%)
  Pallas kernels  24 us (25%)
  local copies, waits for them, and re-layouts  4.46 us (5%)
  between operations  1.49 us (2%)
    ppermute x17, starting transfers between devices, send(): return lax.ppermute(value, AXES, pairs)  34.6 us
    ppermute x17, waiting for transfers between devices, send(): return lax.ppermute(value, AXES, pairs)  30 us
    pallas_call x1, Pallas kernels, body(): call(near_kernel, 'near_tile', (), [SMEM, VMEM, anywhere, VMEM, VMEM], [V...  4.64 us
    pallas_call x1, Pallas kernels, body(): call(far_kernel, 'far_tile', (), [SMEM, VMEM, anywhere, VMEM, VMEM], [VME...  4.59 us
    unnamed x6, local copies, waits for them, and re-layouts  4.37 us
    pallas_call x1, Pallas kernels, body(): call(own_kernel, 'own_tile', (steps,), [SMEM, wide, whole(4, width)], [fl...  4.31 us
    pallas_call x1, Pallas kernels, body(): call(lambda *refs: cross_kernel(steps, *refs), 'cross_tile', (), [SMEM] +...  2.96 us
  transfers between devices with their start and end apart: 17, of which 9 were waited for; matrix products, arithmetic and copies ran while one was open for 0% of the time, Pallas kernels for 23%

profile of v16, /device:TPU:0, one launch (start us, length us, event | category | flops | bytes accessed | tf_op | source)
XLA Modules:
  0.0 94.6 jit_solution(9892287939399394531)
XLA Ops:
  0.6 1.3 %collective-permute-start.4 = (bf16[4096,512]{1,0:T(8,128)(2,1)}, bf16[4096,512]{1,0:T(8,128)(2,1)}, u32[]{:S(2)}, u32[]{:S(2)}) collective-permute-start(bf16[4096,512]{1,0:T(8,128)(2,1)} %x_ref.1), channel_id=1, source_target_pairs={{1,9},{3,11},{5,13},{7,15},{8,0},{9,17},{10,2},{11,19},{12,4},{13,... | collective-permute-start | bytes 12582920 | tf_op jit(solution)/shard_map/ppermute | solution.py:234
  1.9 1.3 %collective-permute-start.7 = (bf16[4096,512]{1,0:T(8,128)(2,1)}, bf16[4096,512]{1,0:T(8,128)(2,1)}, u32[]{:S(2)}, u32[]{:S(2)}) collective-permute-start(bf16[4096,512]{1,0:T(8,128)(2,1)} %x_ref.1), channel_id=1, source_target_pairs={{1,5},{3,7},{4,0},{6,2},{9,13},{11,15},{12,8},{14,10},{17,21},{19,... | collective-permute-start | bytes 12582920 | tf_op jit(solution)/shard_map/ppermute | solution.py:234
  3.2 0.0 copy-start
  3.2 2.2 %copy-done = bf16[4096,512]{1,0:T(8,128)(2,1)S(1)} copy-done((bf16[4096,512]{1,0:T(8,128)(2,1)S(1)}, bf16[4096,512]{1,0:T(8,128)(2,1)}, u32[]{:S(2)}) %copy-start) | copy-done | bytes 4194328
  5.4 1.9 %local_stats.1.own_ref = f32[2,512]{1,0:T(2,128)S(1)} custom-call(bf16[4096,512]{1,0:T(8,128)(2,1)S(1)} %copy-done), custom_call_target="tpu_custom_call" | custom-call | flops 10485760 | bytes 4194304 | tf_op jit(solution)/shard_map/local_stats/pallas_call | solution.py:267
  7.3 10.2 %collective-permute-start.2 = (f32[2,512]{1,0:T(2,128)S(1)}, f32[2,512]{1,0:T(2,128)S(1)}, u32[]{:S(2)}, u32[]{:S(2)}) collective-permute-start(f32[2,512]{1,0:T(2,128)S(1)} %local_stats.1.own_ref), channel_id=1, source_target_pairs={{0,3},{1,2},{2,1},{3,0},{4,7},{5,6},{6,5},{7,4},{8,11},{9,10},{10,... | collective-permute-start | bytes 12296 | tf_op jit(solution)/shard_map/ppermute | solution.py:234
  17.5 0.5 collective-permute-start.1
  18.0 0.0 collective-permute-start
  18.7 0.1 stack.23.pos_ref.refs_0_
  18.7 0.0 collective-permute-done.2.cross_ref
  18.8 2.3 %collective-permute-done.1.far_ref = f32[2,512]{1,0:T(2,128)S(1)} collective-permute-done((f32[2,512]{1,0:T(2,128)S(1)}, f32[2,512]{1,0:T(2,128)S(1)}, u32[]{:S(2)}, u32[]{:S(2)}) %collective-permute-start.1) | collective-permute-done | bytes 4128 | tf_op jit(solution)/shard_map/ppermute | solution.py:234
  21.1 0.0 collective-permute-done.sib_ref
  21.1 0.6 stats.1.stat_ref
  21.7 0.0 copy-start.1
  21.7 2.2 %copy-done.1 = bf16[4096,512]{1,0:T(8,128)(2,1)S(1)} copy-done((bf16[4096,512]{1,0:T(8,128)(2,1)S(1)}, bf16[4096,512]{1,0:T(8,128)(2,1)}, u32[]{:S(2)}) %copy-start.1) | copy-done | bytes 4194328
  23.8 4.3 %own_tile.1 = (bf16[512,4096]{1,0:T(8,128)(2,1)S(1)}, f32[2,128,512]{2,1,0:T(8,128)S(1)}, f32[2,128,512]{2,1,0:T(8,128)S(1)}) custom-call(s32[5]{0:T(128)S(1)} %stack.23.pos_ref.refs_0_, bf16[4096,512]{1,0:T(8,128)(2,1)S(1)} %copy-done.1, f32[4,512]{1,0:T(4,128)S(1)} %stats.1.stat_ref), custom_call_target="tpu_custom_call" | custom-call | flops 2147483648 | bytes 8388608 | tf_op jit(solution)/shard_map/own_tile/pallas_call | solution.py:274
  28.2 0.1 collective-permute-start.3
  28.2 1.9 %collective-permute-done.3.got_ref = f32[2,128,512]{2,1,0:T(8,128)S(1)} collective-permute-done((f32[2,128,512]{2,1,0:T(8,128)S(1)}, f32[2,128,512]{2,1,0:T(8,128)S(1)}, u32[]{:S(2)}, u32[]{:S(2)}) %collective-permute-start.3) | collective-permute-done | bytes 524320 | tf_op jit(solution)/shard_map/ppermute | solution.py:234
  30.1 0.6 own_tile_strips.1
  30.8 0.6 collective-permute-start.6
  31.3 1.9 %collective-permute-start.5 = (f32[4,512]{1,0:T(4,128)S(1)}, f32[4,512]{1,0:T(4,128)S(1)}, u32[]{:S(2)}, u32[]{:S(2)}) collective-permute-start(f32[4,512]{1,0:T(4,128)S(1)} %stats.1.stat_ref), channel_id=1, source_target_pairs={{0,9},{2,11},{4,13},{6,15},{8,17},{9,0},{10,19},{11,2},{12,21},{13... | collective-permute-start | bytes 24584 | tf_op jit(solution)/shard_map/ppermute | solution.py:234
  33.3 1.9 %collective-permute-start.8 = (f32[4,512]{1,0:T(4,128)S(1)}, f32[4,512]{1,0:T(4,128)S(1)}, u32[]{:S(2)}, u32[]{:S(2)}) collective-permute-start(f32[4,512]{1,0:T(4,128)S(1)} %stats.1.stat_ref), channel_id=1, source_target_pairs={{0,5},{2,7},{5,0},{7,2},{8,13},{10,15},{13,8},{15,10},{16,21},{18,... | collective-permute-start | bytes 24584 | tf_op jit(solution)/shard_map/ppermute | solution.py:234
  35.2 1.3 %collective-permute-done.5.wstat_ref.refs_4_ = f32[4,512]{1,0:T(4,128)S(1)} collective-permute-done((f32[4,512]{1,0:T(4,128)S(1)}, f32[4,512]{1,0:T(4,128)S(1)}, u32[]{:S(2)}, u32[]{:S(2)}) %collective-permute-start.5) | collective-permute-done | bytes 8224 | tf_op jit(solution)/shard_map/ppermute | solution.py:234
  36.4 16.0 %collective-permute-done.4.w_ref = bf16[4096,512]{1,0:T(8,128)(2,1)} collective-permute-done((bf16[4096,512]{1,0:T(8,128)(2,1)}, bf16[4096,512]{1,0:T(8,128)(2,1)}, u32[]{:S(2)}, u32[]{:S(2)}) %collective-permute-start.4) | collective-permute-done | bytes 4194336 | tf_op jit(solution)/shard_map/ppermute | solution.py:234
  52.4 4.6 %far_tile.1 = (f32[3,256,256]{2,1,0:T(8,128)S(1)}, bf16[3,256,256]{2,1,0:T(8,128)(2,1)S(1)}, bf16[4096,512]{1,0:T(8,128)(2,1)S(1)}) custom-call(s32[5]{0:T(128)S(1)} %stack.23.pos_ref.refs_0_, bf16[512,4096]{1,0:T(8,128)(2,1)S(1)} %get-tuple-element.34.turned_ref, bf16[4096,512]{1,0:T(8,128)(2,1)} %collective-permute-done.4.w_ref, ...), custom_call_target="tpu_custom_call" | custom-call | flops 2147483648 | bytes 12582912 | tf_op jit(solution)/shard_map/far_tile/pallas_call | solution.py:287
  57.0 0.0 collective-permute-done.6.diag_got
  57.1 2.0 %collective-permute-start.10 = (bf16[3,256,256]{2,1,0:T(8,128)(2,1)S(1)}, bf16[3,256,256]{2,1,0:T(8,128)(2,1)S(1)}, u32[]{:S(2)}, u32[]{:S(2)}) collective-permute-start(bf16[3,256,256]{2,1,0:T(8,128)(2,1)S(1)} %get-tuple-element.44), channel_id=1, source_target_pairs={{0,2},{1,3},{2,0},{3,1},{4,6},{5,7},{6,4},{7,5},{8,10},{9,11},{10,... | collective-permute-start | bytes 1179656 | tf_op jit(solution)/shard_map/ppermute | solution.py:234
  59.1 4.6 %near_tile.1 = (f32[3,256,256]{2,1,0:T(8,128)S(1)}, bf16[3,256,256]{2,1,0:T(8,128)(2,1)S(1)}, bf16[512,4096]{1,0:T(8,128)(2,1)S(1)}) custom-call(s32[5]{0:T(128)S(1)} %stack.23.pos_ref.refs_0_, bf16[512,4096]{1,0:T(8,128)(2,1)S(1)} %get-tuple-element.34.turned_ref, bf16[4096,512]{1,0:T(8,128)(2,1)} %collective-permute-done.7.y_ref, ...), custom_call_target="tpu_custom_call" | custom-call | flops 2147483648 | bytes 12582912 | tf_op jit(solution)/shard_map/near_tile/pallas_call | solution.py:294
  63.7 2.0 %collective-permute-start.9 = (bf16[3,256,256]{2,1,0:T(8,128)(2,1)S(1)}, bf16[3,256,256]{2,1,0:T(8,128)(2,1)S(1)}, u32[]{:S(2)}, u32[]{:S(2)}) collective-permute-start(bf16[3,256,256]{2,1,0:T(8,128)(2,1)S(1)} %get-tuple-element.39), channel_id=1, source_target_pairs={{0,2},{2,0},{5,7},{7,5},{8,10},{10,8},{13,15},{15,13},{16,18},{18,... | collective-permute-start | bytes 1179656 | tf_op jit(solution)/shard_map/ppermute | solution.py:234
  65.7 3.0 %cross_tile.1 = (f32[3,256,256]{2,1,0:T(8,128)S(1)}, bf16[3,256,256]{2,1,0:T(8,128)(2,1)S(1)}) custom-call(s32[5]{0:T(128)S(1)} %stack.23.pos_ref.refs_0_, bf16[512,4096]{1,0:T(8,128)(2,1)S(1)} %get-tuple-element.41.refs_1_, bf16[4096,512]{1,0:T(8,128)(2,1)S(1)} %get-tuple-element.42.refs_2_, f32[4,512]{1,0:T(4,128)S(1)} %collective-permute-done.8.ystat_ref.refs_3_, ...), custom_call_target="tpu_custom_call" | custom-call | flops 2147483648 | bytes 8388608 | tf_op jit(solution)/shard_map/cross_tile/pallas_call | solution.py:299
  68.7 3.8 %collective-permute-start.12 = (bf16[3,256,256]{2,1,0:T(8,128)(2,1)S(1)}, bf16[3,256,256]{2,1,0:T(8,128)(2,1)S(1)}, u32[]{:S(2)}, u32[]{:S(2)}) collective-permute-start(bf16[3,256,256]{2,1,0:T(8,128)(2,1)S(1)} %get-tuple-element.52), channel_id=1, source_target_pairs={{0,2},{2,0},{5,7},{7,5},{8,10},{10,8},{13,15},{15,13},{16,18},{18,... | collective-permute-start | bytes 1179656 | tf_op jit(solution)/shard_map/ppermute | solution.py:234
  72.5 0.7 far_strips.1
  73.2 0.1 collective-permute-done.9.got
  73.4 0.7 near_strips.1
  74.1 1.9 %collective-permute-start.11 = (f32[256,512]{1,0:T(8,128)S(1)}, f32[256,512]{1,0:T(8,128)S(1)}, u32[]{:S(2)}, u32[]{:S(2)}) collective-permute-start(f32[256,512]{1,0:T(8,128)S(1)} %get-tuple-element.50), channel_id=1, source_target_pairs={{0,5},{2,7},{5,0},{7,2},{8,13},{10,15},{13,8},{15,10},{16,21},{18,... | collective-permute-start | bytes 1572872 | tf_op jit(solution)/shard_map/ppermute | solution.py:234
  76.1 1.9 %collective-permute-start.15 = (bf16[256,512]{1,0:T(8,128)(2,1)S(1)}, bf16[256,512]{1,0:T(8,128)(2,1)S(1)}, u32[]{:S(2)}, u32[]{:S(2)}) collective-permute-start(bf16[256,512]{1,0:T(8,128)(2,1)S(1)} %get-tuple-element.46), channel_id=1, source_target_pairs={{0,9},{2,11},{4,13},{6,15},{8,17},{9,0},{10,19},{11,2},{12,21},{13... | collective-permute-start | bytes 786440 | tf_op jit(solution)/shard_map/ppermute | solution.py:234
  78.0 0.4 collective-permute-done.12.got
  78.4 0.7 cross_strips.1
  79.1 3.1 %collective-permute-start.14 = (bf16[256,512]{1,0:T(8,128)(2,1)S(1)}, bf16[256,512]{1,0:T(8,128)(2,1)S(1)}, u32[]{:S(2)}, u32[]{:S(2)}) collective-permute-start(bf16[256,512]{1,0:T(8,128)(2,1)S(1)} %get-tuple-element.55), channel_id=1, source_target_pairs={{0,9},{2,11},{8,17},{10,19},{13,4},{15,6},{16,25},{18,27},{21,12},... | collective-permute-start | bytes 786440 | tf_op jit(solution)/shard_map/ppermute | solution.py:234
  82.2 1.9 %collective-permute-start.13 = (bf16[256,512]{1,0:T(8,128)(2,1)S(1)}, bf16[256,512]{1,0:T(8,128)(2,1)S(1)}, u32[]{:S(2)}, u32[]{:S(2)}) collective-permute-start(bf16[256,512]{1,0:T(8,128)(2,1)S(1)} %get-tuple-element.54), channel_id=1, source_target_pairs={{0,5},{2,7},{5,0},{7,2},{8,13},{10,15},{13,8},{15,10},{16,21},{18,... | collective-permute-start | bytes 786440 | tf_op jit(solution)/shard_map/ppermute | solution.py:234
  84.1 0.0 collective-permute-done.15.from_z_c
  84.2 1.9 %collective-permute-done.14.from_z_d = bf16[256,512]{1,0:T(8,128)(2,1)S(1)} collective-permute-done((bf16[256,512]{1,0:T(8,128)(2,1)S(1)}, bf16[256,512]{1,0:T(8,128)(2,1)S(1)}, u32[]{:S(2)}, u32[]{:S(2)}) %collective-permute-start.14) | collective-permute-done | bytes 262176 | tf_op jit(solution)/shard_map/ppermute | solution.py:234
  86.1 0.0 collective-permute-done.11.from_y_b
  86.1 3.8 %collective-permute-done.13.from_y_d = bf16[256,512]{1,0:T(8,128)(2,1)S(1)} collective-permute-done((bf16[256,512]{1,0:T(8,128)(2,1)S(1)}, bf16[256,512]{1,0:T(8,128)(2,1)S(1)}, u32[]{:S(2)}, u32[]{:S(2)}) %collective-permute-start.13) | collective-permute-done | bytes 262176 | tf_op jit(solution)/shard_map/ppermute | solution.py:234
  89.9 0.7 combine.1
  90.6 0.1 collective-permute-start.16
  90.7 2.3 %collective-permute-done.16.sib = f32[3,128,512]{2,1,0:T(8,128)S(1)} collective-permute-done((f32[3,128,512]{2,1,0:T(8,128)S(1)}, f32[3,128,512]{2,1,0:T(8,128)S(1)}, u32[]{:S(2)}, u32[]{:S(2)}) %collective-permute-start.16) | collective-permute-done | bytes 786464 | tf_op jit(solution)/shard_map/ppermute | solution.py:234
  93.0 1.7 %finish.1 = (bf16[1,3,128,512]{3,2,1,0:T(8,128)(2,1)}, bf16[1,2,128,512]{3,2,1,0:T(8,128)(2,1)}) custom-call(s32[5]{0:T(128)S(1)} %stack.23.pos_ref.refs_0_, s32[1,3]{1,0:T(1,128)S(1)} %copy-done.2, f32[128,512]{1,0:T(8,128)S(1)} %get-tuple-element.33.diag_mine, f32[128,512]{1,0:T(8,128)S(1)} %collective-permute-done.6.diag_got, ...), custom_call_target="tpu_custom_call" | custom-call | tf_op jit(solution)/shard_map/finish/pallas_call | solution.py:323
  (5 shorter events, 0.0 us)
Async XLA Ops:
  0.6 51.8 %collective-permute-start.4 = (bf16[4096,512]{1,0:T(8,128)(2,1)}, bf16[4096,512]{1,0:T(8,128)(2,1)}, u32[]{:S(2)}, u32[]{:S(2)}) collective-permute-start(bf16[4096,512]{1,0:T(8,128)(2,1)} %x_ref.1), channel_id=1, source_target_pairs={{1,9},{3,11},{5,13},{7,15},{8,0},{9,17},{10,2},{11,19},{12,4},{13,... | collective-permute-start | bytes 12582920 | tf_op jit(solution)/shard_map/ppermute | solution.py:234
  1.9 57.1 %collective-permute-start.7 = (bf16[4096,512]{1,0:T(8,128)(2,1)}, bf16[4096,512]{1,0:T(8,128)(2,1)}, u32[]{:S(2)}, u32[]{:S(2)}) collective-permute-start(bf16[4096,512]{1,0:T(8,128)(2,1)} %x_ref.1), channel_id=1, source_target_pairs={{1,5},{3,7},{4,0},{6,2},{9,13},{11,15},{12,8},{14,10},{17,21},{19,... | collective-permute-start | bytes 12582920 | tf_op jit(solution)/shard_map/ppermute | solution.py:234
  3.2 2.2 %copy-start = (bf16[4096,512]{1,0:T(8,128)(2,1)S(1)}, bf16[4096,512]{1,0:T(8,128)(2,1)}, u32[]{:S(2)}) copy-start(bf16[4096,512]{1,0:T(8,128)(2,1)} %x_ref.1) | copy-start | bytes 12582916
  5.4 15.7 %copy-start.2 = (s32[1,3]{1,0:T(1,128)S(1)}, s32[1,3]{1,0:T(1,128)}, u32[]{:S(2)}) copy-start(s32[1,3]{1,0:T(1,128)} %offsets_ref.3) | copy-start | bytes 40
  7.3 11.5 %collective-permute-start.2 = (f32[2,512]{1,0:T(2,128)S(1)}, f32[2,512]{1,0:T(2,128)S(1)}, u32[]{:S(2)}, u32[]{:S(2)}) collective-permute-start(f32[2,512]{1,0:T(2,128)S(1)} %local_stats.1.own_ref), channel_id=1, source_target_pairs={{0,3},{1,2},{2,1},{3,0},{4,7},{5,6},{6,5},{7,4},{8,11},{9,10},{10,... | collective-permute-start | bytes 12296 | tf_op jit(solution)/shard_map/ppermute | solution.py:234
  17.5 3.6 %collective-permute-start.1 = (f32[2,512]{1,0:T(2,128)S(1)}, f32[2,512]{1,0:T(2,128)S(1)}, u32[]{:S(2)}, u32[]{:S(2)}) collective-permute-start(f32[2,512]{1,0:T(2,128)S(1)} %local_stats.1.own_ref), channel_id=1, source_target_pairs={{0,2},{1,3},{2,0},{3,1},{4,6},{5,7},{6,4},{7,5},{8,10},{9,11},{10,... | collective-permute-start | bytes 12296 | tf_op jit(solution)/shard_map/ppermute | solution.py:234
  18.0 3.1 %collective-permute-start = (f32[2,512]{1,0:T(2,128)S(1)}, f32[2,512]{1,0:T(2,128)S(1)}, u32[]{:S(2)}, u32[]{:S(2)}) collective-permute-start(f32[2,512]{1,0:T(2,128)S(1)} %local_stats.1.own_ref), channel_id=1, source_target_pairs={{0,1},{1,0},{2,3},{3,2},{4,5},{5,4},{6,7},{7,6},{8,9},{9,8},{10,11... | collective-permute-start | bytes 12296 | tf_op jit(solution)/shard_map/ppermute | solution.py:234
  21.7 2.2 %copy-start.1 = (bf16[4096,512]{1,0:T(8,128)(2,1)S(1)}, bf16[4096,512]{1,0:T(8,128)(2,1)}, u32[]{:S(2)}) copy-start(bf16[4096,512]{1,0:T(8,128)(2,1)} %x_ref.1) | copy-start | bytes 12582916
  28.2 2.0 %collective-permute-start.3 = (f32[2,128,512]{2,1,0:T(8,128)S(1)}, f32[2,128,512]{2,1,0:T(8,128)S(1)}, u32[]{:S(2)}, u32[]{:S(2)}) collective-permute-start(f32[2,128,512]{2,1,0:T(8,128)S(1)} %get-tuple-element.32), channel_id=1, source_target_pairs={{0,1},{1,0},{2,3},{3,2},{4,5},{5,4},{6,7},{7,6},{8,9},{9,8},{10,11... | collective-permute-start | bytes 1572872 | tf_op jit(solution)/shard_map/ppermute | solution.py:234
  30.8 26.3 %collective-permute-start.6 = (f32[128,512]{1,0:T(8,128)S(1)}, f32[128,512]{1,0:T(8,128)S(1)}, u32[]{:S(2)}, u32[]{:S(2)}) collective-permute-start(f32[128,512]{1,0:T(8,128)S(1)} %get-tuple-element.36), channel_id=1, source_target_pairs={{0,2},{1,3},{2,0},{3,1},{4,6},{5,7},{6,4},{7,5},{8,10},{9,11},{10,... | collective-permute-start | bytes 786440 | tf_op jit(solution)/shard_map/ppermute | solution.py:234
  31.3 5.1 %collective-permute-start.5 = (f32[4,512]{1,0:T(4,128)S(1)}, f32[4,512]{1,0:T(4,128)S(1)}, u32[]{:S(2)}, u32[]{:S(2)}) collective-permute-start(f32[4,512]{1,0:T(4,128)S(1)} %stats.1.stat_ref), channel_id=1, source_target_pairs={{0,9},{2,11},{4,13},{6,15},{8,17},{9,0},{10,19},{11,2},{12,21},{13... | collective-permute-start | bytes 24584 | tf_op jit(solution)/shard_map/ppermute | solution.py:234
  33.3 25.8 %collective-permute-start.8 = (f32[4,512]{1,0:T(4,128)S(1)}, f32[4,512]{1,0:T(4,128)S(1)}, u32[]{:S(2)}, u32[]{:S(2)}) collective-permute-start(f32[4,512]{1,0:T(4,128)S(1)} %stats.1.stat_ref), channel_id=1, source_target_pairs={{0,5},{2,7},{5,0},{7,2},{8,13},{10,15},{13,8},{15,10},{16,21},{18,... | collective-permute-start | bytes 24584 | tf_op jit(solution)/shard_map/ppermute | solution.py:234
  57.1 11.6 %collective-permute-start.10 = (bf16[3,256,256]{2,1,0:T(8,128)(2,1)S(1)}, bf16[3,256,256]{2,1,0:T(8,128)(2,1)S(1)}, u32[]{:S(2)}, u32[]{:S(2)}) collective-permute-start(bf16[3,256,256]{2,1,0:T(8,128)(2,1)S(1)} %get-tuple-element.44), channel_id=1, source_target_pairs={{0,2},{1,3},{2,0},{3,1},{4,6},{5,7},{6,4},{7,5},{8,10},{9,11},{10,... | collective-permute-start | bytes 1179656 | tf_op jit(solution)/shard_map/ppermute | solution.py:234
  63.7 9.7 %collective-permute-start.9 = (bf16[3,256,256]{2,1,0:T(8,128)(2,1)S(1)}, bf16[3,256,256]{2,1,0:T(8,128)(2,1)S(1)}, u32[]{:S(2)}, u32[]{:S(2)}) collective-permute-start(bf16[3,256,256]{2,1,0:T(8,128)(2,1)S(1)} %get-tuple-element.39), channel_id=1, source_target_pairs={{0,2},{2,0},{5,7},{7,5},{8,10},{10,8},{13,15},{15,13},{16,18},{18,... | collective-permute-start | bytes 1179656 | tf_op jit(solution)/shard_map/ppermute | solution.py:234
  68.7 9.7 %collective-permute-start.12 = (bf16[3,256,256]{2,1,0:T(8,128)(2,1)S(1)}, bf16[3,256,256]{2,1,0:T(8,128)(2,1)S(1)}, u32[]{:S(2)}, u32[]{:S(2)}) collective-permute-start(bf16[3,256,256]{2,1,0:T(8,128)(2,1)S(1)} %get-tuple-element.52), channel_id=1, source_target_pairs={{0,2},{2,0},{5,7},{7,5},{8,10},{10,8},{13,15},{15,13},{16,18},{18,... | collective-permute-start | bytes 1179656 | tf_op jit(solution)/shard_map/ppermute | solution.py:234
  74.1 11.9 %collective-permute-start.11 = (f32[256,512]{1,0:T(8,128)S(1)}, f32[256,512]{1,0:T(8,128)S(1)}, u32[]{:S(2)}, u32[]{:S(2)}) collective-permute-start(f32[256,512]{1,0:T(8,128)S(1)} %get-tuple-element.50), channel_id=1, source_target_pairs={{0,5},{2,7},{5,0},{7,2},{8,13},{10,15},{13,8},{15,10},{16,21},{18,... | collective-permute-start | bytes 1572872 | tf_op jit(solution)/shard_map/ppermute | solution.py:234
  76.1 8.1 %collective-permute-start.15 = (bf16[256,512]{1,0:T(8,128)(2,1)S(1)}, bf16[256,512]{1,0:T(8,128)(2,1)S(1)}, u32[]{:S(2)}, u32[]{:S(2)}) collective-permute-start(bf16[256,512]{1,0:T(8,128)(2,1)S(1)} %get-tuple-element.46), channel_id=1, source_target_pairs={{0,9},{2,11},{4,13},{6,15},{8,17},{9,0},{10,19},{11,2},{12,21},{13... | collective-permute-start | bytes 786440 | tf_op jit(solution)/shard_map/ppermute | solution.py:234
  79.1 7.0 %collective-permute-start.14 = (bf16[256,512]{1,0:T(8,128)(2,1)S(1)}, bf16[256,512]{1,0:T(8,128)(2,1)S(1)}, u32[]{:S(2)}, u32[]{:S(2)}) collective-permute-start(bf16[256,512]{1,0:T(8,128)(2,1)S(1)} %get-tuple-element.55), channel_id=1, source_target_pairs={{0,9},{2,11},{8,17},{10,19},{13,4},{15,6},{16,25},{18,27},{21,12},... | collective-permute-start | bytes 786440 | tf_op jit(solution)/shard_map/ppermute | solution.py:234
  82.2 7.7 %collective-permute-start.13 = (bf16[256,512]{1,0:T(8,128)(2,1)S(1)}, bf16[256,512]{1,0:T(8,128)(2,1)S(1)}, u32[]{:S(2)}, u32[]{:S(2)}) collective-permute-start(bf16[256,512]{1,0:T(8,128)(2,1)S(1)} %get-tuple-element.54), channel_id=1, source_target_pairs={{0,5},{2,7},{5,0},{7,2},{8,13},{10,15},{13,8},{15,10},{16,21},{18,... | collective-permute-start | bytes 786440 | tf_op jit(solution)/shard_map/ppermute | solution.py:234
  90.6 2.4 %collective-permute-start.16 = (f32[3,128,512]{2,1,0:T(8,128)S(1)}, f32[3,128,512]{2,1,0:T(8,128)S(1)}, u32[]{:S(2)}, u32[]{:S(2)}) collective-permute-start(f32[3,128,512]{2,1,0:T(8,128)S(1)} %get-tuple-element.59), channel_id=1, source_target_pairs={{0,1},{1,0},{2,3},{3,2},{4,5},{5,4},{6,7},{7,6},{8,9},{9,8},{10,11... | collective-permute-start | bytes 2359304 | tf_op jit(solution)/shard_map/ppermute | solution.py:234

commit v17 on v15

--- a/solution.py
+++ b/solution.py
@@ -281,7 +281,7 @@
     diag_got = send(diag_other, across)
 
     anywhere = pl.BlockSpec(memory_space=pl.ANY)
-    parts = [pltpu.VMEM((steps, step_rows, width), BF16), pltpu.SemaphoreType.DMA((steps,))]
+    parts = [pltpu.VMEM((2 * steps, step_rows // 2, width), BF16), pltpu.SemaphoreType.DMA((2 * steps,))]
     sums = pltpu.VMEM((width, width), F32)
     pair = [shape(3, half, half), shape(3, half, half, dtype=HALVES)]
     keep_c, send_c, w = call(

time: 92.7 us -> 93.1 us (level)
  no operation moved by 1% of the time
where the time goes in v17:
time: 93.1 us; the launch traced here: 92.6 us
  starting transfers between devices  33.3 us (36%)
  waiting for transfers between devices  28.8 us (31%)
  Pallas kernels  24.5 us (26%)
  local copies, waits for them, and re-layouts  4.46 us (5%)
  between operations  1.49 us (2%)
    ppermute x17, starting transfers between devices, send(): return lax.ppermute(value, AXES, pairs)  33.3 us
    ppermute x17, waiting for transfers between devices, send(): return lax.ppermute(value, AXES, pairs)  28.8 us
    pallas_call x1, Pallas kernels, body(): call(near_kernel, 'near_tile', (), [SMEM, VMEM, anywhere, VMEM, VMEM], [V...  4.82 us
    pallas_call x1, Pallas kernels, body(): call(far_kernel, 'far_tile', (), [SMEM, VMEM, anywhere, VMEM, VMEM], [VME...  4.82 us
    unnamed x6, local copies, waits for them, and re-layouts  4.37 us
    pallas_call x1, Pallas kernels, body(): call(own_kernel, 'own_tile', (steps,), [SMEM, wide, whole(4, width)], [fl...  4.31 us
    pallas_call x1, Pallas kernels, body(): call(lambda *refs: cross_kernel(steps, *refs), 'cross_tile', (), [SMEM] +...  2.96 us
    pallas_call x1, Pallas kernels, body(): call(lambda *refs: local_kernel(steps, *refs), 'local_stats', (steps,), [...  1.87 us
  transfers between devices with their start and end apart: 17, of which 10 were waited for; matrix products, arithmetic and copies ran while one was open for 0% of the time, Pallas kernels for 24%

profile of v17, /device:TPU:0, one launch (start us, length us, event | category | flops | bytes accessed | tf_op | source)
XLA Modules:
  0.0 92.6 jit_solution(3306529938213575093)
XLA Ops:
  0.6 1.3 %collective-permute-start.4 = (bf16[4096,512]{1,0:T(8,128)(2,1)}, bf16[4096,512]{1,0:T(8,128)(2,1)}, u32[]{:S(2)}, u32[]{:S(2)}) collective-permute-start(bf16[4096,512]{1,0:T(8,128)(2,1)} %x_ref.1), channel_id=1, source_target_pairs={{1,9},{3,11},{5,13},{7,15},{8,0},{9,17},{10,2},{11,19},{12,4},{13,... | collective-permute-start | bytes 12582920 | tf_op jit(solution)/shard_map/ppermute | solution.py:234
  1.9 1.3 %collective-permute-start.7 = (bf16[4096,512]{1,0:T(8,128)(2,1)}, bf16[4096,512]{1,0:T(8,128)(2,1)}, u32[]{:S(2)}, u32[]{:S(2)}) collective-permute-start(bf16[4096,512]{1,0:T(8,128)(2,1)} %x_ref.1), channel_id=1, source_target_pairs={{1,5},{3,7},{4,0},{6,2},{9,13},{11,15},{12,8},{14,10},{17,21},{19,... | collective-permute-start | bytes 12582920 | tf_op jit(solution)/shard_map/ppermute | solution.py:234
  3.2 0.0 copy-start
  3.2 2.2 %copy-done = bf16[4096,512]{1,0:T(8,128)(2,1)S(1)} copy-done((bf16[4096,512]{1,0:T(8,128)(2,1)S(1)}, bf16[4096,512]{1,0:T(8,128)(2,1)}, u32[]{:S(2)}) %copy-start) | copy-done | bytes 4194328
  5.4 1.9 %local_stats.1.own_ref = f32[2,512]{1,0:T(2,128)S(1)} custom-call(bf16[4096,512]{1,0:T(8,128)(2,1)S(1)} %copy-done), custom_call_target="tpu_custom_call" | custom-call | flops 10485760 | bytes 4194304 | tf_op jit(solution)/shard_map/local_stats/pallas_call | solution.py:267
  7.3 10.2 %collective-permute-start.2 = (f32[2,512]{1,0:T(2,128)S(1)}, f32[2,512]{1,0:T(2,128)S(1)}, u32[]{:S(2)}, u32[]{:S(2)}) collective-permute-start(f32[2,512]{1,0:T(2,128)S(1)} %local_stats.1.own_ref), channel_id=1, source_target_pairs={{0,3},{1,2},{2,1},{3,0},{4,7},{5,6},{6,5},{7,4},{8,11},{9,10},{10,... | collective-permute-start | bytes 12296 | tf_op jit(solution)/shard_map/ppermute | solution.py:234
  17.5 0.5 collective-permute-start.1
  18.0 0.0 collective-permute-start
  18.7 0.1 stack.23.pos_ref.refs_0_
  18.7 0.0 collective-permute-done.2.cross_ref
  18.8 2.3 %collective-permute-done.1.far_ref = f32[2,512]{1,0:T(2,128)S(1)} collective-permute-done((f32[2,512]{1,0:T(2,128)S(1)}, f32[2,512]{1,0:T(2,128)S(1)}, u32[]{:S(2)}, u32[]{:S(2)}) %collective-permute-start.1) | collective-permute-done | bytes 4128 | tf_op jit(solution)/shard_map/ppermute | solution.py:234
  21.1 0.0 collective-permute-done.sib_ref
  21.1 0.6 stats.1.stat_ref
  21.7 0.0 copy-start.1
  21.7 2.2 %copy-done.1 = bf16[4096,512]{1,0:T(8,128)(2,1)S(1)} copy-done((bf16[4096,512]{1,0:T(8,128)(2,1)S(1)}, bf16[4096,512]{1,0:T(8,128)(2,1)}, u32[]{:S(2)}) %copy-start.1) | copy-done | bytes 4194328
  23.8 4.3 %own_tile.1 = (bf16[512,4096]{1,0:T(8,128)(2,1)S(1)}, f32[2,128,512]{2,1,0:T(8,128)S(1)}, f32[2,128,512]{2,1,0:T(8,128)S(1)}) custom-call(s32[5]{0:T(128)S(1)} %stack.23.pos_ref.refs_0_, bf16[4096,512]{1,0:T(8,128)(2,1)S(1)} %copy-done.1, f32[4,512]{1,0:T(4,128)S(1)} %stats.1.stat_ref), custom_call_target="tpu_custom_call" | custom-call | flops 2147483648 | bytes 8388608 | tf_op jit(solution)/shard_map/own_tile/pallas_call | solution.py:274
  28.2 0.1 collective-permute-start.3
  28.2 1.9 %collective-permute-done.3.got_ref = f32[2,128,512]{2,1,0:T(8,128)S(1)} collective-permute-done((f32[2,128,512]{2,1,0:T(8,128)S(1)}, f32[2,128,512]{2,1,0:T(8,128)S(1)}, u32[]{:S(2)}, u32[]{:S(2)}) %collective-permute-start.3) | collective-permute-done | bytes 524320 | tf_op jit(solution)/shard_map/ppermute | solution.py:234
  30.1 0.6 own_tile_strips.1
  30.8 0.6 collective-permute-start.6
  31.3 1.9 %collective-permute-start.5 = (f32[4,512]{1,0:T(4,128)S(1)}, f32[4,512]{1,0:T(4,128)S(1)}, u32[]{:S(2)}, u32[]{:S(2)}) collective-permute-start(f32[4,512]{1,0:T(4,128)S(1)} %stats.1.stat_ref), channel_id=1, source_target_pairs={{0,9},{2,11},{4,13},{6,15},{8,17},{9,0},{10,19},{11,2},{12,21},{13... | collective-permute-start | bytes 24584 | tf_op jit(solution)/shard_map/ppermute | solution.py:234
  33.3 1.9 %collective-permute-start.8 = (f32[4,512]{1,0:T(4,128)S(1)}, f32[4,512]{1,0:T(4,128)S(1)}, u32[]{:S(2)}, u32[]{:S(2)}) collective-permute-start(f32[4,512]{1,0:T(4,128)S(1)} %stats.1.stat_ref), channel_id=1, source_target_pairs={{0,5},{2,7},{5,0},{7,2},{8,13},{10,15},{13,8},{15,10},{16,21},{18,... | collective-permute-start | bytes 24584 | tf_op jit(solution)/shard_map/ppermute | solution.py:234
  35.2 1.3 %collective-permute-done.5.wstat_ref.refs_4_ = f32[4,512]{1,0:T(4,128)S(1)} collective-permute-done((f32[4,512]{1,0:T(4,128)S(1)}, f32[4,512]{1,0:T(4,128)S(1)}, u32[]{:S(2)}, u32[]{:S(2)}) %collective-permute-start.5) | collective-permute-done | bytes 8224 | tf_op jit(solution)/shard_map/ppermute | solution.py:234
  36.4 16.0 %collective-permute-done.4.w_ref = bf16[4096,512]{1,0:T(8,128)(2,1)} collective-permute-done((bf16[4096,512]{1,0:T(8,128)(2,1)}, bf16[4096,512]{1,0:T(8,128)(2,1)}, u32[]{:S(2)}, u32[]{:S(2)}) %collective-permute-start.4) | collective-permute-done | bytes 4194336 | tf_op jit(solution)/shard_map/ppermute | solution.py:234
  52.4 4.8 %far_tile.1 = (f32[3,256,256]{2,1,0:T(8,128)S(1)}, bf16[3,256,256]{2,1,0:T(8,128)(2,1)S(1)}, bf16[4096,512]{1,0:T(8,128)(2,1)S(1)}) custom-call(s32[5]{0:T(128)S(1)} %stack.23.pos_ref.refs_0_, bf16[512,4096]{1,0:T(8,128)(2,1)S(1)} %get-tuple-element.32.turned_ref, bf16[4096,512]{1,0:T(8,128)(2,1)} %collective-permute-done.4.w_ref, ...), custom_call_target="tpu_custom_call" | custom-call | flops 2147483648 | bytes 12582912 | tf_op jit(solution)/shard_map/far_tile/pallas_call | solution.py:287
  57.3 0.0 collective-permute-done.6.diag_got
  57.3 2.0 %collective-permute-start.10 = (bf16[3,256,256]{2,1,0:T(8,128)(2,1)S(1)}, bf16[3,256,256]{2,1,0:T(8,128)(2,1)S(1)}, u32[]{:S(2)}, u32[]{:S(2)}) collective-permute-start(bf16[3,256,256]{2,1,0:T(8,128)(2,1)S(1)} %get-tuple-element.42), channel_id=1, source_target_pairs={{0,2},{1,3},{2,0},{3,1},{4,6},{5,7},{6,4},{7,5},{8,10},{9,11},{10,... | collective-permute-start | bytes 1179656 | tf_op jit(solution)/shard_map/ppermute | solution.py:234
  59.3 4.8 %near_tile.1 = (f32[3,256,256]{2,1,0:T(8,128)S(1)}, bf16[3,256,256]{2,1,0:T(8,128)(2,1)S(1)}, bf16[512,4096]{1,0:T(8,128)(2,1)S(1)}) custom-call(s32[5]{0:T(128)S(1)} %stack.23.pos_ref.refs_0_, bf16[512,4096]{1,0:T(8,128)(2,1)S(1)} %get-tuple-element.32.turned_ref, bf16[4096,512]{1,0:T(8,128)(2,1)} %collective-permute-done.7.y_ref, ...), custom_call_target="tpu_custom_call" | custom-call | flops 2147483648 | bytes 12582912 | tf_op jit(solution)/shard_map/near_tile/pallas_call | solution.py:294
  64.1 2.0 %collective-permute-start.9 = (bf16[3,256,256]{2,1,0:T(8,128)(2,1)S(1)}, bf16[3,256,256]{2,1,0:T(8,128)(2,1)S(1)}, u32[]{:S(2)}, u32[]{:S(2)}) collective-permute-start(bf16[3,256,256]{2,1,0:T(8,128)(2,1)S(1)} %get-tuple-element.37), channel_id=1, source_target_pairs={{0,2},{2,0},{5,7},{7,5},{8,10},{10,8},{13,15},{15,13},{16,18},{18,... | collective-permute-start | bytes 1179656 | tf_op jit(solution)/shard_map/ppermute | solution.py:234
  66.1 3.0 %cross_tile.1 = (f32[3,256,256]{2,1,0:T(8,128)S(1)}, bf16[3,256,256]{2,1,0:T(8,128)(2,1)S(1)}) custom-call(s32[5]{0:T(128)S(1)} %stack.23.pos_ref.refs_0_, bf16[512,4096]{1,0:T(8,128)(2,1)S(1)} %get-tuple-element.39.refs_1_, bf16[4096,512]{1,0:T(8,128)(2,1)S(1)} %get-tuple-element.40.refs_2_, f32[4,512]{1,0:T(4,128)S(1)} %collective-permute-done.8.ystat_ref.refs_3_, ...), custom_call_target="tpu_custom_call" | custom-call | flops 2147483648 | bytes 8388608 | tf_op jit(solution)/shard_map/cross_tile/pallas_call | solution.py:299
  69.1 0.0 collective-permute-done.10.got
  69.1 3.8 %collective-permute-start.12 = (bf16[3,256,256]{2,1,0:T(8,128)(2,1)S(1)}, bf16[3,256,256]{2,1,0:T(8,128)(2,1)S(1)}, u32[]{:S(2)}, u32[]{:S(2)}) collective-permute-start(bf16[3,256,256]{2,1,0:T(8,128)(2,1)S(1)} %get-tuple-element.50), channel_id=1, source_target_pairs={{0,2},{2,0},{5,7},{7,5},{8,10},{10,8},{13,15},{15,13},{16,18},{18,... | collective-permute-start | bytes 1179656 | tf_op jit(solution)/shard_map/ppermute | solution.py:234
  72.9 0.7 far_strips.1
  73.7 0.1 collective-permute-done.9.got
  73.8 0.7 near_strips.1
  74.5 1.9 %collective-permute-start.11 = (f32[256,512]{1,0:T(8,128)S(1)}, f32[256,512]{1,0:T(8,128)S(1)}, u32[]{:S(2)}, u32[]{:S(2)}) collective-permute-start(f32[256,512]{1,0:T(8,128)S(1)} %get-tuple-element.48), channel_id=1, source_target_pairs={{0,5},{2,7},{5,0},{7,2},{8,13},{10,15},{13,8},{15,10},{16,21},{18,... | collective-permute-start | bytes 1572872 | tf_op jit(solution)/shard_map/ppermute | solution.py:234
  76.5 1.9 %collective-permute-start.14 = (bf16[256,512]{1,0:T(8,128)(2,1)S(1)}, bf16[256,512]{1,0:T(8,128)(2,1)S(1)}, u32[]{:S(2)}, u32[]{:S(2)}) collective-permute-start(bf16[256,512]{1,0:T(8,128)(2,1)S(1)} %get-tuple-element.44), channel_id=1, source_target_pairs={{0,9},{2,11},{4,13},{6,15},{8,17},{9,0},{10,19},{11,2},{12,21},{13... | collective-permute-start | bytes 786440 | tf_op jit(solution)/shard_map/ppermute | solution.py:234
  78.4 0.4 collective-permute-done.12.got
  78.8 0.7 cross_strips.1
  79.5 2.0 %collective-permute-start.13 = (bf16[256,512]{1,0:T(8,128)(2,1)S(1)}, bf16[256,512]{1,0:T(8,128)(2,1)S(1)}, u32[]{:S(2)}, u32[]{:S(2)}) collective-permute-start(bf16[256,512]{1,0:T(8,128)(2,1)S(1)} %get-tuple-element.52), channel_id=1, source_target_pairs={{0,5},{2,7},{5,0},{7,2},{8,13},{10,15},{13,8},{15,10},{16,21},{18,... | collective-permute-start | bytes 786440 | tf_op jit(solution)/shard_map/ppermute | solution.py:234
  81.5 1.8 %collective-permute-start.15 = (bf16[256,512]{1,0:T(8,128)(2,1)S(1)}, bf16[256,512]{1,0:T(8,128)(2,1)S(1)}, u32[]{:S(2)}, u32[]{:S(2)}) collective-permute-start(bf16[256,512]{1,0:T(8,128)(2,1)S(1)} %get-tuple-element.53), channel_id=1, source_target_pairs={{0,9},{2,11},{8,17},{10,19},{13,4},{15,6},{16,25},{18,27},{21,12},... | collective-permute-start | bytes 786440 | tf_op jit(solution)/shard_map/ppermute | solution.py:234
  83.3 0.8 collective-permute-done.14.from_z_c
  84.2 0.9 collective-permute-done.11.from_y_b
  85.0 2.8 %collective-permute-done.13.from_y_d = bf16[256,512]{1,0:T(8,128)(2,1)S(1)} collective-permute-done((bf16[256,512]{1,0:T(8,128)(2,1)S(1)}, bf16[256,512]{1,0:T(8,128)(2,1)S(1)}, u32[]{:S(2)}, u32[]{:S(2)}) %collective-permute-start.13) | collective-permute-done | bytes 262176 | tf_op jit(solution)/shard_map/ppermute | solution.py:234
  87.9 0.7 combine.1
  88.6 0.1 collective-permute-start.16
  88.6 2.3 %collective-permute-done.16.sib = f32[3,128,512]{2,1,0:T(8,128)S(1)} collective-permute-done((f32[3,128,512]{2,1,0:T(8,128)S(1)}, f32[3,128,512]{2,1,0:T(8,128)S(1)}, u32[]{:S(2)}, u32[]{:S(2)}) %collective-permute-start.16) | collective-permute-done | bytes 786464 | tf_op jit(solution)/shard_map/ppermute | solution.py:234
  90.9 1.7 %finish.1 = (bf16[1,3,128,512]{3,2,1,0:T(8,128)(2,1)}, bf16[1,2,128,512]{3,2,1,0:T(8,128)(2,1)}) custom-call(s32[5]{0:T(128)S(1)} %stack.23.pos_ref.refs_0_, s32[1,3]{1,0:T(1,128)S(1)} %copy-done.2, f32[128,512]{1,0:T(8,128)S(1)} %get-tuple-element.31.diag_mine, f32[128,512]{1,0:T(8,128)S(1)} %collective-permute-done.6.diag_got, ...), custom_call_target="tpu_custom_call" | custom-call | tf_op jit(solution)/shard_map/finish/pallas_call | solution.py:322
  (5 shorter events, 0.0 us)
Async XLA Ops:
  0.6 51.8 %collective-permute-start.4 = (bf16[4096,512]{1,0:T(8,128)(2,1)}, bf16[4096,512]{1,0:T(8,128)(2,1)}, u32[]{:S(2)}, u32[]{:S(2)}) collective-permute-start(bf16[4096,512]{1,0:T(8,128)(2,1)} %x_ref.1), channel_id=1, source_target_pairs={{1,9},{3,11},{5,13},{7,15},{8,0},{9,17},{10,2},{11,19},{12,4},{13,... | collective-permute-start | bytes 12582920 | tf_op jit(solution)/shard_map/ppermute | solution.py:234
  1.9 57.4 %collective-permute-start.7 = (bf16[4096,512]{1,0:T(8,128)(2,1)}, bf16[4096,512]{1,0:T(8,128)(2,1)}, u32[]{:S(2)}, u32[]{:S(2)}) collective-permute-start(bf16[4096,512]{1,0:T(8,128)(2,1)} %x_ref.1), channel_id=1, source_target_pairs={{1,5},{3,7},{4,0},{6,2},{9,13},{11,15},{12,8},{14,10},{17,21},{19,... | collective-permute-start | bytes 12582920 | tf_op jit(solution)/shard_map/ppermute | solution.py:234
  3.2 2.2 %copy-start = (bf16[4096,512]{1,0:T(8,128)(2,1)S(1)}, bf16[4096,512]{1,0:T(8,128)(2,1)}, u32[]{:S(2)}) copy-start(bf16[4096,512]{1,0:T(8,128)(2,1)} %x_ref.1) | copy-start | bytes 12582916
  5.4 15.7 %copy-start.2 = (s32[1,3]{1,0:T(1,128)S(1)}, s32[1,3]{1,0:T(1,128)}, u32[]{:S(2)}) copy-start(s32[1,3]{1,0:T(1,128)} %offsets_ref.3) | copy-start | bytes 40
  7.3 11.5 %collective-permute-start.2 = (f32[2,512]{1,0:T(2,128)S(1)}, f32[2,512]{1,0:T(2,128)S(1)}, u32[]{:S(2)}, u32[]{:S(2)}) collective-permute-start(f32[2,512]{1,0:T(2,128)S(1)} %local_stats.1.own_ref), channel_id=1, source_target_pairs={{0,3},{1,2},{2,1},{3,0},{4,7},{5,6},{6,5},{7,4},{8,11},{9,10},{10,... | collective-permute-start | bytes 12296 | tf_op jit(solution)/shard_map/ppermute | solution.py:234
  17.5 3.6 %collective-permute-start.1 = (f32[2,512]{1,0:T(2,128)S(1)}, f32[2,512]{1,0:T(2,128)S(1)}, u32[]{:S(2)}, u32[]{:S(2)}) collective-permute-start(f32[2,512]{1,0:T(2,128)S(1)} %local_stats.1.own_ref), channel_id=1, source_target_pairs={{0,2},{1,3},{2,0},{3,1},{4,6},{5,7},{6,4},{7,5},{8,10},{9,11},{10,... | collective-permute-start | bytes 12296 | tf_op jit(solution)/shard_map/ppermute | solution.py:234
  18.0 3.1 %collective-permute-start = (f32[2,512]{1,0:T(2,128)S(1)}, f32[2,512]{1,0:T(2,128)S(1)}, u32[]{:S(2)}, u32[]{:S(2)}) collective-permute-start(f32[2,512]{1,0:T(2,128)S(1)} %local_stats.1.own_ref), channel_id=1, source_target_pairs={{0,1},{1,0},{2,3},{3,2},{4,5},{5,4},{6,7},{7,6},{8,9},{9,8},{10,11... | collective-permute-start | bytes 12296 | tf_op jit(solution)/shard_map/ppermute | solution.py:234
  21.7 2.2 %copy-start.1 = (bf16[4096,512]{1,0:T(8,128)(2,1)S(1)}, bf16[4096,512]{1,0:T(8,128)(2,1)}, u32[]{:S(2)}) copy-start(bf16[4096,512]{1,0:T(8,128)(2,1)} %x_ref.1) | copy-start | bytes 12582916
  28.2 2.0 %collective-permute-start.3 = (f32[2,128,512]{2,1,0:T(8,128)S(1)}, f32[2,128,512]{2,1,0:T(8,128)S(1)}, u32[]{:S(2)}, u32[]{:S(2)}) collective-permute-start(f32[2,128,512]{2,1,0:T(8,128)S(1)} %get-tuple-element.30), channel_id=1, source_target_pairs={{0,1},{1,0},{2,3},{3,2},{4,5},{5,4},{6,7},{7,6},{8,9},{9,8},{10,11... | collective-permute-start | bytes 1572872 | tf_op jit(solution)/shard_map/ppermute | solution.py:234
  30.8 26.5 %collective-permute-start.6 = (f32[128,512]{1,0:T(8,128)S(1)}, f32[128,512]{1,0:T(8,128)S(1)}, u32[]{:S(2)}, u32[]{:S(2)}) collective-permute-start(f32[128,512]{1,0:T(8,128)S(1)} %get-tuple-element.34), channel_id=1, source_target_pairs={{0,2},{1,3},{2,0},{3,1},{4,6},{5,7},{6,4},{7,5},{8,10},{9,11},{10,... | collective-permute-start | bytes 786440 | tf_op jit(solution)/shard_map/ppermute | solution.py:234
  31.3 5.1 %collective-permute-start.5 = (f32[4,512]{1,0:T(4,128)S(1)}, f32[4,512]{1,0:T(4,128)S(1)}, u32[]{:S(2)}, u32[]{:S(2)}) collective-permute-start(f32[4,512]{1,0:T(4,128)S(1)} %stats.1.stat_ref), channel_id=1, source_target_pairs={{0,9},{2,11},{4,13},{6,15},{8,17},{9,0},{10,19},{11,2},{12,21},{13... | collective-permute-start | bytes 24584 | tf_op jit(solution)/shard_map/ppermute | solution.py:234
  33.3 26.0 %collective-permute-start.8 = (f32[4,512]{1,0:T(4,128)S(1)}, f32[4,512]{1,0:T(4,128)S(1)}, u32[]{:S(2)}, u32[]{:S(2)}) collective-permute-start(f32[4,512]{1,0:T(4,128)S(1)} %stats.1.stat_ref), channel_id=1, source_target_pairs={{0,5},{2,7},{5,0},{7,2},{8,13},{10,15},{13,8},{15,10},{16,21},{18,... | collective-permute-start | bytes 24584 | tf_op jit(solution)/shard_map/ppermute | solution.py:234
  57.3 11.8 %collective-permute-start.10 = (bf16[3,256,256]{2,1,0:T(8,128)(2,1)S(1)}, bf16[3,256,256]{2,1,0:T(8,128)(2,1)S(1)}, u32[]{:S(2)}, u32[]{:S(2)}) collective-permute-start(bf16[3,256,256]{2,1,0:T(8,128)(2,1)S(1)} %get-tuple-element.42), channel_id=1, source_target_pairs={{0,2},{1,3},{2,0},{3,1},{4,6},{5,7},{6,4},{7,5},{8,10},{9,11},{10,... | collective-permute-start | bytes 1179656 | tf_op jit(solution)/shard_map/ppermute | solution.py:234
  64.1 9.7 %collective-permute-start.9 = (bf16[3,256,256]{2,1,0:T(8,128)(2,1)S(1)}, bf16[3,256,256]{2,1,0:T(8,128)(2,1)S(1)}, u32[]{:S(2)}, u32[]{:S(2)}) collective-permute-start(bf16[3,256,256]{2,1,0:T(8,128)(2,1)S(1)} %get-tuple-element.37), channel_id=1, source_target_pairs={{0,2},{2,0},{5,7},{7,5},{8,10},{10,8},{13,15},{15,13},{16,18},{18,... | collective-permute-start | bytes 1179656 | tf_op jit(solution)/shard_map/ppermute | solution.py:234
  69.1 9.7 %collective-permute-start.12 = (bf16[3,256,256]{2,1,0:T(8,128)(2,1)S(1)}, bf16[3,256,256]{2,1,0:T(8,128)(2,1)S(1)}, u32[]{:S(2)}, u32[]{:S(2)}) collective-permute-start(bf16[3,256,256]{2,1,0:T(8,128)(2,1)S(1)} %get-tuple-element.50), channel_id=1, source_target_pairs={{0,2},{2,0},{5,7},{7,5},{8,10},{10,8},{13,15},{15,13},{16,18},{18,... | collective-permute-start | bytes 1179656 | tf_op jit(solution)/shard_map/ppermute | solution.py:234
  74.5 10.5 %collective-permute-start.11 = (f32[256,512]{1,0:T(8,128)S(1)}, f32[256,512]{1,0:T(8,128)S(1)}, u32[]{:S(2)}, u32[]{:S(2)}) collective-permute-start(f32[256,512]{1,0:T(8,128)S(1)} %get-tuple-element.48), channel_id=1, source_target_pairs={{0,5},{2,7},{5,0},{7,2},{8,13},{10,15},{13,8},{15,10},{16,21},{18,... | collective-permute-start | bytes 1572872 | tf_op jit(solution)/shard_map/ppermute | solution.py:234
  76.5 7.7 %collective-permute-start.14 = (bf16[256,512]{1,0:T(8,128)(2,1)S(1)}, bf16[256,512]{1,0:T(8,128)(2,1)S(1)}, u32[]{:S(2)}, u32[]{:S(2)}) collective-permute-start(bf16[256,512]{1,0:T(8,128)(2,1)S(1)} %get-tuple-element.44), channel_id=1, source_target_pairs={{0,9},{2,11},{4,13},{6,15},{8,17},{9,0},{10,19},{11,2},{12,21},{13... | collective-permute-start | bytes 786440 | tf_op jit(solution)/shard_map/ppermute | solution.py:234
  79.5 8.4 %collective-permute-start.13 = (bf16[256,512]{1,0:T(8,128)(2,1)S(1)}, bf16[256,512]{1,0:T(8,128)(2,1)S(1)}, u32[]{:S(2)}, u32[]{:S(2)}) collective-permute-start(bf16[256,512]{1,0:T(8,128)(2,1)S(1)} %get-tuple-element.52), channel_id=1, source_target_pairs={{0,5},{2,7},{5,0},{7,2},{8,13},{10,15},{13,8},{15,10},{16,21},{18,... | collective-permute-start | bytes 786440 | tf_op jit(solution)/shard_map/ppermute | solution.py:234
  81.5 6.3 %collective-permute-start.15 = (bf16[256,512]{1,0:T(8,128)(2,1)S(1)}, bf16[256,512]{1,0:T(8,128)(2,1)S(1)}, u32[]{:S(2)}, u32[]{:S(2)}) collective-permute-start(bf16[256,512]{1,0:T(8,128)(2,1)S(1)} %get-tuple-element.53), channel_id=1, source_target_pairs={{0,9},{2,11},{8,17},{10,19},{13,4},{15,6},{16,25},{18,27},{21,12},... | collective-permute-start | bytes 786440 | tf_op jit(solution)/shard_map/ppermute | solution.py:234
  88.6 2.4 %collective-permute-start.16 = (f32[3,128,512]{2,1,0:T(8,128)S(1)}, f32[3,128,512]{2,1,0:T(8,128)S(1)}, u32[]{:S(2)}, u32[]{:S(2)}) collective-permute-start(f32[3,128,512]{2,1,0:T(8,128)S(1)} %get-tuple-element.55), channel_id=1, source_target_pairs={{0,1},{1,0},{2,3},{3,2},{4,5},{5,4},{6,7},{7,6},{8,9},{9,8},{10,11... | collective-permute-start | bytes 2359304 | tf_op jit(solution)/shard_map/ppermute | solution.py:234

commit v18 on v17

--- a/solution.py
+++ b/solution.py
@@ -281,7 +281,8 @@
     diag_got = send(diag_other, across)
 
     anywhere = pl.BlockSpec(memory_space=pl.ANY)
-    parts = [pltpu.VMEM((2 * steps, step_rows // 2, width), BF16), pltpu.SemaphoreType.DMA((2 * steps,))]
+    halves = max(steps // 2, 1)
+    parts = [pltpu.VMEM((halves, depth // halves, width), BF16), pltpu.SemaphoreType.DMA((halves,))]
     sums = pltpu.VMEM((width, width), F32)
     pair = [shape(3, half, half), shape(3, half, half, dtype=HALVES)]
     keep_c, send_c, w = call(

time: 93.1 us -> 93 us (level)
  no operation moved by 1% of the time
where the time goes in v18:
time: 93 us; the launch traced here: 92.5 us
  starting transfers between devices  33.3 us (36%)
  waiting for transfers between devices  28.8 us (31%)
  Pallas kernels  24.4 us (26%)
  local copies, waits for them, and re-layouts  4.46 us (5%)
  between operations  1.49 us (2%)
    ppermute x17, starting transfers between devices, send(): return lax.ppermute(value, AXES, pairs)  33.3 us
    ppermute x17, waiting for transfers between devices, send(): return lax.ppermute(value, AXES, pairs)  28.8 us
    pallas_call x1, Pallas kernels, body(): call(near_kernel, 'near_tile', (), [SMEM, VMEM, anywhere, VMEM, VMEM], [V...  4.83 us
    pallas_call x1, Pallas kernels, body(): call(far_kernel, 'far_tile', (), [SMEM, VMEM, anywhere, VMEM, VMEM], [VME...  4.76 us
    unnamed x6, local copies, waits for them, and re-layouts  4.37 us
    pallas_call x1, Pallas kernels, body(): call(own_kernel, 'own_tile', (steps,), [SMEM, wide, whole(4, width)], [fl...  4.31 us
    pallas_call x1, Pallas kernels, body(): call(lambda *refs: cross_kernel(steps, *refs), 'cross_tile', (), [SMEM] +...  2.96 us
    pallas_call x1, Pallas kernels, body(): call(lambda *refs: local_kernel(steps, *refs), 'local_stats', (steps,), [...  1.87 us
  transfers between devices with their start and end apart: 17, of which 10 were waited for; matrix products, arithmetic and copies ran while one was open for 0% of the time, Pallas kernels for 24%

profile of v18, /device:TPU:0, one launch (start us, length us, event | category | flops | bytes accessed | tf_op | source)
XLA Modules:
  0.0 92.5 jit_solution(3863263604211618471)
XLA Ops:
  0.6 1.3 %collective-permute-start.4 = (bf16[4096,512]{1,0:T(8,128)(2,1)}, bf16[4096,512]{1,0:T(8,128)(2,1)}, u32[]{:S(2)}, u32[]{:S(2)}) collective-permute-start(bf16[4096,512]{1,0:T(8,128)(2,1)} %x_ref.1), channel_id=1, source_target_pairs={{1,9},{3,11},{5,13},{7,15},{8,0},{9,17},{10,2},{11,19},{12,4},{13,... | collective-permute-start | bytes 12582920 | tf_op jit(solution)/shard_map/ppermute | solution.py:234
  1.9 1.3 %collective-permute-start.7 = (bf16[4096,512]{1,0:T(8,128)(2,1)}, bf16[4096,512]{1,0:T(8,128)(2,1)}, u32[]{:S(2)}, u32[]{:S(2)}) collective-permute-start(bf16[4096,512]{1,0:T(8,128)(2,1)} %x_ref.1), channel_id=1, source_target_pairs={{1,5},{3,7},{4,0},{6,2},{9,13},{11,15},{12,8},{14,10},{17,21},{19,... | collective-permute-start | bytes 12582920 | tf_op jit(solution)/shard_map/ppermute | solution.py:234
  3.2 0.0 copy-start
  3.2 2.2 %copy-done = bf16[4096,512]{1,0:T(8,128)(2,1)S(1)} copy-done((bf16[4096,512]{1,0:T(8,128)(2,1)S(1)}, bf16[4096,512]{1,0:T(8,128)(2,1)}, u32[]{:S(2)}) %copy-start) | copy-done | bytes 4194328
  5.4 1.9 %local_stats.1.own_ref = f32[2,512]{1,0:T(2,128)S(1)} custom-call(bf16[4096,512]{1,0:T(8,128)(2,1)S(1)} %copy-done), custom_call_target="tpu_custom_call" | custom-call | flops 10485760 | bytes 4194304 | tf_op jit(solution)/shard_map/local_stats/pallas_call | solution.py:267
  7.3 10.2 %collective-permute-start.2 = (f32[2,512]{1,0:T(2,128)S(1)}, f32[2,512]{1,0:T(2,128)S(1)}, u32[]{:S(2)}, u32[]{:S(2)}) collective-permute-start(f32[2,512]{1,0:T(2,128)S(1)} %local_stats.1.own_ref), channel_id=1, source_target_pairs={{0,3},{1,2},{2,1},{3,0},{4,7},{5,6},{6,5},{7,4},{8,11},{9,10},{10,... | collective-permute-start | bytes 12296 | tf_op jit(solution)/shard_map/ppermute | solution.py:234
  17.5 0.5 collective-permute-start.1
  18.0 0.0 collective-permute-start
  18.7 0.1 stack.23.pos_ref.refs_0_
  18.7 0.0 collective-permute-done.2.cross_ref
  18.8 2.3 %collective-permute-done.1.far_ref = f32[2,512]{1,0:T(2,128)S(1)} collective-permute-done((f32[2,512]{1,0:T(2,128)S(1)}, f32[2,512]{1,0:T(2,128)S(1)}, u32[]{:S(2)}, u32[]{:S(2)}) %collective-permute-start.1) | collective-permute-done | bytes 4128 | tf_op jit(solution)/shard_map/ppermute | solution.py:234
  21.1 0.0 collective-permute-done.sib_ref
  21.1 0.6 stats.1.stat_ref
  21.7 0.0 copy-start.1
  21.7 2.2 %copy-done.1 = bf16[4096,512]{1,0:T(8,128)(2,1)S(1)} copy-done((bf16[4096,512]{1,0:T(8,128)(2,1)S(1)}, bf16[4096,512]{1,0:T(8,128)(2,1)}, u32[]{:S(2)}) %copy-start.1) | copy-done | bytes 4194328
  23.8 4.3 %own_tile.1 = (bf16[512,4096]{1,0:T(8,128)(2,1)S(1)}, f32[2,128,512]{2,1,0:T(8,128)S(1)}, f32[2,128,512]{2,1,0:T(8,128)S(1)}) custom-call(s32[5]{0:T(128)S(1)} %stack.23.pos_ref.refs_0_, bf16[4096,512]{1,0:T(8,128)(2,1)S(1)} %copy-done.1, f32[4,512]{1,0:T(4,128)S(1)} %stats.1.stat_ref), custom_call_target="tpu_custom_call" | custom-call | flops 2147483648 | bytes 8388608 | tf_op jit(solution)/shard_map/own_tile/pallas_call | solution.py:274
  28.2 0.1 collective-permute-start.3
  28.2 1.9 %collective-permute-done.3.got_ref = f32[2,128,512]{2,1,0:T(8,128)S(1)} collective-permute-done((f32[2,128,512]{2,1,0:T(8,128)S(1)}, f32[2,128,512]{2,1,0:T(8,128)S(1)}, u32[]{:S(2)}, u32[]{:S(2)}) %collective-permute-start.3) | collective-permute-done | bytes 524320 | tf_op jit(solution)/shard_map/ppermute | solution.py:234
  30.1 0.6 own_tile_strips.1
  30.8 0.6 collective-permute-start.6
  31.3 1.9 %collective-permute-start.5 = (f32[4,512]{1,0:T(4,128)S(1)}, f32[4,512]{1,0:T(4,128)S(1)}, u32[]{:S(2)}, u32[]{:S(2)}) collective-permute-start(f32[4,512]{1,0:T(4,128)S(1)} %stats.1.stat_ref), channel_id=1, source_target_pairs={{0,9},{2,11},{4,13},{6,15},{8,17},{9,0},{10,19},{11,2},{12,21},{13... | collective-permute-start | bytes 24584 | tf_op jit(solution)/shard_map/ppermute | solution.py:234
  33.3 1.9 %collective-permute-start.8 = (f32[4,512]{1,0:T(4,128)S(1)}, f32[4,512]{1,0:T(4,128)S(1)}, u32[]{:S(2)}, u32[]{:S(2)}) collective-permute-start(f32[4,512]{1,0:T(4,128)S(1)} %stats.1.stat_ref), channel_id=1, source_target_pairs={{0,5},{2,7},{5,0},{7,2},{8,13},{10,15},{13,8},{15,10},{16,21},{18,... | collective-permute-start | bytes 24584 | tf_op jit(solution)/shard_map/ppermute | solution.py:234
  35.2 1.3 %collective-permute-done.5.wstat_ref.refs_4_ = f32[4,512]{1,0:T(4,128)S(1)} collective-permute-done((f32[4,512]{1,0:T(4,128)S(1)}, f32[4,512]{1,0:T(4,128)S(1)}, u32[]{:S(2)}, u32[]{:S(2)}) %collective-permute-start.5) | collective-permute-done | bytes 8224 | tf_op jit(solution)/shard_map/ppermute | solution.py:234
  36.4 16.0 %collective-permute-done.4.w_ref = bf16[4096,512]{1,0:T(8,128)(2,1)} collective-permute-done((bf16[4096,512]{1,0:T(8,128)(2,1)}, bf16[4096,512]{1,0:T(8,128)(2,1)}, u32[]{:S(2)}, u32[]{:S(2)}) %collective-permute-start.4) | collective-permute-done | bytes 4194336 | tf_op jit(solution)/shard_map/ppermute | solution.py:234
  52.4 4.8 %far_tile.1 = (f32[3,256,256]{2,1,0:T(8,128)S(1)}, bf16[3,256,256]{2,1,0:T(8,128)(2,1)S(1)}, bf16[4096,512]{1,0:T(8,128)(2,1)S(1)}) custom-call(s32[5]{0:T(128)S(1)} %stack.23.pos_ref.refs_0_, bf16[512,4096]{1,0:T(8,128)(2,1)S(1)} %get-tuple-element.32.turned_ref, bf16[4096,512]{1,0:T(8,128)(2,1)} %collective-permute-done.4.w_ref, ...), custom_call_target="tpu_custom_call" | custom-call | flops 2147483648 | bytes 12582912 | tf_op jit(solution)/shard_map/far_tile/pallas_call | solution.py:288
  57.2 0.0 collective-permute-done.6.diag_got
  57.2 2.0 %collective-permute-start.10 = (bf16[3,256,256]{2,1,0:T(8,128)(2,1)S(1)}, bf16[3,256,256]{2,1,0:T(8,128)(2,1)S(1)}, u32[]{:S(2)}, u32[]{:S(2)}) collective-permute-start(bf16[3,256,256]{2,1,0:T(8,128)(2,1)S(1)} %get-tuple-element.42), channel_id=1, source_target_pairs={{0,2},{1,3},{2,0},{3,1},{4,6},{5,7},{6,4},{7,5},{8,10},{9,11},{10,... | collective-permute-start | bytes 1179656 | tf_op jit(solution)/shard_map/ppermute | solution.py:234
  59.2 4.8 %near_tile.1 = (f32[3,256,256]{2,1,0:T(8,128)S(1)}, bf16[3,256,256]{2,1,0:T(8,128)(2,1)S(1)}, bf16[512,4096]{1,0:T(8,128)(2,1)S(1)}) custom-call(s32[5]{0:T(128)S(1)} %stack.23.pos_ref.refs_0_, bf16[512,4096]{1,0:T(8,128)(2,1)S(1)} %get-tuple-element.32.turned_ref, bf16[4096,512]{1,0:T(8,128)(2,1)} %collective-permute-done.7.y_ref, ...), custom_call_target="tpu_custom_call" | custom-call | flops 2147483648 | bytes 12582912 | tf_op jit(solution)/shard_map/near_tile/pallas_call | solution.py:295
  64.1 2.0 %collective-permute-start.9 = (bf16[3,256,256]{2,1,0:T(8,128)(2,1)S(1)}, bf16[3,256,256]{2,1,0:T(8,128)(2,1)S(1)}, u32[]{:S(2)}, u32[]{:S(2)}) collective-permute-start(bf16[3,256,256]{2,1,0:T(8,128)(2,1)S(1)} %get-tuple-element.37), channel_id=1, source_target_pairs={{0,2},{2,0},{5,7},{7,5},{8,10},{10,8},{13,15},{15,13},{16,18},{18,... | collective-permute-start | bytes 1179656 | tf_op jit(solution)/shard_map/ppermute | solution.py:234
  66.1 3.0 %cross_tile.1 = (f32[3,256,256]{2,1,0:T(8,128)S(1)}, bf16[3,256,256]{2,1,0:T(8,128)(2,1)S(1)}) custom-call(s32[5]{0:T(128)S(1)} %stack.23.pos_ref.refs_0_, bf16[512,4096]{1,0:T(8,128)(2,1)S(1)} %get-tuple-element.39.refs_1_, bf16[4096,512]{1,0:T(8,128)(2,1)S(1)} %get-tuple-element.40.refs_2_, f32[4,512]{1,0:T(4,128)S(1)} %collective-permute-done.8.ystat_ref.refs_3_, ...), custom_call_target="tpu_custom_call" | custom-call | flops 2147483648 | bytes 8388608 | tf_op jit(solution)/shard_map/cross_tile/pallas_call | solution.py:300
  69.0 3.8 %collective-permute-start.12 = (bf16[3,256,256]{2,1,0:T(8,128)(2,1)S(1)}, bf16[3,256,256]{2,1,0:T(8,128)(2,1)S(1)}, u32[]{:S(2)}, u32[]{:S(2)}) collective-permute-start(bf16[3,256,256]{2,1,0:T(8,128)(2,1)S(1)} %get-tuple-element.50), channel_id=1, source_target_pairs={{0,2},{2,0},{5,7},{7,5},{8,10},{10,8},{13,15},{15,13},{16,18},{18,... | collective-permute-start | bytes 1179656 | tf_op jit(solution)/shard_map/ppermute | solution.py:234
  72.9 0.7 far_strips.1
  73.6 0.1 collective-permute-done.9.got
  73.7 0.7 near_strips.1
  74.5 1.9 %collective-permute-start.11 = (f32[256,512]{1,0:T(8,128)S(1)}, f32[256,512]{1,0:T(8,128)S(1)}, u32[]{:S(2)}, u32[]{:S(2)}) collective-permute-start(f32[256,512]{1,0:T(8,128)S(1)} %get-tuple-element.48), channel_id=1, source_target_pairs={{0,5},{2,7},{5,0},{7,2},{8,13},{10,15},{13,8},{15,10},{16,21},{18,... | collective-permute-start | bytes 1572872 | tf_op jit(solution)/shard_map/ppermute | solution.py:234
  76.4 1.9 %collective-permute-start.14 = (bf16[256,512]{1,0:T(8,128)(2,1)S(1)}, bf16[256,512]{1,0:T(8,128)(2,1)S(1)}, u32[]{:S(2)}, u32[]{:S(2)}) collective-permute-start(bf16[256,512]{1,0:T(8,128)(2,1)S(1)} %get-tuple-element.44), channel_id=1, source_target_pairs={{0,9},{2,11},{4,13},{6,15},{8,17},{9,0},{10,19},{11,2},{12,21},{13... | collective-permute-start | bytes 786440 | tf_op jit(solution)/shard_map/ppermute | solution.py:234
  78.3 0.4 collective-permute-done.12.got
  78.7 0.7 cross_strips.1
  79.4 2.0 %collective-permute-start.13 = (bf16[256,512]{1,0:T(8,128)(2,1)S(1)}, bf16[256,512]{1,0:T(8,128)(2,1)S(1)}, u32[]{:S(2)}, u32[]{:S(2)}) collective-permute-start(bf16[256,512]{1,0:T(8,128)(2,1)S(1)} %get-tuple-element.52), channel_id=1, source_target_pairs={{0,5},{2,7},{5,0},{7,2},{8,13},{10,15},{13,8},{15,10},{16,21},{18,... | collective-permute-start | bytes 786440 | tf_op jit(solution)/shard_map/ppermute | solution.py:234
  81.5 1.8 %collective-permute-start.15 = (bf16[256,512]{1,0:T(8,128)(2,1)S(1)}, bf16[256,512]{1,0:T(8,128)(2,1)S(1)}, u32[]{:S(2)}, u32[]{:S(2)}) collective-permute-start(bf16[256,512]{1,0:T(8,128)(2,1)S(1)} %get-tuple-element.53), channel_id=1, source_target_pairs={{0,9},{2,11},{8,17},{10,19},{13,4},{15,6},{16,25},{18,27},{21,12},... | collective-permute-start | bytes 786440 | tf_op jit(solution)/shard_map/ppermute | solution.py:234
  83.3 0.8 collective-permute-done.14.from_z_c
  84.1 0.9 collective-permute-done.11.from_y_b
  85.0 2.8 %collective-permute-done.13.from_y_d = bf16[256,512]{1,0:T(8,128)(2,1)S(1)} collective-permute-done((bf16[256,512]{1,0:T(8,128)(2,1)S(1)}, bf16[256,512]{1,0:T(8,128)(2,1)S(1)}, u32[]{:S(2)}, u32[]{:S(2)}) %collective-permute-start.13) | collective-permute-done | bytes 262176 | tf_op jit(solution)/shard_map/ppermute | solution.py:234
  87.8 0.0 collective-permute-done.15.from_z_d
  87.8 0.7 combine.1
  88.5 0.1 collective-permute-start.16
  88.6 2.3 %collective-permute-done.16.sib = f32[3,128,512]{2,1,0:T(8,128)S(1)} collective-permute-done((f32[3,128,512]{2,1,0:T(8,128)S(1)}, f32[3,128,512]{2,1,0:T(8,128)S(1)}, u32[]{:S(2)}, u32[]{:S(2)}) %collective-permute-start.16) | collective-permute-done | bytes 786464 | tf_op jit(solution)/shard_map/ppermute | solution.py:234
  90.9 1.7 %finish.1 = (bf16[1,3,128,512]{3,2,1,0:T(8,128)(2,1)}, bf16[1,2,128,512]{3,2,1,0:T(8,128)(2,1)}) custom-call(s32[5]{0:T(128)S(1)} %stack.23.pos_ref.refs_0_, s32[1,3]{1,0:T(1,128)S(1)} %copy-done.2, f32[128,512]{1,0:T(8,128)S(1)} %get-tuple-element.31.diag_mine, f32[128,512]{1,0:T(8,128)S(1)} %collective-permute-done.6.diag_got, ...), custom_call_target="tpu_custom_call" | custom-call | tf_op jit(solution)/shard_map/finish/pallas_call | solution.py:323
  (5 shorter events, 0.0 us)
Async XLA Ops:
  0.6 51.8 %collective-permute-start.4 = (bf16[4096,512]{1,0:T(8,128)(2,1)}, bf16[4096,512]{1,0:T(8,128)(2,1)}, u32[]{:S(2)}, u32[]{:S(2)}) collective-permute-start(bf16[4096,512]{1,0:T(8,128)(2,1)} %x_ref.1), channel_id=1, source_target_pairs={{1,9},{3,11},{5,13},{7,15},{8,0},{9,17},{10,2},{11,19},{12,4},{13,... | collective-permute-start | bytes 12582920 | tf_op jit(solution)/shard_map/ppermute | solution.py:234
  1.9 57.3 %collective-permute-start.7 = (bf16[4096,512]{1,0:T(8,128)(2,1)}, bf16[4096,512]{1,0:T(8,128)(2,1)}, u32[]{:S(2)}, u32[]{:S(2)}) collective-permute-start(bf16[4096,512]{1,0:T(8,128)(2,1)} %x_ref.1), channel_id=1, source_target_pairs={{1,5},{3,7},{4,0},{6,2},{9,13},{11,15},{12,8},{14,10},{17,21},{19,... | collective-permute-start | bytes 12582920 | tf_op jit(solution)/shard_map/ppermute | solution.py:234
  3.2 2.2 %copy-start = (bf16[4096,512]{1,0:T(8,128)(2,1)S(1)}, bf16[4096,512]{1,0:T(8,128)(2,1)}, u32[]{:S(2)}) copy-start(bf16[4096,512]{1,0:T(8,128)(2,1)} %x_ref.1) | copy-start | bytes 12582916
  5.4 15.7 %copy-start.2 = (s32[1,3]{1,0:T(1,128)S(1)}, s32[1,3]{1,0:T(1,128)}, u32[]{:S(2)}) copy-start(s32[1,3]{1,0:T(1,128)} %offsets_ref.3) | copy-start | bytes 40
  7.3 11.5 %collective-permute-start.2 = (f32[2,512]{1,0:T(2,128)S(1)}, f32[2,512]{1,0:T(2,128)S(1)}, u32[]{:S(2)}, u32[]{:S(2)}) collective-permute-start(f32[2,512]{1,0:T(2,128)S(1)} %local_stats.1.own_ref), channel_id=1, source_target_pairs={{0,3},{1,2},{2,1},{3,0},{4,7},{5,6},{6,5},{7,4},{8,11},{9,10},{10,... | collective-permute-start | bytes 12296 | tf_op jit(solution)/shard_map/ppermute | solution.py:234
  17.5 3.6 %collective-permute-start.1 = (f32[2,512]{1,0:T(2,128)S(1)}, f32[2,512]{1,0:T(2,128)S(1)}, u32[]{:S(2)}, u32[]{:S(2)}) collective-permute-start(f32[2,512]{1,0:T(2,128)S(1)} %local_stats.1.own_ref), channel_id=1, source_target_pairs={{0,2},{1,3},{2,0},{3,1},{4,6},{5,7},{6,4},{7,5},{8,10},{9,11},{10,... | collective-permute-start | bytes 12296 | tf_op jit(solution)/shard_map/ppermute | solution.py:234
  18.0 3.1 %collective-permute-start = (f32[2,512]{1,0:T(2,128)S(1)}, f32[2,512]{1,0:T(2,128)S(1)}, u32[]{:S(2)}, u32[]{:S(2)}) collective-permute-start(f32[2,512]{1,0:T(2,128)S(1)} %local_stats.1.own_ref), channel_id=1, source_target_pairs={{0,1},{1,0},{2,3},{3,2},{4,5},{5,4},{6,7},{7,6},{8,9},{9,8},{10,11... | collective-permute-start | bytes 12296 | tf_op jit(solution)/shard_map/ppermute | solution.py:234
  21.7 2.2 %copy-start.1 = (bf16[4096,512]{1,0:T(8,128)(2,1)S(1)}, bf16[4096,512]{1,0:T(8,128)(2,1)}, u32[]{:S(2)}) copy-start(bf16[4096,512]{1,0:T(8,128)(2,1)} %x_ref.1) | copy-start | bytes 12582916
  28.2 2.0 %collective-permute-start.3 = (f32[2,128,512]{2,1,0:T(8,128)S(1)}, f32[2,128,512]{2,1,0:T(8,128)S(1)}, u32[]{:S(2)}, u32[]{:S(2)}) collective-permute-start(f32[2,128,512]{2,1,0:T(8,128)S(1)} %get-tuple-element.30), channel_id=1, source_target_pairs={{0,1},{1,0},{2,3},{3,2},{4,5},{5,4},{6,7},{7,6},{8,9},{9,8},{10,11... | collective-permute-start | bytes 1572872 | tf_op jit(solution)/shard_map/ppermute | solution.py:234
  30.8 26.5 %collective-permute-start.6 = (f32[128,512]{1,0:T(8,128)S(1)}, f32[128,512]{1,0:T(8,128)S(1)}, u32[]{:S(2)}, u32[]{:S(2)}) collective-permute-start(f32[128,512]{1,0:T(8,128)S(1)} %get-tuple-element.34), channel_id=1, source_target_pairs={{0,2},{1,3},{2,0},{3,1},{4,6},{5,7},{6,4},{7,5},{8,10},{9,11},{10,... | collective-permute-start | bytes 786440 | tf_op jit(solution)/shard_map/ppermute | solution.py:234
  31.3 5.1 %collective-permute-start.5 = (f32[4,512]{1,0:T(4,128)S(1)}, f32[4,512]{1,0:T(4,128)S(1)}, u32[]{:S(2)}, u32[]{:S(2)}) collective-permute-start(f32[4,512]{1,0:T(4,128)S(1)} %stats.1.stat_ref), channel_id=1, source_target_pairs={{0,9},{2,11},{4,13},{6,15},{8,17},{9,0},{10,19},{11,2},{12,21},{13... | collective-permute-start | bytes 24584 | tf_op jit(solution)/shard_map/ppermute | solution.py:234
  33.3 26.0 %collective-permute-start.8 = (f32[4,512]{1,0:T(4,128)S(1)}, f32[4,512]{1,0:T(4,128)S(1)}, u32[]{:S(2)}, u32[]{:S(2)}) collective-permute-start(f32[4,512]{1,0:T(4,128)S(1)} %stats.1.stat_ref), channel_id=1, source_target_pairs={{0,5},{2,7},{5,0},{7,2},{8,13},{10,15},{13,8},{15,10},{16,21},{18,... | collective-permute-start | bytes 24584 | tf_op jit(solution)/shard_map/ppermute | solution.py:234
  57.2 11.8 %collective-permute-start.10 = (bf16[3,256,256]{2,1,0:T(8,128)(2,1)S(1)}, bf16[3,256,256]{2,1,0:T(8,128)(2,1)S(1)}, u32[]{:S(2)}, u32[]{:S(2)}) collective-permute-start(bf16[3,256,256]{2,1,0:T(8,128)(2,1)S(1)} %get-tuple-element.42), channel_id=1, source_target_pairs={{0,2},{1,3},{2,0},{3,1},{4,6},{5,7},{6,4},{7,5},{8,10},{9,11},{10,... | collective-permute-start | bytes 1179656 | tf_op jit(solution)/shard_map/ppermute | solution.py:234
  64.1 9.7 %collective-permute-start.9 = (bf16[3,256,256]{2,1,0:T(8,128)(2,1)S(1)}, bf16[3,256,256]{2,1,0:T(8,128)(2,1)S(1)}, u32[]{:S(2)}, u32[]{:S(2)}) collective-permute-start(bf16[3,256,256]{2,1,0:T(8,128)(2,1)S(1)} %get-tuple-element.37), channel_id=1, source_target_pairs={{0,2},{2,0},{5,7},{7,5},{8,10},{10,8},{13,15},{15,13},{16,18},{18,... | collective-permute-start | bytes 1179656 | tf_op jit(solution)/shard_map/ppermute | solution.py:234
  69.0 9.7 %collective-permute-start.12 = (bf16[3,256,256]{2,1,0:T(8,128)(2,1)S(1)}, bf16[3,256,256]{2,1,0:T(8,128)(2,1)S(1)}, u32[]{:S(2)}, u32[]{:S(2)}) collective-permute-start(bf16[3,256,256]{2,1,0:T(8,128)(2,1)S(1)} %get-tuple-element.50), channel_id=1, source_target_pairs={{0,2},{2,0},{5,7},{7,5},{8,10},{10,8},{13,15},{15,13},{16,18},{18,... | collective-permute-start | bytes 1179656 | tf_op jit(solution)/shard_map/ppermute | solution.py:234
  74.5 10.5 %collective-permute-start.11 = (f32[256,512]{1,0:T(8,128)S(1)}, f32[256,512]{1,0:T(8,128)S(1)}, u32[]{:S(2)}, u32[]{:S(2)}) collective-permute-start(f32[256,512]{1,0:T(8,128)S(1)} %get-tuple-element.48), channel_id=1, source_target_pairs={{0,5},{2,7},{5,0},{7,2},{8,13},{10,15},{13,8},{15,10},{16,21},{18,... | collective-permute-start | bytes 1572872 | tf_op jit(solution)/shard_map/ppermute | solution.py:234
  76.4 7.7 %collective-permute-start.14 = (bf16[256,512]{1,0:T(8,128)(2,1)S(1)}, bf16[256,512]{1,0:T(8,128)(2,1)S(1)}, u32[]{:S(2)}, u32[]{:S(2)}) collective-permute-start(bf16[256,512]{1,0:T(8,128)(2,1)S(1)} %get-tuple-element.44), channel_id=1, source_target_pairs={{0,9},{2,11},{4,13},{6,15},{8,17},{9,0},{10,19},{11,2},{12,21},{13... | collective-permute-start | bytes 786440 | tf_op jit(solution)/shard_map/ppermute | solution.py:234
  79.4 8.4 %collective-permute-start.13 = (bf16[256,512]{1,0:T(8,128)(2,1)S(1)}, bf16[256,512]{1,0:T(8,128)(2,1)S(1)}, u32[]{:S(2)}, u32[]{:S(2)}) collective-permute-start(bf16[256,512]{1,0:T(8,128)(2,1)S(1)} %get-tuple-element.52), channel_id=1, source_target_pairs={{0,5},{2,7},{5,0},{7,2},{8,13},{10,15},{13,8},{15,10},{16,21},{18,... | collective-permute-start | bytes 786440 | tf_op jit(solution)/shard_map/ppermute | solution.py:234
  81.5 6.3 %collective-permute-start.15 = (bf16[256,512]{1,0:T(8,128)(2,1)S(1)}, bf16[256,512]{1,0:T(8,128)(2,1)S(1)}, u32[]{:S(2)}, u32[]{:S(2)}) collective-permute-start(bf16[256,512]{1,0:T(8,128)(2,1)S(1)} %get-tuple-element.53), channel_id=1, source_target_pairs={{0,9},{2,11},{8,17},{10,19},{13,4},{15,6},{16,25},{18,27},{21,12},... | collective-permute-start | bytes 786440 | tf_op jit(solution)/shard_map/ppermute | solution.py:234
  88.5 2.4 %collective-permute-start.16 = (f32[3,128,512]{2,1,0:T(8,128)S(1)}, f32[3,128,512]{2,1,0:T(8,128)S(1)}, u32[]{:S(2)}, u32[]{:S(2)}) collective-permute-start(f32[3,128,512]{2,1,0:T(8,128)S(1)} %get-tuple-element.55), channel_id=1, source_target_pairs={{0,1},{1,0},{2,3},{3,2},{4,5},{5,4},{6,7},{7,6},{8,9},{9,8},{10,11... | collective-permute-start | bytes 2359304 | tf_op jit(solution)/shard_map/ppermute | solution.py:234
